TPU v7x, 512 devices: a whole 4x8x8 slice. The times are simulated.
512 devices in a mesh: sweep: 16 (over x_lo, y), cx: 16 (over x_hi, z), cy: 2 (over core).
Axes of the slice: x: 4 (x_hi: 2, x_lo: 2; x = x_hi * 2 + x_lo), y: 8, z: 8, core: 2. Of those that a mesh axis runs over, the one named last changes fastest.
Arguments:
- rhs_vectors: float32 [48, 32, 4, 16, 320], P('sweep', 'cx', 'cy'), may hold values from -6 to 6
- old_iterate: float32 [48, 32, 4, 16, 320], P('sweep', 'cx', 'cy'), may hold values from -6 to 6
- diag_inverse: bfloat16 [48, 32, 4, 320, 320], P('sweep', 'cx', 'cy'), may hold values from -0.051 to 1.051
- coupling: bfloat16 [48, 32, 4, 80, 480], P('sweep', 'cx', 'cy'), may hold values from -0.09 to 1.01
- lift_table: bfloat16 [480, 320], replicated, may hold values from -1 to 1, as said below
- upstream: int32 [48, 32, 4], P('sweep', 'cx', 'cy'), may hold values from 0 to 3, as said below
Outputs:
- new_iterate: float32 [48, 32, 4, 16, 320], P('sweep', 'cx', 'cy')
- residual: float32 [48, 32, 4, 16, 320], P('sweep', 'cx', 'cy')
Inputs may be any that keep to these rules, and one draw needn't show every extreme that they name: `upstream`: for every layer and every aligned patch of 2 x 2 elements of the two cross dimensions, the values form a permutation of the positions p * 2 + q of the patch. `lift_table`: row f * 80 + t is nonzero only at the 4 element rows of trace entry t's variable whose two node indices along face f equal those of entry t.
All inputs are finite; a program needn't handle non-finite values.
Results may differ from a plain program's by a relative error of at most 0.0003.
Values sent between devices are 32-bit elements; how exact they have to be, the bound alone decides.
No kernel may reach another device: no remote copies, remote signals or barrier semaphores. Data moves between devices by JAX's collectives and lax.ppermute only.
A program may use at most 64 MiB of HBM per device.

v0:
```python
import jax
import jax.numpy as jnp
import numpy as np
from jax import lax
from jax.sharding import PartitionSpec as P

NVAR = 5
NPOINT = 4
TRACE = 80
VECS = 16
LAYERS = 3
EX = 2
EY = 2


HIGHEST = lax.Precision.HIGHEST


def passed_along(shard, axis, by):
    peers = lax.axis_size(axis)
    pairs = [(i, i + by) for i in range(peers) if 0 <= i + by < peers]
    return lax.ppermute(shard, axis, pairs)


def with_halo(cells, sides, width):
    for axis, dim in sides:
        count = lax.axis_size(axis)
        ends = count - 1
        head = lax.slice_in_dim(cells, 0, width, axis=dim)
        tail = lax.slice_in_dim(cells, cells.shape[dim] - width, cells.shape[dim], axis=dim)
        cells = jnp.concatenate(
            [
                lax.ppermute(tail, axis, [(i, (i + 1) % count) for i in range(ends)]),
                cells,
                lax.ppermute(head, axis, [((i + 1) % count, i) for i in range(ends)]),
            ],
            axis=dim,
        )
    return cells


def face_table(components, points):
    height = components * points**3
    stride = components * points**2
    edge_at = points - 1
    selector = np.zeros((height, 6 * stride), np.float32)
    for c in range(components):
        for i in range(points):
            for j in range(points):
                for k in range(points):
                    source = ((c * points + i) * points + j) * points + k
                    placed = (
                        (0, k == 0, i, j),
                        (1, k == edge_at, i, j),
                        (2, i == 0, j, k),
                        (3, i == edge_at, j, k),
                        (4, j == 0, i, k),
                        (5, j == edge_at, i, k),
                    )
                    for f, inside, a, b in placed:
                        if inside:
                            selector[source, f * stride + (c * points + a) * points + b] = 1.0
    return selector


def mixed_product(spec, values, table):
    high_part = lax.optimization_barrier(values.astype(jnp.bfloat16))
    low_part = (values - high_part.astype(jnp.float32)).astype(jnp.bfloat16)
    upper = jnp.einsum(spec, high_part, table, preferred_element_type=jnp.float32)
    return upper + jnp.einsum(spec, low_part, table, preferred_element_type=jnp.float32)


def lifted(stacked, coupling, lift_table):
    blocks = coupling.reshape(coupling.shape[:-1] + (6, TRACE))
    shaped = stacked.reshape(stacked.shape[:-1] + (6, TRACE))
    fluxes = mixed_product("...vfi,...ifo->...vfo", shaped, blocks)
    return mixed_product("...n,nr->...r", fluxes.reshape(stacked.shape), lift_table)


def neighbours(traces, up_links):
    elements = EX * EY
    inflow = traces[..., 0:TRACE].reshape(LAYERS, elements, VECS, TRACE)
    scattered = jnp.einsum("lef,levm->lfvm", up_links, inflow, precision=HIGHEST)
    arriving = passed_along(scattered[0], "sweep", -1)
    from_below = jnp.concatenate([scattered[1:], arriving[None]], 0).reshape(
        LAYERS, EX, EY, VECS, TRACE
    )
    padded = with_halo(traces[..., 2 * TRACE : 6 * TRACE], (("cx", 1), ("cy", 2)), 1)
    from_west = padded[:, 0:EX, 1 : EY + 1, :, TRACE : 2 * TRACE]
    from_east = padded[:, 2 : EX + 2, 1 : EY + 1, :, 0:TRACE]
    from_south = padded[:, 1 : EX + 1, 0:EY, :, 3 * TRACE : 4 * TRACE]
    from_north = padded[:, 1 : EX + 1, 2 : EY + 2, :, 2 * TRACE : 3 * TRACE]
    vacant = jnp.zeros_like(from_below)
    return jnp.concatenate([vacant, from_below, from_west, from_east, from_south, from_north], -1)


def propagate(incoming, sources, transfer, up_links):
    collected = []
    current = incoming
    for layer_at in range(LAYERS):
        gathered = jnp.einsum("ef,fbm->ebm", up_links[layer_at], current, precision=HIGHEST)
        collected.append(gathered)
        current = -jnp.einsum("ebi,eim->ebm", gathered, transfer[layer_at], precision=HIGHEST)
        current = current + sources[layer_at]
    return (current, collected)


def local(rhs_vectors, old_iterate, diag_inverse, coupling, lift_table, upstream):
    selector = jnp.asarray(face_table(NVAR, NPOINT), jnp.bfloat16)
    elements = EX * EY
    up_links = (
        upstream.reshape(LAYERS, elements, 1)
        == jnp.arange(elements, dtype=jnp.int32)[None, None, :]
    ).astype(jnp.float32)
    old_stack = neighbours(mixed_product("...r,rn->...n", old_iterate, selector), up_links)
    partial_rhs = rhs_vectors - lifted(old_stack, coupling, lift_table)
    out_columns = diag_inverse[..., NPOINT - 1 :: NPOINT]
    source_out = mixed_product("...vk,...km->...vm", partial_rhs, out_columns).reshape(
        LAYERS, elements, VECS, TRACE
    )
    upwind = coupling[..., 0:TRACE]
    lifted_out = jnp.einsum(
        "ik,...km->...im", lift_table[0:TRACE], out_columns, preferred_element_type=jnp.float32
    )
    transfer = mixed_product("...jm,...ij->...im", lifted_out, upwind).reshape(
        LAYERS, elements, TRACE, TRACE
    )

    def advance(step_at, arriving):
        leaving, unused = propagate(arriving, source_out, transfer, up_links)
        return passed_along(leaving, "sweep", 1)

    arriving = lax.fori_loop(
        0, lax.axis_size("sweep") - 1, advance, jnp.zeros((elements, VECS, TRACE), jnp.float32)
    )
    unused, upwind_traces = propagate(arriving, source_out, transfer, up_links)
    upwind_all = jnp.stack(upwind_traces).reshape(LAYERS, EX, EY, VECS, TRACE)
    upwind_flux = mixed_product("...vi,...io->...vo", upwind_all, upwind)
    full_rhs = partial_rhs - mixed_product("...vi,ir->...vr", upwind_flux, lift_table[0:TRACE])
    new_iterate = mixed_product("...vk,...kj->...vj", full_rhs, diag_inverse)
    new_stack = neighbours(mixed_product("...r,rn->...n", new_iterate, selector), up_links)
    residual = lifted(old_stack - new_stack, coupling, lift_table)
    return (new_iterate, residual)


def solution(mesh):
    return jax.shard_map(
        local,
        mesh=mesh,
        in_specs=(
            P("sweep", "cx", "cy", None, None),
            P("sweep", "cx", "cy", None, None),
            P("sweep", "cx", "cy", None, None),
            P("sweep", "cx", "cy", None, None),
            P(),
            P("sweep", "cx", "cy"),
        ),
        out_specs=(P("sweep", "cx", "cy", None, None), P("sweep", "cx", "cy", None, None)),
        check_vma=False,
    )
```

profile of v0, /device:TPU:7, one launch (start us, length us, event | category | flops | bytes accessed | tf_op | source)
XLA Modules:
  0.0 247.9 jit_solution(16461548197780078621)
XLA Ops:
  4.4 5.4 %collective-permute-start.1 = (f32[4,16,80]{2,0,1:T(4,128)}, f32[4,16,80]{2,0,1:T(4,128)S(1)}, u32[]{:S(2)}, u32[]{:S(2)}) collective-permute-start(f32[4,16,80]{2,0,1:T(4,128)} %slice_bitcast_fusion.1), channel_id=1, source_target_pairs={{32,0},{64,32},{96,64},{128,96},{160,128},{192,160},{224,192},{256... | collective-permute-start | bytes 61448 | tf_op jit(solution)/shard_map/ppermute | solution.py:22
  10.6 4.0 %collective-permute-start.2 = (f32[3,1,2,16,320]{4,3,2,1,0:T(8,128)}, f32[3,1,2,16,320]{4,3,2,1,0:T(8,128)S(1)}, u32[]{:S(2)}, u32[]{:S(2)}) collective-permute-start(f32[3,1,2,16,320]{4,3,2,1,0:T(8,128)} %get-tuple-element.76), channel_id=1, source_target_pairs={{0,2},{2,4},{4,6},{6,8},{8,10},{10,12},{12,14},{14,16},{16,18},{18... | collective-permute-start | bytes 368648 | tf_op jit(solution)/shard_map/ppermute | solution.py:33
  14.6 9.3 %collective-permute-start.3 = (f32[3,1,2,16,320]{4,3,2,1,0:T(8,128)}, f32[3,1,2,16,320]{4,3,2,1,0:T(8,128)}, u32[]{:S(2)}, u32[]{:S(2)}) collective-permute-start(f32[3,1,2,16,320]{4,3,2,1,0:T(8,128)} %get-tuple-element.75), channel_id=1, source_target_pairs={{2,0},{4,2},{6,4},{8,6},{10,8},{12,10},{14,12},{16,14},{18,16},{20... | collective-permute-start | bytes 368648 | tf_op jit(solution)/shard_map/ppermute | solution.py:35
  23.9 23.5 %slice.159 = bf16[3,2,2,320,80]{4,3,2,1,0:T(8,128)(2,1)S(1)} slice(bf16[3,2,2,320,320]{4,3,2,1,0:T(8,128)(2,1)} %param.11), slice={[0:3:1], [0:2:1], [0:2:1], [0:320:1], [3:320:4]} | slice | bytes 1228800
  58.0 3.2 %collective-permute-start.5 = (f32[3,4,1,16,320]{4,3,2,1,0:T(8,128)S(1)}, f32[3,4,1,16,320]{4,3,2,1,0:T(8,128)S(1)}, u32[]{:S(2)}, u32[]{:S(2)}) collective-permute-start(f32[3,4,1,16,320]{4,3,2,1,0:T(8,128)S(1)} %get-tuple-element.69), channel_id=1, source_target_pairs={{1,0},{3,2},{5,4},{7,6},{9,8},{11,10},{13,12},{15,14},{17,16},{19,... | collective-permute-start | bytes 737288 | tf_op jit(solution)/shard_map/ppermute | solution.py:35
  65.1 2.0 concatenate.89
  67.1 2.2 reshape.75
  73.6 2.1 reshape.77
  78.2 122.3 %while.10 = (s32[]{:T(128)}, f32[4,16,80]{2,1,0:T(8,128)S(1)}, f32[3,4,4]{2,1,0:T(4,128)S(1)}, f32[3,4,80,80]{3,2,1,0:T(8,128)S(1)}, f32[3,4,16,80]{3,2,1,0:T(8,128)S(1)}, /*index=5*/s32[]{:T(128)}) while((s32[]{:T(128)}, f32[4,16,80]{2,1,0:T(8,128)S(1)}, f32[3,4,4]{2,1,0:T(4,128)S(1)}, f32[3,4,80,80]{3,2,1,0:T(8,128)S(1)}, ...), condition=%wide.region_1.0_spmd, body=%wide.region_0.0_spmd.sunk | while | flops 15513602 | bytes 997485 | solution.py:133
  79.5 1.9 collective-permute-start
  81.5 5.1 %collective-permute-done = f32[4,16,80]{2,1,0:T(8,128)S(1)} collective-permute-done((f32[4,16,80]{2,1,0:T(8,128)S(1)}, f32[4,16,80]{2,1,0:T(8,128)S(1)}, u32[]{:S(2)}, u32[]{:S(2)}) %collective-permute-start) | collective-permute-done | bytes 20512 | tf_op jit(solution)/shard_map/while/body/eval_jaxpr/ppermute | solution.py:22
  88.0 1.9 collective-permute-start
  89.9 4.8 %collective-permute-done = f32[4,16,80]{2,1,0:T(8,128)S(1)} collective-permute-done((f32[4,16,80]{2,1,0:T(8,128)S(1)}, f32[4,16,80]{2,1,0:T(8,128)S(1)}, u32[]{:S(2)}, u32[]{:S(2)}) %collective-permute-start) | collective-permute-done | bytes 20512 | tf_op jit(solution)/shard_map/while/body/eval_jaxpr/ppermute | solution.py:22
  96.1 1.9 collective-permute-start
  98.0 4.8 %collective-permute-done = f32[4,16,80]{2,1,0:T(8,128)S(1)} collective-permute-done((f32[4,16,80]{2,1,0:T(8,128)S(1)}, f32[4,16,80]{2,1,0:T(8,128)S(1)}, u32[]{:S(2)}, u32[]{:S(2)}) %collective-permute-start) | collective-permute-done | bytes 20512 | tf_op jit(solution)/shard_map/while/body/eval_jaxpr/ppermute | solution.py:22
  104.2 1.9 collective-permute-start
  106.2 4.8 %collective-permute-done = f32[4,16,80]{2,1,0:T(8,128)S(1)} collective-permute-done((f32[4,16,80]{2,1,0:T(8,128)S(1)}, f32[4,16,80]{2,1,0:T(8,128)S(1)}, u32[]{:S(2)}, u32[]{:S(2)}) %collective-permute-start) | collective-permute-done | bytes 20512 | tf_op jit(solution)/shard_map/while/body/eval_jaxpr/ppermute | solution.py:22
  114.3 4.8 %collective-permute-done = f32[4,16,80]{2,1,0:T(8,128)S(1)} collective-permute-done((f32[4,16,80]{2,1,0:T(8,128)S(1)}, f32[4,16,80]{2,1,0:T(8,128)S(1)}, u32[]{:S(2)}, u32[]{:S(2)}) %collective-permute-start) | collective-permute-done | bytes 20512 | tf_op jit(solution)/shard_map/while/body/eval_jaxpr/ppermute | solution.py:22
  122.4 4.8 %collective-permute-done = f32[4,16,80]{2,1,0:T(8,128)S(1)} collective-permute-done((f32[4,16,80]{2,1,0:T(8,128)S(1)}, f32[4,16,80]{2,1,0:T(8,128)S(1)}, u32[]{:S(2)}, u32[]{:S(2)}) %collective-permute-start) | collective-permute-done | bytes 20512 | tf_op jit(solution)/shard_map/while/body/eval_jaxpr/ppermute | solution.py:22
  130.5 4.8 %collective-permute-done = f32[4,16,80]{2,1,0:T(8,128)S(1)} collective-permute-done((f32[4,16,80]{2,1,0:T(8,128)S(1)}, f32[4,16,80]{2,1,0:T(8,128)S(1)}, u32[]{:S(2)}, u32[]{:S(2)}) %collective-permute-start) | collective-permute-done | bytes 20512 | tf_op jit(solution)/shard_map/while/body/eval_jaxpr/ppermute | solution.py:22
  138.7 4.8 %collective-permute-done = f32[4,16,80]{2,1,0:T(8,128)S(1)} collective-permute-done((f32[4,16,80]{2,1,0:T(8,128)S(1)}, f32[4,16,80]{2,1,0:T(8,128)S(1)}, u32[]{:S(2)}, u32[]{:S(2)}) %collective-permute-start) | collective-permute-done | bytes 20512 | tf_op jit(solution)/shard_map/while/body/eval_jaxpr/ppermute | solution.py:22
  146.8 4.8 %collective-permute-done = f32[4,16,80]{2,1,0:T(8,128)S(1)} collective-permute-done((f32[4,16,80]{2,1,0:T(8,128)S(1)}, f32[4,16,80]{2,1,0:T(8,128)S(1)}, u32[]{:S(2)}, u32[]{:S(2)}) %collective-permute-start) | collective-permute-done | bytes 20512 | tf_op jit(solution)/shard_map/while/body/eval_jaxpr/ppermute | solution.py:22
  154.9 4.8 %collective-permute-done = f32[4,16,80]{2,1,0:T(8,128)S(1)} collective-permute-done((f32[4,16,80]{2,1,0:T(8,128)S(1)}, f32[4,16,80]{2,1,0:T(8,128)S(1)}, u32[]{:S(2)}, u32[]{:S(2)}) %collective-permute-start) | collective-permute-done | bytes 20512 | tf_op jit(solution)/shard_map/while/body/eval_jaxpr/ppermute | solution.py:22
  163.1 4.8 %collective-permute-done = f32[4,16,80]{2,1,0:T(8,128)S(1)} collective-permute-done((f32[4,16,80]{2,1,0:T(8,128)S(1)}, f32[4,16,80]{2,1,0:T(8,128)S(1)}, u32[]{:S(2)}, u32[]{:S(2)}) %collective-permute-start) | collective-permute-done | bytes 20512 | tf_op jit(solution)/shard_map/while/body/eval_jaxpr/ppermute | solution.py:22
  171.2 4.8 %collective-permute-done = f32[4,16,80]{2,1,0:T(8,128)S(1)} collective-permute-done((f32[4,16,80]{2,1,0:T(8,128)S(1)}, f32[4,16,80]{2,1,0:T(8,128)S(1)}, u32[]{:S(2)}, u32[]{:S(2)}) %collective-permute-start) | collective-permute-done | bytes 20512 | tf_op jit(solution)/shard_map/while/body/eval_jaxpr/ppermute | solution.py:22
  179.3 4.8 %collective-permute-done = f32[4,16,80]{2,1,0:T(8,128)S(1)} collective-permute-done((f32[4,16,80]{2,1,0:T(8,128)S(1)}, f32[4,16,80]{2,1,0:T(8,128)S(1)}, u32[]{:S(2)}, u32[]{:S(2)}) %collective-permute-start) | collective-permute-done | bytes 20512 | tf_op jit(solution)/shard_map/while/body/eval_jaxpr/ppermute | solution.py:22
  187.5 4.8 %collective-permute-done = f32[4,16,80]{2,1,0:T(8,128)S(1)} collective-permute-done((f32[4,16,80]{2,1,0:T(8,128)S(1)}, f32[4,16,80]{2,1,0:T(8,128)S(1)}, u32[]{:S(2)}, u32[]{:S(2)}) %collective-permute-start) | collective-permute-done | bytes 20512 | tf_op jit(solution)/shard_map/while/body/eval_jaxpr/ppermute | solution.py:22
  195.6 4.8 %collective-permute-done = f32[4,16,80]{2,1,0:T(8,128)S(1)} collective-permute-done((f32[4,16,80]{2,1,0:T(8,128)S(1)}, f32[4,16,80]{2,1,0:T(8,128)S(1)}, u32[]{:S(2)}, u32[]{:S(2)}) %collective-permute-start) | collective-permute-done | bytes 20512 | tf_op jit(solution)/shard_map/while/body/eval_jaxpr/ppermute | solution.py:22
  207.7 1.9 collective-permute-start.7
  209.6 7.0 %collective-permute-start.8 = (f32[3,1,2,16,320]{4,3,2,1,0:T(8,128)S(1)}, f32[3,1,2,16,320]{4,3,2,1,0:T(8,128)S(1)}, u32[]{:S(2)}, u32[]{:S(2)}) collective-permute-start(f32[3,1,2,16,320]{4,3,2,1,0:T(8,128)S(1)} %get-tuple-element.73), channel_id=1, source_target_pairs={{2,0},{4,2},{6,4},{8,6},{10,8},{12,10},{14,12},{16,14},{18,16},{20... | collective-permute-start | bytes 368648 | tf_op jit(solution)/shard_map/ppermute | solution.py:35
  218.8 2.5 %collective-permute-done.6 = f32[4,16,80]{2,0,1:T(4,128)S(1)} collective-permute-done((f32[4,16,80]{2,0,1:T(4,128)S(1)}, f32[4,16,80]{2,0,1:T(4,128)S(1)}, u32[]{:S(2)}, u32[]{:S(2)}) %collective-permute-start.6) | collective-permute-done | bytes 20512 | tf_op jit(solution)/shard_map/ppermute | solution.py:22
  222.7 20.3 %collective-permute-start.10 = (f32[3,4,1,16,320]{4,3,2,1,0:T(8,128)S(1)}, f32[3,4,1,16,320]{4,3,2,1,0:T(8,128)S(1)}, u32[]{:S(2)}, u32[]{:S(2)}) collective-permute-start(f32[3,4,1,16,320]{4,3,2,1,0:T(8,128)S(1)} %get-tuple-element.67), channel_id=1, source_target_pairs={{1,0},{3,2},{5,4},{7,6},{9,8},{11,10},{13,12},{15,14},{17,16},{19,... | collective-permute-start | bytes 737288 | tf_op jit(solution)/shard_map/ppermute | solution.py:35
  (233 shorter events, 82.1 us)
Async XLA Ops:
  3.3 11.3 %copy-start.11 = (f32[3,2,2,16,480]{4,3,2,1,0:T(8,128)}, f32[3,2,2,16,480]{4,3,2,1,0:T(8,128)S(1)}, u32[]{:S(2)}) copy-start(f32[3,2,2,16,480]{4,3,2,1,0:T(8,128)S(1)} %fusion.24) | copy-start | bytes 1105924
  4.4 50.6 %collective-permute-start.1 = (f32[4,16,80]{2,0,1:T(4,128)}, f32[4,16,80]{2,0,1:T(4,128)S(1)}, u32[]{:S(2)}, u32[]{:S(2)}) collective-permute-start(f32[4,16,80]{2,0,1:T(4,128)} %slice_bitcast_fusion.1), channel_id=1, source_target_pairs={{32,0},{64,32},{96,64},{128,96},{160,128},{192,160},{224,192},{256... | collective-permute-start | bytes 61448 | tf_op jit(solution)/shard_map/ppermute | solution.py:22
  10.6 45.1 %collective-permute-start.2 = (f32[3,1,2,16,320]{4,3,2,1,0:T(8,128)}, f32[3,1,2,16,320]{4,3,2,1,0:T(8,128)S(1)}, u32[]{:S(2)}, u32[]{:S(2)}) collective-permute-start(f32[3,1,2,16,320]{4,3,2,1,0:T(8,128)} %get-tuple-element.76), channel_id=1, source_target_pairs={{0,2},{2,4},{4,6},{6,8},{8,10},{10,12},{12,14},{14,16},{16,18},{18... | collective-permute-start | bytes 368648 | tf_op jit(solution)/shard_map/ppermute | solution.py:33
  14.6 34.2 %copy-start.3 = (bf16[3,2,2,80,480]{4,3,2,1,0:T(8,128)(2,1)S(1)}, bf16[3,2,2,80,480]{4,3,2,1,0:T(8,128)(2,1)}, u32[]{:S(2)}) copy-start(bf16[3,2,2,80,480]{4,3,2,1,0:T(8,128)(2,1)} %param.12) | copy-start | bytes 2764804
  14.6 41.1 %collective-permute-start.3 = (f32[3,1,2,16,320]{4,3,2,1,0:T(8,128)}, f32[3,1,2,16,320]{4,3,2,1,0:T(8,128)}, u32[]{:S(2)}, u32[]{:S(2)}) collective-permute-start(f32[3,1,2,16,320]{4,3,2,1,0:T(8,128)} %get-tuple-element.75), channel_id=1, source_target_pairs={{2,0},{4,2},{6,4},{8,6},{10,8},{12,10},{14,12},{16,14},{18,16},{20... | collective-permute-start | bytes 368648 | tf_op jit(solution)/shard_map/ppermute | solution.py:35
  49.4 3.3 %copy-start.6 = (f32[3,2,2,80,80]{4,3,2,1,0:T(8,128)}, f32[3,2,2,80,80]{4,3,2,1,0:T(8,128)S(1)}, u32[]{:S(2)}) copy-start(f32[3,2,2,80,80]{4,3,2,1,0:T(8,128)S(1)} %convolution_add_fusion.2) | copy-start | bytes 921604
  56.7 6.1 %collective-permute-start.4 = (f32[3,4,1,16,320]{4,3,2,1,0:T(8,128)S(1)}, f32[3,4,1,16,320]{4,3,2,1,0:T(8,128)S(1)}, u32[]{:S(2)}, u32[]{:S(2)}) collective-permute-start(f32[3,4,1,16,320]{4,3,2,1,0:T(8,128)S(1)} %get-tuple-element.70), channel_id=1, source_target_pairs={{0,1},{2,3},{4,5},{6,7},{8,9},{10,11},{12,13},{14,15},{16,17},{18,... | collective-permute-start | bytes 737288 | tf_op jit(solution)/shard_map/ppermute | solution.py:33
  58.0 5.5 %collective-permute-start.5 = (f32[3,4,1,16,320]{4,3,2,1,0:T(8,128)S(1)}, f32[3,4,1,16,320]{4,3,2,1,0:T(8,128)S(1)}, u32[]{:S(2)}, u32[]{:S(2)}) collective-permute-start(f32[3,4,1,16,320]{4,3,2,1,0:T(8,128)S(1)} %get-tuple-element.69), channel_id=1, source_target_pairs={{1,0},{3,2},{5,4},{7,6},{9,8},{11,10},{13,12},{15,14},{17,16},{19,... | collective-permute-start | bytes 737288 | tf_op jit(solution)/shard_map/ppermute | solution.py:35
  72.5 4.3 %copy-start.1 = (bf16[480,320]{0,1:T(8,128)(2,1)S(1)}, bf16[480,320]{0,1:T(8,128)(2,1)}, u32[]{:S(2)}) copy-start(bf16[480,320]{0,1:T(8,128)(2,1)} %param.13) | copy-start | bytes 921604
  78.2 125.4 %copy-start.4 = (bf16[3,2,2,80,480]{4,3,2,1,0:T(8,128)(2,1)S(1)}, bf16[3,2,2,80,480]{4,3,2,1,0:T(8,128)(2,1)}, u32[]{:S(2)}) copy-start(bf16[3,2,2,80,480]{4,3,2,1,0:T(8,128)(2,1)} %param.12) | copy-start | bytes 2764804
  79.5 7.1 %collective-permute-start = (f32[4,16,80]{2,1,0:T(8,128)S(1)}, f32[4,16,80]{2,1,0:T(8,128)S(1)}, u32[]{:S(2)}, u32[]{:S(2)}) collective-permute-start(f32[4,16,80]{2,1,0:T(8,128)S(1)} %fusion.153), channel_id=1, source_target_pairs={{0,32},{32,64},{64,96},{96,128},{128,160},{160,192},{192,224},{224... | collective-permute-start | bytes 61448 | tf_op jit(solution)/shard_map/while/body/eval_jaxpr/ppermute | solution.py:22
  88.0 6.8 %collective-permute-start = (f32[4,16,80]{2,1,0:T(8,128)S(1)}, f32[4,16,80]{2,1,0:T(8,128)S(1)}, u32[]{:S(2)}, u32[]{:S(2)}) collective-permute-start(f32[4,16,80]{2,1,0:T(8,128)S(1)} %fusion.153), channel_id=1, source_target_pairs={{0,32},{32,64},{64,96},{96,128},{128,160},{160,192},{192,224},{224... | collective-permute-start | bytes 61448 | tf_op jit(solution)/shard_map/while/body/eval_jaxpr/ppermute | solution.py:22
  96.1 6.8 %collective-permute-start = (f32[4,16,80]{2,1,0:T(8,128)S(1)}, f32[4,16,80]{2,1,0:T(8,128)S(1)}, u32[]{:S(2)}, u32[]{:S(2)}) collective-permute-start(f32[4,16,80]{2,1,0:T(8,128)S(1)} %fusion.153), channel_id=1, source_target_pairs={{0,32},{32,64},{64,96},{96,128},{128,160},{160,192},{192,224},{224... | collective-permute-start | bytes 61448 | tf_op jit(solution)/shard_map/while/body/eval_jaxpr/ppermute | solution.py:22
  104.2 6.8 %collective-permute-start = (f32[4,16,80]{2,1,0:T(8,128)S(1)}, f32[4,16,80]{2,1,0:T(8,128)S(1)}, u32[]{:S(2)}, u32[]{:S(2)}) collective-permute-start(f32[4,16,80]{2,1,0:T(8,128)S(1)} %fusion.153), channel_id=1, source_target_pairs={{0,32},{32,64},{64,96},{96,128},{128,160},{160,192},{192,224},{224... | collective-permute-start | bytes 61448 | tf_op jit(solution)/shard_map/while/body/eval_jaxpr/ppermute | solution.py:22
  112.4 6.8 %collective-permute-start = (f32[4,16,80]{2,1,0:T(8,128)S(1)}, f32[4,16,80]{2,1,0:T(8,128)S(1)}, u32[]{:S(2)}, u32[]{:S(2)}) collective-permute-start(f32[4,16,80]{2,1,0:T(8,128)S(1)} %fusion.153), channel_id=1, source_target_pairs={{0,32},{32,64},{64,96},{96,128},{128,160},{160,192},{192,224},{224... | collective-permute-start | bytes 61448 | tf_op jit(solution)/shard_map/while/body/eval_jaxpr/ppermute | solution.py:22
  120.5 6.8 %collective-permute-start = (f32[4,16,80]{2,1,0:T(8,128)S(1)}, f32[4,16,80]{2,1,0:T(8,128)S(1)}, u32[]{:S(2)}, u32[]{:S(2)}) collective-permute-start(f32[4,16,80]{2,1,0:T(8,128)S(1)} %fusion.153), channel_id=1, source_target_pairs={{0,32},{32,64},{64,96},{96,128},{128,160},{160,192},{192,224},{224... | collective-permute-start | bytes 61448 | tf_op jit(solution)/shard_map/while/body/eval_jaxpr/ppermute | solution.py:22
  128.6 6.8 %collective-permute-start = (f32[4,16,80]{2,1,0:T(8,128)S(1)}, f32[4,16,80]{2,1,0:T(8,128)S(1)}, u32[]{:S(2)}, u32[]{:S(2)}) collective-permute-start(f32[4,16,80]{2,1,0:T(8,128)S(1)} %fusion.153), channel_id=1, source_target_pairs={{0,32},{32,64},{64,96},{96,128},{128,160},{160,192},{192,224},{224... | collective-permute-start | bytes 61448 | tf_op jit(solution)/shard_map/while/body/eval_jaxpr/ppermute | solution.py:22
  136.7 6.8 %collective-permute-start = (f32[4,16,80]{2,1,0:T(8,128)S(1)}, f32[4,16,80]{2,1,0:T(8,128)S(1)}, u32[]{:S(2)}, u32[]{:S(2)}) collective-permute-start(f32[4,16,80]{2,1,0:T(8,128)S(1)} %fusion.153), channel_id=1, source_target_pairs={{0,32},{32,64},{64,96},{96,128},{128,160},{160,192},{192,224},{224... | collective-permute-start | bytes 61448 | tf_op jit(solution)/shard_map/while/body/eval_jaxpr/ppermute | solution.py:22
  144.9 6.8 %collective-permute-start = (f32[4,16,80]{2,1,0:T(8,128)S(1)}, f32[4,16,80]{2,1,0:T(8,128)S(1)}, u32[]{:S(2)}, u32[]{:S(2)}) collective-permute-start(f32[4,16,80]{2,1,0:T(8,128)S(1)} %fusion.153), channel_id=1, source_target_pairs={{0,32},{32,64},{64,96},{96,128},{128,160},{160,192},{192,224},{224... | collective-permute-start | bytes 61448 | tf_op jit(solution)/shard_map/while/body/eval_jaxpr/ppermute | solution.py:22
  153.0 6.8 %collective-permute-start = (f32[4,16,80]{2,1,0:T(8,128)S(1)}, f32[4,16,80]{2,1,0:T(8,128)S(1)}, u32[]{:S(2)}, u32[]{:S(2)}) collective-permute-start(f32[4,16,80]{2,1,0:T(8,128)S(1)} %fusion.153), channel_id=1, source_target_pairs={{0,32},{32,64},{64,96},{96,128},{128,160},{160,192},{192,224},{224... | collective-permute-start | bytes 61448 | tf_op jit(solution)/shard_map/while/body/eval_jaxpr/ppermute | solution.py:22
  161.1 6.8 %collective-permute-start = (f32[4,16,80]{2,1,0:T(8,128)S(1)}, f32[4,16,80]{2,1,0:T(8,128)S(1)}, u32[]{:S(2)}, u32[]{:S(2)}) collective-permute-start(f32[4,16,80]{2,1,0:T(8,128)S(1)} %fusion.153), channel_id=1, source_target_pairs={{0,32},{32,64},{64,96},{96,128},{128,160},{160,192},{192,224},{224... | collective-permute-start | bytes 61448 | tf_op jit(solution)/shard_map/while/body/eval_jaxpr/ppermute | solution.py:22
  169.3 6.8 %collective-permute-start = (f32[4,16,80]{2,1,0:T(8,128)S(1)}, f32[4,16,80]{2,1,0:T(8,128)S(1)}, u32[]{:S(2)}, u32[]{:S(2)}) collective-permute-start(f32[4,16,80]{2,1,0:T(8,128)S(1)} %fusion.153), channel_id=1, source_target_pairs={{0,32},{32,64},{64,96},{96,128},{128,160},{160,192},{192,224},{224... | collective-permute-start | bytes 61448 | tf_op jit(solution)/shard_map/while/body/eval_jaxpr/ppermute | solution.py:22
  177.4 6.8 %collective-permute-start = (f32[4,16,80]{2,1,0:T(8,128)S(1)}, f32[4,16,80]{2,1,0:T(8,128)S(1)}, u32[]{:S(2)}, u32[]{:S(2)}) collective-permute-start(f32[4,16,80]{2,1,0:T(8,128)S(1)} %fusion.153), channel_id=1, source_target_pairs={{0,32},{32,64},{64,96},{96,128},{128,160},{160,192},{192,224},{224... | collective-permute-start | bytes 61448 | tf_op jit(solution)/shard_map/while/body/eval_jaxpr/ppermute | solution.py:22
  185.5 6.8 %collective-permute-start = (f32[4,16,80]{2,1,0:T(8,128)S(1)}, f32[4,16,80]{2,1,0:T(8,128)S(1)}, u32[]{:S(2)}, u32[]{:S(2)}) collective-permute-start(f32[4,16,80]{2,1,0:T(8,128)S(1)} %fusion.153), channel_id=1, source_target_pairs={{0,32},{32,64},{64,96},{96,128},{128,160},{160,192},{192,224},{224... | collective-permute-start | bytes 61448 | tf_op jit(solution)/shard_map/while/body/eval_jaxpr/ppermute | solution.py:22
  193.7 6.8 %collective-permute-start = (f32[4,16,80]{2,1,0:T(8,128)S(1)}, f32[4,16,80]{2,1,0:T(8,128)S(1)}, u32[]{:S(2)}, u32[]{:S(2)}) collective-permute-start(f32[4,16,80]{2,1,0:T(8,128)S(1)} %fusion.153), channel_id=1, source_target_pairs={{0,32},{32,64},{64,96},{96,128},{128,160},{160,192},{192,224},{224... | collective-permute-start | bytes 61448 | tf_op jit(solution)/shard_map/while/body/eval_jaxpr/ppermute | solution.py:22
  200.4 3.8 %copy-start.10 = (f32[3,2,2,16,320]{4,3,2,1,0:T(8,128)S(1)}, f32[3,2,2,16,320]{4,3,2,1,0:T(8,128)}, u32[]{:S(2)}) copy-start(f32[3,2,2,16,320]{4,3,2,1,0:T(8,128)} %copy-done.9) | copy-start | bytes 737284
  207.7 13.6 %collective-permute-start.7 = (f32[3,1,2,16,320]{4,3,2,1,0:T(8,128)S(1)}, f32[3,1,2,16,320]{4,3,2,1,0:T(8,128)S(1)}, u32[]{:S(2)}, u32[]{:S(2)}) collective-permute-start(f32[3,1,2,16,320]{4,3,2,1,0:T(8,128)S(1)} %get-tuple-element.74), channel_id=1, source_target_pairs={{0,2},{2,4},{4,6},{6,8},{8,10},{10,12},{12,14},{14,16},{16,18},{18... | collective-permute-start | bytes 368648 | tf_op jit(solution)/shard_map/ppermute | solution.py:33
  209.6 11.7 %collective-permute-start.8 = (f32[3,1,2,16,320]{4,3,2,1,0:T(8,128)S(1)}, f32[3,1,2,16,320]{4,3,2,1,0:T(8,128)S(1)}, u32[]{:S(2)}, u32[]{:S(2)}) collective-permute-start(f32[3,1,2,16,320]{4,3,2,1,0:T(8,128)S(1)} %get-tuple-element.73), channel_id=1, source_target_pairs={{2,0},{4,2},{6,4},{8,6},{10,8},{12,10},{14,12},{16,14},{18,16},{20... | collective-permute-start | bytes 368648 | tf_op jit(solution)/shard_map/ppermute | solution.py:35
  216.6 4.7 %collective-permute-start.6 = (f32[4,16,80]{2,0,1:T(4,128)S(1)}, f32[4,16,80]{2,0,1:T(4,128)S(1)}, u32[]{:S(2)}, u32[]{:S(2)}) collective-permute-start(f32[4,16,80]{2,0,1:T(4,128)S(1)} %slice_bitcast_fusion), channel_id=1, source_target_pairs={{32,0},{64,32},{96,64},{128,96},{160,128},{192,160},{224,192},{256... | collective-permute-start | bytes 61448 | tf_op jit(solution)/shard_map/ppermute | solution.py:22
  221.4 21.7 %collective-permute-start.9 = (f32[3,4,1,16,320]{4,3,2,1,0:T(8,128)S(1)}, f32[3,4,1,16,320]{4,3,2,1,0:T(8,128)S(1)}, u32[]{:S(2)}, u32[]{:S(2)}) collective-permute-start(f32[3,4,1,16,320]{4,3,2,1,0:T(8,128)S(1)} %get-tuple-element.68), channel_id=1, source_target_pairs={{0,1},{2,3},{4,5},{6,7},{8,9},{10,11},{12,13},{14,15},{16,17},{18,... | collective-permute-start | bytes 737288 | tf_op jit(solution)/shard_map/ppermute | solution.py:33
  222.7 21.6 %copy-start.15 = (f32[3,2,2,16,6,80]{5,3,2,1,0,4:T(8,128)S(1)}, f32[3,2,2,16,6,80]{5,3,2,1,0,4:T(8,128)}, u32[]{:S(2)}) copy-start(f32[3,2,2,16,6,80]{5,3,2,1,0,4:T(8,128)} %copy-done.14) | copy-start | bytes 1105924
  222.7 21.4 %collective-permute-start.10 = (f32[3,4,1,16,320]{4,3,2,1,0:T(8,128)S(1)}, f32[3,4,1,16,320]{4,3,2,1,0:T(8,128)S(1)}, u32[]{:S(2)}, u32[]{:S(2)}) collective-permute-start(f32[3,4,1,16,320]{4,3,2,1,0:T(8,128)S(1)} %get-tuple-element.67), channel_id=1, source_target_pairs={{1,0},{3,2},{5,4},{7,6},{9,8},{11,10},{13,12},{15,14},{17,16},{19,... | collective-permute-start | bytes 737288 | tf_op jit(solution)/shard_map/ppermute | solution.py:35
  (11 other events, 16.8 us)
where the time goes:
time: 249 us; the launch traced here: 248 us
  starting transfers between devices  84.3 us (34%)
  waiting for transfers between devices  76.4 us (31%)
  local copies, waits for them, and re-layouts  41.2 us (17%)
  matrix products  35.3 us (14%)
  other arithmetic  8.74 us (4%)
    ppermute x17, waiting for transfers between devices, passed_along(): return lax.ppermute(shard, axis, pairs)  75.4 us
    ppermute x4, starting transfers between devices, with_halo(): lax.ppermute(head, axis, [((i + 1) % count, i) for i in range(ends)])  39.7 us
    ppermute x17, starting transfers between devices, passed_along(): return lax.ppermute(shard, axis, pairs)  36.1 us
    unnamed x40, local copies, waits for them, and re-layouts  28.3 us
    dot_general x47, matrix products, propagate(): jnp.einsum('ebi,eim->ebm', gathered, transfer[layer_at], precision=HIGHEST)  14.1 us
    dot_general x48, matrix products, propagate(): jnp.einsum('ef,fbm->ebm', up_links[layer_at], current, precision=HIGHEST)  8.89 us
    ppermute x4, starting transfers between devices, with_halo(): lax.ppermute(tail, axis, [(i, (i + 1) % count) for i in range(ends)])  8.49 us
    dot_general x11, matrix products, mixed_product(): jnp.einsum(spec, low_part, table, preferred_element_type=jnp.float32)  6.16 us
  transfers between devices with their start and end apart: 25, of which 17 were waited for; matrix products, arithmetic and copies ran while one was open for 14% of the time, Pallas kernels for 0%

commit v1 on v0

v1 whole, which is shorter than its diff:
```python
import jax
import jax.numpy as jnp
from jax import lax
from jax.experimental import pallas as pl
from jax.experimental.pallas import tpu as pltpu
from jax.sharding import PartitionSpec as P

NPOINT = 4
ROWS = 320
TRACE = 80
VECS = 16
LAYERS = 3
EX = 2
EY = 2
PATCH = EX * EY
CELLS = LAYERS * PATCH
LANES = 128
DEEP = 2 * LANES
GROUP = 4
NODES = NPOINT**3
MAP_ROWS = TRACE + VECS
BF16 = jnp.bfloat16
F32 = jnp.float32

FACE_ROWS = ((0, 16, 4), (3, 16, 4), (0, 4, 1), (48, 4, 1), (0, 16, 1), (12, 16, 1))
SLOT_FACES = (0, 3, 2, 5, 4)


def split(x):
    high = x.astype(BF16)
    low = (x - high.astype(F32)).astype(BF16)
    return high, low


def stacked(x):
    return jnp.concatenate(split(x), axis=0)


def dot(a, b):
    return jnp.dot(a, b, preferred_element_type=F32)


def dot_rows(a, b):
    return lax.dot_general(a, b, (((1,), (1,)), ((), ())), preferred_element_type=F32)


def halves(x):
    rows = x.shape[0] // 2
    return x[:rows] + x[rows:]


def deep_rows(table):
    high, low = split(table)
    gap = jnp.zeros((LANES - TRACE, table.shape[1]), BF16)
    return jnp.concatenate([high, gap, low, gap], axis=0)


def deep_lhs(x):
    high, low = split(x)
    return jnp.concatenate(
        [jnp.concatenate([high, high], axis=1), jnp.concatenate([low, low], axis=1)], axis=0
    )


def times(x, deep):
    return halves(dot(deep_lhs(x), deep))


def lane_take(x, index):
    return jnp.take_along_axis(x, index, axis=1)


def lane_ids(rows):
    return lax.broadcasted_iota(jnp.int32, (rows, LANES), 1)


def blocks_of(x):
    rest = ROWS - 2 * LANES
    tail = jnp.concatenate([x[:, 2 * LANES :], jnp.zeros((x.shape[0], LANES - rest), x.dtype)], axis=1)
    return x[:, :LANES], x[:, LANES : 2 * LANES], tail


def face_of(blocks, face):
    start, a_step, b_step = FACE_ROWS[face]
    lane = lane_ids(blocks[0].shape[0])
    entry = lane & 15
    index = (lane >> 4 & 1) * NODES + start + (entry >> 2) * a_step + (entry & 3) * b_step
    first, second, third = [lane_take(block, index) for block in blocks]
    third = jnp.where(lane < TRACE, third, 0.0)
    return jnp.where(lane < 32, first, jnp.where(lane < 64, second, third))


def put_faces(layer, cells, up, traces, inner, outer, across, below):
    core = lax.axis_index("cy")
    even = lax.rem(lax.axis_index("cx"), 2) == 0
    blocks = blocks_of(jnp.concatenate(cells, axis=0))
    faces = [face_of(blocks, face) for face in SLOT_FACES]
    block = lambda e, s: faces[s][VECS * e : VECS * (e + 1)]
    for e in range(PATCH):
        for s in range(len(SLOT_FACES)):
            traces[layer * PATCH + e, :, s * LANES : (s + 1) * LANES] = stacked(block(e, s))
    for b in range(EY):
        east, west = block(EY + b, 1), block(b, 2)
        inner[layer * EY + b] = jnp.where(even, east, west)
        outer[layer * EY + b] = jnp.where(even, west, east)
    for a in range(EX):
        across[layer * EX + a] = jnp.where(core == 0, block(a * EY + 1, 3), block(a * EY, 4))
    if layer == 0:
        for e in range(PATCH):
            below[up[e]] = block(e, 0)


def open_kernel(links, old, up, traces, inner, outer, across, below):
    for at in range(CELLS):
        up[at] = links[at % PATCH // EY, at % EY, at // PATCH]
    for layer in range(LAYERS):
        cells = [old[layer * PATCH + e] for e in range(PATCH)]
        put_faces(layer, cells, up, traces, inner, outer, across, below)


def place_downstream(up, traces, from_above, down):
    for layer in range(1, LAYERS):
        for e in range(PATCH):
            down[(layer - 1) * PATCH + up[layer * PATCH + e]] = traces[layer * PATCH + e, :, 0:LANES]
    for e in range(PATCH):
        down[(LAYERS - 1) * PATCH + e] = stacked(from_above[e])


def lifted_layer(layer, traces, down, inner, outer, from_across, coupling, lift):
    core = lax.axis_index("cy")
    even = lax.rem(lax.axis_index("cx"), 2) == 0
    lane = lax.broadcasted_iota(jnp.int32, (2 * VECS, DEEP), 1)
    left, right = [], []
    for e in range(PATCH):
        a, b = e // EY, e % EY
        own = lambda cell, s: traces[layer * PATCH + cell, :, s * LANES : (s + 1) * LANES]
        near, far = inner[layer * EY + b], outer[layer * EY + b]
        slot1 = down[layer * PATCH + e]
        slot2 = own(b, 1) if a == 1 else stacked(jnp.where(even, far, near))
        slot3 = own(EY + b, 2) if a == 0 else stacked(jnp.where(even, near, far))
        other = from_across[layer * EX + a]
        slot4 = own(a * EY, 3) if b == 1 else stacked(jnp.where(core == 1, other, 0.0))
        slot5 = own(a * EY + 1, 4) if b == 0 else stacked(jnp.where(core == 0, other, 0.0))
        first = jnp.concatenate([slot1, slot2, slot3], axis=0)[:, :TRACE]
        second = jnp.concatenate([slot3, slot4, slot5], axis=0)[:, :TRACE]
        block = coupling[layer * PATCH + e]
        y = dot(first, block[:, :DEEP])
        r = 2 * VECS
        kept = jnp.where(
            lane < TRACE,
            0.0,
            jnp.where(lane < 2 * TRACE, y[:r], jnp.where(lane < 3 * TRACE, y[r : 2 * r], y[2 * r :])),
        )
        left.append(stacked(halves(kept)))
        z = dot(second, block[:, DEEP:])
        tail = lane[:, : 6 * TRACE - DEEP] + DEEP
        kept = jnp.where(
            tail < 4 * TRACE, z[:r], jnp.where(tail < 5 * TRACE, z[r : 2 * r], z[2 * r :])
        )
        right.append(stacked(halves(kept)))
    out = dot_rows(jnp.concatenate(left, axis=0), lift[:, :DEEP]) + dot_rows(
        jnp.concatenate(right, axis=0), lift[:, DEEP:]
    )
    return [halves(out[2 * VECS * e : 2 * VECS * (e + 1)]) for e in range(PATCH)]


def left_of(deep):
    high, low = deep[:TRACE], deep[LANES : LANES + TRACE]
    return jnp.concatenate(
        [jnp.concatenate([high, high], axis=1), jnp.concatenate([low, low], axis=1)], axis=0
    )


def transfer_kernel(up, diag, coupling, lift, weights, passing, composed, first_two):
    one = lax.broadcasted_iota(jnp.int32, (TRACE, TRACE), 0)
    two = lax.broadcasted_iota(jnp.int32, (TRACE, TRACE), 1)
    inflow = dot_rows((one == two).astype(F32).astype(BF16), lift[:, :TRACE]).astype(BF16)
    upper, lower = inflow[:NODES, :DEEP], inflow[NODES:, DEEP:]
    for at in range(CELLS):
        block = diag[at]
        lifted_rows = jnp.concatenate([dot(upper, block[:DEEP]), dot(lower, block[DEEP:])], axis=0)
        upwind = coupling[at][:, :LANES]
        weight = dot(jnp.concatenate([upwind, upwind], axis=1), deep_rows(lifted_rows))
        weights[at] = deep_rows(weight)
        passing[at] = deep_rows(face_of(blocks_of(weight), 1))
    for e in range(PATCH):
        first_two[e] = halves(dot(left_of(passing[up[PATCH + e]]), passing[PATCH + e]))
    for e in range(PATCH):
        composed[e] = -times(first_two[up[2 * PATCH + e]], passing[2 * PATCH + e])


def pack(maps, ends):
    lane = lane_ids(MAP_ROWS)
    fourth = maps[3]
    one = jnp.where(lane < TRACE, maps[0], pltpu.roll(fourth, TRACE, 1))
    two = jnp.where(lane < TRACE, maps[1], pltpu.roll(fourth, 2 * TRACE - LANES, 1))
    return jnp.concatenate([one, two, maps[2], ends], axis=0)


def unpack(packed):
    lane = lane_ids(MAP_ROWS)
    one, two, three = [packed[MAP_ROWS * at : MAP_ROWS * (at + 1)] for at in range(3)]
    fourth = jnp.where(
        lane < LANES - TRACE, pltpu.roll(one, LANES - TRACE, 1), pltpu.roll(two, 2 * LANES - 2 * TRACE, 1)
    )
    used = lane < TRACE
    maps = [jnp.where(used, x, 0.0) for x in (one, two, three, fourth)]
    return maps, packed[3 * MAP_ROWS : 3 * MAP_ROWS + 8]


def chosen(items, at):
    out = items[0]
    for number in range(1, PATCH):
        out = jnp.where(at == number, items[number], out)
    return out


def rows_of(ends):
    return [ends[at : at + 1] for at in range(PATCH)]


def ends_of(rows):
    return jnp.concatenate(list(rows) + [jnp.zeros((8 - PATCH, LANES), F32)], axis=0)


def placed(states, ends):
    out = []
    for position in range(PATCH):
        total = jnp.where(ends[0] == position, states[0], 0.0)
        for at in range(1, PATCH):
            total = total + jnp.where(ends[at] == position, states[at], 0.0)
        out.append(total)
    return out


def after(first, second):
    nothing = jnp.zeros((TRACE, LANES), F32)
    added = jnp.concatenate([nothing, second[TRACE:]], axis=0) if first.shape[0] > VECS else second[TRACE:]
    return times(first, deep_rows(second[:TRACE])) + added


def source_kernel(
    up, rhs, traces, outer, from_above, inner, from_across, diag, coupling, lift, passing, composed,
    solved, sources, packed, down, current, maps,
):
    place_downstream(up, traces, from_above, down)
    for layer in range(LAYERS):
        lifts = lifted_layer(layer, traces, down, inner, outer, from_across, coupling, lift)
        for e in range(PATCH):
            at = layer * PATCH + e
            y = halves(dot(stacked(rhs[at] - lifts[e]), diag[at]))
            solved[at] = y
            sources[at] = face_of(blocks_of(y), 1)
    for e in range(PATCH):
        current[e] = sources[e]
    for layer in range(1, LAYERS):
        moved = []
        for e in range(PATCH):
            at = layer * PATCH + e
            moved.append(sources[at] - times(current[up[at]], passing[at]))
        for e in range(PATCH):
            current[e] = moved[e]
    row = lax.broadcasted_iota(jnp.int32, (8, LANES), 0)
    ends = jnp.zeros((8, LANES), F32)
    for e in range(PATCH):
        start = up[up[PATCH + up[2 * PATCH + e]]]
        maps[start, 0:TRACE] = composed[e]
        maps[start, TRACE:MAP_ROWS] = current[e]
        ends = jnp.where(row == start, float(e), ends)
    packed[...] = pack([maps[e] for e in range(PATCH)], ends)


def joined(mine, theirs, bit):
    later = (lax.axis_index("sweep") >> bit & 1) == 1
    first, first_ends = unpack(jnp.where(later, theirs, mine))
    second, second_ends = unpack(jnp.where(later, mine, theirs))
    first_ends, second_ends = rows_of(first_ends), rows_of(second_ends)
    maps = [after(first[at], chosen(second, first_ends[at])) for at in range(PATCH)]
    return maps, [chosen(second_ends, first_ends[at]) for at in range(PATCH)], first, first_ends, later


def pair_kernel(mine, theirs, packed):
    maps, ends, *unused = joined(mine[...], theirs[...], 0)
    packed[...] = pack(maps, ends_of(ends))


def group_kernel(mine, theirs, packed, leaving):
    maps, ends, *unused = joined(mine[...], theirs[...], 1)
    packed[...] = pack(maps, ends_of(ends))
    for at, state in enumerate(placed([x[TRACE:] for x in maps], ends)):
        leaving[at] = state


def prefix_kernel(pair, theirs, prefixes, ends):
    me = lax.axis_index("sweep")
    partner, partner_ends = unpack(pair[...])
    row = lax.broadcasted_iota(jnp.int32, (MAP_ROWS, LANES), 0)
    same = (row == lane_ids(MAP_ROWS)).astype(F32)
    later = (me & 1) == 1
    own = [jnp.where(later, x, same) for x in partner]
    own_ends = [jnp.where(later, x, float(at)) for at, x in enumerate(rows_of(partner_ends))]
    first, first_ends = unpack(theirs[...])
    first_ends = rows_of(first_ends)
    later = (me >> 1 & 1) == 1
    out = []
    for at in range(PATCH):
        whole = after(first[at], chosen(own, first_ends[at]))
        prefixes[at] = jnp.where(later, whole, own[at])
        out.append(jnp.where(later, chosen(own_ends, first_ends[at]), own_ends[at]))
    ends[...] = ends_of(out)


def onward_kernel(entering, packed, leaving):
    maps, ends = unpack(packed[...])
    states = [after(entering[at], maps[at]) for at in range(PATCH)]
    for at, state in enumerate(placed(states, rows_of(ends))):
        leaving[at] = state


def finish_kernel(
    up, second, third, fourth, before, prefixes, ends, old, solved, sources, weights, passing,
    new, traces, inner, outer, across, below, arrived, current,
):
    maps, map_ends = unpack(before[...])
    states = [after(fourth[at], maps[at]) for at in range(PATCH)]
    last = placed(states, rows_of(map_ends))
    entering = [second[at] + third[at] + last[at] for at in range(PATCH)]
    states = [after(entering[at], prefixes[at]) for at in range(PATCH)]
    for at, state in enumerate(placed(states, rows_of(ends))):
        arrived[at] = state
    for layer in range(LAYERS):
        inflow = []
        for e in range(PATCH):
            link = up[layer * PATCH + e]
            inflow.append(arrived[link] if layer == 0 else current[link])
        if layer < LAYERS - 1:
            for e in range(PATCH):
                at = layer * PATCH + e
                current[e] = sources[at] - times(inflow[e], passing[at])
        changes = []
        for e in range(PATCH):
            at = layer * PATCH + e
            x = solved[at] - times(inflow[e], weights[at])
            new[at] = x
            changes.append(old[at] - x)
        put_faces(layer, changes, up, traces, inner, outer, across, below)


def residual_kernel(up, traces, outer, from_above, inner, from_across, coupling, lift, out, down):
    place_downstream(up, traces, from_above, down)
    for layer in range(LAYERS):
        lifts = lifted_layer(layer, traces, down, inner, outer, from_across, coupling, lift)
        for e in range(PATCH):
            out[layer * PATCH + e] = lifts[e]


VMEM = pl.BlockSpec(memory_space=pltpu.VMEM)
SMEM = pl.BlockSpec(memory_space=pltpu.SMEM)


def call(kernel, scalars, outs, scratch=(), scalar_outs=(), micros=1):
    def run(*args):
        return pl.pallas_call(
            kernel,
            in_specs=[SMEM] * scalars + [VMEM] * (len(args) - scalars),
            out_specs=[SMEM if i in scalar_outs else VMEM for i in range(len(outs))],
            out_shape=[jax.ShapeDtypeStruct(shape, kind) for shape, kind in outs],
            scratch_shapes=list(scratch),
            compiler_params=pltpu.CompilerParams(vmem_limit_bytes=16 * 1024 * 1024),
            cost_estimate=pl.CostEstimate(
                flops=micros * 1_000_000_000, bytes_accessed=micros * 3_600_000, transcendentals=0
            ),
        )(*args)

    return run


FACE_OUTS = [
    ((CELLS, 2 * VECS, len(SLOT_FACES) * LANES), BF16),
    ((LAYERS * EY, VECS, LANES), F32),
    ((LAYERS * EY, VECS, LANES), F32),
    ((LAYERS * EX, VECS, LANES), F32),
    ((PATCH, VECS, LANES), F32),
]
FIELD = ((CELLS, VECS, ROWS), F32)
STATES = ((PATCH, VECS, LANES), F32)
PACKED = ((3 * MAP_ROWS + 8, LANES), F32)
DOWN = pltpu.VMEM((CELLS, 2 * VECS, LANES), BF16)
HELD = pltpu.VMEM((PATCH, VECS, LANES), F32)


def exchange_sides(inner, outer, across, below):
    wide, deep = lax.axis_size("cx"), lax.axis_size("sweep")
    outer = lax.ppermute(outer, "cx", [(i, i + 1 if i % 2 else i - 1) for i in range(1, wide - 1)])
    below = lax.ppermute(below, "sweep", [(i + 1, i) for i in range(deep - 1)])
    inner = lax.ppermute(inner, "cx", [(i, i ^ 1) for i in range(wide)])
    across = lax.ppermute(across, "cy", [(0, 1), (1, 0)])
    return outer, below, inner, across


def swapped(packed, by):
    return lax.ppermute(packed, "sweep", [(i, i ^ by) for i in range(lax.axis_size("sweep"))])


def passed(states, source, target):
    return lax.ppermute(states, "sweep", [(GROUP * source + p, GROUP * target + p) for p in range(GROUP)])


def local(rhs_vectors, old_iterate, diag_inverse, coupling, lift_table, upstream):
    old = old_iterate.reshape(CELLS, VECS, ROWS)
    rhs = rhs_vectors.reshape(CELLS, VECS, ROWS)
    diag = diag_inverse.reshape(CELLS, ROWS, ROWS)
    blocks = coupling.reshape(CELLS, TRACE, 6 * TRACE)
    lift = lift_table.T
    up, traces, *sends = call(open_kernel, 1, [((CELLS,), jnp.int32)] + FACE_OUTS, scalar_outs=(0,), micros=2)(
        upstream.transpose(1, 2, 0), old
    )
    halos = exchange_sides(*sends)
    weights, passing, composed = call(
        transfer_kernel,
        1,
        [((CELLS, DEEP, ROWS), BF16), ((CELLS, DEEP, LANES), BF16), ((PATCH, TRACE, LANES), F32)],
        [pltpu.VMEM((PATCH, TRACE, LANES), F32)],
    )(up, diag, blocks, lift)
    solved, sources, single = call(
        source_kernel,
        1,
        [FIELD, ((CELLS, VECS, LANES), F32), PACKED],
        [DOWN, HELD, pltpu.VMEM((PATCH, MAP_ROWS, LANES), F32)],
    )(up, rhs, traces, *halos, diag, blocks, lift, passing, composed)
    partner = swapped(single, 1)
    (pair,) = call(pair_kernel, 0, [PACKED])(single, partner)
    partner_pair = swapped(pair, 2)
    group, leaving = call(group_kernel, 0, [PACKED, STATES])(pair, partner_pair)
    second = passed(leaving, 0, 1)
    before = passed(group, 2, 3)
    prefixes, ends = call(prefix_kernel, 0, [((PATCH, MAP_ROWS, LANES), F32), ((8, LANES), F32)])(
        partner, partner_pair
    )
    (leaving,) = call(onward_kernel, 0, [STATES])(second, group)
    third = passed(leaving, 1, 2)
    fourth = passed(leaving, 1, 3)
    new, traces, *sends = call(finish_kernel, 1, [FIELD] + FACE_OUTS, [HELD, HELD])(
        up, second, third, fourth, before, prefixes, ends, old, solved, sources, weights, passing
    )
    halos = exchange_sides(*sends)
    (residual,) = call(residual_kernel, 1, [FIELD], [DOWN])(up, traces, *halos, blocks, lift)
    shape = rhs_vectors.shape
    return new.reshape(shape), residual.reshape(shape)


def solution(mesh):
    field = P("sweep", "cx", "cy", None, None)
    return jax.shard_map(
        local,
        mesh=mesh,
        in_specs=(field, field, field, field, P(), P("sweep", "cx", "cy")),
        out_specs=(field, field),
        check_vma=False,
    )
```

time: 249 us -> 87.7 us (0.35)
  waiting for transfers between devices: 76.4 us -> 26 us
  starting transfers between devices: 84.3 us -> 44.5 us
  local copies, waits for them, and re-layouts: 41.2 us -> 1.66 us
  matrix products: 35.3 us -> 0 us
  Pallas kernels: 0 us -> 13.7 us
  other arithmetic: 8.74 us -> 0 us
    ppermute x25 -> x14, waiting for transfers between devices: 76.4 us -> 26 us  [the longest x2 15.4 us: swapped(): lax.ppermute(packed, 'sweep', [(i, i ^ by) for i in range(lax.axis_size('...]
    ppermute x25 -> x14, starting transfers between devices: 84.3 us -> 44.5 us  [the longest x2 13.9 us: exchange_sides(): lax.ppermute(outer, 'cx', [(i, i + 1 if i % 2 else i - 1) for i in range(...]
    dot_general x120 -> x0, matrix products: 35.3 us -> none  [the longest x47 14.1 us: propagate(): jnp.einsum('ebi,eim->ebm', gathered, transfer[layer_at], precision=HIGHEST)]
    unnamed x40 -> x14, local copies, waits for them, and re-layouts: 28.3 us -> 1.66 us
    pallas_call x0 -> x9, Pallas kernels: none -> 13.7 us  [run(): pl.pallas_call(kernel, in_specs=[SMEM] * scalars + [VMEM] * (len(args) -...]
    reshape x3 -> x0, local copies, waits for them, and re-layouts: 4.43 us -> none  [the longest x2 2.27 us: lifted(): fluxes.reshape(stacked.shape)]
    convert_element_type x8 -> x0, other arithmetic: 3.76 us -> none  [the longest x6 3.55 us: mixed_product(): high_part = lax.optimization_barrier(values.astype(jnp.bfloat16))]
    slice x15 -> x0, local copies, waits for them, and re-layouts: 3.21 us -> none  [the longest x2 1.23 us: neighbours(): traces[..., 2 * TRACE:6 * TRACE]]
  transfers between devices with their start and end apart: 25 -> 14, of which waited for: 17 -> 4; matrix products, arithmetic and copies ran while one was open for 14% -> 0% of each run, Pallas kernels for 0% -> 5%
where the time goes in v1:
time: 87.7 us; the launch traced here: 86.8 us
  starting transfers between devices  44.5 us (51%)
  waiting for transfers between devices  26 us (30%)
  Pallas kernels  13.7 us (16%)
  local copies, waits for them, and re-layouts  1.66 us (2%)
  between operations  0.9 us (1%)
    ppermute x2, waiting for transfers between devices, swapped(): lax.ppermute(packed, 'sweep', [(i, i ^ by) for i in range(lax.axis_size('...  15.4 us
    ppermute x2, starting transfers between devices, exchange_sides(): lax.ppermute(outer, 'cx', [(i, i + 1 if i % 2 else i - 1) for i in range(...  13.9 us
    pallas_call x9, Pallas kernels, run(): pl.pallas_call(kernel, in_specs=[SMEM] * scalars + [VMEM] * (len(args) -...  13.7 us
    ppermute x2, starting transfers between devices, exchange_sides(): across = lax.ppermute(across, 'cy', [(0, 1), (1, 0)])  8.33 us
    ppermute x4, waiting for transfers between devices, passed(): lax.ppermute(states, 'sweep', [(GROUP * source + p, GROUP * target + p) f...  7.81 us
    ppermute x2, starting transfers between devices, exchange_sides(): below = lax.ppermute(below, 'sweep', [(i + 1, i) for i in range(deep - 1)])  7.41 us
    ppermute x4, starting transfers between devices, passed(): lax.ppermute(states, 'sweep', [(GROUP * source + p, GROUP * target + p) f...  6.27 us
    ppermute x2, starting transfers between devices, exchange_sides(): inner = lax.ppermute(inner, 'cx', [(i, i ^ 1) for i in range(wide)])  4.7 us
  transfers between devices with their start and end apart: 14, of which 4 were waited for; matrix products, arithmetic and copies ran while one was open for 0% of the time, Pallas kernels for 5%

profile of v1, /device:TPU:7, one launch (start us, length us, event | category | flops | bytes accessed | tf_op | source)
XLA Modules:
  0.0 86.8 jit_solution(3460635122208811134)
XLA Ops:
  0.6 0.0 copy-start.4
  0.6 1.0 %copy-done.4 = f32[3,2,2,16,320]{4,3,2,1,0:T(8,128)S(1)} copy-done((f32[3,2,2,16,320]{4,3,2,1,0:T(8,128)S(1)}, f32[3,2,2,16,320]{4,3,2,1,0:T(8,128)}, u32[]{:S(2)}) %copy-start.4) | copy-done | bytes 245784
  1.6 0.7 copy-done.6
  2.3 1.6 %shard_map.77 = (s32[12]{0:T(128)S(1)}, bf16[12,32,640]{2,1,0:T(8,128)(2,1)S(1)}, f32[6,16,128]{2,1,0:T(8,128)S(1)}, f32[6,16,128]{2,1,0:T(8,128)S(1)}, f32[6,16...) custom-call(s32[2,2,3]{2,1,0:T(2,128)S(1)} %bitcast.19, f32[12,16,320]{2,1,0:T(8,128)S(1)} %bitcast.17), custom_call_target="tpu_custom_call" | custom-call | flops 2000000000 | bytes 7200000 | tf_op jit(solution)/shard_map/pallas_call | solution.py:363
  3.9 0.0 copy-start.3
  3.9 5.5 %collective-permute-start.1 = (f32[4,16,128]{2,1,0:T(8,128)S(1)}, f32[4,16,128]{2,1,0:T(8,128)S(1)}, u32[]{:S(2)}, u32[]{:S(2)}) collective-permute-start(f32[4,16,128]{2,1,0:T(8,128)S(1)} %get-tuple-element.27), channel_id=1, source_target_pairs={{32,0},{64,32},{96,64},{128,96},{160,128},{192,160},{224,192},{256... | collective-permute-start | bytes 98312 | tf_op jit(solution)/shard_map/ppermute | solution.py:395
  9.4 11.2 %collective-permute-start = (f32[6,16,128]{2,1,0:T(8,128)S(1)}, f32[6,16,128]{2,1,0:T(8,128)S(1)}, u32[]{:S(2)}, u32[]{:S(2)}) collective-permute-start(f32[6,16,128]{2,1,0:T(8,128)S(1)} %get-tuple-element.26), channel_id=1, source_target_pairs={{2,4},{4,2},{6,8},{8,6},{10,12},{12,10},{14,16},{16,14},{18,20},{2... | collective-permute-start | bytes 147464 | tf_op jit(solution)/shard_map/ppermute | solution.py:394
  20.6 1.9 %collective-permute-start.2 = (f32[6,16,128]{2,1,0:T(8,128)S(1)}, f32[6,16,128]{2,1,0:T(8,128)S(1)}, u32[]{:S(2)}, u32[]{:S(2)}) collective-permute-start(f32[6,16,128]{2,1,0:T(8,128)S(1)} %get-tuple-element.28), channel_id=1, source_target_pairs={{0,2},{2,0},{4,6},{6,4},{8,10},{10,8},{12,14},{14,12},{16,18},{18,... | collective-permute-start | bytes 147464 | tf_op jit(solution)/shard_map/ppermute | solution.py:396
  22.6 3.1 %collective-permute-start.3 = (f32[6,16,128]{2,1,0:T(8,128)S(1)}, f32[6,16,128]{2,1,0:T(8,128)S(1)}, u32[]{:S(2)}, u32[]{:S(2)}) collective-permute-start(f32[6,16,128]{2,1,0:T(8,128)S(1)} %get-tuple-element.29), channel_id=1, source_target_pairs={{0,1},{1,0},{2,3},{3,2},{4,5},{5,4},{6,7},{7,6},{8,9},{9,8},{10,11... | collective-permute-start | bytes 147464 | tf_op jit(solution)/shard_map/ppermute | solution.py:397
  25.7 3.7 %shard_map.78 = (bf16[12,256,320]{2,1,0:T(8,128)(2,1)S(1)}, bf16[12,256,128]{2,1,0:T(8,128)(2,1)S(1)}, f32[4,80,128]{2,1,0:T(8,128)S(1)}) custom-call(s32[12]{0:T(128)S(1)} %get-tuple-element.24.up, bf16[12,320,320]{2,1,0:T(8,128)(2,1)S(1)} %bitcast.8, bf16[12,80,480]{2,1,0:T(8,128)(2,1)S(1)} %bitcast.10, bf16[320,480]{1,0:T(8,128)(2,1)S(1)} %bitcast.13), custom_call_target="tpu_custom_call" | custom-call | flops 1000000000 | bytes 3600000 | tf_op jit(solution)/shard_map/pallas_call | solution.py:363
  29.5 2.6 %shard_map.79 = (f32[12,16,320]{2,1,0:T(8,128)S(1)}, f32[12,16,128]{2,1,0:T(8,128)S(1)}, f32[296,128]{1,0:T(8,128)S(1)}) custom-call(s32[12]{0:T(128)S(1)} %get-tuple-element.24.up, f32[12,16,320]{2,1,0:T(8,128)S(1)} %bitcast.16, bf16[12,32,640]{2,1,0:T(8,128)(2,1)S(1)} %get-tuple-element.25.traces, f32[6,16,128]{2,1,0:T(8,128)S(1)} %collective-permute-done.outer, ...), custom_call_target="tpu_custom_call" | custom-call | flops 1000000000 | bytes 3600000 | tf_op jit(solution)/shard_map/pallas_call | solution.py:363
  32.0 1.9 %collective-permute-start.4 = (f32[296,128]{1,0:T(8,128)S(1)}, f32[296,128]{1,0:T(8,128)S(1)}, u32[]{:S(2)}, u32[]{:S(2)}) collective-permute-start(f32[296,128]{1,0:T(8,128)S(1)} %get-tuple-element.32.mine), channel_id=1, source_target_pairs={{0,32},{32,0},{64,96},{96,64},{128,160},{160,128},{192,224},{224,1... | collective-permute-start | bytes 454664 | tf_op jit(solution)/shard_map/ppermute | solution.py:402
  34.0 5.5 %collective-permute-done.4.theirs.pair = f32[296,128]{1,0:T(8,128)S(1)} collective-permute-done((f32[296,128]{1,0:T(8,128)S(1)}, f32[296,128]{1,0:T(8,128)S(1)}, u32[]{:S(2)}, u32[]{:S(2)}) %collective-permute-start.4) | collective-permute-done | bytes 151584 | tf_op jit(solution)/shard_map/ppermute | solution.py:402
  39.5 0.4 shard_map.80.mine
  39.9 1.9 %collective-permute-start.5 = (f32[296,128]{1,0:T(8,128)S(1)}, f32[296,128]{1,0:T(8,128)S(1)}, u32[]{:S(2)}, u32[]{:S(2)}) collective-permute-start(f32[296,128]{1,0:T(8,128)S(1)} %shard_map.80.mine), channel_id=1, source_target_pairs={{0,64},{32,96},{64,0},{96,32},{128,192},{160,224},{192,128},{224,1... | collective-permute-start | bytes 454664 | tf_op jit(solution)/shard_map/ppermute | solution.py:402
  41.9 9.9 %collective-permute-done.5.theirs = f32[296,128]{1,0:T(8,128)S(1)} collective-permute-done((f32[296,128]{1,0:T(8,128)S(1)}, f32[296,128]{1,0:T(8,128)S(1)}, u32[]{:S(2)}, u32[]{:S(2)}) %collective-permute-start.5) | collective-permute-done | bytes 151584 | tf_op jit(solution)/shard_map/ppermute | solution.py:402
  51.8 0.4 shard_map.81
  52.2 0.7 collective-permute-start.6
  52.9 0.0 copy-start.5
  52.9 3.6 %collective-permute-start.9 = (f32[296,128]{1,0:T(8,128)S(1)}, f32[296,128]{1,0:T(8,128)S(1)}, u32[]{:S(2)}, u32[]{:S(2)}) collective-permute-start(f32[296,128]{1,0:T(8,128)S(1)} %get-tuple-element.34.packed), channel_id=1, source_target_pairs={{256,384},{288,416},{320,448},{352,480},{257,385},{289,417},{321,4... | collective-permute-start | bytes 454664 | tf_op jit(solution)/shard_map/ppermute | solution.py:406
  56.5 0.2 shard_map.82
  56.8 0.7 collective-permute-start.8
  57.4 1.3 %collective-permute-start.7 = (f32[4,16,128]{2,1,0:T(8,128)S(1)}, f32[4,16,128]{2,1,0:T(8,128)S(1)}, u32[]{:S(2)}, u32[]{:S(2)}) collective-permute-start(f32[4,16,128]{2,1,0:T(8,128)S(1)} %shard_map.82), channel_id=1, source_target_pairs={{128,256},{160,288},{192,320},{224,352},{129,257},{161,289},{193,3... | collective-permute-start | bytes 98312 | tf_op jit(solution)/shard_map/ppermute | solution.py:406
  58.7 0.3 shard_map.83
  59.1 7.8 %collective-permute-done.7.third = f32[4,16,128]{2,1,0:T(8,128)S(1)} collective-permute-done((f32[4,16,128]{2,1,0:T(8,128)S(1)}, f32[4,16,128]{2,1,0:T(8,128)S(1)}, u32[]{:S(2)}, u32[]{:S(2)}) %collective-permute-start.7) | collective-permute-done | bytes 32800 | tf_op jit(solution)/shard_map/ppermute | solution.py:406
  66.9 2.2 %shard_map.84 = (f32[12,16,320]{2,1,0:T(8,128)}, bf16[12,32,640]{2,1,0:T(8,128)(2,1)S(1)}, f32[6,16,128]{2,1,0:T(8,128)S(1)}, f32[6,16,128]{2,1,0:T(8,128)S(1)},...) custom-call(s32[12]{0:T(128)S(1)} %get-tuple-element.24.up, ...), custom_call_target="tpu_custom_call" | custom-call | flops 1000000000 | bytes 3600000 | tf_op jit(solution)/shard_map/pallas_call | solution.py:363
  69.1 2.7 %collective-permute-start.10 = (f32[6,16,128]{2,1,0:T(8,128)S(1)}, f32[6,16,128]{2,1,0:T(8,128)S(1)}, u32[]{:S(2)}, u32[]{:S(2)}) collective-permute-start(f32[6,16,128]{2,1,0:T(8,128)S(1)} %get-tuple-element.42), channel_id=1, source_target_pairs={{2,4},{4,2},{6,8},{8,6},{10,12},{12,10},{14,16},{16,14},{18,20},{2... | collective-permute-start | bytes 147464 | tf_op jit(solution)/shard_map/ppermute | solution.py:394
  71.8 2.8 %collective-permute-start.12 = (f32[6,16,128]{2,1,0:T(8,128)S(1)}, f32[6,16,128]{2,1,0:T(8,128)S(1)}, u32[]{:S(2)}, u32[]{:S(2)}) collective-permute-start(f32[6,16,128]{2,1,0:T(8,128)S(1)} %get-tuple-element.44), channel_id=1, source_target_pairs={{0,2},{2,0},{4,6},{6,4},{8,10},{10,8},{12,14},{14,12},{16,18},{18,... | collective-permute-start | bytes 147464 | tf_op jit(solution)/shard_map/ppermute | solution.py:396
  74.6 5.2 %collective-permute-start.13 = (f32[6,16,128]{2,1,0:T(8,128)S(1)}, f32[6,16,128]{2,1,0:T(8,128)S(1)}, u32[]{:S(2)}, u32[]{:S(2)}) collective-permute-start(f32[6,16,128]{2,1,0:T(8,128)S(1)} %get-tuple-element.45), channel_id=1, source_target_pairs={{0,1},{1,0},{2,3},{3,2},{4,5},{5,4},{6,7},{7,6},{8,9},{9,8},{10,11... | collective-permute-start | bytes 147464 | tf_op jit(solution)/shard_map/ppermute | solution.py:397
  79.8 1.9 %collective-permute-start.11 = (f32[4,16,128]{2,1,0:T(8,128)S(1)}, f32[4,16,128]{2,1,0:T(8,128)S(1)}, u32[]{:S(2)}, u32[]{:S(2)}) collective-permute-start(f32[4,16,128]{2,1,0:T(8,128)S(1)} %get-tuple-element.43), channel_id=1, source_target_pairs={{32,0},{64,32},{96,64},{128,96},{160,128},{192,160},{224,192},{256... | collective-permute-start | bytes 98312 | tf_op jit(solution)/shard_map/ppermute | solution.py:395
  81.8 2.7 %collective-permute-done.11.from_above = f32[4,16,128]{2,1,0:T(8,128)S(1)} collective-permute-done((f32[4,16,128]{2,1,0:T(8,128)S(1)}, f32[4,16,128]{2,1,0:T(8,128)S(1)}, u32[]{:S(2)}, u32[]{:S(2)}) %collective-permute-start.11) | collective-permute-done | bytes 32800 | tf_op jit(solution)/shard_map/ppermute | solution.py:395
  84.5 2.3 %shard_map.85 = f32[12,16,320]{2,1,0:T(8,128)} custom-call(s32[12]{0:T(128)S(1)} %get-tuple-element.24.up, bf16[12,32,640]{2,1,0:T(8,128)(2,1)S(1)} %get-tuple-element.41.traces, f32[6,16,128]{2,1,0:T(8,128)S(1)} %collective-permute-done.10.outer, f32[4,16,128]{2,1,0:T(8,128)S(1)} %collective-permute-done.11.from_above, ...), custom_call_target="tpu_custom_call" | custom-call | flops 1000000000 | bytes 3600000 | tf_op jit(solution)/shard_map/pallas_call | solution.py:363
  (19 shorter events, 0.0 us)
Async XLA Ops:
  0.6 1.0 %copy-start.4 = (f32[3,2,2,16,320]{4,3,2,1,0:T(8,128)S(1)}, f32[3,2,2,16,320]{4,3,2,1,0:T(8,128)}, u32[]{:S(2)}) copy-start(f32[3,2,2,16,320]{4,3,2,1,0:T(8,128)} %param.7) | copy-start | bytes 737284
  1.6 0.7 copy-start.6
  2.3 23.4 %copy-start = (bf16[3,2,2,320,320]{4,3,2,1,0:T(8,128)(2,1)S(1)}, bf16[3,2,2,320,320]{4,3,2,1,0:T(8,128)(2,1)}, u32[]{:S(2)}) copy-start(bf16[3,2,2,320,320]{4,3,2,1,0:T(8,128)(2,1)} %param.8) | copy-start | bytes 7372804
  2.3 23.4 %copy-start.1 = (bf16[3,2,2,80,480]{4,3,2,1,0:T(8,128)(2,1)S(1)}, bf16[3,2,2,80,480]{4,3,2,1,0:T(8,128)(2,1)}, u32[]{:S(2)}) copy-start(bf16[3,2,2,80,480]{4,3,2,1,0:T(8,128)(2,1)} %param.9) | copy-start | bytes 2764804
  2.3 23.5 %copy-start.2 = (bf16[480,320]{0,1:T(8,128)(2,1)S(1)}, bf16[480,320]{0,1:T(8,128)(2,1)}, u32[]{:S(2)}) copy-start(bf16[480,320]{0,1:T(8,128)(2,1)} %param.10) | copy-start | bytes 921604
  3.9 25.6 %copy-start.3 = (f32[3,2,2,16,320]{4,3,2,1,0:T(8,128)S(1)}, f32[3,2,2,16,320]{4,3,2,1,0:T(8,128)}, u32[]{:S(2)}) copy-start(f32[3,2,2,16,320]{4,3,2,1,0:T(8,128)} %param.6) | copy-start | bytes 737284
  3.9 25.5 %collective-permute-start.1 = (f32[4,16,128]{2,1,0:T(8,128)S(1)}, f32[4,16,128]{2,1,0:T(8,128)S(1)}, u32[]{:S(2)}, u32[]{:S(2)}) collective-permute-start(f32[4,16,128]{2,1,0:T(8,128)S(1)} %get-tuple-element.27), channel_id=1, source_target_pairs={{32,0},{64,32},{96,64},{128,96},{160,128},{192,160},{224,192},{256... | collective-permute-start | bytes 98312 | tf_op jit(solution)/shard_map/ppermute | solution.py:395
  9.4 20.0 %collective-permute-start = (f32[6,16,128]{2,1,0:T(8,128)S(1)}, f32[6,16,128]{2,1,0:T(8,128)S(1)}, u32[]{:S(2)}, u32[]{:S(2)}) collective-permute-start(f32[6,16,128]{2,1,0:T(8,128)S(1)} %get-tuple-element.26), channel_id=1, source_target_pairs={{2,4},{4,2},{6,8},{8,6},{10,12},{12,10},{14,16},{16,14},{18,20},{2... | collective-permute-start | bytes 147464 | tf_op jit(solution)/shard_map/ppermute | solution.py:394
  20.6 8.8 %collective-permute-start.2 = (f32[6,16,128]{2,1,0:T(8,128)S(1)}, f32[6,16,128]{2,1,0:T(8,128)S(1)}, u32[]{:S(2)}, u32[]{:S(2)}) collective-permute-start(f32[6,16,128]{2,1,0:T(8,128)S(1)} %get-tuple-element.28), channel_id=1, source_target_pairs={{0,2},{2,0},{4,6},{6,4},{8,10},{10,8},{12,14},{14,12},{16,18},{18,... | collective-permute-start | bytes 147464 | tf_op jit(solution)/shard_map/ppermute | solution.py:396
  22.6 6.9 %collective-permute-start.3 = (f32[6,16,128]{2,1,0:T(8,128)S(1)}, f32[6,16,128]{2,1,0:T(8,128)S(1)}, u32[]{:S(2)}, u32[]{:S(2)}) collective-permute-start(f32[6,16,128]{2,1,0:T(8,128)S(1)} %get-tuple-element.29), channel_id=1, source_target_pairs={{0,1},{1,0},{2,3},{3,2},{4,5},{5,4},{6,7},{7,6},{8,9},{9,8},{10,11... | collective-permute-start | bytes 147464 | tf_op jit(solution)/shard_map/ppermute | solution.py:397
  32.0 7.4 %collective-permute-start.4 = (f32[296,128]{1,0:T(8,128)S(1)}, f32[296,128]{1,0:T(8,128)S(1)}, u32[]{:S(2)}, u32[]{:S(2)}) collective-permute-start(f32[296,128]{1,0:T(8,128)S(1)} %get-tuple-element.32.mine), channel_id=1, source_target_pairs={{0,32},{32,0},{64,96},{96,64},{128,160},{160,128},{192,224},{224,1... | collective-permute-start | bytes 454664 | tf_op jit(solution)/shard_map/ppermute | solution.py:402
  39.9 11.8 %collective-permute-start.5 = (f32[296,128]{1,0:T(8,128)S(1)}, f32[296,128]{1,0:T(8,128)S(1)}, u32[]{:S(2)}, u32[]{:S(2)}) collective-permute-start(f32[296,128]{1,0:T(8,128)S(1)} %shard_map.80.mine), channel_id=1, source_target_pairs={{0,64},{32,96},{64,0},{96,32},{128,192},{160,224},{192,128},{224,1... | collective-permute-start | bytes 454664 | tf_op jit(solution)/shard_map/ppermute | solution.py:402
  52.2 4.3 %collective-permute-start.6 = (f32[4,16,128]{2,1,0:T(8,128)S(1)}, f32[4,16,128]{2,1,0:T(8,128)S(1)}, u32[]{:S(2)}, u32[]{:S(2)}) collective-permute-start(f32[4,16,128]{2,1,0:T(8,128)S(1)} %get-tuple-element.33), channel_id=1, source_target_pairs={{0,128},{32,160},{64,192},{96,224},{1,129},{33,161},{65,193},{97,2... | collective-permute-start | bytes 98312 | tf_op jit(solution)/shard_map/ppermute | solution.py:406
  52.9 14.0 %copy-start.5 = (f32[3,2,2,16,320]{4,3,2,1,0:T(8,128)S(1)}, f32[3,2,2,16,320]{4,3,2,1,0:T(8,128)}, u32[]{:S(2)}) copy-start(f32[3,2,2,16,320]{4,3,2,1,0:T(8,128)} %param.7) | copy-start | bytes 737284
  52.9 14.0 %collective-permute-start.9 = (f32[296,128]{1,0:T(8,128)S(1)}, f32[296,128]{1,0:T(8,128)S(1)}, u32[]{:S(2)}, u32[]{:S(2)}) collective-permute-start(f32[296,128]{1,0:T(8,128)S(1)} %get-tuple-element.34.packed), channel_id=1, source_target_pairs={{256,384},{288,416},{320,448},{352,480},{257,385},{289,417},{321,4... | collective-permute-start | bytes 454664 | tf_op jit(solution)/shard_map/ppermute | solution.py:406
  56.8 2.3 %collective-permute-start.8 = (f32[4,16,128]{2,1,0:T(8,128)S(1)}, f32[4,16,128]{2,1,0:T(8,128)S(1)}, u32[]{:S(2)}, u32[]{:S(2)}) collective-permute-start(f32[4,16,128]{2,1,0:T(8,128)S(1)} %shard_map.82), channel_id=1, source_target_pairs={{128,384},{160,416},{192,448},{224,480},{129,385},{161,417},{193,4... | collective-permute-start | bytes 98312 | tf_op jit(solution)/shard_map/ppermute | solution.py:406
  57.4 9.5 %collective-permute-start.7 = (f32[4,16,128]{2,1,0:T(8,128)S(1)}, f32[4,16,128]{2,1,0:T(8,128)S(1)}, u32[]{:S(2)}, u32[]{:S(2)}) collective-permute-start(f32[4,16,128]{2,1,0:T(8,128)S(1)} %shard_map.82), channel_id=1, source_target_pairs={{128,256},{160,288},{192,320},{224,352},{129,257},{161,289},{193,3... | collective-permute-start | bytes 98312 | tf_op jit(solution)/shard_map/ppermute | solution.py:406
  69.1 15.4 %collective-permute-start.10 = (f32[6,16,128]{2,1,0:T(8,128)S(1)}, f32[6,16,128]{2,1,0:T(8,128)S(1)}, u32[]{:S(2)}, u32[]{:S(2)}) collective-permute-start(f32[6,16,128]{2,1,0:T(8,128)S(1)} %get-tuple-element.42), channel_id=1, source_target_pairs={{2,4},{4,2},{6,8},{8,6},{10,12},{12,10},{14,16},{16,14},{18,20},{2... | collective-permute-start | bytes 147464 | tf_op jit(solution)/shard_map/ppermute | solution.py:394
  71.8 12.6 %collective-permute-start.12 = (f32[6,16,128]{2,1,0:T(8,128)S(1)}, f32[6,16,128]{2,1,0:T(8,128)S(1)}, u32[]{:S(2)}, u32[]{:S(2)}) collective-permute-start(f32[6,16,128]{2,1,0:T(8,128)S(1)} %get-tuple-element.44), channel_id=1, source_target_pairs={{0,2},{2,0},{4,6},{6,4},{8,10},{10,8},{12,14},{14,12},{16,18},{18,... | collective-permute-start | bytes 147464 | tf_op jit(solution)/shard_map/ppermute | solution.py:396
  74.6 9.9 %collective-permute-start.13 = (f32[6,16,128]{2,1,0:T(8,128)S(1)}, f32[6,16,128]{2,1,0:T(8,128)S(1)}, u32[]{:S(2)}, u32[]{:S(2)}) collective-permute-start(f32[6,16,128]{2,1,0:T(8,128)S(1)} %get-tuple-element.45), channel_id=1, source_target_pairs={{0,1},{1,0},{2,3},{3,2},{4,5},{5,4},{6,7},{7,6},{8,9},{9,8},{10,11... | collective-permute-start | bytes 147464 | tf_op jit(solution)/shard_map/ppermute | solution.py:397
  79.8 4.7 %collective-permute-start.11 = (f32[4,16,128]{2,1,0:T(8,128)S(1)}, f32[4,16,128]{2,1,0:T(8,128)S(1)}, u32[]{:S(2)}, u32[]{:S(2)}) collective-permute-start(f32[4,16,128]{2,1,0:T(8,128)S(1)} %get-tuple-element.43), channel_id=1, source_target_pairs={{32,0},{64,32},{96,64},{128,96},{160,128},{192,160},{224,192},{256... | collective-permute-start | bytes 98312 | tf_op jit(solution)/shard_map/ppermute | solution.py:395

commit v2 on v1

--- a/solution.py
+++ b/solution.py
@@ -90,32 +90,45 @@
     return jnp.where(lane < 32, first, jnp.where(lane < 64, second, third))
 
 
-def put_faces(layer, cells, up, traces, inner, outer, across, below):
+def side_table():
+    row = lax.broadcasted_iota(jnp.int32, (ROWS, LANES), 0)
+    lane = lane_ids(1)
+    blocks = []
+    for face in SLOT_FACES:
+        start, a_step, b_step = FACE_ROWS[face]
+        source = (lane >> 4) * NODES + start + (lane >> 2 & 3) * a_step + (lane & 3) * b_step
+        source = jnp.where(lane < TRACE, source, -1)
+        blocks.append(jnp.where(row == source, 1.0, 0.0).astype(BF16))
+    return jnp.concatenate(blocks, axis=1)
+
+
+def put_faces(cells, up, traces, inner, outer, across, below):
     core = lax.axis_index("cy")
     even = lax.rem(lax.axis_index("cx"), 2) == 0
-    blocks = blocks_of(jnp.concatenate(cells, axis=0))
-    faces = [face_of(blocks, face) for face in SLOT_FACES]
-    block = lambda e, s: faces[s][VECS * e : VECS * (e + 1)]
-    for e in range(PATCH):
-        for s in range(len(SLOT_FACES)):
-            traces[layer * PATCH + e, :, s * LANES : (s + 1) * LANES] = stacked(block(e, s))
-    for b in range(EY):
-        east, west = block(EY + b, 1), block(b, 2)
-        inner[layer * EY + b] = jnp.where(even, east, west)
-        outer[layer * EY + b] = jnp.where(even, west, east)
-    for a in range(EX):
-        across[layer * EX + a] = jnp.where(core == 0, block(a * EY + 1, 3), block(a * EY, 4))
-    if layer == 0:
-        for e in range(PATCH):
-            below[up[e]] = block(e, 0)
+    picked = dot(jnp.concatenate([stacked(x) for x in cells], axis=0), side_table())
+    whole = []
+    for at in range(CELLS):
+        piece = picked[2 * VECS * at : 2 * VECS * (at + 1)]
+        traces[at] = piece.astype(BF16)
+        whole.append(halves(piece))
+    for layer in range(LAYERS):
+        block = lambda e, s: whole[layer * PATCH + e][:, s * LANES : (s + 1) * LANES]
+        for b in range(EY):
+            east, west = block(EY + b, 1), block(b, 2)
+            inner[layer * EY + b] = jnp.where(even, east, west)
+            outer[layer * EY + b] = jnp.where(even, west, east)
+        for a in range(EX):
+            across[layer * EX + a] = jnp.where(core == 0, block(a * EY + 1, 3), block(a * EY, 4))
+    for e in range(PATCH):
+        below[up[e]] = whole[e][:, :LANES]
+    for e in range(PATCH, LAYERS * EY):
+        below[e] = jnp.zeros((VECS, LANES), F32)
 
 
 def open_kernel(links, old, up, traces, inner, outer, across, below):
     for at in range(CELLS):
         up[at] = links[at % PATCH // EY, at % EY, at // PATCH]
-    for layer in range(LAYERS):
-        cells = [old[layer * PATCH + e] for e in range(PATCH)]
-        put_faces(layer, cells, up, traces, inner, outer, across, below)
+    put_faces([old[at] for at in range(CELLS)], up, traces, inner, outer, across, below)
 
 
 def place_downstream(up, traces, from_above, down):
@@ -189,23 +202,60 @@
         composed[e] = -times(first_two[up[2 * PATCH + e]], passing[2 * PATCH + e])
 
 
+def turned(x, by):
+    return pltpu.roll(x, by % LANES, 1)
+
+
 def pack(maps, ends):
-    lane = lane_ids(MAP_ROWS)
-    fourth = maps[3]
-    one = jnp.where(lane < TRACE, maps[0], pltpu.roll(fourth, TRACE, 1))
-    two = jnp.where(lane < TRACE, maps[1], pltpu.roll(fourth, 2 * TRACE - LANES, 1))
-    return jnp.concatenate([one, two, maps[2], ends], axis=0)
+    lane = lane_ids(TRACE)
+    square = [x[:TRACE] for x in maps]
+    source = [x[TRACE:] for x in maps]
+    all_sources = jnp.concatenate(source, axis=0)
+    part = lane_ids(VECS) >> 4
+    last = jnp.where(part == 5, turned(source[0], 16), jnp.where(part == 6, turned(source[1], 32), turned(source[2], 48)))
+    one = jnp.where(lane < TRACE, square[0], turned(square[3], TRACE))
+    rest = jnp.concatenate([turned(all_sources, 64), turned(source[3], 48)], axis=0)
+    two = jnp.where(lane < TRACE, square[1], jnp.where(lane < 112, turned(square[3], 32), rest))
+    three = jnp.where(lane < TRACE, square[2], jnp.concatenate([turned(all_sources, TRACE), last], axis=0))
+    return jnp.concatenate([one, two, three, ends], axis=0)
 
 
 def unpack(packed):
-    lane = lane_ids(MAP_ROWS)
-    one, two, three = [packed[MAP_ROWS * at : MAP_ROWS * (at + 1)] for at in range(3)]
-    fourth = jnp.where(
-        lane < LANES - TRACE, pltpu.roll(one, LANES - TRACE, 1), pltpu.roll(two, 2 * LANES - 2 * TRACE, 1)
-    )
-    used = lane < TRACE
-    maps = [jnp.where(used, x, 0.0) for x in (one, two, three, fourth)]
-    return maps, packed[3 * MAP_ROWS : 3 * MAP_ROWS + 8]
+    lane = lane_ids(TRACE)
+    one, two, three = [packed[TRACE * at : TRACE * (at + 1)] for at in range(3)]
+    four = jnp.where(lane < 48, turned(one, 48), turned(two, 96))
+    square = [jnp.where(lane < TRACE, x, 0.0) for x in (one, two, three, four)]
+    lane = lane_ids(PATCH * VECS)
+    most = jnp.where(lane < 48, turned(three[: PATCH * VECS], 48), turned(two[: PATCH * VECS], 64))
+    ends = [turned(three[PATCH * VECS :], by) for by in (112, 96, 80)] + [turned(two[PATCH * VECS :], 80)]
+    lane = lane_ids(VECS)
+    maps = []
+    for at in range(PATCH):
+        source = jnp.where(lane < 64, most[VECS * at : VECS * (at + 1)], jnp.where(lane < TRACE, ends[at], 0.0))
+        maps.append(jnp.concatenate([square[at], source], axis=0))
+    return maps, packed[3 * TRACE : 3 * TRACE + 8]
+
+
+def pack_states(states):
+    lane = lane_ids(VECS)
+    one = jnp.where(lane < TRACE, states[0], turned(states[3], TRACE))
+    two = jnp.where(lane < TRACE, states[1], turned(states[3], 32))
+    return jnp.concatenate([one, two, states[2]], axis=0)
+
+
+def unpack_states(packed):
+    lane = lane_ids(VECS)
+    one, two, three = [packed[VECS * at : VECS * (at + 1)] for at in range(3)]
+    four = jnp.where(lane < 48, turned(one, 48), turned(two, 96))
+    return [jnp.where(lane < TRACE, x, 0.0) for x in (one, two, three, four)]
+
+
+def rows_of(ends):
+    return [ends[at : at + 1] for at in range(PATCH)]
+
+
+def ends_of(rows):
+    return jnp.concatenate(list(rows) + [jnp.zeros((8 - PATCH, LANES), F32)], axis=0)
 
 
 def chosen(items, at):
@@ -213,14 +263,6 @@
     for number in range(1, PATCH):
         out = jnp.where(at == number, items[number], out)
     return out
-
-
-def rows_of(ends):
-    return [ends[at : at + 1] for at in range(PATCH)]
-
-
-def ends_of(rows):
-    return jnp.concatenate(list(rows) + [jnp.zeros((8 - PATCH, LANES), F32)], axis=0)
 
 
 def placed(states, ends):
@@ -240,7 +282,7 @@
 
 
 def source_kernel(
-    up, rhs, traces, outer, from_above, inner, from_across, diag, coupling, lift, passing, composed,
+    up, rhs, traces, from_above, outer, inner, from_across, diag, coupling, lift, passing, composed,
     solved, sources, packed, down, current, maps,
 ):
     place_downstream(up, traces, from_above, down)
@@ -287,8 +329,7 @@
 def group_kernel(mine, theirs, packed, leaving):
     maps, ends, *unused = joined(mine[...], theirs[...], 1)
     packed[...] = pack(maps, ends_of(ends))
-    for at, state in enumerate(placed([x[TRACE:] for x in maps], ends)):
-        leaving[at] = state
+    leaving[...] = pack_states(placed([x[TRACE:] for x in maps], ends))
 
 
 def prefix_kernel(pair, theirs, prefixes, ends):
@@ -312,22 +353,24 @@
 
 def onward_kernel(entering, packed, leaving):
     maps, ends = unpack(packed[...])
-    states = [after(entering[at], maps[at]) for at in range(PATCH)]
-    for at, state in enumerate(placed(states, rows_of(ends))):
-        leaving[at] = state
+    states = unpack_states(entering[...])
+    states = [after(states[at], maps[at]) for at in range(PATCH)]
+    leaving[...] = pack_states(placed(states, rows_of(ends)))
 
 
 def finish_kernel(
-    up, second, third, fourth, before, prefixes, ends, old, solved, sources, weights, passing,
-    new, traces, inner, outer, across, below, arrived, current,
+    up, second, fourth, third, before, prefixes, ends, old, solved, sources, weights, passing,
+    new, traces, inner, outer, across, below, arrived, current, made, sems,
 ):
     maps, map_ends = unpack(before[...])
+    second, fourth, third = [unpack_states(x[...]) for x in (second, fourth, third)]
     states = [after(fourth[at], maps[at]) for at in range(PATCH)]
     last = placed(states, rows_of(map_ends))
     entering = [second[at] + third[at] + last[at] for at in range(PATCH)]
     states = [after(entering[at], prefixes[at]) for at in range(PATCH)]
     for at, state in enumerate(placed(states, rows_of(ends))):
         arrived[at] = state
+    changes, copies = [], []
     for layer in range(LAYERS):
         inflow = []
         for e in range(PATCH):
@@ -337,16 +380,18 @@
             for e in range(PATCH):
                 at = layer * PATCH + e
                 current[e] = sources[at] - times(inflow[e], passing[at])
-        changes = []
         for e in range(PATCH):
             at = layer * PATCH + e
             x = solved[at] - times(inflow[e], weights[at])
-            new[at] = x
+            made[at] = x
             changes.append(old[at] - x)
-        put_faces(layer, changes, up, traces, inner, outer, across, below)
-
-
-def residual_kernel(up, traces, outer, from_above, inner, from_across, coupling, lift, out, down):
+    copy = pltpu.make_async_copy(made, new, sems.at[0])
+    copy.start()
+    put_faces(changes, up, traces, inner, outer, across, below)
+    copy.wait()
+
+
+def residual_kernel(up, traces, from_above, outer, inner, from_across, coupling, lift, out, down):
     place_downstream(up, traces, from_above, down)
     for layer in range(LAYERS):
         lifts = lifted_layer(layer, traces, down, inner, outer, from_across, coupling, lift)
@@ -356,14 +401,15 @@
 
 VMEM = pl.BlockSpec(memory_space=pltpu.VMEM)
 SMEM = pl.BlockSpec(memory_space=pltpu.SMEM)
-
-
-def call(kernel, scalars, outs, scratch=(), scalar_outs=(), micros=1):
+FAR = pl.BlockSpec(memory_space=pl.ANY)
+
+
+def call(kernel, scalars, outs, scratch=(), scalar_outs=(), far_outs=(), micros=1):
     def run(*args):
         return pl.pallas_call(
             kernel,
             in_specs=[SMEM] * scalars + [VMEM] * (len(args) - scalars),
-            out_specs=[SMEM if i in scalar_outs else VMEM for i in range(len(outs))],
+            out_specs=[SMEM if i in scalar_outs else FAR if i in far_outs else VMEM for i in range(len(outs))],
             out_shape=[jax.ShapeDtypeStruct(shape, kind) for shape, kind in outs],
             scratch_shapes=list(scratch),
             compiler_params=pltpu.CompilerParams(vmem_limit_bytes=16 * 1024 * 1024),
@@ -380,11 +426,11 @@
     ((LAYERS * EY, VECS, LANES), F32),
     ((LAYERS * EY, VECS, LANES), F32),
     ((LAYERS * EX, VECS, LANES), F32),
-    ((PATCH, VECS, LANES), F32),
+    ((LAYERS * EY, VECS, LANES), F32),
 ]
 FIELD = ((CELLS, VECS, ROWS), F32)
-STATES = ((PATCH, VECS, LANES), F32)
-PACKED = ((3 * MAP_ROWS + 8, LANES), F32)
+STATES = ((3 * VECS, LANES), F32)
+PACKED = ((3 * TRACE + 8, LANES), F32)
 DOWN = pltpu.VMEM((CELLS, 2 * VECS, LANES), BF16)
 HELD = pltpu.VMEM((PATCH, VECS, LANES), F32)
 
@@ -395,15 +441,16 @@
     below = lax.ppermute(below, "sweep", [(i + 1, i) for i in range(deep - 1)])
     inner = lax.ppermute(inner, "cx", [(i, i ^ 1) for i in range(wide)])
     across = lax.ppermute(across, "cy", [(0, 1), (1, 0)])
-    return outer, below, inner, across
+    return below, outer, inner, across
 
 
 def swapped(packed, by):
     return lax.ppermute(packed, "sweep", [(i, i ^ by) for i in range(lax.axis_size("sweep"))])
 
 
-def passed(states, source, target):
-    return lax.ppermute(states, "sweep", [(GROUP * source + p, GROUP * target + p) for p in range(GROUP)])
+def passed(states, source, target, shift):
+    pairs = [(GROUP * source + p, GROUP * target + (p + shift) % GROUP) for p in range(GROUP)]
+    return lax.ppermute(states, "sweep", pairs)
 
 
 def local(rhs_vectors, old_iterate, diag_inverse, coupling, lift_table, upstream):
@@ -432,16 +479,22 @@
     (pair,) = call(pair_kernel, 0, [PACKED])(single, partner)
     partner_pair = swapped(pair, 2)
     group, leaving = call(group_kernel, 0, [PACKED, STATES])(pair, partner_pair)
-    second = passed(leaving, 0, 1)
-    before = passed(group, 2, 3)
+    second = passed(leaving, 0, 1, 2)
+    before = passed(group, 2, 3, 2)
     prefixes, ends = call(prefix_kernel, 0, [((PATCH, MAP_ROWS, LANES), F32), ((8, LANES), F32)])(
         partner, partner_pair
     )
     (leaving,) = call(onward_kernel, 0, [STATES])(second, group)
-    third = passed(leaving, 1, 2)
-    fourth = passed(leaving, 1, 3)
-    new, traces, *sends = call(finish_kernel, 1, [FIELD] + FACE_OUTS, [HELD, HELD])(
-        up, second, third, fourth, before, prefixes, ends, old, solved, sources, weights, passing
+    third = passed(leaving, 1, 2, 2)
+    fourth = passed(leaving, 1, 3, 0)
+    new, traces, *sends = call(
+        finish_kernel,
+        1,
+        [FIELD] + FACE_OUTS,
+        [HELD, HELD, pltpu.VMEM((CELLS, VECS, ROWS), F32), pltpu.SemaphoreType.DMA((1,))],
+        far_outs=(0,),
+    )(
+        up, second, fourth, third, before, prefixes, ends, old, solved, sources, weights, passing
     )
     halos = exchange_sides(*sends)
     (residual,) = call(residual_kernel, 1, [FIELD], [DOWN])(up, traces, *halos, blocks, lift)

time: 87.7 us -> 81.3 us (0.927)
  waiting for transfers between devices: 26 us -> 20 us
    ppermute x2, waiting for transfers between devices: 2.73 us -> 0.01 us  [exchange_sides(): below = lax.ppermute(below, 'sweep', [(i + 1, i) for i in range(deep - 1)])]
    ppermute x4, waiting for transfers between devices: 7.81 us -> 5.26 us  [passed(): return lax.ppermute(states, 'sweep', pairs)]
    ppermute x4, starting transfers between devices: 6.27 us -> 4.06 us  [passed(): return lax.ppermute(states, 'sweep', pairs)]
    ppermute x2, starting transfers between devices: 7.41 us -> 9.34 us  [exchange_sides(): below = lax.ppermute(below, 'sweep', [(i + 1, i) for i in range(deep - 1)])]
    ppermute x2, waiting for transfers between devices: 15.4 us -> 13.9 us  [swapped(): lax.ppermute(packed, 'sweep', [(i, i ^ by) for i in range(lax.axis_size('...]
where the time goes in v2:
time: 81.3 us; the launch traced here: 80.5 us
  starting transfers between devices  44 us (54%)
  waiting for transfers between devices  20 us (25%)
  Pallas kernels  14 us (17%)
  local copies, waits for them, and re-layouts  1.66 us (2%)
  between operations  0.92 us (1%)
    pallas_call x9, Pallas kernels, run(): pl.pallas_call(kernel, in_specs=[SMEM] * scalars + [VMEM] * (len(args) -...  14 us
    ppermute x2, starting transfers between devices, exchange_sides(): lax.ppermute(outer, 'cx', [(i, i + 1 if i % 2 else i - 1) for i in range(...  13.9 us
    ppermute x2, waiting for transfers between devices, swapped(): lax.ppermute(packed, 'sweep', [(i, i ^ by) for i in range(lax.axis_size('...  13.9 us
    ppermute x2, starting transfers between devices, exchange_sides(): below = lax.ppermute(below, 'sweep', [(i + 1, i) for i in range(deep - 1)])  9.34 us
    ppermute x2, starting transfers between devices, exchange_sides(): across = lax.ppermute(across, 'cy', [(0, 1), (1, 0)])  8.11 us
    ppermute x4, waiting for transfers between devices, passed(): return lax.ppermute(states, 'sweep', pairs)  5.26 us
    ppermute x2, starting transfers between devices, exchange_sides(): inner = lax.ppermute(inner, 'cx', [(i, i ^ 1) for i in range(wide)])  4.73 us
    ppermute x4, starting transfers between devices, passed(): return lax.ppermute(states, 'sweep', pairs)  4.06 us
  transfers between devices with their start and end apart: 14, of which 4 were waited for; matrix products, arithmetic and copies ran while one was open for 0% of the time, Pallas kernels for 5%

profile of v2, /device:TPU:7, one launch (start us, length us, event | category | flops | bytes accessed | tf_op | source)
XLA Modules:
  0.0 80.5 jit_solution(12472750180181381389)
XLA Ops:
  0.6 0.0 copy-start.4
  0.6 1.0 %copy-done.4 = f32[3,2,2,16,320]{4,3,2,1,0:T(8,128)S(1)} copy-done((f32[3,2,2,16,320]{4,3,2,1,0:T(8,128)S(1)}, f32[3,2,2,16,320]{4,3,2,1,0:T(8,128)}, u32[]{:S(2)}) %copy-start.4) | copy-done | bytes 245784
  1.6 0.7 copy-done.6
  2.3 1.5 %shard_map.77 = (s32[12]{0:T(128)S(1)}, bf16[12,32,640]{2,1,0:T(8,128)(2,1)S(1)}, f32[6,16,128]{2,1,0:T(8,128)S(1)}, f32[6,16,128]{2,1,0:T(8,128)S(1)}, f32[6,16...) custom-call(s32[2,2,3]{2,1,0:T(2,128)S(1)} %bitcast.19, f32[12,16,320]{2,1,0:T(8,128)S(1)} %bitcast.17), custom_call_target="tpu_custom_call" | custom-call | flops 2000000000 | bytes 7200000 | tf_op jit(solution)/shard_map/pallas_call | solution.py:409
  3.8 0.0 copy-start.3
  3.8 5.5 %collective-permute-start = (f32[6,16,128]{2,1,0:T(8,128)S(1)}, f32[6,16,128]{2,1,0:T(8,128)S(1)}, u32[]{:S(2)}, u32[]{:S(2)}) collective-permute-start(f32[6,16,128]{2,1,0:T(8,128)S(1)} %get-tuple-element.26), channel_id=1, source_target_pairs={{32,0},{64,32},{96,64},{128,96},{160,128},{192,160},{224,192},{256... | collective-permute-start | bytes 147464 | tf_op jit(solution)/shard_map/ppermute | solution.py:441
  9.3 11.2 %collective-permute-start.1 = (f32[6,16,128]{2,1,0:T(8,128)S(1)}, f32[6,16,128]{2,1,0:T(8,128)S(1)}, u32[]{:S(2)}, u32[]{:S(2)}) collective-permute-start(f32[6,16,128]{2,1,0:T(8,128)S(1)} %get-tuple-element.27), channel_id=1, source_target_pairs={{2,4},{4,2},{6,8},{8,6},{10,12},{12,10},{14,16},{16,14},{18,20},{2... | collective-permute-start | bytes 147464 | tf_op jit(solution)/shard_map/ppermute | solution.py:440
  20.6 1.9 %collective-permute-start.2 = (f32[6,16,128]{2,1,0:T(8,128)S(1)}, f32[6,16,128]{2,1,0:T(8,128)S(1)}, u32[]{:S(2)}, u32[]{:S(2)}) collective-permute-start(f32[6,16,128]{2,1,0:T(8,128)S(1)} %get-tuple-element.28), channel_id=1, source_target_pairs={{0,2},{2,0},{4,6},{6,4},{8,10},{10,8},{12,14},{14,12},{16,18},{18,... | collective-permute-start | bytes 147464 | tf_op jit(solution)/shard_map/ppermute | solution.py:442
  22.5 3.1 %collective-permute-start.3 = (f32[6,16,128]{2,1,0:T(8,128)S(1)}, f32[6,16,128]{2,1,0:T(8,128)S(1)}, u32[]{:S(2)}, u32[]{:S(2)}) collective-permute-start(f32[6,16,128]{2,1,0:T(8,128)S(1)} %get-tuple-element.29), channel_id=1, source_target_pairs={{0,1},{1,0},{2,3},{3,2},{4,5},{5,4},{6,7},{7,6},{8,9},{9,8},{10,11... | collective-permute-start | bytes 147464 | tf_op jit(solution)/shard_map/ppermute | solution.py:443
  25.7 3.7 %shard_map.78 = (bf16[12,256,320]{2,1,0:T(8,128)(2,1)S(1)}, bf16[12,256,128]{2,1,0:T(8,128)(2,1)S(1)}, f32[4,80,128]{2,1,0:T(8,128)S(1)}) custom-call(s32[12]{0:T(128)S(1)} %get-tuple-element.24.up, bf16[12,320,320]{2,1,0:T(8,128)(2,1)S(1)} %bitcast.8, bf16[12,80,480]{2,1,0:T(8,128)(2,1)S(1)} %bitcast.10, bf16[320,480]{1,0:T(8,128)(2,1)S(1)} %bitcast.13), custom_call_target="tpu_custom_call" | custom-call | flops 1000000000 | bytes 3600000 | tf_op jit(solution)/shard_map/pallas_call | solution.py:409
  29.4 2.6 %shard_map.79 = (f32[12,16,320]{2,1,0:T(8,128)S(1)}, f32[12,16,128]{2,1,0:T(8,128)S(1)}, f32[248,128]{1,0:T(8,128)S(1)}) custom-call(s32[12]{0:T(128)S(1)} %get-tuple-element.24.up, f32[12,16,320]{2,1,0:T(8,128)S(1)} %bitcast.16, bf16[12,32,640]{2,1,0:T(8,128)(2,1)S(1)} %get-tuple-element.25.traces, f32[6,16,128]{2,1,0:T(8,128)S(1)} %collective-permute-done.from_above, ...), custom_call_target="tpu_custom_call" | custom-call | flops 1000000000 | bytes 3600000 | tf_op jit(solution)/shard_map/pallas_call | solution.py:409
  32.0 1.9 %collective-permute-start.4 = (f32[248,128]{1,0:T(8,128)S(1)}, f32[248,128]{1,0:T(8,128)S(1)}, u32[]{:S(2)}, u32[]{:S(2)}) collective-permute-start(f32[248,128]{1,0:T(8,128)S(1)} %get-tuple-element.32.mine), channel_id=1, source_target_pairs={{0,32},{32,0},{64,96},{96,64},{128,160},{160,128},{192,224},{224,1... | collective-permute-start | bytes 380936 | tf_op jit(solution)/shard_map/ppermute | solution.py:448
  33.9 5.0 %collective-permute-done.4.theirs.pair = f32[248,128]{1,0:T(8,128)S(1)} collective-permute-done((f32[248,128]{1,0:T(8,128)S(1)}, f32[248,128]{1,0:T(8,128)S(1)}, u32[]{:S(2)}, u32[]{:S(2)}) %collective-permute-start.4) | collective-permute-done | bytes 127008 | tf_op jit(solution)/shard_map/ppermute | solution.py:448
  38.9 0.4 shard_map.80.mine
  39.4 1.9 %collective-permute-start.5 = (f32[248,128]{1,0:T(8,128)S(1)}, f32[248,128]{1,0:T(8,128)S(1)}, u32[]{:S(2)}, u32[]{:S(2)}) collective-permute-start(f32[248,128]{1,0:T(8,128)S(1)} %shard_map.80.mine), channel_id=1, source_target_pairs={{0,64},{32,96},{64,0},{96,32},{128,192},{160,224},{192,128},{224,1... | collective-permute-start | bytes 380936 | tf_op jit(solution)/shard_map/ppermute | solution.py:448
  41.3 8.8 %collective-permute-done.5.theirs = f32[248,128]{1,0:T(8,128)S(1)} collective-permute-done((f32[248,128]{1,0:T(8,128)S(1)}, f32[248,128]{1,0:T(8,128)S(1)}, u32[]{:S(2)}, u32[]{:S(2)}) %collective-permute-start.5) | collective-permute-done | bytes 127008 | tf_op jit(solution)/shard_map/ppermute | solution.py:448
  50.2 0.4 shard_map.81
  50.6 0.7 collective-permute-start.6
  51.3 0.0 copy-start.5
  51.3 1.4 %collective-permute-start.9 = (f32[248,128]{1,0:T(8,128)S(1)}, f32[248,128]{1,0:T(8,128)S(1)}, u32[]{:S(2)}, u32[]{:S(2)}) collective-permute-start(f32[248,128]{1,0:T(8,128)S(1)} %get-tuple-element.34.packed), channel_id=1, source_target_pairs={{256,448},{288,480},{320,384},{352,416},{257,449},{289,481},{321,3... | collective-permute-start | bytes 380936 | tf_op jit(solution)/shard_map/ppermute | solution.py:453
  52.7 0.3 shard_map.82
  53.0 1.3 %collective-permute-start.8 = (f32[48,128]{1,0:T(8,128)S(1)}, f32[48,128]{1,0:T(8,128)S(1)}, u32[]{:S(2)}, u32[]{:S(2)}) collective-permute-start(f32[48,128]{1,0:T(8,128)S(1)} %shard_map.82), channel_id=1, source_target_pairs={{128,320},{160,352},{192,256},{224,288},{129,321},{161,353},{193,2... | collective-permute-start | bytes 73736 | tf_op jit(solution)/shard_map/ppermute | solution.py:453
  54.3 0.7 collective-permute-start.7
  55.0 0.4 shard_map.83
  55.4 5.2 %collective-permute-done.8.third = f32[48,128]{1,0:T(8,128)S(1)} collective-permute-done((f32[48,128]{1,0:T(8,128)S(1)}, f32[48,128]{1,0:T(8,128)S(1)}, u32[]{:S(2)}, u32[]{:S(2)}) %collective-permute-start.8) | collective-permute-done | bytes 24608 | tf_op jit(solution)/shard_map/ppermute | solution.py:453
  60.6 2.4 %shard_map.84 = (f32[12,16,320]{2,1,0:T(8,128)}, bf16[12,32,640]{2,1,0:T(8,128)(2,1)S(1)}, f32[6,16,128]{2,1,0:T(8,128)S(1)}, f32[6,16,128]{2,1,0:T(8,128)S(1)},...) custom-call(s32[12]{0:T(128)S(1)} %get-tuple-element.24.up, f32[48,128]{1,0:T(8,128)S(1)} %collective-permute-done.6.entering.second, ...), custom_call_target="tpu_custom_call" | custom-call | flops 1000000000 | bytes 3600000 | tf_op jit(solution)/shard_map/pallas_call | solution.py:409
  63.0 3.8 %collective-permute-start.10 = (f32[6,16,128]{2,1,0:T(8,128)S(1)}, f32[6,16,128]{2,1,0:T(8,128)S(1)}, u32[]{:S(2)}, u32[]{:S(2)}) collective-permute-start(f32[6,16,128]{2,1,0:T(8,128)S(1)} %get-tuple-element.42), channel_id=1, source_target_pairs={{32,0},{64,32},{96,64},{128,96},{160,128},{192,160},{224,192},{256... | collective-permute-start | bytes 147464 | tf_op jit(solution)/shard_map/ppermute | solution.py:441
  66.9 2.7 %collective-permute-start.11 = (f32[6,16,128]{2,1,0:T(8,128)S(1)}, f32[6,16,128]{2,1,0:T(8,128)S(1)}, u32[]{:S(2)}, u32[]{:S(2)}) collective-permute-start(f32[6,16,128]{2,1,0:T(8,128)S(1)} %get-tuple-element.43), channel_id=1, source_target_pairs={{2,4},{4,2},{6,8},{8,6},{10,12},{12,10},{14,16},{16,14},{18,20},{2... | collective-permute-start | bytes 147464 | tf_op jit(solution)/shard_map/ppermute | solution.py:440
  69.6 2.8 %collective-permute-start.12 = (f32[6,16,128]{2,1,0:T(8,128)S(1)}, f32[6,16,128]{2,1,0:T(8,128)S(1)}, u32[]{:S(2)}, u32[]{:S(2)}) collective-permute-start(f32[6,16,128]{2,1,0:T(8,128)S(1)} %get-tuple-element.44), channel_id=1, source_target_pairs={{0,2},{2,0},{4,6},{6,4},{8,10},{10,8},{12,14},{14,12},{16,18},{18,... | collective-permute-start | bytes 147464 | tf_op jit(solution)/shard_map/ppermute | solution.py:442
  72.4 5.0 %collective-permute-start.13 = (f32[6,16,128]{2,1,0:T(8,128)S(1)}, f32[6,16,128]{2,1,0:T(8,128)S(1)}, u32[]{:S(2)}, u32[]{:S(2)}) collective-permute-start(f32[6,16,128]{2,1,0:T(8,128)S(1)} %get-tuple-element.45), channel_id=1, source_target_pairs={{0,1},{1,0},{2,3},{3,2},{4,5},{5,4},{6,7},{7,6},{8,9},{9,8},{10,11... | collective-permute-start | bytes 147464 | tf_op jit(solution)/shard_map/ppermute | solution.py:443
  77.4 0.8 %collective-permute-done.13.from_across = f32[6,16,128]{2,1,0:T(8,128)S(1)} collective-permute-done((f32[6,16,128]{2,1,0:T(8,128)S(1)}, f32[6,16,128]{2,1,0:T(8,128)S(1)}, u32[]{:S(2)}, u32[]{:S(2)}) %collective-permute-start.13) | collective-permute-done | bytes 49184 | tf_op jit(solution)/shard_map/ppermute | solution.py:443
  78.3 2.3 %shard_map.85 = f32[12,16,320]{2,1,0:T(8,128)} custom-call(s32[12]{0:T(128)S(1)} %get-tuple-element.24.up, bf16[12,32,640]{2,1,0:T(8,128)(2,1)S(1)} %get-tuple-element.41.traces, f32[6,16,128]{2,1,0:T(8,128)S(1)} %collective-permute-done.10.from_above, f32[6,16,128]{2,1,0:T(8,128)S(1)} %collective-permute-done.11.outer, ...), custom_call_target="tpu_custom_call" | custom-call | flops 1000000000 | bytes 3600000 | tf_op jit(solution)/shard_map/pallas_call | solution.py:409
  (19 shorter events, 0.0 us)
Async XLA Ops:
  0.6 1.0 %copy-start.4 = (f32[3,2,2,16,320]{4,3,2,1,0:T(8,128)S(1)}, f32[3,2,2,16,320]{4,3,2,1,0:T(8,128)}, u32[]{:S(2)}) copy-start(f32[3,2,2,16,320]{4,3,2,1,0:T(8,128)} %param.7) | copy-start | bytes 737284
  1.6 0.7 copy-start.6
  2.3 23.4 %copy-start = (bf16[3,2,2,320,320]{4,3,2,1,0:T(8,128)(2,1)S(1)}, bf16[3,2,2,320,320]{4,3,2,1,0:T(8,128)(2,1)}, u32[]{:S(2)}) copy-start(bf16[3,2,2,320,320]{4,3,2,1,0:T(8,128)(2,1)} %param.8) | copy-start | bytes 7372804
  2.3 23.4 %copy-start.1 = (bf16[3,2,2,80,480]{4,3,2,1,0:T(8,128)(2,1)S(1)}, bf16[3,2,2,80,480]{4,3,2,1,0:T(8,128)(2,1)}, u32[]{:S(2)}) copy-start(bf16[3,2,2,80,480]{4,3,2,1,0:T(8,128)(2,1)} %param.9) | copy-start | bytes 2764804
  2.3 23.4 %copy-start.2 = (bf16[480,320]{0,1:T(8,128)(2,1)S(1)}, bf16[480,320]{0,1:T(8,128)(2,1)}, u32[]{:S(2)}) copy-start(bf16[480,320]{0,1:T(8,128)(2,1)} %param.10) | copy-start | bytes 921604
  3.8 25.6 %copy-start.3 = (f32[3,2,2,16,320]{4,3,2,1,0:T(8,128)S(1)}, f32[3,2,2,16,320]{4,3,2,1,0:T(8,128)}, u32[]{:S(2)}) copy-start(f32[3,2,2,16,320]{4,3,2,1,0:T(8,128)} %param.6) | copy-start | bytes 737284
  3.8 25.5 %collective-permute-start = (f32[6,16,128]{2,1,0:T(8,128)S(1)}, f32[6,16,128]{2,1,0:T(8,128)S(1)}, u32[]{:S(2)}, u32[]{:S(2)}) collective-permute-start(f32[6,16,128]{2,1,0:T(8,128)S(1)} %get-tuple-element.26), channel_id=1, source_target_pairs={{32,0},{64,32},{96,64},{128,96},{160,128},{192,160},{224,192},{256... | collective-permute-start | bytes 147464 | tf_op jit(solution)/shard_map/ppermute | solution.py:441
  9.3 20.0 %collective-permute-start.1 = (f32[6,16,128]{2,1,0:T(8,128)S(1)}, f32[6,16,128]{2,1,0:T(8,128)S(1)}, u32[]{:S(2)}, u32[]{:S(2)}) collective-permute-start(f32[6,16,128]{2,1,0:T(8,128)S(1)} %get-tuple-element.27), channel_id=1, source_target_pairs={{2,4},{4,2},{6,8},{8,6},{10,12},{12,10},{14,16},{16,14},{18,20},{2... | collective-permute-start | bytes 147464 | tf_op jit(solution)/shard_map/ppermute | solution.py:440
  20.6 8.8 %collective-permute-start.2 = (f32[6,16,128]{2,1,0:T(8,128)S(1)}, f32[6,16,128]{2,1,0:T(8,128)S(1)}, u32[]{:S(2)}, u32[]{:S(2)}) collective-permute-start(f32[6,16,128]{2,1,0:T(8,128)S(1)} %get-tuple-element.28), channel_id=1, source_target_pairs={{0,2},{2,0},{4,6},{6,4},{8,10},{10,8},{12,14},{14,12},{16,18},{18,... | collective-permute-start | bytes 147464 | tf_op jit(solution)/shard_map/ppermute | solution.py:442
  22.5 6.9 %collective-permute-start.3 = (f32[6,16,128]{2,1,0:T(8,128)S(1)}, f32[6,16,128]{2,1,0:T(8,128)S(1)}, u32[]{:S(2)}, u32[]{:S(2)}) collective-permute-start(f32[6,16,128]{2,1,0:T(8,128)S(1)} %get-tuple-element.29), channel_id=1, source_target_pairs={{0,1},{1,0},{2,3},{3,2},{4,5},{5,4},{6,7},{7,6},{8,9},{9,8},{10,11... | collective-permute-start | bytes 147464 | tf_op jit(solution)/shard_map/ppermute | solution.py:443
  32.0 6.9 %collective-permute-start.4 = (f32[248,128]{1,0:T(8,128)S(1)}, f32[248,128]{1,0:T(8,128)S(1)}, u32[]{:S(2)}, u32[]{:S(2)}) collective-permute-start(f32[248,128]{1,0:T(8,128)S(1)} %get-tuple-element.32.mine), channel_id=1, source_target_pairs={{0,32},{32,0},{64,96},{96,64},{128,160},{160,128},{192,224},{224,1... | collective-permute-start | bytes 380936 | tf_op jit(solution)/shard_map/ppermute | solution.py:448
  39.4 10.8 %collective-permute-start.5 = (f32[248,128]{1,0:T(8,128)S(1)}, f32[248,128]{1,0:T(8,128)S(1)}, u32[]{:S(2)}, u32[]{:S(2)}) collective-permute-start(f32[248,128]{1,0:T(8,128)S(1)} %shard_map.80.mine), channel_id=1, source_target_pairs={{0,64},{32,96},{64,0},{96,32},{128,192},{160,224},{192,128},{224,1... | collective-permute-start | bytes 380936 | tf_op jit(solution)/shard_map/ppermute | solution.py:448
  50.6 2.1 %collective-permute-start.6 = (f32[48,128]{1,0:T(8,128)S(1)}, f32[48,128]{1,0:T(8,128)S(1)}, u32[]{:S(2)}, u32[]{:S(2)}) collective-permute-start(f32[48,128]{1,0:T(8,128)S(1)} %get-tuple-element.33), channel_id=1, source_target_pairs={{0,192},{32,224},{64,128},{96,160},{1,193},{33,225},{65,129},{97,1... | collective-permute-start | bytes 73736 | tf_op jit(solution)/shard_map/ppermute | solution.py:453
  51.3 9.4 %copy-start.5 = (f32[3,2,2,16,320]{4,3,2,1,0:T(8,128)S(1)}, f32[3,2,2,16,320]{4,3,2,1,0:T(8,128)}, u32[]{:S(2)}) copy-start(f32[3,2,2,16,320]{4,3,2,1,0:T(8,128)} %param.7) | copy-start | bytes 737284
  51.3 9.3 %collective-permute-start.9 = (f32[248,128]{1,0:T(8,128)S(1)}, f32[248,128]{1,0:T(8,128)S(1)}, u32[]{:S(2)}, u32[]{:S(2)}) collective-permute-start(f32[248,128]{1,0:T(8,128)S(1)} %get-tuple-element.34.packed), channel_id=1, source_target_pairs={{256,448},{288,480},{320,384},{352,416},{257,449},{289,481},{321,3... | collective-permute-start | bytes 380936 | tf_op jit(solution)/shard_map/ppermute | solution.py:453
  53.0 7.6 %collective-permute-start.8 = (f32[48,128]{1,0:T(8,128)S(1)}, f32[48,128]{1,0:T(8,128)S(1)}, u32[]{:S(2)}, u32[]{:S(2)}) collective-permute-start(f32[48,128]{1,0:T(8,128)S(1)} %shard_map.82), channel_id=1, source_target_pairs={{128,320},{160,352},{192,256},{224,288},{129,321},{161,353},{193,2... | collective-permute-start | bytes 73736 | tf_op jit(solution)/shard_map/ppermute | solution.py:453
  54.3 6.3 %collective-permute-start.7 = (f32[48,128]{1,0:T(8,128)S(1)}, f32[48,128]{1,0:T(8,128)S(1)}, u32[]{:S(2)}, u32[]{:S(2)}) collective-permute-start(f32[48,128]{1,0:T(8,128)S(1)} %shard_map.82), channel_id=1, source_target_pairs={{128,384},{160,416},{192,448},{224,480},{129,385},{161,417},{193,4... | collective-permute-start | bytes 73736 | tf_op jit(solution)/shard_map/ppermute | solution.py:453
  63.0 14.4 %collective-permute-start.10 = (f32[6,16,128]{2,1,0:T(8,128)S(1)}, f32[6,16,128]{2,1,0:T(8,128)S(1)}, u32[]{:S(2)}, u32[]{:S(2)}) collective-permute-start(f32[6,16,128]{2,1,0:T(8,128)S(1)} %get-tuple-element.42), channel_id=1, source_target_pairs={{32,0},{64,32},{96,64},{128,96},{160,128},{192,160},{224,192},{256... | collective-permute-start | bytes 147464 | tf_op jit(solution)/shard_map/ppermute | solution.py:441
  66.9 10.5 %collective-permute-start.11 = (f32[6,16,128]{2,1,0:T(8,128)S(1)}, f32[6,16,128]{2,1,0:T(8,128)S(1)}, u32[]{:S(2)}, u32[]{:S(2)}) collective-permute-start(f32[6,16,128]{2,1,0:T(8,128)S(1)} %get-tuple-element.43), channel_id=1, source_target_pairs={{2,4},{4,2},{6,8},{8,6},{10,12},{12,10},{14,16},{16,14},{18,20},{2... | collective-permute-start | bytes 147464 | tf_op jit(solution)/shard_map/ppermute | solution.py:440
  69.6 7.8 %collective-permute-start.12 = (f32[6,16,128]{2,1,0:T(8,128)S(1)}, f32[6,16,128]{2,1,0:T(8,128)S(1)}, u32[]{:S(2)}, u32[]{:S(2)}) collective-permute-start(f32[6,16,128]{2,1,0:T(8,128)S(1)} %get-tuple-element.44), channel_id=1, source_target_pairs={{0,2},{2,0},{4,6},{6,4},{8,10},{10,8},{12,14},{14,12},{16,18},{18,... | collective-permute-start | bytes 147464 | tf_op jit(solution)/shard_map/ppermute | solution.py:442
  72.4 5.8 %collective-permute-start.13 = (f32[6,16,128]{2,1,0:T(8,128)S(1)}, f32[6,16,128]{2,1,0:T(8,128)S(1)}, u32[]{:S(2)}, u32[]{:S(2)}) collective-permute-start(f32[6,16,128]{2,1,0:T(8,128)S(1)} %get-tuple-element.45), channel_id=1, source_target_pairs={{0,1},{1,0},{2,3},{3,2},{4,5},{5,4},{6,7},{7,6},{8,9},{9,8},{10,11... | collective-permute-start | bytes 147464 | tf_op jit(solution)/shard_map/ppermute | solution.py:443

commit v3 on v2

--- a/solution.py
+++ b/solution.py
@@ -102,104 +102,146 @@
     return jnp.concatenate(blocks, axis=1)
 
 
-def put_faces(cells, up, traces, inner, outer, across, below):
+def rows_of(ends):
+    return [ends[at : at + 1] for at in range(PATCH)]
+
+
+def ends_of(rows):
+    return jnp.concatenate(list(rows) + [jnp.zeros((8 - PATCH, LANES), F32)], axis=0)
+
+
+def chosen(items, at):
+    out = items[0]
+    for number in range(1, PATCH):
+        out = jnp.where(at == number, items[number], out)
+    return out
+
+
+def placed(states, ends):
+    out = []
+    for position in range(PATCH):
+        total = jnp.where(ends[0] == position, states[0], 0.0)
+        for at in range(1, PATCH):
+            total = total + jnp.where(ends[at] == position, states[at], 0.0)
+        out.append(total)
+    return out
+
+
+def ups_of(ups):
+    return [[ups[layer * PATCH + e : layer * PATCH + e + 1] for e in range(PATCH)] for layer in range(LAYERS)]
+
+
+def position_kernel(links, ups):
+    found = []
+    lane = lax.broadcasted_iota(jnp.int32, (EY, LAYERS), 1)
+    for layer in range(LAYERS):
+        for a in range(EX):
+            value = jnp.sum(jnp.where(lane == layer, links[a], 0).astype(F32), axis=1, keepdims=True)
+            found.append(jnp.broadcast_to(value, (EY, LANES)))
+    ups[...] = jnp.concatenate(found + [jnp.zeros((16 - CELLS, LANES), F32)], axis=0)
+
+
+def put_faces(cells, ups, traces, inner, outer, across, below):
     core = lax.axis_index("cy")
     even = lax.rem(lax.axis_index("cx"), 2) == 0
     picked = dot(jnp.concatenate([stacked(x) for x in cells], axis=0), side_table())
-    whole = []
-    for at in range(CELLS):
-        piece = picked[2 * VECS * at : 2 * VECS * (at + 1)]
-        traces[at] = piece.astype(BF16)
-        whole.append(halves(piece))
+    pieces = [picked[2 * VECS * at : 2 * VECS * (at + 1)] for at in range(CELLS)]
+    whole = [halves(piece) for piece in pieces]
     for layer in range(LAYERS):
         block = lambda e, s: whole[layer * PATCH + e][:, s * LANES : (s + 1) * LANES]
+        for e in range(PATCH):
+            traces[layer * PATCH + e, :, LANES:] = pieces[layer * PATCH + e][:, LANES:].astype(BF16)
         for b in range(EY):
             east, west = block(EY + b, 1), block(b, 2)
             inner[layer * EY + b] = jnp.where(even, east, west)
             outer[layer * EY + b] = jnp.where(even, west, east)
         for a in range(EX):
             across[layer * EX + a] = jnp.where(core == 0, block(a * EY + 1, 3), block(a * EY, 4))
-    for e in range(PATCH):
-        below[up[e]] = whole[e][:, :LANES]
+        if layer == 0:
+            for e, state in enumerate(placed([block(e, 0) for e in range(PATCH)], ups[layer])):
+                below[e] = state
+        else:
+            inflows = [pieces[layer * PATCH + e][:, :LANES] for e in range(PATCH)]
+            for e, piece in enumerate(placed(inflows, ups[layer])):
+                traces[(layer - 1) * PATCH + e, :, :LANES] = piece.astype(BF16)
     for e in range(PATCH, LAYERS * EY):
         below[e] = jnp.zeros((VECS, LANES), F32)
 
 
-def open_kernel(links, old, up, traces, inner, outer, across, below):
-    for at in range(CELLS):
-        up[at] = links[at % PATCH // EY, at % EY, at // PATCH]
-    put_faces([old[at] for at in range(CELLS)], up, traces, inner, outer, across, below)
-
-
-def place_downstream(up, traces, from_above, down):
-    for layer in range(1, LAYERS):
-        for e in range(PATCH):
-            down[(layer - 1) * PATCH + up[layer * PATCH + e]] = traces[layer * PATCH + e, :, 0:LANES]
-    for e in range(PATCH):
-        down[(LAYERS - 1) * PATCH + e] = stacked(from_above[e])
-
-
-def lifted_layer(layer, traces, down, inner, outer, from_across, coupling, lift):
+def open_kernel(ups, old, traces, inner, outer, across, below):
+    put_faces([old[at] for at in range(CELLS)], ups_of(ups), traces, inner, outer, across, below)
+
+
+def near_slots(layer, e, traces):
+    a, b = e // EY, e % EY
+    own = lambda cell, s: traces[layer * PATCH + cell, :, s * LANES : (s + 1) * LANES]
+    slots = {}
+    if layer < LAYERS - 1:
+        slots[1] = own(e, 0)
+    slots[2 if a == 1 else 3] = own(b, 1) if a == 1 else own(EY + b, 2)
+    slots[4 if b == 1 else 5] = own(a * EY, 3) if b == 1 else own(a * EY + 1, 4)
+    return slots
+
+
+def far_slots(layer, e, from_above, outer, inner, from_across):
     core = lax.axis_index("cy")
     even = lax.rem(lax.axis_index("cx"), 2) == 0
+    a, b = e // EY, e % EY
+    close, wide = inner[layer * EY + b], outer[layer * EY + b]
+    other = from_across[layer * EX + a]
+    slots = {}
+    if layer == LAYERS - 1:
+        slots[1] = stacked(from_above[e])
+    slots[2 if a == 0 else 3] = stacked(jnp.where(even, wide, close) if a == 0 else jnp.where(even, close, wide))
+    slots[4 if b == 0 else 5] = stacked(jnp.where(core == (1 if b == 0 else 0), other, 0.0))
+    return slots
+
+
+def lifted_layer(layer, stacks, coupling, lift):
     lane = lax.broadcasted_iota(jnp.int32, (2 * VECS, DEEP), 1)
-    left, right = [], []
-    for e in range(PATCH):
-        a, b = e // EY, e % EY
-        own = lambda cell, s: traces[layer * PATCH + cell, :, s * LANES : (s + 1) * LANES]
-        near, far = inner[layer * EY + b], outer[layer * EY + b]
-        slot1 = down[layer * PATCH + e]
-        slot2 = own(b, 1) if a == 1 else stacked(jnp.where(even, far, near))
-        slot3 = own(EY + b, 2) if a == 0 else stacked(jnp.where(even, near, far))
-        other = from_across[layer * EX + a]
-        slot4 = own(a * EY, 3) if b == 1 else stacked(jnp.where(core == 1, other, 0.0))
-        slot5 = own(a * EY + 1, 4) if b == 0 else stacked(jnp.where(core == 0, other, 0.0))
-        first = jnp.concatenate([slot1, slot2, slot3], axis=0)[:, :TRACE]
-        second = jnp.concatenate([slot3, slot4, slot5], axis=0)[:, :TRACE]
+    halfs = ((0, (1, 2, 3)), (DEEP, (3, 4, 5)))
+    sides = [[], []]
+    r = 2 * VECS
+    for e, slots in enumerate(stacks):
         block = coupling[layer * PATCH + e]
-        y = dot(first, block[:, :DEEP])
-        r = 2 * VECS
-        kept = jnp.where(
-            lane < TRACE,
-            0.0,
-            jnp.where(lane < 2 * TRACE, y[:r], jnp.where(lane < 3 * TRACE, y[r : 2 * r], y[2 * r :])),
-        )
-        left.append(stacked(halves(kept)))
-        z = dot(second, block[:, DEEP:])
-        tail = lane[:, : 6 * TRACE - DEEP] + DEEP
-        kept = jnp.where(
-            tail < 4 * TRACE, z[:r], jnp.where(tail < 5 * TRACE, z[r : 2 * r], z[2 * r :])
-        )
-        right.append(stacked(halves(kept)))
-    out = dot_rows(jnp.concatenate(left, axis=0), lift[:, :DEEP]) + dot_rows(
-        jnp.concatenate(right, axis=0), lift[:, DEEP:]
+        for side, (begin, numbers) in zip(sides, halfs):
+            present = [slot for slot in numbers if slot in slots]
+            y = dot(
+                jnp.concatenate([slots[slot] for slot in present], axis=0)[:, :TRACE],
+                block[:, begin : begin + DEEP],
+            )
+            at = lane[:, : y.shape[1]] + begin
+            kept = jnp.zeros((r, y.shape[1]), F32)
+            for i, slot in enumerate(present):
+                inside = (at >= slot * TRACE) & (at < (slot + 1) * TRACE)
+                kept = jnp.where(inside, y[r * i : r * (i + 1)], kept)
+            side.append(stacked(halves(kept)))
+    out = dot_rows(jnp.concatenate(sides[0], axis=0), lift[:, :DEEP]) + dot_rows(
+        jnp.concatenate(sides[1], axis=0), lift[:, DEEP:]
     )
-    return [halves(out[2 * VECS * e : 2 * VECS * (e + 1)]) for e in range(PATCH)]
-
-
-def left_of(deep):
-    high, low = deep[:TRACE], deep[LANES : LANES + TRACE]
-    return jnp.concatenate(
-        [jnp.concatenate([high, high], axis=1), jnp.concatenate([low, low], axis=1)], axis=0
-    )
-
-
-def transfer_kernel(up, diag, coupling, lift, weights, passing, composed, first_two):
+    return [halves(out[r * e : r * (e + 1)]) for e in range(PATCH)]
+
+
+def transfer_kernel(ups, diag, coupling, lift, weights, passing, composed):
+    ups = ups_of(ups)
     one = lax.broadcasted_iota(jnp.int32, (TRACE, TRACE), 0)
     two = lax.broadcasted_iota(jnp.int32, (TRACE, TRACE), 1)
     inflow = dot_rows((one == two).astype(F32).astype(BF16), lift[:, :TRACE]).astype(BF16)
     upper, lower = inflow[:NODES, :DEEP], inflow[NODES:, DEEP:]
+    first = []
     for at in range(CELLS):
         block = diag[at]
         lifted_rows = jnp.concatenate([dot(upper, block[:DEEP]), dot(lower, block[DEEP:])], axis=0)
         upwind = coupling[at][:, :LANES]
         weight = dot(jnp.concatenate([upwind, upwind], axis=1), deep_rows(lifted_rows))
         weights[at] = deep_rows(weight)
-        passing[at] = deep_rows(face_of(blocks_of(weight), 1))
+        passed_on = face_of(blocks_of(weight), 1)
+        passing[at] = deep_rows(passed_on)
+        if at < PATCH:
+            first.append(passed_on)
+    both = [times(chosen(first, ups[1][e]), passing[PATCH + e]) for e in range(PATCH)]
     for e in range(PATCH):
-        first_two[e] = halves(dot(left_of(passing[up[PATCH + e]]), passing[PATCH + e]))
-    for e in range(PATCH):
-        composed[e] = -times(first_two[up[2 * PATCH + e]], passing[2 * PATCH + e])
+        composed[e] = -times(chosen(both, ups[2][e]), passing[2 * PATCH + e])
 
 
 def turned(x, by):
@@ -250,31 +292,6 @@
     return [jnp.where(lane < TRACE, x, 0.0) for x in (one, two, three, four)]
 
 
-def rows_of(ends):
-    return [ends[at : at + 1] for at in range(PATCH)]
-
-
-def ends_of(rows):
-    return jnp.concatenate(list(rows) + [jnp.zeros((8 - PATCH, LANES), F32)], axis=0)
-
-
-def chosen(items, at):
-    out = items[0]
-    for number in range(1, PATCH):
-        out = jnp.where(at == number, items[number], out)
-    return out
-
-
-def placed(states, ends):
-    out = []
-    for position in range(PATCH):
-        total = jnp.where(ends[0] == position, states[0], 0.0)
-        for at in range(1, PATCH):
-            total = total + jnp.where(ends[at] == position, states[at], 0.0)
-        out.append(total)
-    return out
-
-
 def after(first, second):
     nothing = jnp.zeros((TRACE, LANES), F32)
     added = jnp.concatenate([nothing, second[TRACE:]], axis=0) if first.shape[0] > VECS else second[TRACE:]
@@ -282,34 +299,33 @@
 
 
 def source_kernel(
-    up, rhs, traces, from_above, outer, inner, from_across, diag, coupling, lift, passing, composed,
-    solved, sources, packed, down, current, maps,
+    ups, rhs, traces, from_above, outer, inner, from_across, diag, coupling, lift, passing, composed,
+    solved, sources, packed,
 ):
-    place_downstream(up, traces, from_above, down)
+    ups = ups_of(ups)
+    outflows = []
     for layer in range(LAYERS):
-        lifts = lifted_layer(layer, traces, down, inner, outer, from_across, coupling, lift)
+        stacks = [
+            near_slots(layer, e, traces) | far_slots(layer, e, from_above, outer, inner, from_across)
+            for e in range(PATCH)
+        ]
+        lifts = lifted_layer(layer, stacks, coupling, lift)
         for e in range(PATCH):
             at = layer * PATCH + e
             y = halves(dot(stacked(rhs[at] - lifts[e]), diag[at]))
             solved[at] = y
-            sources[at] = face_of(blocks_of(y), 1)
-    for e in range(PATCH):
-        current[e] = sources[e]
+            outflows.append(face_of(blocks_of(y), 1))
+            sources[at] = outflows[at]
+    current = outflows[:PATCH]
     for layer in range(1, LAYERS):
-        moved = []
-        for e in range(PATCH):
-            at = layer * PATCH + e
-            moved.append(sources[at] - times(current[up[at]], passing[at]))
-        for e in range(PATCH):
-            current[e] = moved[e]
-    row = lax.broadcasted_iota(jnp.int32, (8, LANES), 0)
-    ends = jnp.zeros((8, LANES), F32)
-    for e in range(PATCH):
-        start = up[up[PATCH + up[2 * PATCH + e]]]
-        maps[start, 0:TRACE] = composed[e]
-        maps[start, TRACE:MAP_ROWS] = current[e]
-        ends = jnp.where(row == start, float(e), ends)
-    packed[...] = pack([maps[e] for e in range(PATCH)], ends)
+        current = [
+            outflows[layer * PATCH + e] - times(chosen(current, ups[layer][e]), passing[layer * PATCH + e])
+            for e in range(PATCH)
+        ]
+    starts = [chosen(ups[0], chosen(ups[1], ups[2][e])) for e in range(PATCH)]
+    maps = placed([jnp.concatenate([composed[e], current[e]], axis=0) for e in range(PATCH)], starts)
+    ends = placed([jnp.full((1, LANES), float(e), F32) for e in range(PATCH)], starts)
+    packed[...] = pack(maps, ends_of(ends))
 
 
 def joined(mine, theirs, bit):
@@ -359,8 +375,8 @@
 
 
 def finish_kernel(
-    up, second, fourth, third, before, prefixes, ends, old, solved, sources, weights, passing,
-    new, traces, inner, outer, across, below, arrived, current, made, sems,
+    ups, second, fourth, third, before, prefixes, ends, old, solved, sources, weights, passing,
+    new, traces, inner, outer, across, below, made, sems,
 ):
     maps, map_ends = unpack(before[...])
     second, fourth, third = [unpack_states(x[...]) for x in (second, fourth, third)]
@@ -368,18 +384,14 @@
     last = placed(states, rows_of(map_ends))
     entering = [second[at] + third[at] + last[at] for at in range(PATCH)]
     states = [after(entering[at], prefixes[at]) for at in range(PATCH)]
-    for at, state in enumerate(placed(states, rows_of(ends))):
-        arrived[at] = state
-    changes, copies = [], []
+    current = placed(states, rows_of(ends))
+    ups = ups_of(ups)
+    changes = []
     for layer in range(LAYERS):
-        inflow = []
-        for e in range(PATCH):
-            link = up[layer * PATCH + e]
-            inflow.append(arrived[link] if layer == 0 else current[link])
-        if layer < LAYERS - 1:
-            for e in range(PATCH):
-                at = layer * PATCH + e
-                current[e] = sources[at] - times(inflow[e], passing[at])
+        inflow = [chosen(current, ups[layer][e]) for e in range(PATCH)]
+        current = [
+            sources[layer * PATCH + e] - times(inflow[e], passing[layer * PATCH + e]) for e in range(PATCH)
+        ]
         for e in range(PATCH):
             at = layer * PATCH + e
             x = solved[at] - times(inflow[e], weights[at])
@@ -387,29 +399,34 @@
             changes.append(old[at] - x)
     copy = pltpu.make_async_copy(made, new, sems.at[0])
     copy.start()
-    put_faces(changes, up, traces, inner, outer, across, below)
+    put_faces(changes, ups, traces, inner, outer, across, below)
     copy.wait()
 
 
-def residual_kernel(up, traces, from_above, outer, inner, from_across, coupling, lift, out, down):
-    place_downstream(up, traces, from_above, down)
+def near_residual_kernel(traces, coupling, lift, out):
     for layer in range(LAYERS):
-        lifts = lifted_layer(layer, traces, down, inner, outer, from_across, coupling, lift)
-        for e in range(PATCH):
-            out[layer * PATCH + e] = lifts[e]
+        stacks = [near_slots(layer, e, traces) for e in range(PATCH)]
+        for e, x in enumerate(lifted_layer(layer, stacks, coupling, lift)):
+            out[layer * PATCH + e] = x
+
+
+def residual_kernel(near, from_above, outer, inner, from_across, coupling, lift, out):
+    for layer in range(LAYERS):
+        stacks = [far_slots(layer, e, from_above, outer, inner, from_across) for e in range(PATCH)]
+        for e, x in enumerate(lifted_layer(layer, stacks, coupling, lift)):
+            out[layer * PATCH + e] = near[layer * PATCH + e] + x
 
 
 VMEM = pl.BlockSpec(memory_space=pltpu.VMEM)
-SMEM = pl.BlockSpec(memory_space=pltpu.SMEM)
 FAR = pl.BlockSpec(memory_space=pl.ANY)
 
 
-def call(kernel, scalars, outs, scratch=(), scalar_outs=(), far_outs=(), micros=1):
+def call(kernel, outs, scratch=(), far_outs=(), micros=1):
     def run(*args):
         return pl.pallas_call(
             kernel,
-            in_specs=[SMEM] * scalars + [VMEM] * (len(args) - scalars),
-            out_specs=[SMEM if i in scalar_outs else FAR if i in far_outs else VMEM for i in range(len(outs))],
+            in_specs=[VMEM] * len(args),
+            out_specs=[FAR if i in far_outs else VMEM for i in range(len(outs))],
             out_shape=[jax.ShapeDtypeStruct(shape, kind) for shape, kind in outs],
             scratch_shapes=list(scratch),
             compiler_params=pltpu.CompilerParams(vmem_limit_bytes=16 * 1024 * 1024),
@@ -431,8 +448,6 @@
 FIELD = ((CELLS, VECS, ROWS), F32)
 STATES = ((3 * VECS, LANES), F32)
 PACKED = ((3 * TRACE + 8, LANES), F32)
-DOWN = pltpu.VMEM((CELLS, 2 * VECS, LANES), BF16)
-HELD = pltpu.VMEM((PATCH, VECS, LANES), F32)
 
 
 def exchange_sides(inner, outer, across, below):
@@ -459,45 +474,37 @@
     diag = diag_inverse.reshape(CELLS, ROWS, ROWS)
     blocks = coupling.reshape(CELLS, TRACE, 6 * TRACE)
     lift = lift_table.T
-    up, traces, *sends = call(open_kernel, 1, [((CELLS,), jnp.int32)] + FACE_OUTS, scalar_outs=(0,), micros=2)(
-        upstream.transpose(1, 2, 0), old
-    )
+    (ups,) = call(position_kernel, [((16, LANES), F32)], micros=2)(upstream.transpose(1, 2, 0))
+    traces, *sends = call(open_kernel, FACE_OUTS, micros=2)(ups, old)
     halos = exchange_sides(*sends)
     weights, passing, composed = call(
         transfer_kernel,
-        1,
         [((CELLS, DEEP, ROWS), BF16), ((CELLS, DEEP, LANES), BF16), ((PATCH, TRACE, LANES), F32)],
-        [pltpu.VMEM((PATCH, TRACE, LANES), F32)],
-    )(up, diag, blocks, lift)
-    solved, sources, single = call(
-        source_kernel,
-        1,
-        [FIELD, ((CELLS, VECS, LANES), F32), PACKED],
-        [DOWN, HELD, pltpu.VMEM((PATCH, MAP_ROWS, LANES), F32)],
-    )(up, rhs, traces, *halos, diag, blocks, lift, passing, composed)
+    )(ups, diag, blocks, lift)
+    solved, sources, single = call(source_kernel, [FIELD, ((CELLS, VECS, LANES), F32), PACKED])(
+        ups, rhs, traces, *halos, diag, blocks, lift, passing, composed
+    )
     partner = swapped(single, 1)
-    (pair,) = call(pair_kernel, 0, [PACKED])(single, partner)
+    (pair,) = call(pair_kernel, [PACKED])(single, partner)
     partner_pair = swapped(pair, 2)
-    group, leaving = call(group_kernel, 0, [PACKED, STATES])(pair, partner_pair)
+    group, leaving = call(group_kernel, [PACKED, STATES])(pair, partner_pair)
     second = passed(leaving, 0, 1, 2)
     before = passed(group, 2, 3, 2)
-    prefixes, ends = call(prefix_kernel, 0, [((PATCH, MAP_ROWS, LANES), F32), ((8, LANES), F32)])(
+    prefixes, ends = call(prefix_kernel, [((PATCH, MAP_ROWS, LANES), F32), ((8, LANES), F32)])(
         partner, partner_pair
     )
-    (leaving,) = call(onward_kernel, 0, [STATES])(second, group)
+    (leaving,) = call(onward_kernel, [STATES])(second, group)
     third = passed(leaving, 1, 2, 2)
     fourth = passed(leaving, 1, 3, 0)
     new, traces, *sends = call(
         finish_kernel,
-        1,
         [FIELD] + FACE_OUTS,
-        [HELD, HELD, pltpu.VMEM((CELLS, VECS, ROWS), F32), pltpu.SemaphoreType.DMA((1,))],
+        [pltpu.VMEM((CELLS, VECS, ROWS), F32), pltpu.SemaphoreType.DMA((1,))],
         far_outs=(0,),
-    )(
-        up, second, fourth, third, before, prefixes, ends, old, solved, sources, weights, passing
-    )
+    )(ups, second, fourth, third, before, prefixes, ends, old, solved, sources, weights, passing)
     halos = exchange_sides(*sends)
-    (residual,) = call(residual_kernel, 1, [FIELD], [DOWN])(up, traces, *halos, blocks, lift)
+    (near,) = call(near_residual_kernel, [FIELD])(traces, blocks, lift)
+    (residual,) = call(residual_kernel, [FIELD])(near, *halos, blocks, lift)
     shape = rhs_vectors.shape
     return new.reshape(shape), residual.reshape(shape)
 

time: 81.3 us -> 77.6 us (0.954)
  Pallas kernels: 14 us -> 11.3 us
  waiting for transfers between devices: 20 us -> 19.1 us
    pallas_call x9 -> x11, Pallas kernels: 14 us -> 11.3 us  [run(): pl.pallas_call(kernel, in_specs=[VMEM] * len(args), out_specs=[FAR if i i...]
    ppermute x2, waiting for transfers between devices: 0.83 us -> 0.01 us  [exchange_sides(): across = lax.ppermute(across, 'cy', [(0, 1), (1, 0)])]
    unnamed x14 -> x12, local copies, waits for them, and re-layouts: 1.66 us -> 1.57 us
  transfers between devices with their start and end apart: 14 -> 14, of which waited for: 4 -> 3; matrix products, arithmetic and copies ran while one was open for 0% -> 0% of each run, Pallas kernels for 5% -> 6%
where the time goes in v3:
time: 77.6 us; the launch traced here: 76.9 us
  starting transfers between devices  44 us (57%)
  waiting for transfers between devices  19.1 us (25%)
  Pallas kernels  11.3 us (15%)
  local copies, waits for them, and re-layouts  1.57 us (2%)
  between operations  0.93 us (1%)
    ppermute x2, starting transfers between devices, exchange_sides(): lax.ppermute(outer, 'cx', [(i, i + 1 if i % 2 else i - 1) for i in range(...  13.9 us
    ppermute x2, waiting for transfers between devices, swapped(): lax.ppermute(packed, 'sweep', [(i, i ^ by) for i in range(lax.axis_size('...  13.8 us
    pallas_call x11, Pallas kernels, run(): pl.pallas_call(kernel, in_specs=[VMEM] * len(args), out_specs=[FAR if i i...  11.3 us
    ppermute x2, starting transfers between devices, exchange_sides(): below = lax.ppermute(below, 'sweep', [(i + 1, i) for i in range(deep - 1)])  9.52 us
    ppermute x2, starting transfers between devices, exchange_sides(): across = lax.ppermute(across, 'cy', [(0, 1), (1, 0)])  8.07 us
    ppermute x4, waiting for transfers between devices, passed(): return lax.ppermute(states, 'sweep', pairs)  5.26 us
    ppermute x2, starting transfers between devices, exchange_sides(): inner = lax.ppermute(inner, 'cx', [(i, i ^ 1) for i in range(wide)])  4.75 us
    ppermute x4, starting transfers between devices, passed(): return lax.ppermute(states, 'sweep', pairs)  3.93 us
  transfers between devices with their start and end apart: 14, of which 3 were waited for; matrix products, arithmetic and copies ran while one was open for 0% of the time, Pallas kernels for 6%

profile of v3, /device:TPU:7, one launch (start us, length us, event | category | flops | bytes accessed | tf_op | source)
XLA Modules:
  0.0 76.9 jit_solution(6348469994941997308)
XLA Ops:
  0.6 0.7 copy-done.5
  1.3 0.1 shard_map.77.ups
  1.4 0.9 %copy-done.4 = f32[3,2,2,16,320]{4,3,2,1,0:T(8,128)S(1)} copy-done((f32[3,2,2,16,320]{4,3,2,1,0:T(8,128)S(1)}, f32[3,2,2,16,320]{4,3,2,1,0:T(8,128)}, u32[]{:S(2)}) %copy-start.4) | copy-done | bytes 245784
  2.3 0.4 shard_map.78
  2.7 0.0 copy-start.3
  2.7 5.6 %collective-permute-start = (f32[6,16,128]{2,1,0:T(8,128)S(1)}, f32[6,16,128]{2,1,0:T(8,128)S(1)}, u32[]{:S(2)}, u32[]{:S(2)}) collective-permute-start(f32[6,16,128]{2,1,0:T(8,128)S(1)} %get-tuple-element.24), channel_id=1, source_target_pairs={{32,0},{64,32},{96,64},{128,96},{160,128},{192,160},{224,192},{256... | collective-permute-start | bytes 147464 | tf_op jit(solution)/shard_map/ppermute | solution.py:456
  8.4 11.2 %collective-permute-start.1 = (f32[6,16,128]{2,1,0:T(8,128)S(1)}, f32[6,16,128]{2,1,0:T(8,128)S(1)}, u32[]{:S(2)}, u32[]{:S(2)}) collective-permute-start(f32[6,16,128]{2,1,0:T(8,128)S(1)} %get-tuple-element.25), channel_id=1, source_target_pairs={{2,4},{4,2},{6,8},{8,6},{10,12},{12,10},{14,16},{16,14},{18,20},{2... | collective-permute-start | bytes 147464 | tf_op jit(solution)/shard_map/ppermute | solution.py:455
  19.6 1.9 %collective-permute-start.2 = (f32[6,16,128]{2,1,0:T(8,128)S(1)}, f32[6,16,128]{2,1,0:T(8,128)S(1)}, u32[]{:S(2)}, u32[]{:S(2)}) collective-permute-start(f32[6,16,128]{2,1,0:T(8,128)S(1)} %get-tuple-element.26), channel_id=1, source_target_pairs={{0,2},{2,0},{4,6},{6,4},{8,10},{10,8},{12,14},{14,12},{16,18},{18,... | collective-permute-start | bytes 147464 | tf_op jit(solution)/shard_map/ppermute | solution.py:457
  21.5 3.1 %collective-permute-start.3 = (f32[6,16,128]{2,1,0:T(8,128)S(1)}, f32[6,16,128]{2,1,0:T(8,128)S(1)}, u32[]{:S(2)}, u32[]{:S(2)}) collective-permute-start(f32[6,16,128]{2,1,0:T(8,128)S(1)} %get-tuple-element.27), channel_id=1, source_target_pairs={{0,1},{1,0},{2,3},{3,2},{4,5},{5,4},{6,7},{7,6},{8,9},{9,8},{10,11... | collective-permute-start | bytes 147464 | tf_op jit(solution)/shard_map/ppermute | solution.py:458
  24.7 2.9 %shard_map.79 = (bf16[12,256,320]{2,1,0:T(8,128)(2,1)S(1)}, bf16[12,256,128]{2,1,0:T(8,128)(2,1)S(1)}, f32[4,80,128]{2,1,0:T(8,128)S(1)}) custom-call(f32[16,128]{1,0:T(8,128)S(1)} %shard_map.77.ups, bf16[12,320,320]{2,1,0:T(8,128)(2,1)S(1)} %bitcast.8, bf16[12,80,480]{2,1,0:T(8,128)(2,1)S(1)} %bitcast.10, bf16[320,480]{1,0:T(8,128)(2,1)S(1)} %bitcast.14), custom_call_target="tpu_custom_call" | custom-call | flops 1000000000 | bytes 3600000 | tf_op jit(solution)/shard_map/pallas_call | solution.py:426
  27.7 2.1 %shard_map.80 = (f32[12,16,320]{2,1,0:T(8,128)S(1)}, f32[12,16,128]{2,1,0:T(8,128)S(1)}, f32[248,128]{1,0:T(8,128)S(1)}) custom-call(f32[16,128]{1,0:T(8,128)S(1)} %shard_map.77.ups, f32[12,16,320]{2,1,0:T(8,128)S(1)} %bitcast.18, bf16[12,32,640]{2,1,0:T(8,128)(2,1)S(1)} %get-tuple-element.23.traces, f32[6,16,128]{2,1,0:T(8,128)S(1)} %collective-permute-done.from_above, ...), custom_call_target="tpu_custom_call" | custom-call | flops 1000000000 | bytes 3600000 | tf_op jit(solution)/shard_map/pallas_call | solution.py:426
  29.8 1.9 %collective-permute-start.4 = (f32[248,128]{1,0:T(8,128)S(1)}, f32[248,128]{1,0:T(8,128)S(1)}, u32[]{:S(2)}, u32[]{:S(2)}) collective-permute-start(f32[248,128]{1,0:T(8,128)S(1)} %get-tuple-element.30.mine), channel_id=1, source_target_pairs={{0,32},{32,0},{64,96},{96,64},{128,160},{160,128},{192,224},{224,1... | collective-permute-start | bytes 380936 | tf_op jit(solution)/shard_map/ppermute | solution.py:463
  31.7 5.0 %collective-permute-done.4.theirs.pair = f32[248,128]{1,0:T(8,128)S(1)} collective-permute-done((f32[248,128]{1,0:T(8,128)S(1)}, f32[248,128]{1,0:T(8,128)S(1)}, u32[]{:S(2)}, u32[]{:S(2)}) %collective-permute-start.4) | collective-permute-done | bytes 127008 | tf_op jit(solution)/shard_map/ppermute | solution.py:463
  36.7 0.4 shard_map.81.mine
  37.2 1.9 %collective-permute-start.5 = (f32[248,128]{1,0:T(8,128)S(1)}, f32[248,128]{1,0:T(8,128)S(1)}, u32[]{:S(2)}, u32[]{:S(2)}) collective-permute-start(f32[248,128]{1,0:T(8,128)S(1)} %shard_map.81.mine), channel_id=1, source_target_pairs={{0,64},{32,96},{64,0},{96,32},{128,192},{160,224},{192,128},{224,1... | collective-permute-start | bytes 380936 | tf_op jit(solution)/shard_map/ppermute | solution.py:463
  39.1 8.8 %collective-permute-done.5.theirs = f32[248,128]{1,0:T(8,128)S(1)} collective-permute-done((f32[248,128]{1,0:T(8,128)S(1)}, f32[248,128]{1,0:T(8,128)S(1)}, u32[]{:S(2)}, u32[]{:S(2)}) %collective-permute-start.5) | collective-permute-done | bytes 127008 | tf_op jit(solution)/shard_map/ppermute | solution.py:463
  47.9 0.4 shard_map.82
  48.4 0.7 collective-permute-start.6
  49.1 1.3 %collective-permute-start.9 = (f32[248,128]{1,0:T(8,128)S(1)}, f32[248,128]{1,0:T(8,128)S(1)}, u32[]{:S(2)}, u32[]{:S(2)}) collective-permute-start(f32[248,128]{1,0:T(8,128)S(1)} %get-tuple-element.32.packed), channel_id=1, source_target_pairs={{256,448},{288,480},{320,384},{352,416},{257,449},{289,481},{321,3... | collective-permute-start | bytes 380936 | tf_op jit(solution)/shard_map/ppermute | solution.py:468
  50.4 0.3 shard_map.83
  50.7 1.3 %collective-permute-start.8 = (f32[48,128]{1,0:T(8,128)S(1)}, f32[48,128]{1,0:T(8,128)S(1)}, u32[]{:S(2)}, u32[]{:S(2)}) collective-permute-start(f32[48,128]{1,0:T(8,128)S(1)} %shard_map.83), channel_id=1, source_target_pairs={{128,320},{160,352},{192,256},{224,288},{129,321},{161,353},{193,2... | collective-permute-start | bytes 73736 | tf_op jit(solution)/shard_map/ppermute | solution.py:468
  52.0 0.7 collective-permute-start.7
  52.6 0.4 shard_map.84
  53.0 5.2 %collective-permute-done.8.third = f32[48,128]{1,0:T(8,128)S(1)} collective-permute-done((f32[48,128]{1,0:T(8,128)S(1)}, f32[48,128]{1,0:T(8,128)S(1)}, u32[]{:S(2)}, u32[]{:S(2)}) %collective-permute-start.8) | collective-permute-done | bytes 24608 | tf_op jit(solution)/shard_map/ppermute | solution.py:468
  58.3 1.7 %shard_map.85 = (f32[12,16,320]{2,1,0:T(8,128)}, bf16[12,32,640]{2,1,0:T(8,128)(2,1)S(1)}, f32[6,16,128]{2,1,0:T(8,128)S(1)}, f32[6,16,128]{2,1,0:T(8,128)S(1)},...) custom-call(f32[16,128]{1,0:T(8,128)S(1)} %shard_map.77.ups, f32[48,128]{1,0:T(8,128)S(1)} %collective-permute-done.6.entering.second, ...), custom_call_target="tpu_custom_call" | custom-call | flops 1000000000 | bytes 3600000 | tf_op jit(solution)/shard_map/pallas_call | solution.py:426
  59.9 3.9 %collective-permute-start.10 = (f32[6,16,128]{2,1,0:T(8,128)S(1)}, f32[6,16,128]{2,1,0:T(8,128)S(1)}, u32[]{:S(2)}, u32[]{:S(2)}) collective-permute-start(f32[6,16,128]{2,1,0:T(8,128)S(1)} %get-tuple-element.40), channel_id=1, source_target_pairs={{32,0},{64,32},{96,64},{128,96},{160,128},{192,160},{224,192},{256... | collective-permute-start | bytes 147464 | tf_op jit(solution)/shard_map/ppermute | solution.py:456
  63.8 2.7 %collective-permute-start.11 = (f32[6,16,128]{2,1,0:T(8,128)S(1)}, f32[6,16,128]{2,1,0:T(8,128)S(1)}, u32[]{:S(2)}, u32[]{:S(2)}) collective-permute-start(f32[6,16,128]{2,1,0:T(8,128)S(1)} %get-tuple-element.41), channel_id=1, source_target_pairs={{2,4},{4,2},{6,8},{8,6},{10,12},{12,10},{14,16},{16,14},{18,20},{2... | collective-permute-start | bytes 147464 | tf_op jit(solution)/shard_map/ppermute | solution.py:455
  66.6 2.8 %collective-permute-start.12 = (f32[6,16,128]{2,1,0:T(8,128)S(1)}, f32[6,16,128]{2,1,0:T(8,128)S(1)}, u32[]{:S(2)}, u32[]{:S(2)}) collective-permute-start(f32[6,16,128]{2,1,0:T(8,128)S(1)} %get-tuple-element.42), channel_id=1, source_target_pairs={{0,2},{2,0},{4,6},{6,4},{8,10},{10,8},{12,14},{14,12},{16,18},{18,... | collective-permute-start | bytes 147464 | tf_op jit(solution)/shard_map/ppermute | solution.py:457
  69.4 4.9 %collective-permute-start.13 = (f32[6,16,128]{2,1,0:T(8,128)S(1)}, f32[6,16,128]{2,1,0:T(8,128)S(1)}, u32[]{:S(2)}, u32[]{:S(2)}) collective-permute-start(f32[6,16,128]{2,1,0:T(8,128)S(1)} %get-tuple-element.43), channel_id=1, source_target_pairs={{0,1},{1,0},{2,3},{3,2},{4,5},{5,4},{6,7},{7,6},{8,9},{9,8},{10,11... | collective-permute-start | bytes 147464 | tf_op jit(solution)/shard_map/ppermute | solution.py:458
  74.3 0.9 %shard_map.86.near = f32[12,16,320]{2,1,0:T(8,128)S(1)} custom-call(bf16[12,32,640]{2,1,0:T(8,128)(2,1)S(1)} %get-tuple-element.39.traces, bf16[12,80,480]{2,1,0:T(8,128)(2,1)S(1)} %bitcast.12, bf16[320,480]{1,0:T(8,128)(2,1)S(1)} %bitcast.16), custom_call_target="tpu_custom_call" | custom-call | flops 1000000000 | bytes 3600000 | tf_op jit(solution)/shard_map/pallas_call | solution.py:426
  75.2 0.0 collective-permute-done.10.from_above
  75.3 1.7 %shard_map.87 = f32[12,16,320]{2,1,0:T(8,128)} custom-call(f32[12,16,320]{2,1,0:T(8,128)S(1)} %shard_map.86.near, f32[6,16,128]{2,1,0:T(8,128)S(1)} %collective-permute-done.10.from_above, f32[6,16,128]{2,1,0:T(8,128)S(1)} %collective-permute-done.11.outer, f32[6,16,128]{2,1,0:T(8,128)S(1)} %collective-permute-done.12.inner, ...), custom_call_target="tpu_custom_call" | custom-call | flops 1000000000 | bytes 3600000 | tf_op jit(solution)/shard_map/pallas_call | solution.py:426
  (19 shorter events, 0.0 us)
Async XLA Ops:
  0.6 0.7 copy-start.5
  1.3 1.0 %copy-start.4 = (f32[3,2,2,16,320]{4,3,2,1,0:T(8,128)S(1)}, f32[3,2,2,16,320]{4,3,2,1,0:T(8,128)}, u32[]{:S(2)}) copy-start(f32[3,2,2,16,320]{4,3,2,1,0:T(8,128)} %param.7) | copy-start | bytes 737284
  2.3 22.4 %copy-start = (bf16[3,2,2,320,320]{4,3,2,1,0:T(8,128)(2,1)S(1)}, bf16[3,2,2,320,320]{4,3,2,1,0:T(8,128)(2,1)}, u32[]{:S(2)}) copy-start(bf16[3,2,2,320,320]{4,3,2,1,0:T(8,128)(2,1)} %param.8) | copy-start | bytes 7372804
  2.3 22.4 %copy-start.1 = (bf16[3,2,2,80,480]{4,3,2,1,0:T(8,128)(2,1)S(1)}, bf16[3,2,2,80,480]{4,3,2,1,0:T(8,128)(2,1)}, u32[]{:S(2)}) copy-start(bf16[3,2,2,80,480]{4,3,2,1,0:T(8,128)(2,1)} %param.9) | copy-start | bytes 2764804
  2.3 22.4 %copy-start.2 = (bf16[480,320]{0,1:T(8,128)(2,1)S(1)}, bf16[480,320]{0,1:T(8,128)(2,1)}, u32[]{:S(2)}) copy-start(bf16[480,320]{0,1:T(8,128)(2,1)} %param.10) | copy-start | bytes 921604
  2.7 25.0 %copy-start.3 = (f32[3,2,2,16,320]{4,3,2,1,0:T(8,128)S(1)}, f32[3,2,2,16,320]{4,3,2,1,0:T(8,128)}, u32[]{:S(2)}) copy-start(f32[3,2,2,16,320]{4,3,2,1,0:T(8,128)} %param.6) | copy-start | bytes 737284
  2.7 24.9 %collective-permute-start = (f32[6,16,128]{2,1,0:T(8,128)S(1)}, f32[6,16,128]{2,1,0:T(8,128)S(1)}, u32[]{:S(2)}, u32[]{:S(2)}) collective-permute-start(f32[6,16,128]{2,1,0:T(8,128)S(1)} %get-tuple-element.24), channel_id=1, source_target_pairs={{32,0},{64,32},{96,64},{128,96},{160,128},{192,160},{224,192},{256... | collective-permute-start | bytes 147464 | tf_op jit(solution)/shard_map/ppermute | solution.py:456
  8.4 19.3 %collective-permute-start.1 = (f32[6,16,128]{2,1,0:T(8,128)S(1)}, f32[6,16,128]{2,1,0:T(8,128)S(1)}, u32[]{:S(2)}, u32[]{:S(2)}) collective-permute-start(f32[6,16,128]{2,1,0:T(8,128)S(1)} %get-tuple-element.25), channel_id=1, source_target_pairs={{2,4},{4,2},{6,8},{8,6},{10,12},{12,10},{14,16},{16,14},{18,20},{2... | collective-permute-start | bytes 147464 | tf_op jit(solution)/shard_map/ppermute | solution.py:455
  19.6 8.1 %collective-permute-start.2 = (f32[6,16,128]{2,1,0:T(8,128)S(1)}, f32[6,16,128]{2,1,0:T(8,128)S(1)}, u32[]{:S(2)}, u32[]{:S(2)}) collective-permute-start(f32[6,16,128]{2,1,0:T(8,128)S(1)} %get-tuple-element.26), channel_id=1, source_target_pairs={{0,2},{2,0},{4,6},{6,4},{8,10},{10,8},{12,14},{14,12},{16,18},{18,... | collective-permute-start | bytes 147464 | tf_op jit(solution)/shard_map/ppermute | solution.py:457
  21.5 6.2 %collective-permute-start.3 = (f32[6,16,128]{2,1,0:T(8,128)S(1)}, f32[6,16,128]{2,1,0:T(8,128)S(1)}, u32[]{:S(2)}, u32[]{:S(2)}) collective-permute-start(f32[6,16,128]{2,1,0:T(8,128)S(1)} %get-tuple-element.27), channel_id=1, source_target_pairs={{0,1},{1,0},{2,3},{3,2},{4,5},{5,4},{6,7},{7,6},{8,9},{9,8},{10,11... | collective-permute-start | bytes 147464 | tf_op jit(solution)/shard_map/ppermute | solution.py:458
  29.8 6.9 %collective-permute-start.4 = (f32[248,128]{1,0:T(8,128)S(1)}, f32[248,128]{1,0:T(8,128)S(1)}, u32[]{:S(2)}, u32[]{:S(2)}) collective-permute-start(f32[248,128]{1,0:T(8,128)S(1)} %get-tuple-element.30.mine), channel_id=1, source_target_pairs={{0,32},{32,0},{64,96},{96,64},{128,160},{160,128},{192,224},{224,1... | collective-permute-start | bytes 380936 | tf_op jit(solution)/shard_map/ppermute | solution.py:463
  37.2 10.8 %collective-permute-start.5 = (f32[248,128]{1,0:T(8,128)S(1)}, f32[248,128]{1,0:T(8,128)S(1)}, u32[]{:S(2)}, u32[]{:S(2)}) collective-permute-start(f32[248,128]{1,0:T(8,128)S(1)} %shard_map.81.mine), channel_id=1, source_target_pairs={{0,64},{32,96},{64,0},{96,32},{128,192},{160,224},{192,128},{224,1... | collective-permute-start | bytes 380936 | tf_op jit(solution)/shard_map/ppermute | solution.py:463
  48.4 2.0 %collective-permute-start.6 = (f32[48,128]{1,0:T(8,128)S(1)}, f32[48,128]{1,0:T(8,128)S(1)}, u32[]{:S(2)}, u32[]{:S(2)}) collective-permute-start(f32[48,128]{1,0:T(8,128)S(1)} %get-tuple-element.31), channel_id=1, source_target_pairs={{0,192},{32,224},{64,128},{96,160},{1,193},{33,225},{65,129},{97,1... | collective-permute-start | bytes 73736 | tf_op jit(solution)/shard_map/ppermute | solution.py:468
  49.1 9.2 %collective-permute-start.9 = (f32[248,128]{1,0:T(8,128)S(1)}, f32[248,128]{1,0:T(8,128)S(1)}, u32[]{:S(2)}, u32[]{:S(2)}) collective-permute-start(f32[248,128]{1,0:T(8,128)S(1)} %get-tuple-element.32.packed), channel_id=1, source_target_pairs={{256,448},{288,480},{320,384},{352,416},{257,449},{289,481},{321,3... | collective-permute-start | bytes 380936 | tf_op jit(solution)/shard_map/ppermute | solution.py:468
  50.7 7.6 %collective-permute-start.8 = (f32[48,128]{1,0:T(8,128)S(1)}, f32[48,128]{1,0:T(8,128)S(1)}, u32[]{:S(2)}, u32[]{:S(2)}) collective-permute-start(f32[48,128]{1,0:T(8,128)S(1)} %shard_map.83), channel_id=1, source_target_pairs={{128,320},{160,352},{192,256},{224,288},{129,321},{161,353},{193,2... | collective-permute-start | bytes 73736 | tf_op jit(solution)/shard_map/ppermute | solution.py:468
  52.0 6.3 %collective-permute-start.7 = (f32[48,128]{1,0:T(8,128)S(1)}, f32[48,128]{1,0:T(8,128)S(1)}, u32[]{:S(2)}, u32[]{:S(2)}) collective-permute-start(f32[48,128]{1,0:T(8,128)S(1)} %shard_map.83), channel_id=1, source_target_pairs={{128,384},{160,416},{192,448},{224,480},{129,385},{161,417},{193,4... | collective-permute-start | bytes 73736 | tf_op jit(solution)/shard_map/ppermute | solution.py:468
  59.9 15.3 %collective-permute-start.10 = (f32[6,16,128]{2,1,0:T(8,128)S(1)}, f32[6,16,128]{2,1,0:T(8,128)S(1)}, u32[]{:S(2)}, u32[]{:S(2)}) collective-permute-start(f32[6,16,128]{2,1,0:T(8,128)S(1)} %get-tuple-element.40), channel_id=1, source_target_pairs={{32,0},{64,32},{96,64},{128,96},{160,128},{192,160},{224,192},{256... | collective-permute-start | bytes 147464 | tf_op jit(solution)/shard_map/ppermute | solution.py:456
  63.8 11.4 %collective-permute-start.11 = (f32[6,16,128]{2,1,0:T(8,128)S(1)}, f32[6,16,128]{2,1,0:T(8,128)S(1)}, u32[]{:S(2)}, u32[]{:S(2)}) collective-permute-start(f32[6,16,128]{2,1,0:T(8,128)S(1)} %get-tuple-element.41), channel_id=1, source_target_pairs={{2,4},{4,2},{6,8},{8,6},{10,12},{12,10},{14,16},{16,14},{18,20},{2... | collective-permute-start | bytes 147464 | tf_op jit(solution)/shard_map/ppermute | solution.py:455
  66.6 8.7 %collective-permute-start.12 = (f32[6,16,128]{2,1,0:T(8,128)S(1)}, f32[6,16,128]{2,1,0:T(8,128)S(1)}, u32[]{:S(2)}, u32[]{:S(2)}) collective-permute-start(f32[6,16,128]{2,1,0:T(8,128)S(1)} %get-tuple-element.42), channel_id=1, source_target_pairs={{0,2},{2,0},{4,6},{6,4},{8,10},{10,8},{12,14},{14,12},{16,18},{18,... | collective-permute-start | bytes 147464 | tf_op jit(solution)/shard_map/ppermute | solution.py:457
  69.4 5.9 %collective-permute-start.13 = (f32[6,16,128]{2,1,0:T(8,128)S(1)}, f32[6,16,128]{2,1,0:T(8,128)S(1)}, u32[]{:S(2)}, u32[]{:S(2)}) collective-permute-start(f32[6,16,128]{2,1,0:T(8,128)S(1)} %get-tuple-element.43), channel_id=1, source_target_pairs={{0,1},{1,0},{2,3},{3,2},{4,5},{5,4},{6,7},{7,6},{8,9},{9,8},{10,11... | collective-permute-start | bytes 147464 | tf_op jit(solution)/shard_map/ppermute | solution.py:458

commit v4 on v3

--- a/solution.py
+++ b/solution.py
@@ -131,53 +131,62 @@
     return [[ups[layer * PATCH + e : layer * PATCH + e + 1] for e in range(PATCH)] for layer in range(LAYERS)]
 
 
-def position_kernel(links, ups):
+def position_rows(links):
     found = []
     lane = lax.broadcasted_iota(jnp.int32, (EY, LAYERS), 1)
     for layer in range(LAYERS):
         for a in range(EX):
             value = jnp.sum(jnp.where(lane == layer, links[a], 0).astype(F32), axis=1, keepdims=True)
             found.append(jnp.broadcast_to(value, (EY, LANES)))
-    ups[...] = jnp.concatenate(found + [jnp.zeros((16 - CELLS, LANES), F32)], axis=0)
-
-
-def put_faces(cells, ups, traces, inner, outer, across, below):
+    return jnp.concatenate(found + [jnp.zeros((16 - CELLS, LANES), F32)], axis=0)
+
+
+def put_sides(cells, traces, inner, outer, across):
     core = lax.axis_index("cy")
     even = lax.rem(lax.axis_index("cx"), 2) == 0
     picked = dot(jnp.concatenate([stacked(x) for x in cells], axis=0), side_table())
     pieces = [picked[2 * VECS * at : 2 * VECS * (at + 1)] for at in range(CELLS)]
-    whole = [halves(piece) for piece in pieces]
+    whole = [halves(piece[:, LANES:]) for piece in pieces]
     for layer in range(LAYERS):
-        block = lambda e, s: whole[layer * PATCH + e][:, s * LANES : (s + 1) * LANES]
+        block = lambda e, s: whole[layer * PATCH + e][:, (s - 1) * LANES : s * LANES]
         for e in range(PATCH):
-            traces[layer * PATCH + e, :, LANES:] = pieces[layer * PATCH + e][:, LANES:].astype(BF16)
+            traces[layer * PATCH + e] = pieces[layer * PATCH + e][:, LANES:].astype(BF16)
         for b in range(EY):
             east, west = block(EY + b, 1), block(b, 2)
             inner[layer * EY + b] = jnp.where(even, east, west)
             outer[layer * EY + b] = jnp.where(even, west, east)
         for a in range(EX):
             across[layer * EX + a] = jnp.where(core == 0, block(a * EY + 1, 3), block(a * EY, 4))
-        if layer == 0:
-            for e, state in enumerate(placed([block(e, 0) for e in range(PATCH)], ups[layer])):
-                below[e] = state
-        else:
-            inflows = [pieces[layer * PATCH + e][:, :LANES] for e in range(PATCH)]
-            for e, piece in enumerate(placed(inflows, ups[layer])):
-                traces[(layer - 1) * PATCH + e, :, :LANES] = piece.astype(BF16)
+    return [piece[:, :LANES] for piece in pieces]
+
+
+def put_inflows(pieces, ups, down, below):
+    for e, state in enumerate(placed([halves(pieces[e]) for e in range(PATCH)], ups[0])):
+        below[e] = state
     for e in range(PATCH, LAYERS * EY):
         below[e] = jnp.zeros((VECS, LANES), F32)
-
-
-def open_kernel(ups, old, traces, inner, outer, across, below):
-    put_faces([old[at] for at in range(CELLS)], ups_of(ups), traces, inner, outer, across, below)
-
-
-def near_slots(layer, e, traces):
+    for layer in range(1, LAYERS):
+        for e, piece in enumerate(placed(pieces[layer * PATCH : (layer + 1) * PATCH], ups[layer])):
+            down[(layer - 1) * PATCH + e] = piece.astype(BF16)
+
+
+def open_kernel(old, traces, inner, outer, across, faces):
+    for at, piece in enumerate(put_sides([old[at] for at in range(CELLS)], traces, inner, outer, across)):
+        faces[at] = piece
+
+
+def position_kernel(links, faces, ups, down, below):
+    rows = position_rows(links)
+    ups[...] = rows
+    put_inflows([faces[at] for at in range(CELLS)], ups_of(rows), down, below)
+
+
+def near_slots(layer, e, traces, down):
     a, b = e // EY, e % EY
-    own = lambda cell, s: traces[layer * PATCH + cell, :, s * LANES : (s + 1) * LANES]
+    own = lambda cell, s: traces[layer * PATCH + cell, :, (s - 1) * LANES : s * LANES]
     slots = {}
     if layer < LAYERS - 1:
-        slots[1] = own(e, 0)
+        slots[1] = down[layer * PATCH + e]
     slots[2 if a == 1 else 3] = own(b, 1) if a == 1 else own(EY + b, 2)
     slots[4 if b == 1 else 5] = own(a * EY, 3) if b == 1 else own(a * EY + 1, 4)
     return slots
@@ -197,51 +206,52 @@
     return slots
 
 
-def lifted_layer(layer, stacks, coupling, lift):
+def lift_all(stacks, coupling, lift, left, right):
     lane = lax.broadcasted_iota(jnp.int32, (2 * VECS, DEEP), 1)
-    halfs = ((0, (1, 2, 3)), (DEEP, (3, 4, 5)))
-    sides = [[], []]
     r = 2 * VECS
-    for e, slots in enumerate(stacks):
-        block = coupling[layer * PATCH + e]
-        for side, (begin, numbers) in zip(sides, halfs):
+    for at, slots in enumerate(stacks):
+        for begin, numbers, kept_rows in ((0, (1, 2, 3), left), (DEEP, (3, 4, 5), right)):
             present = [slot for slot in numbers if slot in slots]
             y = dot(
                 jnp.concatenate([slots[slot] for slot in present], axis=0)[:, :TRACE],
-                block[:, begin : begin + DEEP],
+                coupling[at, :, begin : min(begin + DEEP, 6 * TRACE)],
             )
-            at = lane[:, : y.shape[1]] + begin
+            place = lane[:, : y.shape[1]] + begin
             kept = jnp.zeros((r, y.shape[1]), F32)
             for i, slot in enumerate(present):
-                inside = (at >= slot * TRACE) & (at < (slot + 1) * TRACE)
+                inside = (place >= slot * TRACE) & (place < (slot + 1) * TRACE)
                 kept = jnp.where(inside, y[r * i : r * (i + 1)], kept)
-            side.append(stacked(halves(kept)))
-    out = dot_rows(jnp.concatenate(sides[0], axis=0), lift[:, :DEEP]) + dot_rows(
-        jnp.concatenate(sides[1], axis=0), lift[:, DEEP:]
-    )
-    return [halves(out[r * e : r * (e + 1)]) for e in range(PATCH)]
-
-
-def transfer_kernel(ups, diag, coupling, lift, weights, passing, composed):
+            kept_rows[r * at : r * (at + 1)] = stacked(halves(kept))
+    out = dot_rows(left[...], lift[:, :DEEP]) + dot_rows(right[...], lift[:, DEEP:])
+    return [halves(out[r * at : r * (at + 1)]) for at in range(CELLS)]
+
+
+def transfer_kernel(ups, diag, coupling, lift, lifted_rows, passing, composed, outflows, first):
     ups = ups_of(ups)
     one = lax.broadcasted_iota(jnp.int32, (TRACE, TRACE), 0)
     two = lax.broadcasted_iota(jnp.int32, (TRACE, TRACE), 1)
     inflow = dot_rows((one == two).astype(F32).astype(BF16), lift[:, :TRACE]).astype(BF16)
     upper, lower = inflow[:NODES, :DEEP], inflow[NODES:, DEEP:]
-    first = []
     for at in range(CELLS):
-        block = diag[at]
-        lifted_rows = jnp.concatenate([dot(upper, block[:DEEP]), dot(lower, block[DEEP:])], axis=0)
-        upwind = coupling[at][:, :LANES]
-        weight = dot(jnp.concatenate([upwind, upwind], axis=1), deep_rows(lifted_rows))
-        weights[at] = deep_rows(weight)
-        passed_on = face_of(blocks_of(weight), 1)
+        lifts = jnp.concatenate([dot(upper, diag[at, :DEEP]), dot(lower, diag[at, DEEP:])], axis=0)
+        lifted_rows[at] = deep_rows(lifts)
+        outflows[at] = deep_rows(face_of(blocks_of(lifts), 1))
+    for at in range(CELLS):
+        upwind = coupling[at, :, :LANES]
+        passed_on = dot(jnp.concatenate([upwind, upwind], axis=1), outflows[at])
         passing[at] = deep_rows(passed_on)
         if at < PATCH:
-            first.append(passed_on)
-    both = [times(chosen(first, ups[1][e]), passing[PATCH + e]) for e in range(PATCH)]
+            first[at] = passed_on
+    source = [first[e] for e in range(PATCH)]
+    both = [times(chosen(source, ups[1][e]), passing[PATCH + e]) for e in range(PATCH)]
     for e in range(PATCH):
         composed[e] = -times(chosen(both, ups[2][e]), passing[2 * PATCH + e])
+
+
+def weight_kernel(coupling, lifted_rows, unused, weights):
+    for at in range(CELLS):
+        upwind = coupling[at][:, :LANES]
+        weights[at] = deep_rows(dot(jnp.concatenate([upwind, upwind], axis=1), lifted_rows[at]))
 
 
 def turned(x, by):
@@ -299,23 +309,21 @@
 
 
 def source_kernel(
-    ups, rhs, traces, from_above, outer, inner, from_across, diag, coupling, lift, passing, composed,
-    solved, sources, packed,
+    ups, rhs, traces, down, from_above, outer, inner, from_across, diag, coupling, lift, passing, composed,
+    solved, sources, packed, left, right,
 ):
     ups = ups_of(ups)
+    stacks = [
+        near_slots(layer, e, traces, down) | far_slots(layer, e, from_above, outer, inner, from_across)
+        for layer in range(LAYERS)
+        for e in range(PATCH)
+    ]
     outflows = []
-    for layer in range(LAYERS):
-        stacks = [
-            near_slots(layer, e, traces) | far_slots(layer, e, from_above, outer, inner, from_across)
-            for e in range(PATCH)
-        ]
-        lifts = lifted_layer(layer, stacks, coupling, lift)
-        for e in range(PATCH):
-            at = layer * PATCH + e
-            y = halves(dot(stacked(rhs[at] - lifts[e]), diag[at]))
-            solved[at] = y
-            outflows.append(face_of(blocks_of(y), 1))
-            sources[at] = outflows[at]
+    for at, x in enumerate(lift_all(stacks, coupling, lift, left, right)):
+        y = halves(dot(stacked(rhs[at] - x), diag[at]))
+        solved[at] = y
+        outflows.append(face_of(blocks_of(y), 1))
+        sources[at] = outflows[at]
     current = outflows[:PATCH]
     for layer in range(1, LAYERS):
         current = [
@@ -328,24 +336,31 @@
     packed[...] = pack(maps, ends_of(ends))
 
 
-def joined(mine, theirs, bit):
+def ordered(mine, theirs, bit):
     later = (lax.axis_index("sweep") >> bit & 1) == 1
     first, first_ends = unpack(jnp.where(later, theirs, mine))
     second, second_ends = unpack(jnp.where(later, mine, theirs))
-    first_ends, second_ends = rows_of(first_ends), rows_of(second_ends)
+    return first, rows_of(first_ends), second, rows_of(second_ends)
+
+
+def joined(mine, theirs, bit):
+    first, first_ends, second, second_ends = ordered(mine, theirs, bit)
     maps = [after(first[at], chosen(second, first_ends[at])) for at in range(PATCH)]
-    return maps, [chosen(second_ends, first_ends[at]) for at in range(PATCH)], first, first_ends, later
+    return pack(maps, ends_of([chosen(second_ends, at) for at in first_ends]))
 
 
 def pair_kernel(mine, theirs, packed):
-    maps, ends, *unused = joined(mine[...], theirs[...], 0)
-    packed[...] = pack(maps, ends_of(ends))
-
-
-def group_kernel(mine, theirs, packed, leaving):
-    maps, ends, *unused = joined(mine[...], theirs[...], 1)
-    packed[...] = pack(maps, ends_of(ends))
-    leaving[...] = pack_states(placed([x[TRACE:] for x in maps], ends))
+    packed[...] = joined(mine[...], theirs[...], 0)
+
+
+def group_kernel(mine, theirs, unused, packed):
+    packed[...] = joined(mine[...], theirs[...], 1)
+
+
+def leaving_kernel(mine, theirs, leaving):
+    first, first_ends, second, second_ends = ordered(mine[...], theirs[...], 1)
+    states = [after(first[at][TRACE:], chosen(second, first_ends[at])) for at in range(PATCH)]
+    leaving[...] = pack_states(placed(states, [chosen(second_ends, at) for at in first_ends]))
 
 
 def prefix_kernel(pair, theirs, prefixes, ends):
@@ -376,7 +391,7 @@
 
 def finish_kernel(
     ups, second, fourth, third, before, prefixes, ends, old, solved, sources, weights, passing,
-    new, traces, inner, outer, across, below, made, sems,
+    new, traces, inner, outer, across, below, down, made, sems,
 ):
     maps, map_ends = unpack(before[...])
     second, fourth, third = [unpack_states(x[...]) for x in (second, fourth, third)]
@@ -399,22 +414,22 @@
             changes.append(old[at] - x)
     copy = pltpu.make_async_copy(made, new, sems.at[0])
     copy.start()
-    put_faces(changes, ups, traces, inner, outer, across, below)
+    put_inflows(put_sides(changes, traces, inner, outer, across), ups, down, below)
     copy.wait()
 
 
-def near_residual_kernel(traces, coupling, lift, out):
-    for layer in range(LAYERS):
-        stacks = [near_slots(layer, e, traces) for e in range(PATCH)]
-        for e, x in enumerate(lifted_layer(layer, stacks, coupling, lift)):
-            out[layer * PATCH + e] = x
-
-
-def residual_kernel(near, from_above, outer, inner, from_across, coupling, lift, out):
-    for layer in range(LAYERS):
-        stacks = [far_slots(layer, e, from_above, outer, inner, from_across) for e in range(PATCH)]
-        for e, x in enumerate(lifted_layer(layer, stacks, coupling, lift)):
-            out[layer * PATCH + e] = near[layer * PATCH + e] + x
+def near_residual_kernel(traces, down, coupling, lift, out, left, right):
+    stacks = [near_slots(layer, e, traces, down) for layer in range(LAYERS) for e in range(PATCH)]
+    for at, x in enumerate(lift_all(stacks, coupling, lift, left, right)):
+        out[at] = x
+
+
+def residual_kernel(near, from_above, outer, inner, from_across, coupling, lift, out, left, right):
+    stacks = [
+        far_slots(layer, e, from_above, outer, inner, from_across) for layer in range(LAYERS) for e in range(PATCH)
+    ]
+    for at, x in enumerate(lift_all(stacks, coupling, lift, left, right)):
+        out[at] = near[at] + x
 
 
 VMEM = pl.BlockSpec(memory_space=pltpu.VMEM)
@@ -438,19 +453,22 @@
     return run
 
 
-FACE_OUTS = [
-    ((CELLS, 2 * VECS, len(SLOT_FACES) * LANES), BF16),
+SIDE_OUTS = [
+    ((CELLS, 2 * VECS, (len(SLOT_FACES) - 1) * LANES), BF16),
     ((LAYERS * EY, VECS, LANES), F32),
     ((LAYERS * EY, VECS, LANES), F32),
     ((LAYERS * EX, VECS, LANES), F32),
-    ((LAYERS * EY, VECS, LANES), F32),
 ]
+BELOW = ((LAYERS * EY, VECS, LANES), F32)
+DOWN = (((LAYERS - 1) * PATCH, 2 * VECS, LANES), BF16)
+ROW_TILE = ((16, LANES), F32)
+FLUXES = [pltpu.VMEM((CELLS * 2 * VECS, DEEP), BF16), pltpu.VMEM((CELLS * 2 * VECS, 6 * TRACE - DEEP), BF16)]
 FIELD = ((CELLS, VECS, ROWS), F32)
 STATES = ((3 * VECS, LANES), F32)
 PACKED = ((3 * TRACE + 8, LANES), F32)
 
 
-def exchange_sides(inner, outer, across, below):
+def exchange_sides(below, outer, inner, across):
     wide, deep = lax.axis_size("cx"), lax.axis_size("sweep")
     outer = lax.ppermute(outer, "cx", [(i, i + 1 if i % 2 else i - 1) for i in range(1, wide - 1)])
     below = lax.ppermute(below, "sweep", [(i + 1, i) for i in range(deep - 1)])
@@ -474,37 +492,42 @@
     diag = diag_inverse.reshape(CELLS, ROWS, ROWS)
     blocks = coupling.reshape(CELLS, TRACE, 6 * TRACE)
     lift = lift_table.T
-    (ups,) = call(position_kernel, [((16, LANES), F32)], micros=2)(upstream.transpose(1, 2, 0))
-    traces, *sends = call(open_kernel, FACE_OUTS, micros=2)(ups, old)
-    halos = exchange_sides(*sends)
-    weights, passing, composed = call(
+    traces, inner, outer, across, faces = call(
+        open_kernel, SIDE_OUTS + [((CELLS, 2 * VECS, LANES), F32)], micros=2
+    )(old)
+    ups, down, below = call(position_kernel, [ROW_TILE, DOWN, BELOW])(upstream.transpose(1, 2, 0), faces)
+    halos = exchange_sides(below, outer, inner, across)
+    lifted_rows, passing, composed = call(
         transfer_kernel,
         [((CELLS, DEEP, ROWS), BF16), ((CELLS, DEEP, LANES), BF16), ((PATCH, TRACE, LANES), F32)],
+        [pltpu.VMEM((CELLS, DEEP, LANES), BF16), pltpu.VMEM((PATCH, TRACE, LANES), F32)],
     )(ups, diag, blocks, lift)
-    solved, sources, single = call(source_kernel, [FIELD, ((CELLS, VECS, LANES), F32), PACKED])(
-        ups, rhs, traces, *halos, diag, blocks, lift, passing, composed
+    solved, sources, single = call(source_kernel, [FIELD, ((CELLS, VECS, LANES), F32), PACKED], FLUXES)(
+        ups, rhs, traces, down, *halos, diag, blocks, lift, passing, composed
     )
     partner = swapped(single, 1)
+    (weights,) = call(weight_kernel, [((CELLS, DEEP, ROWS), BF16)])(blocks, lifted_rows, single)
     (pair,) = call(pair_kernel, [PACKED])(single, partner)
     partner_pair = swapped(pair, 2)
-    group, leaving = call(group_kernel, [PACKED, STATES])(pair, partner_pair)
+    (leaving,) = call(leaving_kernel, [STATES])(pair, partner_pair)
     second = passed(leaving, 0, 1, 2)
+    (group,) = call(group_kernel, [PACKED])(pair, partner_pair, leaving)
     before = passed(group, 2, 3, 2)
+    (leaving,) = call(onward_kernel, [STATES])(second, group)
+    third = passed(leaving, 1, 2, 2)
+    fourth = passed(leaving, 1, 3, 0)
     prefixes, ends = call(prefix_kernel, [((PATCH, MAP_ROWS, LANES), F32), ((8, LANES), F32)])(
         partner, partner_pair
     )
-    (leaving,) = call(onward_kernel, [STATES])(second, group)
-    third = passed(leaving, 1, 2, 2)
-    fourth = passed(leaving, 1, 3, 0)
-    new, traces, *sends = call(
+    new, traces, inner, outer, across, below, down = call(
         finish_kernel,
-        [FIELD] + FACE_OUTS,
+        [FIELD] + SIDE_OUTS + [BELOW, DOWN],
         [pltpu.VMEM((CELLS, VECS, ROWS), F32), pltpu.SemaphoreType.DMA((1,))],
         far_outs=(0,),
     )(ups, second, fourth, third, before, prefixes, ends, old, solved, sources, weights, passing)
-    halos = exchange_sides(*sends)
-    (near,) = call(near_residual_kernel, [FIELD])(traces, blocks, lift)
-    (residual,) = call(residual_kernel, [FIELD])(near, *halos, blocks, lift)
+    halos = exchange_sides(below, outer, inner, across)
+    (near,) = call(near_residual_kernel, [FIELD], FLUXES)(traces, down, blocks, lift)
+    (residual,) = call(residual_kernel, [FIELD], FLUXES)(near, *halos, blocks, lift)
     shape = rhs_vectors.shape
     return new.reshape(shape), residual.reshape(shape)
 

time: 77.6 us -> 75.1 us (0.968)
  Pallas kernels: 11.3 us -> 9.65 us
  waiting for transfers between devices: 19.1 us -> 18.2 us
    pallas_call x11 -> x13, Pallas kernels: 11.3 us -> 9.65 us  [run(): pl.pallas_call(kernel, in_specs=[VMEM] * len(args), out_specs=[FAR if i i...]
    ppermute x2, starting transfers between devices: 4.75 us -> 6.2 us  [exchange_sides(): inner = lax.ppermute(inner, 'cx', [(i, i ^ 1) for i in range(wide)])]
    ppermute x2, waiting for transfers between devices: 13.8 us -> 12.7 us  [swapped(): lax.ppermute(packed, 'sweep', [(i, i ^ by) for i in range(lax.axis_size('...]
    ppermute x2, starting transfers between devices: 13.9 us -> 13.1 us  [exchange_sides(): lax.ppermute(outer, 'cx', [(i, i + 1 if i % 2 else i - 1) for i in range(...]
    unnamed x12 -> x14, local copies, waits for them, and re-layouts: 1.57 us -> 1.2 us
  transfers between devices with their start and end apart: 14 -> 14, of which waited for: 3 -> 4; matrix products, arithmetic and copies ran while one was open for 0% -> 0% of each run, Pallas kernels for 6% -> 5%
where the time goes in v4:
time: 75.1 us; the launch traced here: 74.6 us
  starting transfers between devices  44.7 us (60%)
  waiting for transfers between devices  18.2 us (24%)
  Pallas kernels  9.65 us (13%)
  local copies, waits for them, and re-layouts  1.2 us (2%)
  between operations  0.94 us (1%)
    ppermute x2, starting transfers between devices, exchange_sides(): lax.ppermute(outer, 'cx', [(i, i + 1 if i % 2 else i - 1) for i in range(...  13.1 us
    ppermute x2, waiting for transfers between devices, swapped(): lax.ppermute(packed, 'sweep', [(i, i ^ by) for i in range(lax.axis_size('...  12.7 us
    pallas_call x13, Pallas kernels, run(): pl.pallas_call(kernel, in_specs=[VMEM] * len(args), out_specs=[FAR if i i...  9.65 us
    ppermute x2, starting transfers between devices, exchange_sides(): below = lax.ppermute(below, 'sweep', [(i + 1, i) for i in range(deep - 1)])  9.36 us
    ppermute x2, starting transfers between devices, exchange_sides(): across = lax.ppermute(across, 'cy', [(0, 1), (1, 0)])  8.06 us
    ppermute x2, starting transfers between devices, exchange_sides(): inner = lax.ppermute(inner, 'cx', [(i, i ^ 1) for i in range(wide)])  6.2 us
    ppermute x4, waiting for transfers between devices, passed(): return lax.ppermute(states, 'sweep', pairs)  5.26 us
    ppermute x4, starting transfers between devices, passed(): return lax.ppermute(states, 'sweep', pairs)  4.05 us
  transfers between devices with their start and end apart: 14, of which 4 were waited for; matrix products, arithmetic and copies ran while one was open for 0% of the time, Pallas kernels for 5%

profile of v4, /device:TPU:7, one launch (start us, length us, event | category | flops | bytes accessed | tf_op | source)
XLA Modules:
  0.0 74.6 jit_solution(14429288791714877962)
XLA Ops:
  0.6 1.0 %copy-done.4 = f32[3,2,2,16,320]{4,3,2,1,0:T(8,128)S(1)} copy-done((f32[3,2,2,16,320]{4,3,2,1,0:T(8,128)S(1)}, f32[3,2,2,16,320]{4,3,2,1,0:T(8,128)}, u32[]{:S(2)}) %copy-start.4) | copy-done | bytes 245784
  1.6 0.4 shard_map.77
  2.1 0.2 copy-done.6
  2.4 5.5 %collective-permute-start = (f32[6,16,128]{2,1,0:T(8,128)S(1)}, f32[6,16,128]{2,1,0:T(8,128)S(1)}, u32[]{:S(2)}, u32[]{:S(2)}) collective-permute-start(f32[6,16,128]{2,1,0:T(8,128)S(1)} %get-tuple-element.29), channel_id=1, source_target_pairs={{32,0},{64,32},{96,64},{128,96},{160,128},{192,160},{224,192},{256... | collective-permute-start | bytes 147464 | tf_op jit(solution)/shard_map/ppermute | solution.py:474
  7.9 11.2 %collective-permute-start.1 = (f32[6,16,128]{2,1,0:T(8,128)S(1)}, f32[6,16,128]{2,1,0:T(8,128)S(1)}, u32[]{:S(2)}, u32[]{:S(2)}) collective-permute-start(f32[6,16,128]{2,1,0:T(8,128)S(1)} %get-tuple-element.30), channel_id=1, source_target_pairs={{2,4},{4,2},{6,8},{8,6},{10,12},{12,10},{14,16},{16,14},{18,20},{2... | collective-permute-start | bytes 147464 | tf_op jit(solution)/shard_map/ppermute | solution.py:473
  19.2 1.9 %collective-permute-start.2 = (f32[6,16,128]{2,1,0:T(8,128)S(1)}, f32[6,16,128]{2,1,0:T(8,128)S(1)}, u32[]{:S(2)}, u32[]{:S(2)}) collective-permute-start(f32[6,16,128]{2,1,0:T(8,128)S(1)} %get-tuple-element.31), channel_id=1, source_target_pairs={{0,2},{2,0},{4,6},{6,4},{8,10},{10,8},{12,14},{14,12},{16,18},{18,... | collective-permute-start | bytes 147464 | tf_op jit(solution)/shard_map/ppermute | solution.py:475
  21.1 3.1 %collective-permute-start.3 = (f32[6,16,128]{2,1,0:T(8,128)S(1)}, f32[6,16,128]{2,1,0:T(8,128)S(1)}, u32[]{:S(2)}, u32[]{:S(2)}) collective-permute-start(f32[6,16,128]{2,1,0:T(8,128)S(1)} %get-tuple-element.32), channel_id=1, source_target_pairs={{0,1},{1,0},{2,3},{3,2},{4,5},{5,4},{6,7},{7,6},{8,9},{9,8},{10,11... | collective-permute-start | bytes 147464 | tf_op jit(solution)/shard_map/ppermute | solution.py:476
  24.3 1.5 %shard_map.79 = (bf16[12,256,320]{2,1,0:T(8,128)(2,1)S(1)}, bf16[12,256,128]{2,1,0:T(8,128)(2,1)S(1)}, f32[4,80,128]{2,1,0:T(8,128)S(1)}) custom-call(f32[16,128]{1,0:T(8,128)S(1)} %get-tuple-element.26.ups, bf16[12,320,320]{2,1,0:T(8,128)(2,1)S(1)} %bitcast.8, bf16[12,80,480]{2,1,0:T(8,128)(2,1)S(1)} %bitcast.10, bf16[320,480]{1,0:T(8,128)(2,1)S(1)} %bitcast.15), custom_call_target="tpu_custom_call" | custom-call | flops 1000000000 | bytes 3600000 | tf_op jit(solution)/shard_map/pallas_call | solution.py:441
  25.9 1.5 %shard_map.80 = (f32[12,16,320]{2,1,0:T(8,128)S(1)}, f32[12,16,128]{2,1,0:T(8,128)S(1)}, f32[248,128]{1,0:T(8,128)S(1)}) custom-call(f32[16,128]{1,0:T(8,128)S(1)} %get-tuple-element.26.ups, f32[12,16,320]{2,1,0:T(8,128)S(1)} %bitcast.19, bf16[12,32,512]{2,1,0:T(8,128)(2,1)S(1)} %get-tuple-element.27.traces, bf16[8,32,128]{2,1,0:T(8,128)(2,1)S(1)} %get-tuple-element.28.down, ...), custom_call_target="tpu_custom_call" | custom-call | flops 1000000000 | bytes 3600000 | tf_op jit(solution)/shard_map/pallas_call | solution.py:441
  27.4 1.9 %collective-permute-start.4 = (f32[248,128]{1,0:T(8,128)S(1)}, f32[248,128]{1,0:T(8,128)S(1)}, u32[]{:S(2)}, u32[]{:S(2)}) collective-permute-start(f32[248,128]{1,0:T(8,128)S(1)} %get-tuple-element.35.mine.unused), channel_id=1, source_target_pairs={{0,32},{32,0},{64,96},{96,64},{128,160},{160,128},{192,224},{224,1... | collective-permute-start | bytes 380936 | tf_op jit(solution)/shard_map/ppermute | solution.py:481
  29.3 4.4 %collective-permute-done.4.theirs.pair = f32[248,128]{1,0:T(8,128)S(1)} collective-permute-done((f32[248,128]{1,0:T(8,128)S(1)}, f32[248,128]{1,0:T(8,128)S(1)}, u32[]{:S(2)}, u32[]{:S(2)}) %collective-permute-start.4) | collective-permute-done | bytes 127008 | tf_op jit(solution)/shard_map/ppermute | solution.py:481
  33.7 0.4 shard_map.81.mine
  34.2 1.9 %collective-permute-start.5 = (f32[248,128]{1,0:T(8,128)S(1)}, f32[248,128]{1,0:T(8,128)S(1)}, u32[]{:S(2)}, u32[]{:S(2)}) collective-permute-start(f32[248,128]{1,0:T(8,128)S(1)} %shard_map.81.mine), channel_id=1, source_target_pairs={{0,64},{32,96},{64,0},{96,32},{128,192},{160,224},{192,128},{224,1... | collective-permute-start | bytes 380936 | tf_op jit(solution)/shard_map/ppermute | solution.py:481
  36.1 0.5 shard_map.86.weights
  36.6 8.3 %collective-permute-done.5.theirs = f32[248,128]{1,0:T(8,128)S(1)} collective-permute-done((f32[248,128]{1,0:T(8,128)S(1)}, f32[248,128]{1,0:T(8,128)S(1)}, u32[]{:S(2)}, u32[]{:S(2)}) %collective-permute-start.5) | collective-permute-done | bytes 127008 | tf_op jit(solution)/shard_map/ppermute | solution.py:481
  44.9 0.3 shard_map.82.unused
  45.3 0.7 collective-permute-start.6
  45.9 0.4 shard_map.83.packed
  46.4 1.3 %collective-permute-start.9 = (f32[248,128]{1,0:T(8,128)S(1)}, f32[248,128]{1,0:T(8,128)S(1)}, u32[]{:S(2)}, u32[]{:S(2)}) collective-permute-start(f32[248,128]{1,0:T(8,128)S(1)} %shard_map.83.packed), channel_id=1, source_target_pairs={{256,448},{288,480},{320,384},{352,416},{257,449},{289,481},{321,3... | collective-permute-start | bytes 380936 | tf_op jit(solution)/shard_map/ppermute | solution.py:486
  47.7 0.3 shard_map.84
  48.0 1.4 %collective-permute-start.8 = (f32[48,128]{1,0:T(8,128)S(1)}, f32[48,128]{1,0:T(8,128)S(1)}, u32[]{:S(2)}, u32[]{:S(2)}) collective-permute-start(f32[48,128]{1,0:T(8,128)S(1)} %shard_map.84), channel_id=1, source_target_pairs={{128,320},{160,352},{192,256},{224,288},{129,321},{161,353},{193,2... | collective-permute-start | bytes 73736 | tf_op jit(solution)/shard_map/ppermute | solution.py:486
  49.4 0.7 collective-permute-start.7
  50.1 0.4 shard_map.85
  50.5 5.2 %collective-permute-done.8.third = f32[48,128]{1,0:T(8,128)S(1)} collective-permute-done((f32[48,128]{1,0:T(8,128)S(1)}, f32[48,128]{1,0:T(8,128)S(1)}, u32[]{:S(2)}, u32[]{:S(2)}) %collective-permute-start.8) | collective-permute-done | bytes 24608 | tf_op jit(solution)/shard_map/ppermute | solution.py:486
  55.7 1.7 %shard_map.87 = (f32[12,16,320]{2,1,0:T(8,128)}, bf16[12,32,512]{2,1,0:T(8,128)(2,1)S(1)}, f32[6,16,128]{2,1,0:T(8,128)S(1)}, f32[6,16,128]{2,1,0:T(8,128)S(1)},...) custom-call(f32[16,128]{1,0:T(8,128)S(1)} %get-tuple-element.26.ups, ...), custom_call_target="tpu_custom_call" | custom-call | flops 1000000000 | bytes 3600000 | tf_op jit(solution)/shard_map/pallas_call | solution.py:441
  57.4 3.9 %collective-permute-start.10 = (f32[6,16,128]{2,1,0:T(8,128)S(1)}, f32[6,16,128]{2,1,0:T(8,128)S(1)}, u32[]{:S(2)}, u32[]{:S(2)}) collective-permute-start(f32[6,16,128]{2,1,0:T(8,128)S(1)} %get-tuple-element.44), channel_id=1, source_target_pairs={{32,0},{64,32},{96,64},{128,96},{160,128},{192,160},{224,192},{256... | collective-permute-start | bytes 147464 | tf_op jit(solution)/shard_map/ppermute | solution.py:474
  61.3 1.9 %collective-permute-start.11 = (f32[6,16,128]{2,1,0:T(8,128)S(1)}, f32[6,16,128]{2,1,0:T(8,128)S(1)}, u32[]{:S(2)}, u32[]{:S(2)}) collective-permute-start(f32[6,16,128]{2,1,0:T(8,128)S(1)} %get-tuple-element.45), channel_id=1, source_target_pairs={{2,4},{4,2},{6,8},{8,6},{10,12},{12,10},{14,16},{16,14},{18,20},{2... | collective-permute-start | bytes 147464 | tf_op jit(solution)/shard_map/ppermute | solution.py:473
  63.2 4.3 %collective-permute-start.12 = (f32[6,16,128]{2,1,0:T(8,128)S(1)}, f32[6,16,128]{2,1,0:T(8,128)S(1)}, u32[]{:S(2)}, u32[]{:S(2)}) collective-permute-start(f32[6,16,128]{2,1,0:T(8,128)S(1)} %get-tuple-element.46), channel_id=1, source_target_pairs={{0,2},{2,0},{4,6},{6,4},{8,10},{10,8},{12,14},{14,12},{16,18},{18,... | collective-permute-start | bytes 147464 | tf_op jit(solution)/shard_map/ppermute | solution.py:475
  67.5 4.9 %collective-permute-start.13 = (f32[6,16,128]{2,1,0:T(8,128)S(1)}, f32[6,16,128]{2,1,0:T(8,128)S(1)}, u32[]{:S(2)}, u32[]{:S(2)}) collective-permute-start(f32[6,16,128]{2,1,0:T(8,128)S(1)} %get-tuple-element.47), channel_id=1, source_target_pairs={{0,1},{1,0},{2,3},{3,2},{4,5},{5,4},{6,7},{7,6},{8,9},{9,8},{10,11... | collective-permute-start | bytes 147464 | tf_op jit(solution)/shard_map/ppermute | solution.py:476
  72.4 0.6 shard_map.88.near
  73.1 0.2 collective-permute-done.13.from_across
  73.3 1.3 %shard_map.89 = f32[12,16,320]{2,1,0:T(8,128)} custom-call(f32[12,16,320]{2,1,0:T(8,128)S(1)} %shard_map.88.near, f32[6,16,128]{2,1,0:T(8,128)S(1)} %collective-permute-done.10.from_above, f32[6,16,128]{2,1,0:T(8,128)S(1)} %collective-permute-done.11.outer, f32[6,16,128]{2,1,0:T(8,128)S(1)} %collective-permute-done.12.inner, ...), custom_call_target="tpu_custom_call" | custom-call | flops 1000000000 | bytes 3600000 | tf_op jit(solution)/shard_map/pallas_call | solution.py:441
  (23 shorter events, 0.2 us)
Async XLA Ops:
  0.6 1.0 %copy-start.4 = (f32[3,2,2,16,320]{4,3,2,1,0:T(8,128)S(1)}, f32[3,2,2,16,320]{4,3,2,1,0:T(8,128)}, u32[]{:S(2)}) copy-start(f32[3,2,2,16,320]{4,3,2,1,0:T(8,128)} %param.7) | copy-start | bytes 737284
  1.6 0.7 copy-start.6
  1.6 22.6 %copy-start.1 = (bf16[3,2,2,80,480]{4,3,2,1,0:T(8,128)(2,1)S(1)}, bf16[3,2,2,80,480]{4,3,2,1,0:T(8,128)(2,1)}, u32[]{:S(2)}) copy-start(bf16[3,2,2,80,480]{4,3,2,1,0:T(8,128)(2,1)} %param.9) | copy-start | bytes 2764804
  2.0 22.2 %copy-start = (bf16[3,2,2,320,320]{4,3,2,1,0:T(8,128)(2,1)S(1)}, bf16[3,2,2,320,320]{4,3,2,1,0:T(8,128)(2,1)}, u32[]{:S(2)}) copy-start(bf16[3,2,2,320,320]{4,3,2,1,0:T(8,128)(2,1)} %param.8) | copy-start | bytes 7372804
  2.1 22.2 %copy-start.2 = (bf16[480,320]{0,1:T(8,128)(2,1)S(1)}, bf16[480,320]{0,1:T(8,128)(2,1)}, u32[]{:S(2)}) copy-start(bf16[480,320]{0,1:T(8,128)(2,1)} %param.10) | copy-start | bytes 921604
  2.4 23.4 %copy-start.3 = (f32[3,2,2,16,320]{4,3,2,1,0:T(8,128)S(1)}, f32[3,2,2,16,320]{4,3,2,1,0:T(8,128)}, u32[]{:S(2)}) copy-start(f32[3,2,2,16,320]{4,3,2,1,0:T(8,128)} %param.6) | copy-start | bytes 737284
  2.4 23.4 %collective-permute-start = (f32[6,16,128]{2,1,0:T(8,128)S(1)}, f32[6,16,128]{2,1,0:T(8,128)S(1)}, u32[]{:S(2)}, u32[]{:S(2)}) collective-permute-start(f32[6,16,128]{2,1,0:T(8,128)S(1)} %get-tuple-element.29), channel_id=1, source_target_pairs={{32,0},{64,32},{96,64},{128,96},{160,128},{192,160},{224,192},{256... | collective-permute-start | bytes 147464 | tf_op jit(solution)/shard_map/ppermute | solution.py:474
  7.9 17.9 %collective-permute-start.1 = (f32[6,16,128]{2,1,0:T(8,128)S(1)}, f32[6,16,128]{2,1,0:T(8,128)S(1)}, u32[]{:S(2)}, u32[]{:S(2)}) collective-permute-start(f32[6,16,128]{2,1,0:T(8,128)S(1)} %get-tuple-element.30), channel_id=1, source_target_pairs={{2,4},{4,2},{6,8},{8,6},{10,12},{12,10},{14,16},{16,14},{18,20},{2... | collective-permute-start | bytes 147464 | tf_op jit(solution)/shard_map/ppermute | solution.py:473
  19.2 6.7 %collective-permute-start.2 = (f32[6,16,128]{2,1,0:T(8,128)S(1)}, f32[6,16,128]{2,1,0:T(8,128)S(1)}, u32[]{:S(2)}, u32[]{:S(2)}) collective-permute-start(f32[6,16,128]{2,1,0:T(8,128)S(1)} %get-tuple-element.31), channel_id=1, source_target_pairs={{0,2},{2,0},{4,6},{6,4},{8,10},{10,8},{12,14},{14,12},{16,18},{18,... | collective-permute-start | bytes 147464 | tf_op jit(solution)/shard_map/ppermute | solution.py:475
  21.1 4.8 %collective-permute-start.3 = (f32[6,16,128]{2,1,0:T(8,128)S(1)}, f32[6,16,128]{2,1,0:T(8,128)S(1)}, u32[]{:S(2)}, u32[]{:S(2)}) collective-permute-start(f32[6,16,128]{2,1,0:T(8,128)S(1)} %get-tuple-element.32), channel_id=1, source_target_pairs={{0,1},{1,0},{2,3},{3,2},{4,5},{5,4},{6,7},{7,6},{8,9},{9,8},{10,11... | collective-permute-start | bytes 147464 | tf_op jit(solution)/shard_map/ppermute | solution.py:476
  27.4 6.3 %collective-permute-start.4 = (f32[248,128]{1,0:T(8,128)S(1)}, f32[248,128]{1,0:T(8,128)S(1)}, u32[]{:S(2)}, u32[]{:S(2)}) collective-permute-start(f32[248,128]{1,0:T(8,128)S(1)} %get-tuple-element.35.mine.unused), channel_id=1, source_target_pairs={{0,32},{32,0},{64,96},{96,64},{128,160},{160,128},{192,224},{224,1... | collective-permute-start | bytes 380936 | tf_op jit(solution)/shard_map/ppermute | solution.py:481
  34.2 10.7 %collective-permute-start.5 = (f32[248,128]{1,0:T(8,128)S(1)}, f32[248,128]{1,0:T(8,128)S(1)}, u32[]{:S(2)}, u32[]{:S(2)}) collective-permute-start(f32[248,128]{1,0:T(8,128)S(1)} %shard_map.81.mine), channel_id=1, source_target_pairs={{0,64},{32,96},{64,0},{96,32},{128,192},{160,224},{192,128},{224,1... | collective-permute-start | bytes 380936 | tf_op jit(solution)/shard_map/ppermute | solution.py:481
  45.3 2.4 %collective-permute-start.6 = (f32[48,128]{1,0:T(8,128)S(1)}, f32[48,128]{1,0:T(8,128)S(1)}, u32[]{:S(2)}, u32[]{:S(2)}) collective-permute-start(f32[48,128]{1,0:T(8,128)S(1)} %shard_map.82.unused), channel_id=1, source_target_pairs={{0,192},{32,224},{64,128},{96,160},{1,193},{33,225},{65,129},{97,1... | collective-permute-start | bytes 73736 | tf_op jit(solution)/shard_map/ppermute | solution.py:486
  46.4 9.3 %collective-permute-start.9 = (f32[248,128]{1,0:T(8,128)S(1)}, f32[248,128]{1,0:T(8,128)S(1)}, u32[]{:S(2)}, u32[]{:S(2)}) collective-permute-start(f32[248,128]{1,0:T(8,128)S(1)} %shard_map.83.packed), channel_id=1, source_target_pairs={{256,448},{288,480},{320,384},{352,416},{257,449},{289,481},{321,3... | collective-permute-start | bytes 380936 | tf_op jit(solution)/shard_map/ppermute | solution.py:486
  48.0 7.7 %copy-start.5 = (f32[3,2,2,16,320]{4,3,2,1,0:T(8,128)S(1)}, f32[3,2,2,16,320]{4,3,2,1,0:T(8,128)}, u32[]{:S(2)}) copy-start(f32[3,2,2,16,320]{4,3,2,1,0:T(8,128)} %param.7) | copy-start | bytes 737284
  48.0 7.7 %collective-permute-start.8 = (f32[48,128]{1,0:T(8,128)S(1)}, f32[48,128]{1,0:T(8,128)S(1)}, u32[]{:S(2)}, u32[]{:S(2)}) collective-permute-start(f32[48,128]{1,0:T(8,128)S(1)} %shard_map.84), channel_id=1, source_target_pairs={{128,320},{160,352},{192,256},{224,288},{129,321},{161,353},{193,2... | collective-permute-start | bytes 73736 | tf_op jit(solution)/shard_map/ppermute | solution.py:486
  49.4 6.3 %collective-permute-start.7 = (f32[48,128]{1,0:T(8,128)S(1)}, f32[48,128]{1,0:T(8,128)S(1)}, u32[]{:S(2)}, u32[]{:S(2)}) collective-permute-start(f32[48,128]{1,0:T(8,128)S(1)} %shard_map.84), channel_id=1, source_target_pairs={{128,384},{160,416},{192,448},{224,480},{129,385},{161,417},{193,4... | collective-permute-start | bytes 73736 | tf_op jit(solution)/shard_map/ppermute | solution.py:486
  57.4 15.7 %collective-permute-start.10 = (f32[6,16,128]{2,1,0:T(8,128)S(1)}, f32[6,16,128]{2,1,0:T(8,128)S(1)}, u32[]{:S(2)}, u32[]{:S(2)}) collective-permute-start(f32[6,16,128]{2,1,0:T(8,128)S(1)} %get-tuple-element.44), channel_id=1, source_target_pairs={{32,0},{64,32},{96,64},{128,96},{160,128},{192,160},{224,192},{256... | collective-permute-start | bytes 147464 | tf_op jit(solution)/shard_map/ppermute | solution.py:474
  61.3 11.8 %collective-permute-start.11 = (f32[6,16,128]{2,1,0:T(8,128)S(1)}, f32[6,16,128]{2,1,0:T(8,128)S(1)}, u32[]{:S(2)}, u32[]{:S(2)}) collective-permute-start(f32[6,16,128]{2,1,0:T(8,128)S(1)} %get-tuple-element.45), channel_id=1, source_target_pairs={{2,4},{4,2},{6,8},{8,6},{10,12},{12,10},{14,16},{16,14},{18,20},{2... | collective-permute-start | bytes 147464 | tf_op jit(solution)/shard_map/ppermute | solution.py:473
  63.2 9.9 %collective-permute-start.12 = (f32[6,16,128]{2,1,0:T(8,128)S(1)}, f32[6,16,128]{2,1,0:T(8,128)S(1)}, u32[]{:S(2)}, u32[]{:S(2)}) collective-permute-start(f32[6,16,128]{2,1,0:T(8,128)S(1)} %get-tuple-element.46), channel_id=1, source_target_pairs={{0,2},{2,0},{4,6},{6,4},{8,10},{10,8},{12,14},{14,12},{16,18},{18,... | collective-permute-start | bytes 147464 | tf_op jit(solution)/shard_map/ppermute | solution.py:475
  67.5 5.8 %collective-permute-start.13 = (f32[6,16,128]{2,1,0:T(8,128)S(1)}, f32[6,16,128]{2,1,0:T(8,128)S(1)}, u32[]{:S(2)}, u32[]{:S(2)}) collective-permute-start(f32[6,16,128]{2,1,0:T(8,128)S(1)} %get-tuple-element.47), channel_id=1, source_target_pairs={{0,1},{1,0},{2,3},{3,2},{4,5},{5,4},{6,7},{7,6},{8,9},{9,8},{10,11... | collective-permute-start | bytes 147464 | tf_op jit(solution)/shard_map/ppermute | solution.py:476

commit v5 on v4

--- a/solution.py
+++ b/solution.py
@@ -141,10 +141,10 @@
     return jnp.concatenate(found + [jnp.zeros((16 - CELLS, LANES), F32)], axis=0)
 
 
-def put_sides(cells, traces, inner, outer, across):
+def put_sides(rows, traces, inner, outer, across):
     core = lax.axis_index("cy")
     even = lax.rem(lax.axis_index("cx"), 2) == 0
-    picked = dot(jnp.concatenate([stacked(x) for x in cells], axis=0), side_table())
+    picked = dot(rows[...], side_table())
     pieces = [picked[2 * VECS * at : 2 * VECS * (at + 1)] for at in range(CELLS)]
     whole = [halves(piece[:, LANES:]) for piece in pieces]
     for layer in range(LAYERS):
@@ -170,8 +170,10 @@
             down[(layer - 1) * PATCH + e] = piece.astype(BF16)
 
 
-def open_kernel(old, traces, inner, outer, across, faces):
-    for at, piece in enumerate(put_sides([old[at] for at in range(CELLS)], traces, inner, outer, across)):
+def open_kernel(old, traces, inner, outer, across, faces, rows):
+    for at in range(CELLS):
+        rows[2 * VECS * at : 2 * VECS * (at + 1)] = stacked(old[at])
+    for at, piece in enumerate(put_sides(rows, traces, inner, outer, across)):
         faces[at] = piece
 
 
@@ -309,18 +311,16 @@
 
 
 def source_kernel(
-    ups, rhs, traces, down, from_above, outer, inner, from_across, diag, coupling, lift, passing, composed,
+    ups, rest, from_above, outer, inner, from_across, diag, coupling, lift, passing, composed,
     solved, sources, packed, left, right,
 ):
     ups = ups_of(ups)
     stacks = [
-        near_slots(layer, e, traces, down) | far_slots(layer, e, from_above, outer, inner, from_across)
-        for layer in range(LAYERS)
-        for e in range(PATCH)
+        far_slots(layer, e, from_above, outer, inner, from_across) for layer in range(LAYERS) for e in range(PATCH)
     ]
     outflows = []
     for at, x in enumerate(lift_all(stacks, coupling, lift, left, right)):
-        y = halves(dot(stacked(rhs[at] - x), diag[at]))
+        y = halves(dot(stacked(rest[at] - x), diag[at]))
         solved[at] = y
         outflows.append(face_of(blocks_of(y), 1))
         sources[at] = outflows[at]
@@ -391,7 +391,7 @@
 
 def finish_kernel(
     ups, second, fourth, third, before, prefixes, ends, old, solved, sources, weights, passing,
-    new, traces, inner, outer, across, below, down, made, sems,
+    new, traces, inner, outer, across, below, down, made, operands, rows, sems,
 ):
     maps, map_ends = unpack(before[...])
     second, fourth, third = [unpack_states(x[...]) for x in (second, fourth, third)]
@@ -401,21 +401,29 @@
     states = [after(entering[at], prefixes[at]) for at in range(PATCH)]
     current = placed(states, rows_of(ends))
     ups = ups_of(ups)
-    changes = []
     for layer in range(LAYERS):
         inflow = [chosen(current, ups[layer][e]) for e in range(PATCH)]
-        current = [
-            sources[layer * PATCH + e] - times(inflow[e], passing[layer * PATCH + e]) for e in range(PATCH)
-        ]
         for e in range(PATCH):
-            at = layer * PATCH + e
-            x = solved[at] - times(inflow[e], weights[at])
-            made[at] = x
-            changes.append(old[at] - x)
+            operands[layer * PATCH + e] = deep_lhs(inflow[e])
+        if layer < LAYERS - 1:
+            current = [
+                sources[layer * PATCH + e] - halves(dot(operands[layer * PATCH + e], passing[layer * PATCH + e]))
+                for e in range(PATCH)
+            ]
+    for at in range(CELLS):
+        x = solved[at] - halves(dot(operands[at], weights[at]))
+        made[at] = x
+        rows[2 * VECS * at : 2 * VECS * (at + 1)] = stacked(old[at] - x)
     copy = pltpu.make_async_copy(made, new, sems.at[0])
     copy.start()
-    put_inflows(put_sides(changes, traces, inner, outer, across), ups, down, below)
+    put_inflows(put_sides(rows, traces, inner, outer, across), ups, down, below)
     copy.wait()
+
+
+def near_source_kernel(rhs, traces, down, coupling, lift, out, left, right):
+    stacks = [near_slots(layer, e, traces, down) for layer in range(LAYERS) for e in range(PATCH)]
+    for at, x in enumerate(lift_all(stacks, coupling, lift, left, right)):
+        out[at] = rhs[at] - x
 
 
 def near_residual_kernel(traces, down, coupling, lift, out, left, right):
@@ -462,6 +470,7 @@
 BELOW = ((LAYERS * EY, VECS, LANES), F32)
 DOWN = (((LAYERS - 1) * PATCH, 2 * VECS, LANES), BF16)
 ROW_TILE = ((16, LANES), F32)
+CELL_ROWS = pltpu.VMEM((CELLS * 2 * VECS, ROWS), BF16)
 FLUXES = [pltpu.VMEM((CELLS * 2 * VECS, DEEP), BF16), pltpu.VMEM((CELLS * 2 * VECS, 6 * TRACE - DEEP), BF16)]
 FIELD = ((CELLS, VECS, ROWS), F32)
 STATES = ((3 * VECS, LANES), F32)
@@ -493,7 +502,7 @@
     blocks = coupling.reshape(CELLS, TRACE, 6 * TRACE)
     lift = lift_table.T
     traces, inner, outer, across, faces = call(
-        open_kernel, SIDE_OUTS + [((CELLS, 2 * VECS, LANES), F32)], micros=2
+        open_kernel, SIDE_OUTS + [((CELLS, 2 * VECS, LANES), F32)], [CELL_ROWS], micros=2
     )(old)
     ups, down, below = call(position_kernel, [ROW_TILE, DOWN, BELOW])(upstream.transpose(1, 2, 0), faces)
     halos = exchange_sides(below, outer, inner, across)
@@ -502,8 +511,9 @@
         [((CELLS, DEEP, ROWS), BF16), ((CELLS, DEEP, LANES), BF16), ((PATCH, TRACE, LANES), F32)],
         [pltpu.VMEM((CELLS, DEEP, LANES), BF16), pltpu.VMEM((PATCH, TRACE, LANES), F32)],
     )(ups, diag, blocks, lift)
+    (rest,) = call(near_source_kernel, [FIELD], FLUXES)(rhs, traces, down, blocks, lift)
     solved, sources, single = call(source_kernel, [FIELD, ((CELLS, VECS, LANES), F32), PACKED], FLUXES)(
-        ups, rhs, traces, down, *halos, diag, blocks, lift, passing, composed
+        ups, rest, *halos, diag, blocks, lift, passing, composed
     )
     partner = swapped(single, 1)
     (weights,) = call(weight_kernel, [((CELLS, DEEP, ROWS), BF16)])(blocks, lifted_rows, single)
@@ -522,7 +532,12 @@
     new, traces, inner, outer, across, below, down = call(
         finish_kernel,
         [FIELD] + SIDE_OUTS + [BELOW, DOWN],
-        [pltpu.VMEM((CELLS, VECS, ROWS), F32), pltpu.SemaphoreType.DMA((1,))],
+        [
+            pltpu.VMEM((CELLS, VECS, ROWS), F32),
+            pltpu.VMEM((CELLS, 2 * VECS, DEEP), BF16),
+            CELL_ROWS,
+            pltpu.SemaphoreType.DMA((1,)),
+        ],
         far_outs=(0,),
     )(ups, second, fourth, third, before, prefixes, ends, old, solved, sources, weights, passing)
     halos = exchange_sides(below, outer, inner, across)

time: 75.1 us -> 76.2 us (1.015)
  Pallas kernels: 9.65 us -> 10.5 us
    ppermute x2, starting transfers between devices: 6.2 us -> 5.3 us  [exchange_sides(): inner = lax.ppermute(inner, 'cx', [(i, i ^ 1) for i in range(wide)])]
    pallas_call x13 -> x14, Pallas kernels: 9.65 us -> 10.5 us  [run(): pl.pallas_call(kernel, in_specs=[VMEM] * len(args), out_specs=[FAR if i i...]
  transfers between devices with their start and end apart: 14 -> 14, of which waited for: 4 -> 4; matrix products, arithmetic and copies ran while one was open for 0% -> 0% of each run, Pallas kernels for 5% -> 6%
where the time goes in v5:
time: 76.2 us; the launch traced here: 75.4 us
  starting transfers between devices  44 us (58%)
  waiting for transfers between devices  18.8 us (25%)
  Pallas kernels  10.5 us (14%)
  local copies, waits for them, and re-layouts  1.17 us (2%)
  between operations  0.94 us (1%)
    ppermute x2, starting transfers between devices, exchange_sides(): lax.ppermute(outer, 'cx', [(i, i + 1 if i % 2 else i - 1) for i in range(...  13.4 us
    ppermute x2, waiting for transfers between devices, swapped(): lax.ppermute(packed, 'sweep', [(i, i ^ by) for i in range(lax.axis_size('...  13.3 us
    pallas_call x14, Pallas kernels, run(): pl.pallas_call(kernel, in_specs=[VMEM] * len(args), out_specs=[FAR if i i...  10.5 us
    ppermute x2, starting transfers between devices, exchange_sides(): below = lax.ppermute(below, 'sweep', [(i + 1, i) for i in range(deep - 1)])  9.38 us
    ppermute x2, starting transfers between devices, exchange_sides(): across = lax.ppermute(across, 'cy', [(0, 1), (1, 0)])  8.07 us
    ppermute x2, starting transfers between devices, exchange_sides(): inner = lax.ppermute(inner, 'cx', [(i, i ^ 1) for i in range(wide)])  5.3 us
    ppermute x4, waiting for transfers between devices, passed(): return lax.ppermute(states, 'sweep', pairs)  5.26 us
    ppermute x4, starting transfers between devices, passed(): return lax.ppermute(states, 'sweep', pairs)  4.05 us
  transfers between devices with their start and end apart: 14, of which 4 were waited for; matrix products, arithmetic and copies ran while one was open for 0% of the time, Pallas kernels for 6%

profile of v5, /device:TPU:7, one launch (start us, length us, event | category | flops | bytes accessed | tf_op | source)
XLA Modules:
  0.0 75.4 jit_solution(5263070448787586964)
XLA Ops:
  0.6 1.0 %copy-done.3 = f32[3,2,2,16,320]{4,3,2,1,0:T(8,128)S(1)} copy-done((f32[3,2,2,16,320]{4,3,2,1,0:T(8,128)S(1)}, f32[3,2,2,16,320]{4,3,2,1,0:T(8,128)}, u32[]{:S(2)}) %copy-start.3) | copy-done | bytes 245784
  1.6 0.5 shard_map.77
  2.4 5.5 %collective-permute-start = (f32[6,16,128]{2,1,0:T(8,128)S(1)}, f32[6,16,128]{2,1,0:T(8,128)S(1)}, u32[]{:S(2)}, u32[]{:S(2)}) collective-permute-start(f32[6,16,128]{2,1,0:T(8,128)S(1)} %get-tuple-element.29), channel_id=1, source_target_pairs={{32,0},{64,32},{96,64},{128,96},{160,128},{192,160},{224,192},{256... | collective-permute-start | bytes 147464 | tf_op jit(solution)/shard_map/ppermute | solution.py:483
  7.9 11.2 %collective-permute-start.1 = (f32[6,16,128]{2,1,0:T(8,128)S(1)}, f32[6,16,128]{2,1,0:T(8,128)S(1)}, u32[]{:S(2)}, u32[]{:S(2)}) collective-permute-start(f32[6,16,128]{2,1,0:T(8,128)S(1)} %get-tuple-element.30), channel_id=1, source_target_pairs={{2,4},{4,2},{6,8},{8,6},{10,12},{12,10},{14,16},{16,14},{18,20},{2... | collective-permute-start | bytes 147464 | tf_op jit(solution)/shard_map/ppermute | solution.py:482
  19.2 1.9 %collective-permute-start.2 = (f32[6,16,128]{2,1,0:T(8,128)S(1)}, f32[6,16,128]{2,1,0:T(8,128)S(1)}, u32[]{:S(2)}, u32[]{:S(2)}) collective-permute-start(f32[6,16,128]{2,1,0:T(8,128)S(1)} %get-tuple-element.31), channel_id=1, source_target_pairs={{0,2},{2,0},{4,6},{6,4},{8,10},{10,8},{12,14},{14,12},{16,18},{18,... | collective-permute-start | bytes 147464 | tf_op jit(solution)/shard_map/ppermute | solution.py:484
  21.1 3.1 %collective-permute-start.3 = (f32[6,16,128]{2,1,0:T(8,128)S(1)}, f32[6,16,128]{2,1,0:T(8,128)S(1)}, u32[]{:S(2)}, u32[]{:S(2)}) collective-permute-start(f32[6,16,128]{2,1,0:T(8,128)S(1)} %get-tuple-element.32), channel_id=1, source_target_pairs={{0,1},{1,0},{2,3},{3,2},{4,5},{5,4},{6,7},{7,6},{8,9},{9,8},{10,11... | collective-permute-start | bytes 147464 | tf_op jit(solution)/shard_map/ppermute | solution.py:485
  24.3 1.6 %shard_map.80 = (bf16[12,256,320]{2,1,0:T(8,128)(2,1)S(1)}, bf16[12,256,128]{2,1,0:T(8,128)(2,1)S(1)}, f32[4,80,128]{2,1,0:T(8,128)S(1)}) custom-call(f32[16,128]{1,0:T(8,128)S(1)} %get-tuple-element.26.ups, bf16[12,320,320]{2,1,0:T(8,128)(2,1)S(1)} %bitcast.8, bf16[12,80,480]{2,1,0:T(8,128)(2,1)S(1)} %bitcast.10, bf16[320,480]{1,0:T(8,128)(2,1)S(1)} %bitcast.16), custom_call_target="tpu_custom_call" | custom-call | flops 1000000000 | bytes 3600000 | tf_op jit(solution)/shard_map/pallas_call | solution.py:449
  25.8 0.6 shard_map.79.rest
  26.5 1.4 %shard_map.81 = (f32[12,16,320]{2,1,0:T(8,128)S(1)}, f32[12,16,128]{2,1,0:T(8,128)S(1)}, f32[248,128]{1,0:T(8,128)S(1)}) custom-call(f32[16,128]{1,0:T(8,128)S(1)} %get-tuple-element.26.ups, f32[12,16,320]{2,1,0:T(8,128)S(1)} %shard_map.79.rest, f32[6,16,128]{2,1,0:T(8,128)S(1)} %collective-permute-done.from_above, ...), custom_call_target="tpu_custom_call" | custom-call | flops 1000000000 | bytes 3600000 | tf_op jit(solution)/shard_map/pallas_call | solution.py:449
  27.9 1.9 %collective-permute-start.4 = (f32[248,128]{1,0:T(8,128)S(1)}, f32[248,128]{1,0:T(8,128)S(1)}, u32[]{:S(2)}, u32[]{:S(2)}) collective-permute-start(f32[248,128]{1,0:T(8,128)S(1)} %get-tuple-element.35.mine.unused), channel_id=1, source_target_pairs={{0,32},{32,0},{64,96},{96,64},{128,160},{160,128},{192,224},{224,1... | collective-permute-start | bytes 380936 | tf_op jit(solution)/shard_map/ppermute | solution.py:490
  29.8 5.0 %collective-permute-done.4.theirs.pair = f32[248,128]{1,0:T(8,128)S(1)} collective-permute-done((f32[248,128]{1,0:T(8,128)S(1)}, f32[248,128]{1,0:T(8,128)S(1)}, u32[]{:S(2)}, u32[]{:S(2)}) %collective-permute-start.4) | collective-permute-done | bytes 127008 | tf_op jit(solution)/shard_map/ppermute | solution.py:490
  34.8 0.4 shard_map.82.mine
  35.3 1.9 %collective-permute-start.5 = (f32[248,128]{1,0:T(8,128)S(1)}, f32[248,128]{1,0:T(8,128)S(1)}, u32[]{:S(2)}, u32[]{:S(2)}) collective-permute-start(f32[248,128]{1,0:T(8,128)S(1)} %shard_map.82.mine), channel_id=1, source_target_pairs={{0,64},{32,96},{64,0},{96,32},{128,192},{160,224},{192,128},{224,1... | collective-permute-start | bytes 380936 | tf_op jit(solution)/shard_map/ppermute | solution.py:490
  37.2 0.5 shard_map.87.weights
  37.7 8.3 %collective-permute-done.5.theirs = f32[248,128]{1,0:T(8,128)S(1)} collective-permute-done((f32[248,128]{1,0:T(8,128)S(1)}, f32[248,128]{1,0:T(8,128)S(1)}, u32[]{:S(2)}, u32[]{:S(2)}) %collective-permute-start.5) | collective-permute-done | bytes 127008 | tf_op jit(solution)/shard_map/ppermute | solution.py:490
  46.1 0.3 shard_map.83.unused
  46.4 0.7 collective-permute-start.6
  47.1 0.4 shard_map.84.packed
  47.5 1.3 %collective-permute-start.9 = (f32[248,128]{1,0:T(8,128)S(1)}, f32[248,128]{1,0:T(8,128)S(1)}, u32[]{:S(2)}, u32[]{:S(2)}) collective-permute-start(f32[248,128]{1,0:T(8,128)S(1)} %shard_map.84.packed), channel_id=1, source_target_pairs={{256,448},{288,480},{320,384},{352,416},{257,449},{289,481},{321,3... | collective-permute-start | bytes 380936 | tf_op jit(solution)/shard_map/ppermute | solution.py:495
  48.8 0.3 shard_map.85
  49.1 1.4 %collective-permute-start.8 = (f32[48,128]{1,0:T(8,128)S(1)}, f32[48,128]{1,0:T(8,128)S(1)}, u32[]{:S(2)}, u32[]{:S(2)}) collective-permute-start(f32[48,128]{1,0:T(8,128)S(1)} %shard_map.85), channel_id=1, source_target_pairs={{128,320},{160,352},{192,256},{224,288},{129,321},{161,353},{193,2... | collective-permute-start | bytes 73736 | tf_op jit(solution)/shard_map/ppermute | solution.py:495
  50.6 0.7 collective-permute-start.7
  51.2 0.4 shard_map.86
  51.6 5.2 %collective-permute-done.8.third = f32[48,128]{1,0:T(8,128)S(1)} collective-permute-done((f32[48,128]{1,0:T(8,128)S(1)}, f32[48,128]{1,0:T(8,128)S(1)}, u32[]{:S(2)}, u32[]{:S(2)}) %collective-permute-start.8) | collective-permute-done | bytes 24608 | tf_op jit(solution)/shard_map/ppermute | solution.py:495
  56.9 2.0 %shard_map.88 = (f32[12,16,320]{2,1,0:T(8,128)}, bf16[12,32,512]{2,1,0:T(8,128)(2,1)S(1)}, f32[6,16,128]{2,1,0:T(8,128)S(1)}, f32[6,16,128]{2,1,0:T(8,128)S(1)},...) custom-call(f32[16,128]{1,0:T(8,128)S(1)} %get-tuple-element.26.ups, ...), custom_call_target="tpu_custom_call" | custom-call | flops 1000000000 | bytes 3600000 | tf_op jit(solution)/shard_map/pallas_call | solution.py:449
  58.9 3.9 %collective-permute-start.10 = (f32[6,16,128]{2,1,0:T(8,128)S(1)}, f32[6,16,128]{2,1,0:T(8,128)S(1)}, u32[]{:S(2)}, u32[]{:S(2)}) collective-permute-start(f32[6,16,128]{2,1,0:T(8,128)S(1)} %get-tuple-element.44), channel_id=1, source_target_pairs={{32,0},{64,32},{96,64},{128,96},{160,128},{192,160},{224,192},{256... | collective-permute-start | bytes 147464 | tf_op jit(solution)/shard_map/ppermute | solution.py:483
  62.8 2.2 %collective-permute-start.11 = (f32[6,16,128]{2,1,0:T(8,128)S(1)}, f32[6,16,128]{2,1,0:T(8,128)S(1)}, u32[]{:S(2)}, u32[]{:S(2)}) collective-permute-start(f32[6,16,128]{2,1,0:T(8,128)S(1)} %get-tuple-element.45), channel_id=1, source_target_pairs={{2,4},{4,2},{6,8},{8,6},{10,12},{12,10},{14,16},{16,14},{18,20},{2... | collective-permute-start | bytes 147464 | tf_op jit(solution)/shard_map/ppermute | solution.py:482
  64.9 3.4 %collective-permute-start.12 = (f32[6,16,128]{2,1,0:T(8,128)S(1)}, f32[6,16,128]{2,1,0:T(8,128)S(1)}, u32[]{:S(2)}, u32[]{:S(2)}) collective-permute-start(f32[6,16,128]{2,1,0:T(8,128)S(1)} %get-tuple-element.46), channel_id=1, source_target_pairs={{0,2},{2,0},{4,6},{6,4},{8,10},{10,8},{12,14},{14,12},{16,18},{18,... | collective-permute-start | bytes 147464 | tf_op jit(solution)/shard_map/ppermute | solution.py:484
  68.3 4.9 %collective-permute-start.13 = (f32[6,16,128]{2,1,0:T(8,128)S(1)}, f32[6,16,128]{2,1,0:T(8,128)S(1)}, u32[]{:S(2)}, u32[]{:S(2)}) collective-permute-start(f32[6,16,128]{2,1,0:T(8,128)S(1)} %get-tuple-element.47), channel_id=1, source_target_pairs={{0,1},{1,0},{2,3},{3,2},{4,5},{5,4},{6,7},{7,6},{8,9},{9,8},{10,11... | collective-permute-start | bytes 147464 | tf_op jit(solution)/shard_map/ppermute | solution.py:485
  73.3 0.6 shard_map.89.near
  73.9 0.2 collective-permute-done.13.from_across
  74.1 1.3 %shard_map.90 = f32[12,16,320]{2,1,0:T(8,128)} custom-call(f32[12,16,320]{2,1,0:T(8,128)S(1)} %shard_map.89.near, f32[6,16,128]{2,1,0:T(8,128)S(1)} %collective-permute-done.10.from_above, f32[6,16,128]{2,1,0:T(8,128)S(1)} %collective-permute-done.11.outer, f32[6,16,128]{2,1,0:T(8,128)S(1)} %collective-permute-done.12.inner, ...), custom_call_target="tpu_custom_call" | custom-call | flops 1000000000 | bytes 3600000 | tf_op jit(solution)/shard_map/pallas_call | solution.py:449
  (24 shorter events, 0.4 us)
Async XLA Ops:
  0.6 1.0 %copy-start.3 = (f32[3,2,2,16,320]{4,3,2,1,0:T(8,128)S(1)}, f32[3,2,2,16,320]{4,3,2,1,0:T(8,128)}, u32[]{:S(2)}) copy-start(f32[3,2,2,16,320]{4,3,2,1,0:T(8,128)} %param.7) | copy-start | bytes 737284
  1.6 0.7 copy-start.6
  1.6 22.6 %copy-start.1 = (bf16[3,2,2,80,480]{4,3,2,1,0:T(8,128)(2,1)S(1)}, bf16[3,2,2,80,480]{4,3,2,1,0:T(8,128)(2,1)}, u32[]{:S(2)}) copy-start(bf16[3,2,2,80,480]{4,3,2,1,0:T(8,128)(2,1)} %param.9) | copy-start | bytes 2764804
  2.1 22.2 %copy-start = (bf16[3,2,2,320,320]{4,3,2,1,0:T(8,128)(2,1)S(1)}, bf16[3,2,2,320,320]{4,3,2,1,0:T(8,128)(2,1)}, u32[]{:S(2)}) copy-start(bf16[3,2,2,320,320]{4,3,2,1,0:T(8,128)(2,1)} %param.8) | copy-start | bytes 7372804
  2.1 22.2 %copy-start.2 = (bf16[480,320]{0,1:T(8,128)(2,1)S(1)}, bf16[480,320]{0,1:T(8,128)(2,1)}, u32[]{:S(2)}) copy-start(bf16[480,320]{0,1:T(8,128)(2,1)} %param.10) | copy-start | bytes 921604
  2.4 23.4 %copy-start.5 = (f32[3,2,2,16,320]{4,3,2,1,0:T(8,128)S(1)}, f32[3,2,2,16,320]{4,3,2,1,0:T(8,128)}, u32[]{:S(2)}) copy-start(f32[3,2,2,16,320]{4,3,2,1,0:T(8,128)} %param.6) | copy-start | bytes 737284
  2.4 24.1 %collective-permute-start = (f32[6,16,128]{2,1,0:T(8,128)S(1)}, f32[6,16,128]{2,1,0:T(8,128)S(1)}, u32[]{:S(2)}, u32[]{:S(2)}) collective-permute-start(f32[6,16,128]{2,1,0:T(8,128)S(1)} %get-tuple-element.29), channel_id=1, source_target_pairs={{32,0},{64,32},{96,64},{128,96},{160,128},{192,160},{224,192},{256... | collective-permute-start | bytes 147464 | tf_op jit(solution)/shard_map/ppermute | solution.py:483
  7.9 18.6 %collective-permute-start.1 = (f32[6,16,128]{2,1,0:T(8,128)S(1)}, f32[6,16,128]{2,1,0:T(8,128)S(1)}, u32[]{:S(2)}, u32[]{:S(2)}) collective-permute-start(f32[6,16,128]{2,1,0:T(8,128)S(1)} %get-tuple-element.30), channel_id=1, source_target_pairs={{2,4},{4,2},{6,8},{8,6},{10,12},{12,10},{14,16},{16,14},{18,20},{2... | collective-permute-start | bytes 147464 | tf_op jit(solution)/shard_map/ppermute | solution.py:482
  19.2 7.3 %collective-permute-start.2 = (f32[6,16,128]{2,1,0:T(8,128)S(1)}, f32[6,16,128]{2,1,0:T(8,128)S(1)}, u32[]{:S(2)}, u32[]{:S(2)}) collective-permute-start(f32[6,16,128]{2,1,0:T(8,128)S(1)} %get-tuple-element.31), channel_id=1, source_target_pairs={{0,2},{2,0},{4,6},{6,4},{8,10},{10,8},{12,14},{14,12},{16,18},{18,... | collective-permute-start | bytes 147464 | tf_op jit(solution)/shard_map/ppermute | solution.py:484
  21.1 5.4 %collective-permute-start.3 = (f32[6,16,128]{2,1,0:T(8,128)S(1)}, f32[6,16,128]{2,1,0:T(8,128)S(1)}, u32[]{:S(2)}, u32[]{:S(2)}) collective-permute-start(f32[6,16,128]{2,1,0:T(8,128)S(1)} %get-tuple-element.32), channel_id=1, source_target_pairs={{0,1},{1,0},{2,3},{3,2},{4,5},{5,4},{6,7},{7,6},{8,9},{9,8},{10,11... | collective-permute-start | bytes 147464 | tf_op jit(solution)/shard_map/ppermute | solution.py:485
  27.9 6.9 %collective-permute-start.4 = (f32[248,128]{1,0:T(8,128)S(1)}, f32[248,128]{1,0:T(8,128)S(1)}, u32[]{:S(2)}, u32[]{:S(2)}) collective-permute-start(f32[248,128]{1,0:T(8,128)S(1)} %get-tuple-element.35.mine.unused), channel_id=1, source_target_pairs={{0,32},{32,0},{64,96},{96,64},{128,160},{160,128},{192,224},{224,1... | collective-permute-start | bytes 380936 | tf_op jit(solution)/shard_map/ppermute | solution.py:490
  35.3 10.8 %collective-permute-start.5 = (f32[248,128]{1,0:T(8,128)S(1)}, f32[248,128]{1,0:T(8,128)S(1)}, u32[]{:S(2)}, u32[]{:S(2)}) collective-permute-start(f32[248,128]{1,0:T(8,128)S(1)} %shard_map.82.mine), channel_id=1, source_target_pairs={{0,64},{32,96},{64,0},{96,32},{128,192},{160,224},{192,128},{224,1... | collective-permute-start | bytes 380936 | tf_op jit(solution)/shard_map/ppermute | solution.py:490
  46.4 2.4 %collective-permute-start.6 = (f32[48,128]{1,0:T(8,128)S(1)}, f32[48,128]{1,0:T(8,128)S(1)}, u32[]{:S(2)}, u32[]{:S(2)}) collective-permute-start(f32[48,128]{1,0:T(8,128)S(1)} %shard_map.83.unused), channel_id=1, source_target_pairs={{0,192},{32,224},{64,128},{96,160},{1,193},{33,225},{65,129},{97,1... | collective-permute-start | bytes 73736 | tf_op jit(solution)/shard_map/ppermute | solution.py:495
  47.5 9.3 %collective-permute-start.9 = (f32[248,128]{1,0:T(8,128)S(1)}, f32[248,128]{1,0:T(8,128)S(1)}, u32[]{:S(2)}, u32[]{:S(2)}) collective-permute-start(f32[248,128]{1,0:T(8,128)S(1)} %shard_map.84.packed), channel_id=1, source_target_pairs={{256,448},{288,480},{320,384},{352,416},{257,449},{289,481},{321,3... | collective-permute-start | bytes 380936 | tf_op jit(solution)/shard_map/ppermute | solution.py:495
  49.1 7.7 %copy-start.4 = (f32[3,2,2,16,320]{4,3,2,1,0:T(8,128)S(1)}, f32[3,2,2,16,320]{4,3,2,1,0:T(8,128)}, u32[]{:S(2)}) copy-start(f32[3,2,2,16,320]{4,3,2,1,0:T(8,128)} %param.7) | copy-start | bytes 737284
  49.1 7.7 %collective-permute-start.8 = (f32[48,128]{1,0:T(8,128)S(1)}, f32[48,128]{1,0:T(8,128)S(1)}, u32[]{:S(2)}, u32[]{:S(2)}) collective-permute-start(f32[48,128]{1,0:T(8,128)S(1)} %shard_map.85), channel_id=1, source_target_pairs={{128,320},{160,352},{192,256},{224,288},{129,321},{161,353},{193,2... | collective-permute-start | bytes 73736 | tf_op jit(solution)/shard_map/ppermute | solution.py:495
  50.6 6.3 %collective-permute-start.7 = (f32[48,128]{1,0:T(8,128)S(1)}, f32[48,128]{1,0:T(8,128)S(1)}, u32[]{:S(2)}, u32[]{:S(2)}) collective-permute-start(f32[48,128]{1,0:T(8,128)S(1)} %shard_map.85), channel_id=1, source_target_pairs={{128,384},{160,416},{192,448},{224,480},{129,385},{161,417},{193,4... | collective-permute-start | bytes 73736 | tf_op jit(solution)/shard_map/ppermute | solution.py:495
  58.9 15.0 %collective-permute-start.10 = (f32[6,16,128]{2,1,0:T(8,128)S(1)}, f32[6,16,128]{2,1,0:T(8,128)S(1)}, u32[]{:S(2)}, u32[]{:S(2)}) collective-permute-start(f32[6,16,128]{2,1,0:T(8,128)S(1)} %get-tuple-element.44), channel_id=1, source_target_pairs={{32,0},{64,32},{96,64},{128,96},{160,128},{192,160},{224,192},{256... | collective-permute-start | bytes 147464 | tf_op jit(solution)/shard_map/ppermute | solution.py:483
  62.8 11.1 %collective-permute-start.11 = (f32[6,16,128]{2,1,0:T(8,128)S(1)}, f32[6,16,128]{2,1,0:T(8,128)S(1)}, u32[]{:S(2)}, u32[]{:S(2)}) collective-permute-start(f32[6,16,128]{2,1,0:T(8,128)S(1)} %get-tuple-element.45), channel_id=1, source_target_pairs={{2,4},{4,2},{6,8},{8,6},{10,12},{12,10},{14,16},{16,14},{18,20},{2... | collective-permute-start | bytes 147464 | tf_op jit(solution)/shard_map/ppermute | solution.py:482
  64.9 9.0 %collective-permute-start.12 = (f32[6,16,128]{2,1,0:T(8,128)S(1)}, f32[6,16,128]{2,1,0:T(8,128)S(1)}, u32[]{:S(2)}, u32[]{:S(2)}) collective-permute-start(f32[6,16,128]{2,1,0:T(8,128)S(1)} %get-tuple-element.46), channel_id=1, source_target_pairs={{0,2},{2,0},{4,6},{6,4},{8,10},{10,8},{12,14},{14,12},{16,18},{18,... | collective-permute-start | bytes 147464 | tf_op jit(solution)/shard_map/ppermute | solution.py:484
  68.3 5.8 %collective-permute-start.13 = (f32[6,16,128]{2,1,0:T(8,128)S(1)}, f32[6,16,128]{2,1,0:T(8,128)S(1)}, u32[]{:S(2)}, u32[]{:S(2)}) collective-permute-start(f32[6,16,128]{2,1,0:T(8,128)S(1)} %get-tuple-element.47), channel_id=1, source_target_pairs={{0,1},{1,0},{2,3},{3,2},{4,5},{5,4},{6,7},{7,6},{8,9},{9,8},{10,11... | collective-permute-start | bytes 147464 | tf_op jit(solution)/shard_map/ppermute | solution.py:485

commit v6 on v4

--- a/solution.py
+++ b/solution.py
@@ -160,11 +160,14 @@
     return [piece[:, :LANES] for piece in pieces]
 
 
-def put_inflows(pieces, ups, down, below):
+def put_below(pieces, ups, below):
     for e, state in enumerate(placed([halves(pieces[e]) for e in range(PATCH)], ups[0])):
         below[e] = state
     for e in range(PATCH, LAYERS * EY):
         below[e] = jnp.zeros((VECS, LANES), F32)
+
+
+def put_down(pieces, ups, down):
     for layer in range(1, LAYERS):
         for e, piece in enumerate(placed(pieces[layer * PATCH : (layer + 1) * PATCH], ups[layer])):
             down[(layer - 1) * PATCH + e] = piece.astype(BF16)
@@ -178,7 +181,9 @@
 def position_kernel(links, faces, ups, down, below):
     rows = position_rows(links)
     ups[...] = rows
-    put_inflows([faces[at] for at in range(CELLS)], ups_of(rows), down, below)
+    pieces = [faces[at] for at in range(CELLS)]
+    put_below(pieces, ups_of(rows), below)
+    put_down(pieces, ups_of(rows), down)
 
 
 def near_slots(layer, e, traces, down):
@@ -199,7 +204,7 @@
     close, wide = inner[layer * EY + b], outer[layer * EY + b]
     other = from_across[layer * EX + a]
     slots = {}
-    if layer == LAYERS - 1:
+    if layer == LAYERS - 1 and from_above is not None:
         slots[1] = stacked(from_above[e])
     slots[2 if a == 0 else 3] = stacked(jnp.where(even, wide, close) if a == 0 else jnp.where(even, close, wide))
     slots[4 if b == 0 else 5] = stacked(jnp.where(core == (1 if b == 0 else 0), other, 0.0))
@@ -248,10 +253,13 @@
         composed[e] = -times(chosen(both, ups[2][e]), passing[2 * PATCH + e])
 
 
-def weight_kernel(coupling, lifted_rows, unused, weights):
+def weight_kernel(coupling, lifted_rows, unused, weights, front):
     for at in range(CELLS):
-        upwind = coupling[at][:, :LANES]
-        weights[at] = deep_rows(dot(jnp.concatenate([upwind, upwind], axis=1), lifted_rows[at]))
+        upwind = coupling[at, :, :LANES]
+        weight = dot(jnp.concatenate([upwind, upwind], axis=1), lifted_rows[at])
+        weights[at] = deep_rows(weight)
+        if at < PATCH:
+            front[at] = face_of(blocks_of(weight), 0)
 
 
 def turned(x, by):
@@ -389,9 +397,18 @@
     leaving[...] = pack_states(placed(states, rows_of(ends)))
 
 
+def ahead_kernel(ups, front, solved, below, unused, packed):
+    maps = [
+        jnp.concatenate([front[e], -face_of(blocks_of(solved[e]), 0)], axis=0) for e in range(PATCH)
+    ]
+    maps = placed(maps, ups_of(ups)[0])
+    maps = [jnp.concatenate([x[:TRACE], x[TRACE:] + below[e]], axis=0) for e, x in enumerate(maps)]
+    packed[...] = pack(maps, jnp.zeros((8, LANES), F32))
+
+
 def finish_kernel(
-    ups, second, fourth, third, before, prefixes, ends, old, solved, sources, weights, passing,
-    new, traces, inner, outer, across, below, down, made, sems,
+    ups, second, third, fourth, before, prefixes, ends, old, solved, sources, weights, passing,
+    new, traces, inner, outer, across, down, leaving, made, sems,
 ):
     maps, map_ends = unpack(before[...])
     second, fourth, third = [unpack_states(x[...]) for x in (second, fourth, third)]
@@ -414,19 +431,24 @@
             changes.append(old[at] - x)
     copy = pltpu.make_async_copy(made, new, sems.at[0])
     copy.start()
-    put_inflows(put_sides(changes, traces, inner, outer, across), ups, down, below)
+    put_down(put_sides(changes, traces, inner, outer, across), ups, down)
+    for e in range(PATCH):
+        leaving[e] = current[e]
     copy.wait()
 
 
-def near_residual_kernel(traces, down, coupling, lift, out, left, right):
+def near_residual_kernel(traces, down, leaving, ahead, coupling, lift, out, left, right):
     stacks = [near_slots(layer, e, traces, down) for layer in range(LAYERS) for e in range(PATCH)]
+    maps, unused = unpack(ahead[...])
+    for e in range(PATCH):
+        stacks[(LAYERS - 1) * PATCH + e][1] = stacked(after(leaving[e], maps[e]))
     for at, x in enumerate(lift_all(stacks, coupling, lift, left, right)):
         out[at] = x
 
 
-def residual_kernel(near, from_above, outer, inner, from_across, coupling, lift, out, left, right):
+def residual_kernel(near, outer, inner, from_across, coupling, lift, out, left, right):
     stacks = [
-        far_slots(layer, e, from_above, outer, inner, from_across) for layer in range(LAYERS) for e in range(PATCH)
+        far_slots(layer, e, None, outer, inner, from_across) for layer in range(LAYERS) for e in range(PATCH)
     ]
     for at, x in enumerate(lift_all(stacks, coupling, lift, left, right)):
         out[at] = near[at] + x
@@ -468,13 +490,16 @@
 PACKED = ((3 * TRACE + 8, LANES), F32)
 
 
-def exchange_sides(below, outer, inner, across):
-    wide, deep = lax.axis_size("cx"), lax.axis_size("sweep")
+def from_next(piece):
+    return lax.ppermute(piece, "sweep", [(i + 1, i) for i in range(lax.axis_size("sweep") - 1)])
+
+
+def exchange_sides(outer, inner, across):
+    wide = lax.axis_size("cx")
     outer = lax.ppermute(outer, "cx", [(i, i + 1 if i % 2 else i - 1) for i in range(1, wide - 1)])
-    below = lax.ppermute(below, "sweep", [(i + 1, i) for i in range(deep - 1)])
     inner = lax.ppermute(inner, "cx", [(i, i ^ 1) for i in range(wide)])
     across = lax.ppermute(across, "cy", [(0, 1), (1, 0)])
-    return below, outer, inner, across
+    return outer, inner, across
 
 
 def swapped(packed, by):
@@ -496,7 +521,7 @@
         open_kernel, SIDE_OUTS + [((CELLS, 2 * VECS, LANES), F32)], micros=2
     )(old)
     ups, down, below = call(position_kernel, [ROW_TILE, DOWN, BELOW])(upstream.transpose(1, 2, 0), faces)
-    halos = exchange_sides(below, outer, inner, across)
+    halos = (from_next(below),) + exchange_sides(outer, inner, across)
     lifted_rows, passing, composed = call(
         transfer_kernel,
         [((CELLS, DEEP, ROWS), BF16), ((CELLS, DEEP, LANES), BF16), ((PATCH, TRACE, LANES), F32)],
@@ -506,7 +531,9 @@
         ups, rhs, traces, down, *halos, diag, blocks, lift, passing, composed
     )
     partner = swapped(single, 1)
-    (weights,) = call(weight_kernel, [((CELLS, DEEP, ROWS), BF16)])(blocks, lifted_rows, single)
+    weights, front = call(weight_kernel, [((CELLS, DEEP, ROWS), BF16), ((PATCH, TRACE, LANES), F32)])(
+        blocks, lifted_rows, single
+    )
     (pair,) = call(pair_kernel, [PACKED])(single, partner)
     partner_pair = swapped(pair, 2)
     (leaving,) = call(leaving_kernel, [STATES])(pair, partner_pair)
@@ -516,17 +543,19 @@
     (leaving,) = call(onward_kernel, [STATES])(second, group)
     third = passed(leaving, 1, 2, 2)
     fourth = passed(leaving, 1, 3, 0)
+    (ahead,) = call(ahead_kernel, [PACKED])(ups, front, solved, below, leaving)
+    ahead = from_next(ahead)
     prefixes, ends = call(prefix_kernel, [((PATCH, MAP_ROWS, LANES), F32), ((8, LANES), F32)])(
         partner, partner_pair
     )
-    new, traces, inner, outer, across, below, down = call(
+    new, traces, inner, outer, across, down, leaving = call(
         finish_kernel,
-        [FIELD] + SIDE_OUTS + [BELOW, DOWN],
+        [FIELD] + SIDE_OUTS + [DOWN, ((PATCH, VECS, LANES), F32)],
         [pltpu.VMEM((CELLS, VECS, ROWS), F32), pltpu.SemaphoreType.DMA((1,))],
         far_outs=(0,),
-    )(ups, second, fourth, third, before, prefixes, ends, old, solved, sources, weights, passing)
-    halos = exchange_sides(below, outer, inner, across)
-    (near,) = call(near_residual_kernel, [FIELD], FLUXES)(traces, down, blocks, lift)
+    )(ups, second, third, fourth, before, prefixes, ends, old, solved, sources, weights, passing)
+    halos = exchange_sides(outer, inner, across)
+    (near,) = call(near_residual_kernel, [FIELD], FLUXES)(traces, down, leaving, ahead, blocks, lift)
     (residual,) = call(residual_kernel, [FIELD], FLUXES)(near, *halos, blocks, lift)
     shape = rhs_vectors.shape
     return new.reshape(shape), residual.reshape(shape)

time: 75.1 us -> 74.2 us (0.988)
  waiting for transfers between devices: 18.2 us -> 12.8 us
  starting transfers between devices: 44.7 us -> 48.7 us
    ppermute x4, waiting for transfers between devices: 5.26 us -> 0.01 us  [passed(): return lax.ppermute(states, 'sweep', pairs)]
    ppermute x2, starting transfers between devices: 9.36 us -> 14.1 us  [from_next(): lax.ppermute(piece, 'sweep', [(i + 1, i) for i in range(lax.axis_size('sw...]
    pallas_call x13 -> x14, Pallas kernels: 9.65 us -> 10 us  [run(): pl.pallas_call(kernel, in_specs=[VMEM] * len(args), out_specs=[FAR if i i...]
  transfers between devices with their start and end apart: 14 -> 14, of which waited for: 4 -> 3; matrix products, arithmetic and copies ran while one was open for 0% -> 0% of each run, Pallas kernels for 5% -> 8%
where the time goes in v6:
time: 74.2 us; the launch traced here: 73.7 us
  starting transfers between devices  48.7 us (66%)
  waiting for transfers between devices  12.8 us (17%)
  Pallas kernels  10 us (13%)
  local copies, waits for them, and re-layouts  1.2 us (2%)
  between operations  0.99 us (1%)
    ppermute x2, starting transfers between devices, from_next(): lax.ppermute(piece, 'sweep', [(i + 1, i) for i in range(lax.axis_size('sw...  14.1 us
    ppermute x2, starting transfers between devices, exchange_sides(): lax.ppermute(outer, 'cx', [(i, i + 1 if i % 2 else i - 1) for i in range(...  13.1 us
    ppermute x2, waiting for transfers between devices, swapped(): lax.ppermute(packed, 'sweep', [(i, i ^ by) for i in range(lax.axis_size('...  12.7 us
    pallas_call x14, Pallas kernels, run(): pl.pallas_call(kernel, in_specs=[VMEM] * len(args), out_specs=[FAR if i i...  10 us
    ppermute x2, starting transfers between devices, exchange_sides(): across = lax.ppermute(across, 'cy', [(0, 1), (1, 0)])  7.51 us
    ppermute x2, starting transfers between devices, exchange_sides(): inner = lax.ppermute(inner, 'cx', [(i, i ^ 1) for i in range(wide)])  6.17 us
    ppermute x4, starting transfers between devices, passed(): return lax.ppermute(states, 'sweep', pairs)  3.92 us
    ppermute x2, starting transfers between devices, swapped(): lax.ppermute(packed, 'sweep', [(i, i ^ by) for i in range(lax.axis_size('...  3.84 us
  transfers between devices with their start and end apart: 14, of which 3 were waited for; matrix products, arithmetic and copies ran while one was open for 0% of the time, Pallas kernels for 8%

profile of v6, /device:TPU:7, one launch (start us, length us, event | category | flops | bytes accessed | tf_op | source)
XLA Modules:
  0.0 73.7 jit_solution(11230150020557031291)
XLA Ops:
  0.6 1.0 %copy-done.4 = f32[3,2,2,16,320]{4,3,2,1,0:T(8,128)S(1)} copy-done((f32[3,2,2,16,320]{4,3,2,1,0:T(8,128)S(1)}, f32[3,2,2,16,320]{4,3,2,1,0:T(8,128)}, u32[]{:S(2)}) %copy-start.4) | copy-done | bytes 245784
  1.6 0.4 shard_map.77
  2.1 0.2 copy-done.6
  2.3 0.1 shard_map.78
  2.4 5.5 %collective-permute-start = (f32[6,16,128]{2,1,0:T(8,128)S(1)}, f32[6,16,128]{2,1,0:T(8,128)S(1)}, u32[]{:S(2)}, u32[]{:S(2)}) collective-permute-start(f32[6,16,128]{2,1,0:T(8,128)S(1)} %get-tuple-element.31.below), channel_id=1, source_target_pairs={{32,0},{64,32},{96,64},{128,96},{160,128},{192,160},{224,192},{256... | collective-permute-start | bytes 147464 | tf_op jit(solution)/shard_map/ppermute | solution.py:494
  7.9 11.2 %collective-permute-start.1 = (f32[6,16,128]{2,1,0:T(8,128)S(1)}, f32[6,16,128]{2,1,0:T(8,128)S(1)}, u32[]{:S(2)}, u32[]{:S(2)}) collective-permute-start(f32[6,16,128]{2,1,0:T(8,128)S(1)} %get-tuple-element.32), channel_id=1, source_target_pairs={{2,4},{4,2},{6,8},{8,6},{10,12},{12,10},{14,16},{16,14},{18,20},{2... | collective-permute-start | bytes 147464 | tf_op jit(solution)/shard_map/ppermute | solution.py:499
  19.2 1.9 %collective-permute-start.2 = (f32[6,16,128]{2,1,0:T(8,128)S(1)}, f32[6,16,128]{2,1,0:T(8,128)S(1)}, u32[]{:S(2)}, u32[]{:S(2)}) collective-permute-start(f32[6,16,128]{2,1,0:T(8,128)S(1)} %get-tuple-element.33), channel_id=1, source_target_pairs={{0,2},{2,0},{4,6},{6,4},{8,10},{10,8},{12,14},{14,12},{16,18},{18,... | collective-permute-start | bytes 147464 | tf_op jit(solution)/shard_map/ppermute | solution.py:500
  21.1 3.1 %collective-permute-start.3 = (f32[6,16,128]{2,1,0:T(8,128)S(1)}, f32[6,16,128]{2,1,0:T(8,128)S(1)}, u32[]{:S(2)}, u32[]{:S(2)}) collective-permute-start(f32[6,16,128]{2,1,0:T(8,128)S(1)} %get-tuple-element.34), channel_id=1, source_target_pairs={{0,1},{1,0},{2,3},{3,2},{4,5},{5,4},{6,7},{7,6},{8,9},{9,8},{10,11... | collective-permute-start | bytes 147464 | tf_op jit(solution)/shard_map/ppermute | solution.py:501
  24.3 1.5 %shard_map.79 = (bf16[12,256,320]{2,1,0:T(8,128)(2,1)S(1)}, bf16[12,256,128]{2,1,0:T(8,128)(2,1)S(1)}, f32[4,80,128]{2,1,0:T(8,128)S(1)}) custom-call(f32[16,128]{1,0:T(8,128)S(1)} %get-tuple-element.28.ups, bf16[12,320,320]{2,1,0:T(8,128)(2,1)S(1)} %bitcast.8, bf16[12,80,480]{2,1,0:T(8,128)(2,1)S(1)} %bitcast.10, bf16[320,480]{1,0:T(8,128)(2,1)S(1)} %bitcast.15), custom_call_target="tpu_custom_call" | custom-call | flops 1000000000 | bytes 3600000 | tf_op jit(solution)/shard_map/pallas_call | solution.py:463
  25.9 1.5 %shard_map.80 = (f32[12,16,320]{2,1,0:T(8,128)S(1)}, f32[12,16,128]{2,1,0:T(8,128)S(1)}, f32[248,128]{1,0:T(8,128)S(1)}) custom-call(f32[16,128]{1,0:T(8,128)S(1)} %get-tuple-element.28.ups, f32[12,16,320]{2,1,0:T(8,128)S(1)} %bitcast.19, bf16[12,32,512]{2,1,0:T(8,128)(2,1)S(1)} %get-tuple-element.29.traces, bf16[8,32,128]{2,1,0:T(8,128)(2,1)S(1)} %get-tuple-element.30.down, ...), custom_call_target="tpu_custom_call" | custom-call | flops 1000000000 | bytes 3600000 | tf_op jit(solution)/shard_map/pallas_call | solution.py:463
  27.4 1.9 %collective-permute-start.4 = (f32[248,128]{1,0:T(8,128)S(1)}, f32[248,128]{1,0:T(8,128)S(1)}, u32[]{:S(2)}, u32[]{:S(2)}) collective-permute-start(f32[248,128]{1,0:T(8,128)S(1)} %get-tuple-element.37.mine.unused), channel_id=1, source_target_pairs={{0,32},{32,0},{64,96},{96,64},{128,160},{160,128},{192,224},{224,1... | collective-permute-start | bytes 380936 | tf_op jit(solution)/shard_map/ppermute | solution.py:506
  29.3 4.4 %collective-permute-done.4.theirs.pair = f32[248,128]{1,0:T(8,128)S(1)} collective-permute-done((f32[248,128]{1,0:T(8,128)S(1)}, f32[248,128]{1,0:T(8,128)S(1)}, u32[]{:S(2)}, u32[]{:S(2)}) %collective-permute-start.4) | collective-permute-done | bytes 127008 | tf_op jit(solution)/shard_map/ppermute | solution.py:506
  33.8 0.4 shard_map.81.mine
  34.2 1.9 %collective-permute-start.5 = (f32[248,128]{1,0:T(8,128)S(1)}, f32[248,128]{1,0:T(8,128)S(1)}, u32[]{:S(2)}, u32[]{:S(2)}) collective-permute-start(f32[248,128]{1,0:T(8,128)S(1)} %shard_map.81.mine), channel_id=1, source_target_pairs={{0,64},{32,96},{64,0},{96,32},{128,192},{160,224},{192,128},{224,1... | collective-permute-start | bytes 380936 | tf_op jit(solution)/shard_map/ppermute | solution.py:506
  36.1 0.5 shard_map.86
  36.7 8.3 %collective-permute-done.5.theirs = f32[248,128]{1,0:T(8,128)S(1)} collective-permute-done((f32[248,128]{1,0:T(8,128)S(1)}, f32[248,128]{1,0:T(8,128)S(1)}, u32[]{:S(2)}, u32[]{:S(2)}) %collective-permute-start.5) | collective-permute-done | bytes 127008 | tf_op jit(solution)/shard_map/ppermute | solution.py:506
  44.9 0.3 shard_map.82.unused
  45.3 0.7 collective-permute-start.6
  46.0 0.4 shard_map.83.packed
  46.4 1.3 %collective-permute-start.9 = (f32[248,128]{1,0:T(8,128)S(1)}, f32[248,128]{1,0:T(8,128)S(1)}, u32[]{:S(2)}, u32[]{:S(2)}) collective-permute-start(f32[248,128]{1,0:T(8,128)S(1)} %shard_map.83.packed), channel_id=1, source_target_pairs={{256,448},{288,480},{320,384},{352,416},{257,449},{289,481},{321,3... | collective-permute-start | bytes 380936 | tf_op jit(solution)/shard_map/ppermute | solution.py:511
  47.7 0.3 shard_map.84.unused
  48.0 1.3 %collective-permute-start.7 = (f32[48,128]{1,0:T(8,128)S(1)}, f32[48,128]{1,0:T(8,128)S(1)}, u32[]{:S(2)}, u32[]{:S(2)}) collective-permute-start(f32[48,128]{1,0:T(8,128)S(1)} %shard_map.84.unused), channel_id=1, source_target_pairs={{128,320},{160,352},{192,256},{224,288},{129,321},{161,353},{193,2... | collective-permute-start | bytes 73736 | tf_op jit(solution)/shard_map/ppermute | solution.py:511
  49.3 0.7 collective-permute-start.8
  50.0 0.2 shard_map.88
  50.2 8.7 %collective-permute-start.10 = (f32[248,128]{1,0:T(8,128)S(1)}, f32[248,128]{1,0:T(8,128)S(1)}, u32[]{:S(2)}, u32[]{:S(2)}) collective-permute-start(f32[248,128]{1,0:T(8,128)S(1)} %shard_map.88), channel_id=1, source_target_pairs={{32,0},{64,32},{96,64},{128,96},{160,128},{192,160},{224,192},{256... | collective-permute-start | bytes 380936 | tf_op jit(solution)/shard_map/ppermute | solution.py:494
  58.9 0.4 shard_map.85
  59.3 1.7 %shard_map.87 = (f32[12,16,320]{2,1,0:T(8,128)}, bf16[12,32,512]{2,1,0:T(8,128)(2,1)S(1)}, f32[6,16,128]{2,1,0:T(8,128)S(1)}, f32[6,16,128]{2,1,0:T(8,128)S(1)},...) custom-call(f32[16,128]{1,0:T(8,128)S(1)} %get-tuple-element.28.ups, ...), custom_call_target="tpu_custom_call" | custom-call | flops 1000000000 | bytes 3600000 | tf_op jit(solution)/shard_map/pallas_call | solution.py:463
  61.0 1.9 %collective-permute-start.11 = (f32[6,16,128]{2,1,0:T(8,128)S(1)}, f32[6,16,128]{2,1,0:T(8,128)S(1)}, u32[]{:S(2)}, u32[]{:S(2)}) collective-permute-start(f32[6,16,128]{2,1,0:T(8,128)S(1)} %get-tuple-element.49), channel_id=1, source_target_pairs={{2,4},{4,2},{6,8},{8,6},{10,12},{12,10},{14,16},{16,14},{18,20},{2... | collective-permute-start | bytes 147464 | tf_op jit(solution)/shard_map/ppermute | solution.py:499
  62.9 4.3 %collective-permute-start.12 = (f32[6,16,128]{2,1,0:T(8,128)S(1)}, f32[6,16,128]{2,1,0:T(8,128)S(1)}, u32[]{:S(2)}, u32[]{:S(2)}) collective-permute-start(f32[6,16,128]{2,1,0:T(8,128)S(1)} %get-tuple-element.50), channel_id=1, source_target_pairs={{0,2},{2,0},{4,6},{6,4},{8,10},{10,8},{12,14},{14,12},{16,18},{18,... | collective-permute-start | bytes 147464 | tf_op jit(solution)/shard_map/ppermute | solution.py:500
  67.2 4.4 %collective-permute-start.13 = (f32[6,16,128]{2,1,0:T(8,128)S(1)}, f32[6,16,128]{2,1,0:T(8,128)S(1)}, u32[]{:S(2)}, u32[]{:S(2)}) collective-permute-start(f32[6,16,128]{2,1,0:T(8,128)S(1)} %get-tuple-element.51), channel_id=1, source_target_pairs={{0,1},{1,0},{2,3},{3,2},{4,5},{5,4},{6,7},{7,6},{8,9},{9,8},{10,11... | collective-permute-start | bytes 147464 | tf_op jit(solution)/shard_map/ppermute | solution.py:501
  71.6 0.7 shard_map.89.near
  72.4 1.3 %shard_map.90 = f32[12,16,320]{2,1,0:T(8,128)} custom-call(f32[12,16,320]{2,1,0:T(8,128)S(1)} %shard_map.89.near, f32[6,16,128]{2,1,0:T(8,128)S(1)} %collective-permute-done.11.outer, f32[6,16,128]{2,1,0:T(8,128)S(1)} %collective-permute-done.12.inner, f32[6,16,128]{2,1,0:T(8,128)S(1)} %collective-permute-done.13.from_across, ...), custom_call_target="tpu_custom_call" | custom-call | flops 1000000000 | bytes 3600000 | tf_op jit(solution)/shard_map/pallas_call | solution.py:463
  (24 shorter events, 0.2 us)
Async XLA Ops:
  0.6 1.0 %copy-start.4 = (f32[3,2,2,16,320]{4,3,2,1,0:T(8,128)S(1)}, f32[3,2,2,16,320]{4,3,2,1,0:T(8,128)}, u32[]{:S(2)}) copy-start(f32[3,2,2,16,320]{4,3,2,1,0:T(8,128)} %param.7) | copy-start | bytes 737284
  1.6 0.7 copy-start.6
  1.6 22.6 %copy-start.1 = (bf16[3,2,2,80,480]{4,3,2,1,0:T(8,128)(2,1)S(1)}, bf16[3,2,2,80,480]{4,3,2,1,0:T(8,128)(2,1)}, u32[]{:S(2)}) copy-start(bf16[3,2,2,80,480]{4,3,2,1,0:T(8,128)(2,1)} %param.9) | copy-start | bytes 2764804
  2.0 22.2 %copy-start = (bf16[3,2,2,320,320]{4,3,2,1,0:T(8,128)(2,1)S(1)}, bf16[3,2,2,320,320]{4,3,2,1,0:T(8,128)(2,1)}, u32[]{:S(2)}) copy-start(bf16[3,2,2,320,320]{4,3,2,1,0:T(8,128)(2,1)} %param.8) | copy-start | bytes 7372804
  2.1 22.2 %copy-start.2 = (bf16[480,320]{0,1:T(8,128)(2,1)S(1)}, bf16[480,320]{0,1:T(8,128)(2,1)}, u32[]{:S(2)}) copy-start(bf16[480,320]{0,1:T(8,128)(2,1)} %param.10) | copy-start | bytes 921604
  2.4 23.4 %copy-start.3 = (f32[3,2,2,16,320]{4,3,2,1,0:T(8,128)S(1)}, f32[3,2,2,16,320]{4,3,2,1,0:T(8,128)}, u32[]{:S(2)}) copy-start(f32[3,2,2,16,320]{4,3,2,1,0:T(8,128)} %param.6) | copy-start | bytes 737284
  2.4 23.4 %collective-permute-start = (f32[6,16,128]{2,1,0:T(8,128)S(1)}, f32[6,16,128]{2,1,0:T(8,128)S(1)}, u32[]{:S(2)}, u32[]{:S(2)}) collective-permute-start(f32[6,16,128]{2,1,0:T(8,128)S(1)} %get-tuple-element.31.below), channel_id=1, source_target_pairs={{32,0},{64,32},{96,64},{128,96},{160,128},{192,160},{224,192},{256... | collective-permute-start | bytes 147464 | tf_op jit(solution)/shard_map/ppermute | solution.py:494
  7.9 17.9 %collective-permute-start.1 = (f32[6,16,128]{2,1,0:T(8,128)S(1)}, f32[6,16,128]{2,1,0:T(8,128)S(1)}, u32[]{:S(2)}, u32[]{:S(2)}) collective-permute-start(f32[6,16,128]{2,1,0:T(8,128)S(1)} %get-tuple-element.32), channel_id=1, source_target_pairs={{2,4},{4,2},{6,8},{8,6},{10,12},{12,10},{14,16},{16,14},{18,20},{2... | collective-permute-start | bytes 147464 | tf_op jit(solution)/shard_map/ppermute | solution.py:499
  19.2 6.7 %collective-permute-start.2 = (f32[6,16,128]{2,1,0:T(8,128)S(1)}, f32[6,16,128]{2,1,0:T(8,128)S(1)}, u32[]{:S(2)}, u32[]{:S(2)}) collective-permute-start(f32[6,16,128]{2,1,0:T(8,128)S(1)} %get-tuple-element.33), channel_id=1, source_target_pairs={{0,2},{2,0},{4,6},{6,4},{8,10},{10,8},{12,14},{14,12},{16,18},{18,... | collective-permute-start | bytes 147464 | tf_op jit(solution)/shard_map/ppermute | solution.py:500
  21.1 4.8 %collective-permute-start.3 = (f32[6,16,128]{2,1,0:T(8,128)S(1)}, f32[6,16,128]{2,1,0:T(8,128)S(1)}, u32[]{:S(2)}, u32[]{:S(2)}) collective-permute-start(f32[6,16,128]{2,1,0:T(8,128)S(1)} %get-tuple-element.34), channel_id=1, source_target_pairs={{0,1},{1,0},{2,3},{3,2},{4,5},{5,4},{6,7},{7,6},{8,9},{9,8},{10,11... | collective-permute-start | bytes 147464 | tf_op jit(solution)/shard_map/ppermute | solution.py:501
  27.4 6.4 %collective-permute-start.4 = (f32[248,128]{1,0:T(8,128)S(1)}, f32[248,128]{1,0:T(8,128)S(1)}, u32[]{:S(2)}, u32[]{:S(2)}) collective-permute-start(f32[248,128]{1,0:T(8,128)S(1)} %get-tuple-element.37.mine.unused), channel_id=1, source_target_pairs={{0,32},{32,0},{64,96},{96,64},{128,160},{160,128},{192,224},{224,1... | collective-permute-start | bytes 380936 | tf_op jit(solution)/shard_map/ppermute | solution.py:506
  34.2 10.7 %collective-permute-start.5 = (f32[248,128]{1,0:T(8,128)S(1)}, f32[248,128]{1,0:T(8,128)S(1)}, u32[]{:S(2)}, u32[]{:S(2)}) collective-permute-start(f32[248,128]{1,0:T(8,128)S(1)} %shard_map.81.mine), channel_id=1, source_target_pairs={{0,64},{32,96},{64,0},{96,32},{128,192},{160,224},{192,128},{224,1... | collective-permute-start | bytes 380936 | tf_op jit(solution)/shard_map/ppermute | solution.py:506
  45.3 2.4 %collective-permute-start.6 = (f32[48,128]{1,0:T(8,128)S(1)}, f32[48,128]{1,0:T(8,128)S(1)}, u32[]{:S(2)}, u32[]{:S(2)}) collective-permute-start(f32[48,128]{1,0:T(8,128)S(1)} %shard_map.82.unused), channel_id=1, source_target_pairs={{0,192},{32,224},{64,128},{96,160},{1,193},{33,225},{65,129},{97,1... | collective-permute-start | bytes 73736 | tf_op jit(solution)/shard_map/ppermute | solution.py:511
  46.4 12.8 %collective-permute-start.9 = (f32[248,128]{1,0:T(8,128)S(1)}, f32[248,128]{1,0:T(8,128)S(1)}, u32[]{:S(2)}, u32[]{:S(2)}) collective-permute-start(f32[248,128]{1,0:T(8,128)S(1)} %shard_map.83.packed), channel_id=1, source_target_pairs={{256,448},{288,480},{320,384},{352,416},{257,449},{289,481},{321,3... | collective-permute-start | bytes 380936 | tf_op jit(solution)/shard_map/ppermute | solution.py:511
  48.0 11.2 %collective-permute-start.7 = (f32[48,128]{1,0:T(8,128)S(1)}, f32[48,128]{1,0:T(8,128)S(1)}, u32[]{:S(2)}, u32[]{:S(2)}) collective-permute-start(f32[48,128]{1,0:T(8,128)S(1)} %shard_map.84.unused), channel_id=1, source_target_pairs={{128,320},{160,352},{192,256},{224,288},{129,321},{161,353},{193,2... | collective-permute-start | bytes 73736 | tf_op jit(solution)/shard_map/ppermute | solution.py:511
  49.3 9.9 %collective-permute-start.8 = (f32[48,128]{1,0:T(8,128)S(1)}, f32[48,128]{1,0:T(8,128)S(1)}, u32[]{:S(2)}, u32[]{:S(2)}) collective-permute-start(f32[48,128]{1,0:T(8,128)S(1)} %shard_map.84.unused), channel_id=1, source_target_pairs={{128,384},{160,416},{192,448},{224,480},{129,385},{161,417},{193,4... | collective-permute-start | bytes 73736 | tf_op jit(solution)/shard_map/ppermute | solution.py:511
  50.2 9.1 %copy-start.5 = (f32[3,2,2,16,320]{4,3,2,1,0:T(8,128)S(1)}, f32[3,2,2,16,320]{4,3,2,1,0:T(8,128)}, u32[]{:S(2)}) copy-start(f32[3,2,2,16,320]{4,3,2,1,0:T(8,128)} %param.7) | copy-start | bytes 737284
  50.2 21.3 %collective-permute-start.10 = (f32[248,128]{1,0:T(8,128)S(1)}, f32[248,128]{1,0:T(8,128)S(1)}, u32[]{:S(2)}, u32[]{:S(2)}) collective-permute-start(f32[248,128]{1,0:T(8,128)S(1)} %shard_map.88), channel_id=1, source_target_pairs={{32,0},{64,32},{96,64},{128,96},{160,128},{192,160},{224,192},{256... | collective-permute-start | bytes 380936 | tf_op jit(solution)/shard_map/ppermute | solution.py:494
  61.0 11.3 %collective-permute-start.11 = (f32[6,16,128]{2,1,0:T(8,128)S(1)}, f32[6,16,128]{2,1,0:T(8,128)S(1)}, u32[]{:S(2)}, u32[]{:S(2)}) collective-permute-start(f32[6,16,128]{2,1,0:T(8,128)S(1)} %get-tuple-element.49), channel_id=1, source_target_pairs={{2,4},{4,2},{6,8},{8,6},{10,12},{12,10},{14,16},{16,14},{18,20},{2... | collective-permute-start | bytes 147464 | tf_op jit(solution)/shard_map/ppermute | solution.py:499
  62.9 9.4 %collective-permute-start.12 = (f32[6,16,128]{2,1,0:T(8,128)S(1)}, f32[6,16,128]{2,1,0:T(8,128)S(1)}, u32[]{:S(2)}, u32[]{:S(2)}) collective-permute-start(f32[6,16,128]{2,1,0:T(8,128)S(1)} %get-tuple-element.50), channel_id=1, source_target_pairs={{0,2},{2,0},{4,6},{6,4},{8,10},{10,8},{12,14},{14,12},{16,18},{18,... | collective-permute-start | bytes 147464 | tf_op jit(solution)/shard_map/ppermute | solution.py:500
  67.2 5.2 %collective-permute-start.13 = (f32[6,16,128]{2,1,0:T(8,128)S(1)}, f32[6,16,128]{2,1,0:T(8,128)S(1)}, u32[]{:S(2)}, u32[]{:S(2)}) collective-permute-start(f32[6,16,128]{2,1,0:T(8,128)S(1)} %get-tuple-element.51), channel_id=1, source_target_pairs={{0,1},{1,0},{2,3},{3,2},{4,5},{5,4},{6,7},{7,6},{8,9},{9,8},{10,11... | collective-permute-start | bytes 147464 | tf_op jit(solution)/shard_map/ppermute | solution.py:501

commit v7 on v6

--- a/solution.py
+++ b/solution.py
@@ -397,7 +397,7 @@
     leaving[...] = pack_states(placed(states, rows_of(ends)))
 
 
-def ahead_kernel(ups, front, solved, below, unused, packed):
+def ahead_kernel(ups, front, solved, below, packed):
     maps = [
         jnp.concatenate([front[e], -face_of(blocks_of(solved[e]), 0)], axis=0) for e in range(PATCH)
     ]
@@ -531,11 +531,13 @@
         ups, rhs, traces, down, *halos, diag, blocks, lift, passing, composed
     )
     partner = swapped(single, 1)
-    weights, front = call(weight_kernel, [((CELLS, DEEP, ROWS), BF16), ((PATCH, TRACE, LANES), F32)])(
-        blocks, lifted_rows, single
-    )
     (pair,) = call(pair_kernel, [PACKED])(single, partner)
     partner_pair = swapped(pair, 2)
+    weights, front = call(weight_kernel, [((CELLS, DEEP, ROWS), BF16), ((PATCH, TRACE, LANES), F32)])(
+        blocks, lifted_rows, pair
+    )
+    (ahead,) = call(ahead_kernel, [PACKED])(ups, front, solved, below)
+    ahead = from_next(ahead)
     (leaving,) = call(leaving_kernel, [STATES])(pair, partner_pair)
     second = passed(leaving, 0, 1, 2)
     (group,) = call(group_kernel, [PACKED])(pair, partner_pair, leaving)
@@ -543,8 +545,6 @@
     (leaving,) = call(onward_kernel, [STATES])(second, group)
     third = passed(leaving, 1, 2, 2)
     fourth = passed(leaving, 1, 3, 0)
-    (ahead,) = call(ahead_kernel, [PACKED])(ups, front, solved, below, leaving)
-    ahead = from_next(ahead)
     prefixes, ends = call(prefix_kernel, [((PATCH, MAP_ROWS, LANES), F32), ((8, LANES), F32)])(
         partner, partner_pair
     )

time: 74.2 us -> 72.7 us (0.980); the launches traced: 73.7 us -> 71.5 us
  starting transfers between devices: 48.7 us -> 45.7 us
  waiting for transfers between devices: 12.8 us -> 13.7 us
    ppermute x4, waiting for transfers between devices: 0.01 us -> 5.26 us  [passed(): return lax.ppermute(states, 'sweep', pairs)]
    ppermute x2, starting transfers between devices: 14.1 us -> 9.73 us  [from_next(): lax.ppermute(piece, 'sweep', [(i + 1, i) for i in range(lax.axis_size('sw...]
    ppermute x2, waiting for transfers between devices: 12.7 us -> 8.3 us  [swapped(): lax.ppermute(packed, 'sweep', [(i, i ^ by) for i in range(lax.axis_size('...]
    ppermute x2, starting transfers between devices: 7.51 us -> 8.77 us  [exchange_sides(): across = lax.ppermute(across, 'cy', [(0, 1), (1, 0)])]
  transfers between devices with their start and end apart: 14 -> 14, of which waited for: 3 -> 4; matrix products, arithmetic and copies ran while one was open for 0% -> 0% of each run, Pallas kernels for 8% -> 9%
where the time goes in v7:
time: 72.7 us; the launch traced here: 71.5 us
  starting transfers between devices  45.7 us (63%)
  waiting for transfers between devices  13.7 us (19%)
  Pallas kernels  10 us (14%)
  local copies, waits for them, and re-layouts  1.2 us (2%)
  between operations  0.96 us (1%)
    ppermute x2, starting transfers between devices, exchange_sides(): lax.ppermute(outer, 'cx', [(i, i + 1 if i % 2 else i - 1) for i in range(...  13.1 us
    pallas_call x14, Pallas kernels, run(): pl.pallas_call(kernel, in_specs=[VMEM] * len(args), out_specs=[FAR if i i...  10 us
    ppermute x2, starting transfers between devices, from_next(): lax.ppermute(piece, 'sweep', [(i + 1, i) for i in range(lax.axis_size('sw...  9.73 us
    ppermute x2, starting transfers between devices, exchange_sides(): across = lax.ppermute(across, 'cy', [(0, 1), (1, 0)])  8.77 us
    ppermute x2, waiting for transfers between devices, swapped(): lax.ppermute(packed, 'sweep', [(i, i ^ by) for i in range(lax.axis_size('...  8.3 us
    ppermute x2, starting transfers between devices, exchange_sides(): inner = lax.ppermute(inner, 'cx', [(i, i ^ 1) for i in range(wide)])  6.14 us
    ppermute x4, waiting for transfers between devices, passed(): return lax.ppermute(states, 'sweep', pairs)  5.26 us
    ppermute x4, starting transfers between devices, passed(): return lax.ppermute(states, 'sweep', pairs)  4.05 us
  transfers between devices with their start and end apart: 14, of which 4 were waited for; matrix products, arithmetic and copies ran while one was open for 0% of the time, Pallas kernels for 9%

profile of v7, /device:TPU:7, one launch (start us, length us, event | category | flops | bytes accessed | tf_op | source)
XLA Modules:
  0.0 71.5 jit_solution(2946979566675055582)
XLA Ops:
  0.6 1.0 %copy-done.4 = f32[3,2,2,16,320]{4,3,2,1,0:T(8,128)S(1)} copy-done((f32[3,2,2,16,320]{4,3,2,1,0:T(8,128)S(1)}, f32[3,2,2,16,320]{4,3,2,1,0:T(8,128)}, u32[]{:S(2)}) %copy-start.4) | copy-done | bytes 245784
  1.6 0.4 shard_map.77
  2.1 0.2 copy-done.6
  2.4 5.5 %collective-permute-start = (f32[6,16,128]{2,1,0:T(8,128)S(1)}, f32[6,16,128]{2,1,0:T(8,128)S(1)}, u32[]{:S(2)}, u32[]{:S(2)}) collective-permute-start(f32[6,16,128]{2,1,0:T(8,128)S(1)} %get-tuple-element.31.below), channel_id=1, source_target_pairs={{32,0},{64,32},{96,64},{128,96},{160,128},{192,160},{224,192},{256... | collective-permute-start | bytes 147464 | tf_op jit(solution)/shard_map/ppermute | solution.py:494
  7.9 11.2 %collective-permute-start.1 = (f32[6,16,128]{2,1,0:T(8,128)S(1)}, f32[6,16,128]{2,1,0:T(8,128)S(1)}, u32[]{:S(2)}, u32[]{:S(2)}) collective-permute-start(f32[6,16,128]{2,1,0:T(8,128)S(1)} %get-tuple-element.32), channel_id=1, source_target_pairs={{2,4},{4,2},{6,8},{8,6},{10,12},{12,10},{14,16},{16,14},{18,20},{2... | collective-permute-start | bytes 147464 | tf_op jit(solution)/shard_map/ppermute | solution.py:499
  19.2 1.9 %collective-permute-start.2 = (f32[6,16,128]{2,1,0:T(8,128)S(1)}, f32[6,16,128]{2,1,0:T(8,128)S(1)}, u32[]{:S(2)}, u32[]{:S(2)}) collective-permute-start(f32[6,16,128]{2,1,0:T(8,128)S(1)} %get-tuple-element.33), channel_id=1, source_target_pairs={{0,2},{2,0},{4,6},{6,4},{8,10},{10,8},{12,14},{14,12},{16,18},{18,... | collective-permute-start | bytes 147464 | tf_op jit(solution)/shard_map/ppermute | solution.py:500
  21.1 3.1 %collective-permute-start.3 = (f32[6,16,128]{2,1,0:T(8,128)S(1)}, f32[6,16,128]{2,1,0:T(8,128)S(1)}, u32[]{:S(2)}, u32[]{:S(2)}) collective-permute-start(f32[6,16,128]{2,1,0:T(8,128)S(1)} %get-tuple-element.34), channel_id=1, source_target_pairs={{0,1},{1,0},{2,3},{3,2},{4,5},{5,4},{6,7},{7,6},{8,9},{9,8},{10,11... | collective-permute-start | bytes 147464 | tf_op jit(solution)/shard_map/ppermute | solution.py:501
  24.3 1.5 %shard_map.79 = (bf16[12,256,320]{2,1,0:T(8,128)(2,1)S(1)}, bf16[12,256,128]{2,1,0:T(8,128)(2,1)S(1)}, f32[4,80,128]{2,1,0:T(8,128)S(1)}) custom-call(f32[16,128]{1,0:T(8,128)S(1)} %get-tuple-element.28.ups, bf16[12,320,320]{2,1,0:T(8,128)(2,1)S(1)} %bitcast.8, bf16[12,80,480]{2,1,0:T(8,128)(2,1)S(1)} %bitcast.10, bf16[320,480]{1,0:T(8,128)(2,1)S(1)} %bitcast.15), custom_call_target="tpu_custom_call" | custom-call | flops 1000000000 | bytes 3600000 | tf_op jit(solution)/shard_map/pallas_call | solution.py:463
  25.9 1.5 %shard_map.80 = (f32[12,16,320]{2,1,0:T(8,128)S(1)}, f32[12,16,128]{2,1,0:T(8,128)S(1)}, f32[248,128]{1,0:T(8,128)S(1)}) custom-call(f32[16,128]{1,0:T(8,128)S(1)} %get-tuple-element.28.ups, f32[12,16,320]{2,1,0:T(8,128)S(1)} %bitcast.19, bf16[12,32,512]{2,1,0:T(8,128)(2,1)S(1)} %get-tuple-element.29.traces, bf16[8,32,128]{2,1,0:T(8,128)(2,1)S(1)} %get-tuple-element.30.down, ...), custom_call_target="tpu_custom_call" | custom-call | flops 1000000000 | bytes 3600000 | tf_op jit(solution)/shard_map/pallas_call | solution.py:463
  27.4 1.9 %collective-permute-start.4 = (f32[248,128]{1,0:T(8,128)S(1)}, f32[248,128]{1,0:T(8,128)S(1)}, u32[]{:S(2)}, u32[]{:S(2)}) collective-permute-start(f32[248,128]{1,0:T(8,128)S(1)} %get-tuple-element.37.mine), channel_id=1, source_target_pairs={{0,32},{32,0},{64,96},{96,64},{128,160},{160,128},{192,224},{224,1... | collective-permute-start | bytes 380936 | tf_op jit(solution)/shard_map/ppermute | solution.py:506
  29.3 4.4 %collective-permute-done.4.theirs.pair = f32[248,128]{1,0:T(8,128)S(1)} collective-permute-done((f32[248,128]{1,0:T(8,128)S(1)}, f32[248,128]{1,0:T(8,128)S(1)}, u32[]{:S(2)}, u32[]{:S(2)}) %collective-permute-start.4) | collective-permute-done | bytes 127008 | tf_op jit(solution)/shard_map/ppermute | solution.py:506
  33.8 0.4 shard_map.81.mine.unused
  34.2 1.9 %collective-permute-start.5 = (f32[248,128]{1,0:T(8,128)S(1)}, f32[248,128]{1,0:T(8,128)S(1)}, u32[]{:S(2)}, u32[]{:S(2)}) collective-permute-start(f32[248,128]{1,0:T(8,128)S(1)} %shard_map.81.mine.unused), channel_id=1, source_target_pairs={{0,64},{32,96},{64,0},{96,32},{128,192},{160,224},{192,128},{224,1... | collective-permute-start | bytes 380936 | tf_op jit(solution)/shard_map/ppermute | solution.py:506
  36.1 0.5 shard_map.86
  36.7 0.2 shard_map.88
  36.9 4.2 %collective-permute-start.10 = (f32[248,128]{1,0:T(8,128)S(1)}, f32[248,128]{1,0:T(8,128)S(1)}, u32[]{:S(2)}, u32[]{:S(2)}) collective-permute-start(f32[248,128]{1,0:T(8,128)S(1)} %shard_map.88), channel_id=1, source_target_pairs={{32,0},{64,32},{96,64},{128,96},{160,128},{192,160},{224,192},{256... | collective-permute-start | bytes 380936 | tf_op jit(solution)/shard_map/ppermute | solution.py:494
  41.1 3.9 %collective-permute-done.5.theirs = f32[248,128]{1,0:T(8,128)S(1)} collective-permute-done((f32[248,128]{1,0:T(8,128)S(1)}, f32[248,128]{1,0:T(8,128)S(1)}, u32[]{:S(2)}, u32[]{:S(2)}) %collective-permute-start.5) | collective-permute-done | bytes 127008 | tf_op jit(solution)/shard_map/ppermute | solution.py:506
  45.0 0.3 shard_map.82.unused
  45.3 0.7 collective-permute-start.6
  46.0 0.4 shard_map.83.packed
  46.5 1.3 %collective-permute-start.9 = (f32[248,128]{1,0:T(8,128)S(1)}, f32[248,128]{1,0:T(8,128)S(1)}, u32[]{:S(2)}, u32[]{:S(2)}) collective-permute-start(f32[248,128]{1,0:T(8,128)S(1)} %shard_map.83.packed), channel_id=1, source_target_pairs={{256,448},{288,480},{320,384},{352,416},{257,449},{289,481},{321,3... | collective-permute-start | bytes 380936 | tf_op jit(solution)/shard_map/ppermute | solution.py:511
  47.8 0.3 shard_map.84
  48.1 1.4 %collective-permute-start.7 = (f32[48,128]{1,0:T(8,128)S(1)}, f32[48,128]{1,0:T(8,128)S(1)}, u32[]{:S(2)}, u32[]{:S(2)}) collective-permute-start(f32[48,128]{1,0:T(8,128)S(1)} %shard_map.84), channel_id=1, source_target_pairs={{128,320},{160,352},{192,256},{224,288},{129,321},{161,353},{193,2... | collective-permute-start | bytes 73736 | tf_op jit(solution)/shard_map/ppermute | solution.py:511
  49.5 0.7 collective-permute-start.8
  50.2 0.4 shard_map.85
  50.5 5.3 %collective-permute-done.7.third = f32[48,128]{1,0:T(8,128)S(1)} collective-permute-done((f32[48,128]{1,0:T(8,128)S(1)}, f32[48,128]{1,0:T(8,128)S(1)}, u32[]{:S(2)}, u32[]{:S(2)}) %collective-permute-start.7) | collective-permute-done | bytes 24608 | tf_op jit(solution)/shard_map/ppermute | solution.py:511
  55.8 1.7 %shard_map.87 = (f32[12,16,320]{2,1,0:T(8,128)}, bf16[12,32,512]{2,1,0:T(8,128)(2,1)S(1)}, f32[6,16,128]{2,1,0:T(8,128)S(1)}, f32[6,16,128]{2,1,0:T(8,128)S(1)},...) custom-call(f32[16,128]{1,0:T(8,128)S(1)} %get-tuple-element.28.ups, ...), custom_call_target="tpu_custom_call" | custom-call | flops 1000000000 | bytes 3600000 | tf_op jit(solution)/shard_map/pallas_call | solution.py:463
  57.5 1.9 %collective-permute-start.11 = (f32[6,16,128]{2,1,0:T(8,128)S(1)}, f32[6,16,128]{2,1,0:T(8,128)S(1)}, u32[]{:S(2)}, u32[]{:S(2)}) collective-permute-start(f32[6,16,128]{2,1,0:T(8,128)S(1)} %get-tuple-element.49), channel_id=1, source_target_pairs={{2,4},{4,2},{6,8},{8,6},{10,12},{12,10},{14,16},{16,14},{18,20},{2... | collective-permute-start | bytes 147464 | tf_op jit(solution)/shard_map/ppermute | solution.py:499
  59.5 4.2 %collective-permute-start.12 = (f32[6,16,128]{2,1,0:T(8,128)S(1)}, f32[6,16,128]{2,1,0:T(8,128)S(1)}, u32[]{:S(2)}, u32[]{:S(2)}) collective-permute-start(f32[6,16,128]{2,1,0:T(8,128)S(1)} %get-tuple-element.50), channel_id=1, source_target_pairs={{0,2},{2,0},{4,6},{6,4},{8,10},{10,8},{12,14},{14,12},{16,18},{18,... | collective-permute-start | bytes 147464 | tf_op jit(solution)/shard_map/ppermute | solution.py:500
  63.7 5.6 %collective-permute-start.13 = (f32[6,16,128]{2,1,0:T(8,128)S(1)}, f32[6,16,128]{2,1,0:T(8,128)S(1)}, u32[]{:S(2)}, u32[]{:S(2)}) collective-permute-start(f32[6,16,128]{2,1,0:T(8,128)S(1)} %get-tuple-element.51), channel_id=1, source_target_pairs={{0,1},{1,0},{2,3},{3,2},{4,5},{5,4},{6,7},{7,6},{8,9},{9,8},{10,11... | collective-permute-start | bytes 147464 | tf_op jit(solution)/shard_map/ppermute | solution.py:501
  69.3 0.7 %shard_map.89.near = f32[12,16,320]{2,1,0:T(8,128)S(1)} custom-call(bf16[12,32,512]{2,1,0:T(8,128)(2,1)S(1)} %get-tuple-element.45.traces, bf16[8,32,128]{2,1,0:T(8,128)(2,1)S(1)} %get-tuple-element.46.down, f32[4,16,128]{2,1,0:T(8,128)S(1)} %get-tuple-element.47.leaving, f32[248,128]{1,0:T(8,128)S(1)} %collective-permute-done.10.ahead, ...), custom_call_target="tpu_custom_call" | custom-call | flops 1000000000 | bytes 3600000 | tf_op jit(solution)/shard_map/pallas_call | solution.py:463
  70.2 1.3 %shard_map.90 = f32[12,16,320]{2,1,0:T(8,128)} custom-call(f32[12,16,320]{2,1,0:T(8,128)S(1)} %shard_map.89.near, f32[6,16,128]{2,1,0:T(8,128)S(1)} %collective-permute-done.11.outer, f32[6,16,128]{2,1,0:T(8,128)S(1)} %collective-permute-done.12.inner, f32[6,16,128]{2,1,0:T(8,128)S(1)} %collective-permute-done.13.from_across, ...), custom_call_target="tpu_custom_call" | custom-call | flops 1000000000 | bytes 3600000 | tf_op jit(solution)/shard_map/pallas_call | solution.py:463
  (24 shorter events, 0.3 us)
Async XLA Ops:
  0.6 1.0 %copy-start.4 = (f32[3,2,2,16,320]{4,3,2,1,0:T(8,128)S(1)}, f32[3,2,2,16,320]{4,3,2,1,0:T(8,128)}, u32[]{:S(2)}) copy-start(f32[3,2,2,16,320]{4,3,2,1,0:T(8,128)} %param.7) | copy-start | bytes 737284
  1.6 0.7 copy-start.6
  1.6 22.6 %copy-start.1 = (bf16[3,2,2,80,480]{4,3,2,1,0:T(8,128)(2,1)S(1)}, bf16[3,2,2,80,480]{4,3,2,1,0:T(8,128)(2,1)}, u32[]{:S(2)}) copy-start(bf16[3,2,2,80,480]{4,3,2,1,0:T(8,128)(2,1)} %param.9) | copy-start | bytes 2764804
  2.0 22.2 %copy-start = (bf16[3,2,2,320,320]{4,3,2,1,0:T(8,128)(2,1)S(1)}, bf16[3,2,2,320,320]{4,3,2,1,0:T(8,128)(2,1)}, u32[]{:S(2)}) copy-start(bf16[3,2,2,320,320]{4,3,2,1,0:T(8,128)(2,1)} %param.8) | copy-start | bytes 7372804
  2.1 22.2 %copy-start.2 = (bf16[480,320]{0,1:T(8,128)(2,1)S(1)}, bf16[480,320]{0,1:T(8,128)(2,1)}, u32[]{:S(2)}) copy-start(bf16[480,320]{0,1:T(8,128)(2,1)} %param.10) | copy-start | bytes 921604
  2.4 23.4 %copy-start.3 = (f32[3,2,2,16,320]{4,3,2,1,0:T(8,128)S(1)}, f32[3,2,2,16,320]{4,3,2,1,0:T(8,128)}, u32[]{:S(2)}) copy-start(f32[3,2,2,16,320]{4,3,2,1,0:T(8,128)} %param.6) | copy-start | bytes 737284
  2.4 23.4 %collective-permute-start = (f32[6,16,128]{2,1,0:T(8,128)S(1)}, f32[6,16,128]{2,1,0:T(8,128)S(1)}, u32[]{:S(2)}, u32[]{:S(2)}) collective-permute-start(f32[6,16,128]{2,1,0:T(8,128)S(1)} %get-tuple-element.31.below), channel_id=1, source_target_pairs={{32,0},{64,32},{96,64},{128,96},{160,128},{192,160},{224,192},{256... | collective-permute-start | bytes 147464 | tf_op jit(solution)/shard_map/ppermute | solution.py:494
  7.9 17.9 %collective-permute-start.1 = (f32[6,16,128]{2,1,0:T(8,128)S(1)}, f32[6,16,128]{2,1,0:T(8,128)S(1)}, u32[]{:S(2)}, u32[]{:S(2)}) collective-permute-start(f32[6,16,128]{2,1,0:T(8,128)S(1)} %get-tuple-element.32), channel_id=1, source_target_pairs={{2,4},{4,2},{6,8},{8,6},{10,12},{12,10},{14,16},{16,14},{18,20},{2... | collective-permute-start | bytes 147464 | tf_op jit(solution)/shard_map/ppermute | solution.py:499
  19.2 6.7 %collective-permute-start.2 = (f32[6,16,128]{2,1,0:T(8,128)S(1)}, f32[6,16,128]{2,1,0:T(8,128)S(1)}, u32[]{:S(2)}, u32[]{:S(2)}) collective-permute-start(f32[6,16,128]{2,1,0:T(8,128)S(1)} %get-tuple-element.33), channel_id=1, source_target_pairs={{0,2},{2,0},{4,6},{6,4},{8,10},{10,8},{12,14},{14,12},{16,18},{18,... | collective-permute-start | bytes 147464 | tf_op jit(solution)/shard_map/ppermute | solution.py:500
  21.1 4.8 %collective-permute-start.3 = (f32[6,16,128]{2,1,0:T(8,128)S(1)}, f32[6,16,128]{2,1,0:T(8,128)S(1)}, u32[]{:S(2)}, u32[]{:S(2)}) collective-permute-start(f32[6,16,128]{2,1,0:T(8,128)S(1)} %get-tuple-element.34), channel_id=1, source_target_pairs={{0,1},{1,0},{2,3},{3,2},{4,5},{5,4},{6,7},{7,6},{8,9},{9,8},{10,11... | collective-permute-start | bytes 147464 | tf_op jit(solution)/shard_map/ppermute | solution.py:501
  27.4 6.4 %collective-permute-start.4 = (f32[248,128]{1,0:T(8,128)S(1)}, f32[248,128]{1,0:T(8,128)S(1)}, u32[]{:S(2)}, u32[]{:S(2)}) collective-permute-start(f32[248,128]{1,0:T(8,128)S(1)} %get-tuple-element.37.mine), channel_id=1, source_target_pairs={{0,32},{32,0},{64,96},{96,64},{128,160},{160,128},{192,224},{224,1... | collective-permute-start | bytes 380936 | tf_op jit(solution)/shard_map/ppermute | solution.py:506
  34.2 10.8 %collective-permute-start.5 = (f32[248,128]{1,0:T(8,128)S(1)}, f32[248,128]{1,0:T(8,128)S(1)}, u32[]{:S(2)}, u32[]{:S(2)}) collective-permute-start(f32[248,128]{1,0:T(8,128)S(1)} %shard_map.81.mine.unused), channel_id=1, source_target_pairs={{0,64},{32,96},{64,0},{96,32},{128,192},{160,224},{192,128},{224,1... | collective-permute-start | bytes 380936 | tf_op jit(solution)/shard_map/ppermute | solution.py:506
  36.9 32.4 %collective-permute-start.10 = (f32[248,128]{1,0:T(8,128)S(1)}, f32[248,128]{1,0:T(8,128)S(1)}, u32[]{:S(2)}, u32[]{:S(2)}) collective-permute-start(f32[248,128]{1,0:T(8,128)S(1)} %shard_map.88), channel_id=1, source_target_pairs={{32,0},{64,32},{96,64},{128,96},{160,128},{192,160},{224,192},{256... | collective-permute-start | bytes 380936 | tf_op jit(solution)/shard_map/ppermute | solution.py:494
  45.3 2.4 %collective-permute-start.6 = (f32[48,128]{1,0:T(8,128)S(1)}, f32[48,128]{1,0:T(8,128)S(1)}, u32[]{:S(2)}, u32[]{:S(2)}) collective-permute-start(f32[48,128]{1,0:T(8,128)S(1)} %shard_map.82.unused), channel_id=1, source_target_pairs={{0,192},{32,224},{64,128},{96,160},{1,193},{33,225},{65,129},{97,1... | collective-permute-start | bytes 73736 | tf_op jit(solution)/shard_map/ppermute | solution.py:511
  46.5 9.3 %collective-permute-start.9 = (f32[248,128]{1,0:T(8,128)S(1)}, f32[248,128]{1,0:T(8,128)S(1)}, u32[]{:S(2)}, u32[]{:S(2)}) collective-permute-start(f32[248,128]{1,0:T(8,128)S(1)} %shard_map.83.packed), channel_id=1, source_target_pairs={{256,448},{288,480},{320,384},{352,416},{257,449},{289,481},{321,3... | collective-permute-start | bytes 380936 | tf_op jit(solution)/shard_map/ppermute | solution.py:511
  48.1 7.7 %copy-start.5 = (f32[3,2,2,16,320]{4,3,2,1,0:T(8,128)S(1)}, f32[3,2,2,16,320]{4,3,2,1,0:T(8,128)}, u32[]{:S(2)}) copy-start(f32[3,2,2,16,320]{4,3,2,1,0:T(8,128)} %param.7) | copy-start | bytes 737284
  48.1 7.7 %collective-permute-start.7 = (f32[48,128]{1,0:T(8,128)S(1)}, f32[48,128]{1,0:T(8,128)S(1)}, u32[]{:S(2)}, u32[]{:S(2)}) collective-permute-start(f32[48,128]{1,0:T(8,128)S(1)} %shard_map.84), channel_id=1, source_target_pairs={{128,320},{160,352},{192,256},{224,288},{129,321},{161,353},{193,2... | collective-permute-start | bytes 73736 | tf_op jit(solution)/shard_map/ppermute | solution.py:511
  49.5 6.3 %collective-permute-start.8 = (f32[48,128]{1,0:T(8,128)S(1)}, f32[48,128]{1,0:T(8,128)S(1)}, u32[]{:S(2)}, u32[]{:S(2)}) collective-permute-start(f32[48,128]{1,0:T(8,128)S(1)} %shard_map.84), channel_id=1, source_target_pairs={{128,384},{160,416},{192,448},{224,480},{129,385},{161,417},{193,4... | collective-permute-start | bytes 73736 | tf_op jit(solution)/shard_map/ppermute | solution.py:511
  57.5 12.5 %collective-permute-start.11 = (f32[6,16,128]{2,1,0:T(8,128)S(1)}, f32[6,16,128]{2,1,0:T(8,128)S(1)}, u32[]{:S(2)}, u32[]{:S(2)}) collective-permute-start(f32[6,16,128]{2,1,0:T(8,128)S(1)} %get-tuple-element.49), channel_id=1, source_target_pairs={{2,4},{4,2},{6,8},{8,6},{10,12},{12,10},{14,16},{16,14},{18,20},{2... | collective-permute-start | bytes 147464 | tf_op jit(solution)/shard_map/ppermute | solution.py:499
  59.5 10.6 %collective-permute-start.12 = (f32[6,16,128]{2,1,0:T(8,128)S(1)}, f32[6,16,128]{2,1,0:T(8,128)S(1)}, u32[]{:S(2)}, u32[]{:S(2)}) collective-permute-start(f32[6,16,128]{2,1,0:T(8,128)S(1)} %get-tuple-element.50), channel_id=1, source_target_pairs={{0,2},{2,0},{4,6},{6,4},{8,10},{10,8},{12,14},{14,12},{16,18},{18,... | collective-permute-start | bytes 147464 | tf_op jit(solution)/shard_map/ppermute | solution.py:500
  63.7 6.5 %collective-permute-start.13 = (f32[6,16,128]{2,1,0:T(8,128)S(1)}, f32[6,16,128]{2,1,0:T(8,128)S(1)}, u32[]{:S(2)}, u32[]{:S(2)}) collective-permute-start(f32[6,16,128]{2,1,0:T(8,128)S(1)} %get-tuple-element.51), channel_id=1, source_target_pairs={{0,1},{1,0},{2,3},{3,2},{4,5},{5,4},{6,7},{7,6},{8,9},{9,8},{10,11... | collective-permute-start | bytes 147464 | tf_op jit(solution)/shard_map/ppermute | solution.py:501

commit v8 on v7

--- a/solution.py
+++ b/solution.py
@@ -371,7 +371,9 @@
     leaving[...] = pack_states(placed(states, [chosen(second_ends, at) for at in first_ends]))
 
 
-def prefix_kernel(pair, theirs, prefixes, ends):
+def entry_kernel(
+    pair, theirs, ups, passing, sources, weights, solved, tables, base, out_tables, out_added, starts
+):
     me = lax.axis_index("sweep")
     partner, partner_ends = unpack(pair[...])
     row = lax.broadcasted_iota(jnp.int32, (MAP_ROWS, LANES), 0)
@@ -382,12 +384,34 @@
     first, first_ends = unpack(theirs[...])
     first_ends = rows_of(first_ends)
     later = (me >> 1 & 1) == 1
-    out = []
+    maps, ends = [], []
     for at in range(PATCH):
         whole = after(first[at], chosen(own, first_ends[at]))
-        prefixes[at] = jnp.where(later, whole, own[at])
-        out.append(jnp.where(later, chosen(own_ends, first_ends[at]), own_ends[at]))
-    ends[...] = ends_of(out)
+        maps.append(jnp.where(later, whole, own[at]))
+        ends.append(jnp.where(later, chosen(own_ends, first_ends[at]), own_ends[at]))
+    maps = placed(maps, ends)
+    begin = placed([jnp.full((1, LANES), float(at), F32) for at in range(PATCH)], ends)
+    ups = ups_of(ups)
+    found, every = [], []
+    nothing = jnp.zeros((TRACE, LANES), F32)
+    for layer in range(LAYERS):
+        begin = [chosen(begin, ups[layer][e]) for e in range(PATCH)]
+        maps = [chosen(maps, ups[layer][e]) for e in range(PATCH)]
+        found += begin
+        every += maps
+        maps = [
+            jnp.concatenate([nothing, sources[layer * PATCH + e]], axis=0)
+            - times(maps[e], passing[layer * PATCH + e])
+            for e in range(PATCH)
+        ]
+    for e in range(PATCH):
+        out_tables[e] = deep_rows(maps[e][:TRACE])
+        out_added[e] = maps[e][TRACE:]
+    for at in range(CELLS):
+        product = times(every[at], weights[at])
+        tables[at] = deep_rows(product[:TRACE])
+        base[at] = solved[at] - product[TRACE:]
+    starts[...] = jnp.concatenate(found + [jnp.zeros((16 - CELLS, LANES), F32)], axis=0)
 
 
 def onward_kernel(entering, packed, leaving):
@@ -407,7 +431,7 @@
 
 
 def finish_kernel(
-    ups, second, third, fourth, before, prefixes, ends, old, solved, sources, weights, passing,
+    ups, second, third, fourth, before, tables, base, out_tables, out_added, starts, old,
     new, traces, inner, outer, across, down, leaving, made, sems,
 ):
     maps, map_ends = unpack(before[...])
@@ -415,25 +439,17 @@
     states = [after(fourth[at], maps[at]) for at in range(PATCH)]
     last = placed(states, rows_of(map_ends))
     entering = [second[at] + third[at] + last[at] for at in range(PATCH)]
-    states = [after(entering[at], prefixes[at]) for at in range(PATCH)]
-    current = placed(states, rows_of(ends))
-    ups = ups_of(ups)
-    changes = []
-    for layer in range(LAYERS):
-        inflow = [chosen(current, ups[layer][e]) for e in range(PATCH)]
-        current = [
-            sources[layer * PATCH + e] - times(inflow[e], passing[layer * PATCH + e]) for e in range(PATCH)
-        ]
-        for e in range(PATCH):
-            at = layer * PATCH + e
-            x = solved[at] - times(inflow[e], weights[at])
-            made[at] = x
-            changes.append(old[at] - x)
+    inflows = [deep_lhs(chosen(entering, starts[at : at + 1])) for at in range(CELLS)]
+    products = [halves(dot(inflows[at], tables[at])) for at in range(CELLS)]
+    found = [base[at] - products[at] for at in range(CELLS)]
+    for at in range(CELLS):
+        made[at] = found[at]
     copy = pltpu.make_async_copy(made, new, sems.at[0])
     copy.start()
-    put_down(put_sides(changes, traces, inner, outer, across), ups, down)
+    changes = [old[at] - found[at] for at in range(CELLS)]
+    put_down(put_sides(changes, traces, inner, outer, across), ups_of(ups), down)
     for e in range(PATCH):
-        leaving[e] = current[e]
+        leaving[e] = halves(dot(inflows[(LAYERS - 1) * PATCH + e], out_tables[e])) + out_added[e]
     copy.wait()
 
 
@@ -545,15 +561,22 @@
     (leaving,) = call(onward_kernel, [STATES])(second, group)
     third = passed(leaving, 1, 2, 2)
     fourth = passed(leaving, 1, 3, 0)
-    prefixes, ends = call(prefix_kernel, [((PATCH, MAP_ROWS, LANES), F32), ((8, LANES), F32)])(
-        partner, partner_pair
-    )
+    maps = call(
+        entry_kernel,
+        [
+            ((CELLS, DEEP, ROWS), BF16),
+            FIELD,
+            ((PATCH, DEEP, LANES), BF16),
+            ((PATCH, VECS, LANES), F32),
+            ROW_TILE,
+        ],
+    )(partner, partner_pair, ups, passing, sources, weights, solved)
     new, traces, inner, outer, across, down, leaving = call(
         finish_kernel,
         [FIELD] + SIDE_OUTS + [DOWN, ((PATCH, VECS, LANES), F32)],
         [pltpu.VMEM((CELLS, VECS, ROWS), F32), pltpu.SemaphoreType.DMA((1,))],
         far_outs=(0,),
-    )(ups, second, third, fourth, before, prefixes, ends, old, solved, sources, weights, passing)
+    )(ups, second, third, fourth, before, *maps, old)
     halos = exchange_sides(outer, inner, across)
     (near,) = call(near_residual_kernel, [FIELD], FLUXES)(traces, down, leaving, ahead, blocks, lift)
     (residual,) = call(residual_kernel, [FIELD], FLUXES)(near, *halos, blocks, lift)

time: 72.7 us -> 72.4 us (level)
  waiting for transfers between devices: 13.7 us -> 12.3 us
  Pallas kernels: 10 us -> 11 us
    ppermute x4, waiting for transfers between devices: 5.26 us -> 3.92 us  [passed(): return lax.ppermute(states, 'sweep', pairs)]
    pallas_call x14, Pallas kernels: 10 us -> 11 us  [run(): pl.pallas_call(kernel, in_specs=[VMEM] * len(args), out_specs=[FAR if i i...]
  transfers between devices with their start and end apart: 14 -> 14, of which waited for: 4 -> 4; matrix products, arithmetic and copies ran while one was open for 0% -> 0% of each run, Pallas kernels for 9% -> 10%
where the time goes in v8:
time: 72.4 us; the launch traced here: 71.2 us
  starting transfers between devices  45.7 us (63%)
  waiting for transfers between devices  12.3 us (17%)
  Pallas kernels  11 us (15%)
  local copies, waits for them, and re-layouts  1.2 us (2%)
  between operations  0.96 us (1%)
    ppermute x2, starting transfers between devices, exchange_sides(): lax.ppermute(outer, 'cx', [(i, i + 1 if i % 2 else i - 1) for i in range(...  13.1 us
    pallas_call x14, Pallas kernels, run(): pl.pallas_call(kernel, in_specs=[VMEM] * len(args), out_specs=[FAR if i i...  11 us
    ppermute x2, starting transfers between devices, from_next(): lax.ppermute(piece, 'sweep', [(i + 1, i) for i in range(lax.axis_size('sw...  9.71 us
    ppermute x2, starting transfers between devices, exchange_sides(): across = lax.ppermute(across, 'cy', [(0, 1), (1, 0)])  8.75 us
    ppermute x2, waiting for transfers between devices, swapped(): lax.ppermute(packed, 'sweep', [(i, i ^ by) for i in range(lax.axis_size('...  8.31 us
    ppermute x2, starting transfers between devices, exchange_sides(): inner = lax.ppermute(inner, 'cx', [(i, i ^ 1) for i in range(wide)])  6.19 us
    ppermute x4, starting transfers between devices, passed(): return lax.ppermute(states, 'sweep', pairs)  4.05 us
    ppermute x4, waiting for transfers between devices, passed(): return lax.ppermute(states, 'sweep', pairs)  3.92 us
  transfers between devices with their start and end apart: 14, of which 4 were waited for; matrix products, arithmetic and copies ran while one was open for 0% of the time, Pallas kernels for 10%

profile of v8, /device:TPU:7, one launch (start us, length us, event | category | flops | bytes accessed | tf_op | source)
XLA Modules:
  0.0 71.2 jit_solution(5051667598223534258)
XLA Ops:
  0.6 1.0 %copy-done.4 = f32[3,2,2,16,320]{4,3,2,1,0:T(8,128)S(1)} copy-done((f32[3,2,2,16,320]{4,3,2,1,0:T(8,128)S(1)}, f32[3,2,2,16,320]{4,3,2,1,0:T(8,128)}, u32[]{:S(2)}) %copy-start.4) | copy-done | bytes 245784
  1.6 0.4 shard_map.77
  2.1 0.2 copy-done.6
  2.4 5.5 %collective-permute-start = (f32[6,16,128]{2,1,0:T(8,128)S(1)}, f32[6,16,128]{2,1,0:T(8,128)S(1)}, u32[]{:S(2)}, u32[]{:S(2)}) collective-permute-start(f32[6,16,128]{2,1,0:T(8,128)S(1)} %get-tuple-element.34.below), channel_id=1, source_target_pairs={{32,0},{64,32},{96,64},{128,96},{160,128},{192,160},{224,192},{256... | collective-permute-start | bytes 147464 | tf_op jit(solution)/shard_map/ppermute | solution.py:510
  7.9 11.2 %collective-permute-start.1 = (f32[6,16,128]{2,1,0:T(8,128)S(1)}, f32[6,16,128]{2,1,0:T(8,128)S(1)}, u32[]{:S(2)}, u32[]{:S(2)}) collective-permute-start(f32[6,16,128]{2,1,0:T(8,128)S(1)} %get-tuple-element.35), channel_id=1, source_target_pairs={{2,4},{4,2},{6,8},{8,6},{10,12},{12,10},{14,16},{16,14},{18,20},{2... | collective-permute-start | bytes 147464 | tf_op jit(solution)/shard_map/ppermute | solution.py:515
  19.2 1.9 %collective-permute-start.2 = (f32[6,16,128]{2,1,0:T(8,128)S(1)}, f32[6,16,128]{2,1,0:T(8,128)S(1)}, u32[]{:S(2)}, u32[]{:S(2)}) collective-permute-start(f32[6,16,128]{2,1,0:T(8,128)S(1)} %get-tuple-element.36), channel_id=1, source_target_pairs={{0,2},{2,0},{4,6},{6,4},{8,10},{10,8},{12,14},{14,12},{16,18},{18,... | collective-permute-start | bytes 147464 | tf_op jit(solution)/shard_map/ppermute | solution.py:516
  21.1 3.1 %collective-permute-start.3 = (f32[6,16,128]{2,1,0:T(8,128)S(1)}, f32[6,16,128]{2,1,0:T(8,128)S(1)}, u32[]{:S(2)}, u32[]{:S(2)}) collective-permute-start(f32[6,16,128]{2,1,0:T(8,128)S(1)} %get-tuple-element.37), channel_id=1, source_target_pairs={{0,1},{1,0},{2,3},{3,2},{4,5},{5,4},{6,7},{7,6},{8,9},{9,8},{10,11... | collective-permute-start | bytes 147464 | tf_op jit(solution)/shard_map/ppermute | solution.py:517
  24.3 1.5 %shard_map.79 = (bf16[12,256,320]{2,1,0:T(8,128)(2,1)S(1)}, bf16[12,256,128]{2,1,0:T(8,128)(2,1)S(1)}, f32[4,80,128]{2,1,0:T(8,128)S(1)}) custom-call(f32[16,128]{1,0:T(8,128)S(1)} %get-tuple-element.31.ups, bf16[12,320,320]{2,1,0:T(8,128)(2,1)S(1)} %bitcast.8, bf16[12,80,480]{2,1,0:T(8,128)(2,1)S(1)} %bitcast.10, bf16[320,480]{1,0:T(8,128)(2,1)S(1)} %bitcast.15), custom_call_target="tpu_custom_call" | custom-call | flops 1000000000 | bytes 3600000 | tf_op jit(solution)/shard_map/pallas_call | solution.py:479
  25.9 1.5 %shard_map.80 = (f32[12,16,320]{2,1,0:T(8,128)S(1)}, f32[12,16,128]{2,1,0:T(8,128)S(1)}, f32[248,128]{1,0:T(8,128)S(1)}) custom-call(f32[16,128]{1,0:T(8,128)S(1)} %get-tuple-element.31.ups, f32[12,16,320]{2,1,0:T(8,128)S(1)} %bitcast.19, bf16[12,32,512]{2,1,0:T(8,128)(2,1)S(1)} %get-tuple-element.32.traces, bf16[8,32,128]{2,1,0:T(8,128)(2,1)S(1)} %get-tuple-element.33.down, ...), custom_call_target="tpu_custom_call" | custom-call | flops 1000000000 | bytes 3600000 | tf_op jit(solution)/shard_map/pallas_call | solution.py:479
  27.4 1.9 %collective-permute-start.4 = (f32[248,128]{1,0:T(8,128)S(1)}, f32[248,128]{1,0:T(8,128)S(1)}, u32[]{:S(2)}, u32[]{:S(2)}) collective-permute-start(f32[248,128]{1,0:T(8,128)S(1)} %get-tuple-element.40.mine), channel_id=1, source_target_pairs={{0,32},{32,0},{64,96},{96,64},{128,160},{160,128},{192,224},{224,1... | collective-permute-start | bytes 380936 | tf_op jit(solution)/shard_map/ppermute | solution.py:522
  29.3 4.4 %collective-permute-done.4.theirs.pair = f32[248,128]{1,0:T(8,128)S(1)} collective-permute-done((f32[248,128]{1,0:T(8,128)S(1)}, f32[248,128]{1,0:T(8,128)S(1)}, u32[]{:S(2)}, u32[]{:S(2)}) %collective-permute-start.4) | collective-permute-done | bytes 127008 | tf_op jit(solution)/shard_map/ppermute | solution.py:522
  33.7 0.4 shard_map.81.mine.unused
  34.2 1.9 %collective-permute-start.5 = (f32[248,128]{1,0:T(8,128)S(1)}, f32[248,128]{1,0:T(8,128)S(1)}, u32[]{:S(2)}, u32[]{:S(2)}) collective-permute-start(f32[248,128]{1,0:T(8,128)S(1)} %shard_map.81.mine.unused), channel_id=1, source_target_pairs={{0,64},{32,96},{64,0},{96,32},{128,192},{160,224},{192,128},{224,1... | collective-permute-start | bytes 380936 | tf_op jit(solution)/shard_map/ppermute | solution.py:522
  36.1 0.5 shard_map.85
  36.7 0.2 shard_map.88
  36.9 4.2 %collective-permute-start.10 = (f32[248,128]{1,0:T(8,128)S(1)}, f32[248,128]{1,0:T(8,128)S(1)}, u32[]{:S(2)}, u32[]{:S(2)}) collective-permute-start(f32[248,128]{1,0:T(8,128)S(1)} %shard_map.88), channel_id=1, source_target_pairs={{32,0},{64,32},{96,64},{128,96},{160,128},{192,160},{224,192},{256... | collective-permute-start | bytes 380936 | tf_op jit(solution)/shard_map/ppermute | solution.py:510
  41.1 3.9 %collective-permute-done.5.theirs = f32[248,128]{1,0:T(8,128)S(1)} collective-permute-done((f32[248,128]{1,0:T(8,128)S(1)}, f32[248,128]{1,0:T(8,128)S(1)}, u32[]{:S(2)}, u32[]{:S(2)}) %collective-permute-start.5) | collective-permute-done | bytes 127008 | tf_op jit(solution)/shard_map/ppermute | solution.py:522
  45.0 0.3 shard_map.82.unused
  45.3 0.7 collective-permute-start.6
  46.0 0.4 shard_map.83.packed
  46.4 1.3 %collective-permute-start.9 = (f32[248,128]{1,0:T(8,128)S(1)}, f32[248,128]{1,0:T(8,128)S(1)}, u32[]{:S(2)}, u32[]{:S(2)}) collective-permute-start(f32[248,128]{1,0:T(8,128)S(1)} %shard_map.83.packed), channel_id=1, source_target_pairs={{256,448},{288,480},{320,384},{352,416},{257,449},{289,481},{321,3... | collective-permute-start | bytes 380936 | tf_op jit(solution)/shard_map/ppermute | solution.py:527
  47.7 0.3 shard_map.84
  48.0 1.4 %collective-permute-start.7 = (f32[48,128]{1,0:T(8,128)S(1)}, f32[48,128]{1,0:T(8,128)S(1)}, u32[]{:S(2)}, u32[]{:S(2)}) collective-permute-start(f32[48,128]{1,0:T(8,128)S(1)} %shard_map.84), channel_id=1, source_target_pairs={{128,320},{160,352},{192,256},{224,288},{129,321},{161,353},{193,2... | collective-permute-start | bytes 73736 | tf_op jit(solution)/shard_map/ppermute | solution.py:527
  49.5 0.7 collective-permute-start.8
  50.2 1.7 %shard_map.86 = (bf16[12,256,320]{2,1,0:T(8,128)(2,1)S(1)}, f32[12,16,320]{2,1,0:T(8,128)S(1)}, bf16[4,256,128]{2,1,0:T(8,128)(2,1)S(1)}, f32[4,16,128]{2,1,0:T(8,128)S(1)}, f32[16,128]{1,0:T(8,128)S(1)}) custom-call(f32[248,128]{1,0:T(8,128)S(1)} %collective-permute-done.4.theirs.pair, f32[248,128]{1,0:T(8,128)S(1)} %collective-permute-done.5.theirs, ...), custom_call_target="tpu_custom_call" | custom-call | flops 1000000000 | bytes 3600000 | tf_op jit(solution)/shard_map/pallas_call | solution.py:479
  51.8 3.9 %collective-permute-done.7.third = f32[48,128]{1,0:T(8,128)S(1)} collective-permute-done((f32[48,128]{1,0:T(8,128)S(1)}, f32[48,128]{1,0:T(8,128)S(1)}, u32[]{:S(2)}, u32[]{:S(2)}) %collective-permute-start.7) | collective-permute-done | bytes 24608 | tf_op jit(solution)/shard_map/ppermute | solution.py:527
  55.8 1.4 %shard_map.87 = (f32[12,16,320]{2,1,0:T(8,128)}, bf16[12,32,512]{2,1,0:T(8,128)(2,1)S(1)}, f32[6,16,128]{2,1,0:T(8,128)S(1)}, f32[6,16,128]{2,1,0:T(8,128)S(1)},...) custom-call(f32[16,128]{1,0:T(8,128)S(1)} %get-tuple-element.31.ups, ...), custom_call_target="tpu_custom_call" | custom-call | flops 1000000000 | bytes 3600000 | tf_op jit(solution)/shard_map/pallas_call | solution.py:479
  57.2 1.9 %collective-permute-start.11 = (f32[6,16,128]{2,1,0:T(8,128)S(1)}, f32[6,16,128]{2,1,0:T(8,128)S(1)}, u32[]{:S(2)}, u32[]{:S(2)}) collective-permute-start(f32[6,16,128]{2,1,0:T(8,128)S(1)} %get-tuple-element.55), channel_id=1, source_target_pairs={{2,4},{4,2},{6,8},{8,6},{10,12},{12,10},{14,16},{16,14},{18,20},{2... | collective-permute-start | bytes 147464 | tf_op jit(solution)/shard_map/ppermute | solution.py:515
  59.1 4.3 %collective-permute-start.12 = (f32[6,16,128]{2,1,0:T(8,128)S(1)}, f32[6,16,128]{2,1,0:T(8,128)S(1)}, u32[]{:S(2)}, u32[]{:S(2)}) collective-permute-start(f32[6,16,128]{2,1,0:T(8,128)S(1)} %get-tuple-element.56), channel_id=1, source_target_pairs={{0,2},{2,0},{4,6},{6,4},{8,10},{10,8},{12,14},{14,12},{16,18},{18,... | collective-permute-start | bytes 147464 | tf_op jit(solution)/shard_map/ppermute | solution.py:516
  63.4 5.6 %collective-permute-start.13 = (f32[6,16,128]{2,1,0:T(8,128)S(1)}, f32[6,16,128]{2,1,0:T(8,128)S(1)}, u32[]{:S(2)}, u32[]{:S(2)}) collective-permute-start(f32[6,16,128]{2,1,0:T(8,128)S(1)} %get-tuple-element.57), channel_id=1, source_target_pairs={{0,1},{1,0},{2,3},{3,2},{4,5},{5,4},{6,7},{7,6},{8,9},{9,8},{10,11... | collective-permute-start | bytes 147464 | tf_op jit(solution)/shard_map/ppermute | solution.py:517
  69.0 0.7 %shard_map.89.near = f32[12,16,320]{2,1,0:T(8,128)S(1)} custom-call(bf16[12,32,512]{2,1,0:T(8,128)(2,1)S(1)} %get-tuple-element.51.traces, bf16[8,32,128]{2,1,0:T(8,128)(2,1)S(1)} %get-tuple-element.52.down, f32[4,16,128]{2,1,0:T(8,128)S(1)} %get-tuple-element.53.leaving, f32[248,128]{1,0:T(8,128)S(1)} %collective-permute-done.10.ahead, ...), custom_call_target="tpu_custom_call" | custom-call | flops 1000000000 | bytes 3600000 | tf_op jit(solution)/shard_map/pallas_call | solution.py:479
  69.9 1.3 %shard_map.90 = f32[12,16,320]{2,1,0:T(8,128)} custom-call(f32[12,16,320]{2,1,0:T(8,128)S(1)} %shard_map.89.near, f32[6,16,128]{2,1,0:T(8,128)S(1)} %collective-permute-done.11.outer, f32[6,16,128]{2,1,0:T(8,128)S(1)} %collective-permute-done.12.inner, f32[6,16,128]{2,1,0:T(8,128)S(1)} %collective-permute-done.13.from_across, ...), custom_call_target="tpu_custom_call" | custom-call | flops 1000000000 | bytes 3600000 | tf_op jit(solution)/shard_map/pallas_call | solution.py:479
  (24 shorter events, 0.3 us)
Async XLA Ops:
  0.6 1.0 %copy-start.4 = (f32[3,2,2,16,320]{4,3,2,1,0:T(8,128)S(1)}, f32[3,2,2,16,320]{4,3,2,1,0:T(8,128)}, u32[]{:S(2)}) copy-start(f32[3,2,2,16,320]{4,3,2,1,0:T(8,128)} %param.7) | copy-start | bytes 737284
  1.6 0.7 copy-start.6
  1.6 22.6 %copy-start.1 = (bf16[3,2,2,80,480]{4,3,2,1,0:T(8,128)(2,1)S(1)}, bf16[3,2,2,80,480]{4,3,2,1,0:T(8,128)(2,1)}, u32[]{:S(2)}) copy-start(bf16[3,2,2,80,480]{4,3,2,1,0:T(8,128)(2,1)} %param.9) | copy-start | bytes 2764804
  2.0 22.2 %copy-start = (bf16[3,2,2,320,320]{4,3,2,1,0:T(8,128)(2,1)S(1)}, bf16[3,2,2,320,320]{4,3,2,1,0:T(8,128)(2,1)}, u32[]{:S(2)}) copy-start(bf16[3,2,2,320,320]{4,3,2,1,0:T(8,128)(2,1)} %param.8) | copy-start | bytes 7372804
  2.1 22.2 %copy-start.2 = (bf16[480,320]{0,1:T(8,128)(2,1)S(1)}, bf16[480,320]{0,1:T(8,128)(2,1)}, u32[]{:S(2)}) copy-start(bf16[480,320]{0,1:T(8,128)(2,1)} %param.10) | copy-start | bytes 921604
  2.4 23.4 %copy-start.3 = (f32[3,2,2,16,320]{4,3,2,1,0:T(8,128)S(1)}, f32[3,2,2,16,320]{4,3,2,1,0:T(8,128)}, u32[]{:S(2)}) copy-start(f32[3,2,2,16,320]{4,3,2,1,0:T(8,128)} %param.6) | copy-start | bytes 737284
  2.4 23.4 %collective-permute-start = (f32[6,16,128]{2,1,0:T(8,128)S(1)}, f32[6,16,128]{2,1,0:T(8,128)S(1)}, u32[]{:S(2)}, u32[]{:S(2)}) collective-permute-start(f32[6,16,128]{2,1,0:T(8,128)S(1)} %get-tuple-element.34.below), channel_id=1, source_target_pairs={{32,0},{64,32},{96,64},{128,96},{160,128},{192,160},{224,192},{256... | collective-permute-start | bytes 147464 | tf_op jit(solution)/shard_map/ppermute | solution.py:510
  7.9 17.9 %collective-permute-start.1 = (f32[6,16,128]{2,1,0:T(8,128)S(1)}, f32[6,16,128]{2,1,0:T(8,128)S(1)}, u32[]{:S(2)}, u32[]{:S(2)}) collective-permute-start(f32[6,16,128]{2,1,0:T(8,128)S(1)} %get-tuple-element.35), channel_id=1, source_target_pairs={{2,4},{4,2},{6,8},{8,6},{10,12},{12,10},{14,16},{16,14},{18,20},{2... | collective-permute-start | bytes 147464 | tf_op jit(solution)/shard_map/ppermute | solution.py:515
  19.2 6.7 %collective-permute-start.2 = (f32[6,16,128]{2,1,0:T(8,128)S(1)}, f32[6,16,128]{2,1,0:T(8,128)S(1)}, u32[]{:S(2)}, u32[]{:S(2)}) collective-permute-start(f32[6,16,128]{2,1,0:T(8,128)S(1)} %get-tuple-element.36), channel_id=1, source_target_pairs={{0,2},{2,0},{4,6},{6,4},{8,10},{10,8},{12,14},{14,12},{16,18},{18,... | collective-permute-start | bytes 147464 | tf_op jit(solution)/shard_map/ppermute | solution.py:516
  21.1 4.8 %collective-permute-start.3 = (f32[6,16,128]{2,1,0:T(8,128)S(1)}, f32[6,16,128]{2,1,0:T(8,128)S(1)}, u32[]{:S(2)}, u32[]{:S(2)}) collective-permute-start(f32[6,16,128]{2,1,0:T(8,128)S(1)} %get-tuple-element.37), channel_id=1, source_target_pairs={{0,1},{1,0},{2,3},{3,2},{4,5},{5,4},{6,7},{7,6},{8,9},{9,8},{10,11... | collective-permute-start | bytes 147464 | tf_op jit(solution)/shard_map/ppermute | solution.py:517
  27.4 6.3 %collective-permute-start.4 = (f32[248,128]{1,0:T(8,128)S(1)}, f32[248,128]{1,0:T(8,128)S(1)}, u32[]{:S(2)}, u32[]{:S(2)}) collective-permute-start(f32[248,128]{1,0:T(8,128)S(1)} %get-tuple-element.40.mine), channel_id=1, source_target_pairs={{0,32},{32,0},{64,96},{96,64},{128,160},{160,128},{192,224},{224,1... | collective-permute-start | bytes 380936 | tf_op jit(solution)/shard_map/ppermute | solution.py:522
  34.2 10.8 %collective-permute-start.5 = (f32[248,128]{1,0:T(8,128)S(1)}, f32[248,128]{1,0:T(8,128)S(1)}, u32[]{:S(2)}, u32[]{:S(2)}) collective-permute-start(f32[248,128]{1,0:T(8,128)S(1)} %shard_map.81.mine.unused), channel_id=1, source_target_pairs={{0,64},{32,96},{64,0},{96,32},{128,192},{160,224},{192,128},{224,1... | collective-permute-start | bytes 380936 | tf_op jit(solution)/shard_map/ppermute | solution.py:522
  36.9 32.1 %collective-permute-start.10 = (f32[248,128]{1,0:T(8,128)S(1)}, f32[248,128]{1,0:T(8,128)S(1)}, u32[]{:S(2)}, u32[]{:S(2)}) collective-permute-start(f32[248,128]{1,0:T(8,128)S(1)} %shard_map.88), channel_id=1, source_target_pairs={{32,0},{64,32},{96,64},{128,96},{160,128},{192,160},{224,192},{256... | collective-permute-start | bytes 380936 | tf_op jit(solution)/shard_map/ppermute | solution.py:510
  45.3 2.4 %collective-permute-start.6 = (f32[48,128]{1,0:T(8,128)S(1)}, f32[48,128]{1,0:T(8,128)S(1)}, u32[]{:S(2)}, u32[]{:S(2)}) collective-permute-start(f32[48,128]{1,0:T(8,128)S(1)} %shard_map.82.unused), channel_id=1, source_target_pairs={{0,192},{32,224},{64,128},{96,160},{1,193},{33,225},{65,129},{97,1... | collective-permute-start | bytes 73736 | tf_op jit(solution)/shard_map/ppermute | solution.py:527
  46.4 9.3 %collective-permute-start.9 = (f32[248,128]{1,0:T(8,128)S(1)}, f32[248,128]{1,0:T(8,128)S(1)}, u32[]{:S(2)}, u32[]{:S(2)}) collective-permute-start(f32[248,128]{1,0:T(8,128)S(1)} %shard_map.83.packed), channel_id=1, source_target_pairs={{256,448},{288,480},{320,384},{352,416},{257,449},{289,481},{321,3... | collective-permute-start | bytes 380936 | tf_op jit(solution)/shard_map/ppermute | solution.py:527
  48.0 7.7 %copy-start.5 = (f32[3,2,2,16,320]{4,3,2,1,0:T(8,128)S(1)}, f32[3,2,2,16,320]{4,3,2,1,0:T(8,128)}, u32[]{:S(2)}) copy-start(f32[3,2,2,16,320]{4,3,2,1,0:T(8,128)} %param.7) | copy-start | bytes 737284
  48.0 7.7 %collective-permute-start.7 = (f32[48,128]{1,0:T(8,128)S(1)}, f32[48,128]{1,0:T(8,128)S(1)}, u32[]{:S(2)}, u32[]{:S(2)}) collective-permute-start(f32[48,128]{1,0:T(8,128)S(1)} %shard_map.84), channel_id=1, source_target_pairs={{128,320},{160,352},{192,256},{224,288},{129,321},{161,353},{193,2... | collective-permute-start | bytes 73736 | tf_op jit(solution)/shard_map/ppermute | solution.py:527
  49.5 6.3 %collective-permute-start.8 = (f32[48,128]{1,0:T(8,128)S(1)}, f32[48,128]{1,0:T(8,128)S(1)}, u32[]{:S(2)}, u32[]{:S(2)}) collective-permute-start(f32[48,128]{1,0:T(8,128)S(1)} %shard_map.84), channel_id=1, source_target_pairs={{128,384},{160,416},{192,448},{224,480},{129,385},{161,417},{193,4... | collective-permute-start | bytes 73736 | tf_op jit(solution)/shard_map/ppermute | solution.py:527
  57.2 12.6 %collective-permute-start.11 = (f32[6,16,128]{2,1,0:T(8,128)S(1)}, f32[6,16,128]{2,1,0:T(8,128)S(1)}, u32[]{:S(2)}, u32[]{:S(2)}) collective-permute-start(f32[6,16,128]{2,1,0:T(8,128)S(1)} %get-tuple-element.55), channel_id=1, source_target_pairs={{2,4},{4,2},{6,8},{8,6},{10,12},{12,10},{14,16},{16,14},{18,20},{2... | collective-permute-start | bytes 147464 | tf_op jit(solution)/shard_map/ppermute | solution.py:515
  59.1 10.7 %collective-permute-start.12 = (f32[6,16,128]{2,1,0:T(8,128)S(1)}, f32[6,16,128]{2,1,0:T(8,128)S(1)}, u32[]{:S(2)}, u32[]{:S(2)}) collective-permute-start(f32[6,16,128]{2,1,0:T(8,128)S(1)} %get-tuple-element.56), channel_id=1, source_target_pairs={{0,2},{2,0},{4,6},{6,4},{8,10},{10,8},{12,14},{14,12},{16,18},{18,... | collective-permute-start | bytes 147464 | tf_op jit(solution)/shard_map/ppermute | solution.py:516
  63.4 6.5 %collective-permute-start.13 = (f32[6,16,128]{2,1,0:T(8,128)S(1)}, f32[6,16,128]{2,1,0:T(8,128)S(1)}, u32[]{:S(2)}, u32[]{:S(2)}) collective-permute-start(f32[6,16,128]{2,1,0:T(8,128)S(1)} %get-tuple-element.57), channel_id=1, source_target_pairs={{0,1},{1,0},{2,3},{3,2},{4,5},{5,4},{6,7},{7,6},{8,9},{9,8},{10,11... | collective-permute-start | bytes 147464 | tf_op jit(solution)/shard_map/ppermute | solution.py:517

commit v9 on v8

--- a/solution.py
+++ b/solution.py
@@ -64,6 +64,12 @@
 
 def times(x, deep):
     return halves(dot(deep_lhs(x), deep))
+
+
+def times_all(items, deeps):
+    operands = [deep_lhs(x) for x in items]
+    products = [dot(x, deep) for x, deep in zip(operands, deeps)]
+    return [halves(x) for x in products]
 
 
 def lane_take(x, index):
@@ -248,9 +254,10 @@
         if at < PATCH:
             first[at] = passed_on
     source = [first[e] for e in range(PATCH)]
-    both = [times(chosen(source, ups[1][e]), passing[PATCH + e]) for e in range(PATCH)]
+    both = times_all([chosen(source, at) for at in ups[1]], [passing[PATCH + e] for e in range(PATCH)])
+    both = times_all([chosen(both, at) for at in ups[2]], [passing[2 * PATCH + e] for e in range(PATCH)])
     for e in range(PATCH):
-        composed[e] = -times(chosen(both, ups[2][e]), passing[2 * PATCH + e])
+        composed[e] = -both[e]
 
 
 def weight_kernel(coupling, lifted_rows, unused, weights, front):
@@ -327,21 +334,36 @@
         for e in range(PATCH)
     ]
     outflows = []
-    for at, x in enumerate(lift_all(stacks, coupling, lift, left, right)):
-        y = halves(dot(stacked(rhs[at] - x), diag[at]))
-        solved[at] = y
-        outflows.append(face_of(blocks_of(y), 1))
-        sources[at] = outflows[at]
+    lifts = lift_all(stacks, coupling, lift, left, right)
+    for layer in range(LAYERS):
+        own = range(layer * PATCH, (layer + 1) * PATCH)
+        operands = [stacked(rhs[at] - lifts[at]) for at in own]
+        results = [halves(dot(x, diag[at])) for x, at in zip(operands, own)]
+        for at, y in zip(own, results):
+            solved[at] = y
+        outflows += [face_of(blocks_of(y), 1) for y in results]
+        for at in own:
+            sources[at] = outflows[at]
     current = outflows[:PATCH]
     for layer in range(1, LAYERS):
-        current = [
-            outflows[layer * PATCH + e] - times(chosen(current, ups[layer][e]), passing[layer * PATCH + e])
-            for e in range(PATCH)
-        ]
+        moved = times_all(
+            [chosen(current, ups[layer][e]) for e in range(PATCH)],
+            [passing[layer * PATCH + e] for e in range(PATCH)],
+        )
+        current = [outflows[layer * PATCH + e] - moved[e] for e in range(PATCH)]
     starts = [chosen(ups[0], chosen(ups[1], ups[2][e])) for e in range(PATCH)]
     maps = placed([jnp.concatenate([composed[e], current[e]], axis=0) for e in range(PATCH)], starts)
     ends = placed([jnp.full((1, LANES), float(e), F32) for e in range(PATCH)], starts)
     packed[...] = pack(maps, ends_of(ends))
+
+
+def after_all(firsts, seconds):
+    tables = [deep_rows(x[:TRACE]) for x in seconds]
+    added = [x[TRACE:] for x in seconds]
+    if firsts[0].shape[0] > VECS:
+        nothing = jnp.zeros((TRACE, LANES), F32)
+        added = [jnp.concatenate([nothing, x], axis=0) for x in added]
+    return [x + y for x, y in zip(times_all(firsts, tables), added)]
 
 
 def ordered(mine, theirs, bit):
@@ -353,7 +375,7 @@
 
 def joined(mine, theirs, bit):
     first, first_ends, second, second_ends = ordered(mine, theirs, bit)
-    maps = [after(first[at], chosen(second, first_ends[at])) for at in range(PATCH)]
+    maps = after_all(first, [chosen(second, at) for at in first_ends])
     return pack(maps, ends_of([chosen(second_ends, at) for at in first_ends]))
 
 
@@ -367,7 +389,7 @@
 
 def leaving_kernel(mine, theirs, leaving):
     first, first_ends, second, second_ends = ordered(mine[...], theirs[...], 1)
-    states = [after(first[at][TRACE:], chosen(second, first_ends[at])) for at in range(PATCH)]
+    states = after_all([x[TRACE:] for x in first], [chosen(second, at) for at in first_ends])
     leaving[...] = pack_states(placed(states, [chosen(second_ends, at) for at in first_ends]))
 
 
@@ -417,7 +439,7 @@
 def onward_kernel(entering, packed, leaving):
     maps, ends = unpack(packed[...])
     states = unpack_states(entering[...])
-    states = [after(states[at], maps[at]) for at in range(PATCH)]
+    states = after_all(states, maps)
     leaving[...] = pack_states(placed(states, rows_of(ends)))
 
 
@@ -436,7 +458,7 @@
 ):
     maps, map_ends = unpack(before[...])
     second, fourth, third = [unpack_states(x[...]) for x in (second, fourth, third)]
-    states = [after(fourth[at], maps[at]) for at in range(PATCH)]
+    states = after_all(fourth, maps)
     last = placed(states, rows_of(map_ends))
     entering = [second[at] + third[at] + last[at] for at in range(PATCH)]
     inflows = [deep_lhs(chosen(entering, starts[at : at + 1])) for at in range(CELLS)]

time: 72.4 us -> 72.4 us (level)
  no operation moved by 1% of the time
where the time goes in v9:
time: 72.4 us; the launch traced here: 71.2 us
  starting transfers between devices  45.7 us (63%)
  waiting for transfers between devices  12.3 us (17%)
  Pallas kernels  11 us (15%)
  local copies, waits for them, and re-layouts  1.2 us (2%)
  between operations  0.96 us (1%)
    ppermute x2, starting transfers between devices, exchange_sides(): lax.ppermute(outer, 'cx', [(i, i + 1 if i % 2 else i - 1) for i in range(...  13.1 us
    pallas_call x14, Pallas kernels, run(): pl.pallas_call(kernel, in_specs=[VMEM] * len(args), out_specs=[FAR if i i...  11 us
    ppermute x2, starting transfers between devices, from_next(): lax.ppermute(piece, 'sweep', [(i + 1, i) for i in range(lax.axis_size('sw...  9.71 us
    ppermute x2, starting transfers between devices, exchange_sides(): across = lax.ppermute(across, 'cy', [(0, 1), (1, 0)])  8.75 us
    ppermute x2, waiting for transfers between devices, swapped(): lax.ppermute(packed, 'sweep', [(i, i ^ by) for i in range(lax.axis_size('...  8.31 us
    ppermute x2, starting transfers between devices, exchange_sides(): inner = lax.ppermute(inner, 'cx', [(i, i ^ 1) for i in range(wide)])  6.19 us
    ppermute x4, starting transfers between devices, passed(): return lax.ppermute(states, 'sweep', pairs)  4.05 us
    ppermute x4, waiting for transfers between devices, passed(): return lax.ppermute(states, 'sweep', pairs)  3.92 us
  transfers between devices with their start and end apart: 14, of which 4 were waited for; matrix products, arithmetic and copies ran while one was open for 0% of the time, Pallas kernels for 10%

profile of v9, /device:TPU:7, one launch (start us, length us, event | category | flops | bytes accessed | tf_op | source)
XLA Modules:
  0.0 71.2 jit_solution(5051667598223534258)
XLA Ops:
  0.6 1.0 %copy-done.4 = f32[3,2,2,16,320]{4,3,2,1,0:T(8,128)S(1)} copy-done((f32[3,2,2,16,320]{4,3,2,1,0:T(8,128)S(1)}, f32[3,2,2,16,320]{4,3,2,1,0:T(8,128)}, u32[]{:S(2)}) %copy-start.4) | copy-done | bytes 245784
  1.6 0.4 shard_map.77
  2.1 0.2 copy-done.6
  2.4 5.5 %collective-permute-start = (f32[6,16,128]{2,1,0:T(8,128)S(1)}, f32[6,16,128]{2,1,0:T(8,128)S(1)}, u32[]{:S(2)}, u32[]{:S(2)}) collective-permute-start(f32[6,16,128]{2,1,0:T(8,128)S(1)} %get-tuple-element.34.below), channel_id=1, source_target_pairs={{32,0},{64,32},{96,64},{128,96},{160,128},{192,160},{224,192},{256... | collective-permute-start | bytes 147464 | tf_op jit(solution)/shard_map/ppermute | solution.py:532
  7.9 11.2 %collective-permute-start.1 = (f32[6,16,128]{2,1,0:T(8,128)S(1)}, f32[6,16,128]{2,1,0:T(8,128)S(1)}, u32[]{:S(2)}, u32[]{:S(2)}) collective-permute-start(f32[6,16,128]{2,1,0:T(8,128)S(1)} %get-tuple-element.35), channel_id=1, source_target_pairs={{2,4},{4,2},{6,8},{8,6},{10,12},{12,10},{14,16},{16,14},{18,20},{2... | collective-permute-start | bytes 147464 | tf_op jit(solution)/shard_map/ppermute | solution.py:537
  19.2 1.9 %collective-permute-start.2 = (f32[6,16,128]{2,1,0:T(8,128)S(1)}, f32[6,16,128]{2,1,0:T(8,128)S(1)}, u32[]{:S(2)}, u32[]{:S(2)}) collective-permute-start(f32[6,16,128]{2,1,0:T(8,128)S(1)} %get-tuple-element.36), channel_id=1, source_target_pairs={{0,2},{2,0},{4,6},{6,4},{8,10},{10,8},{12,14},{14,12},{16,18},{18,... | collective-permute-start | bytes 147464 | tf_op jit(solution)/shard_map/ppermute | solution.py:538
  21.1 3.1 %collective-permute-start.3 = (f32[6,16,128]{2,1,0:T(8,128)S(1)}, f32[6,16,128]{2,1,0:T(8,128)S(1)}, u32[]{:S(2)}, u32[]{:S(2)}) collective-permute-start(f32[6,16,128]{2,1,0:T(8,128)S(1)} %get-tuple-element.37), channel_id=1, source_target_pairs={{0,1},{1,0},{2,3},{3,2},{4,5},{5,4},{6,7},{7,6},{8,9},{9,8},{10,11... | collective-permute-start | bytes 147464 | tf_op jit(solution)/shard_map/ppermute | solution.py:539
  24.3 1.5 %shard_map.79 = (bf16[12,256,320]{2,1,0:T(8,128)(2,1)S(1)}, bf16[12,256,128]{2,1,0:T(8,128)(2,1)S(1)}, f32[4,80,128]{2,1,0:T(8,128)S(1)}) custom-call(f32[16,128]{1,0:T(8,128)S(1)} %get-tuple-element.31.ups, bf16[12,320,320]{2,1,0:T(8,128)(2,1)S(1)} %bitcast.8, bf16[12,80,480]{2,1,0:T(8,128)(2,1)S(1)} %bitcast.10, bf16[320,480]{1,0:T(8,128)(2,1)S(1)} %bitcast.15), custom_call_target="tpu_custom_call" | custom-call | flops 1000000000 | bytes 3600000 | tf_op jit(solution)/shard_map/pallas_call | solution.py:501
  25.9 1.5 %shard_map.80 = (f32[12,16,320]{2,1,0:T(8,128)S(1)}, f32[12,16,128]{2,1,0:T(8,128)S(1)}, f32[248,128]{1,0:T(8,128)S(1)}) custom-call(f32[16,128]{1,0:T(8,128)S(1)} %get-tuple-element.31.ups, f32[12,16,320]{2,1,0:T(8,128)S(1)} %bitcast.19, bf16[12,32,512]{2,1,0:T(8,128)(2,1)S(1)} %get-tuple-element.32.traces, bf16[8,32,128]{2,1,0:T(8,128)(2,1)S(1)} %get-tuple-element.33.down, ...), custom_call_target="tpu_custom_call" | custom-call | flops 1000000000 | bytes 3600000 | tf_op jit(solution)/shard_map/pallas_call | solution.py:501
  27.4 1.9 %collective-permute-start.4 = (f32[248,128]{1,0:T(8,128)S(1)}, f32[248,128]{1,0:T(8,128)S(1)}, u32[]{:S(2)}, u32[]{:S(2)}) collective-permute-start(f32[248,128]{1,0:T(8,128)S(1)} %get-tuple-element.40.mine), channel_id=1, source_target_pairs={{0,32},{32,0},{64,96},{96,64},{128,160},{160,128},{192,224},{224,1... | collective-permute-start | bytes 380936 | tf_op jit(solution)/shard_map/ppermute | solution.py:544
  29.3 4.4 %collective-permute-done.4.theirs.pair = f32[248,128]{1,0:T(8,128)S(1)} collective-permute-done((f32[248,128]{1,0:T(8,128)S(1)}, f32[248,128]{1,0:T(8,128)S(1)}, u32[]{:S(2)}, u32[]{:S(2)}) %collective-permute-start.4) | collective-permute-done | bytes 127008 | tf_op jit(solution)/shard_map/ppermute | solution.py:544
  33.7 0.4 shard_map.81.mine.unused
  34.2 1.9 %collective-permute-start.5 = (f32[248,128]{1,0:T(8,128)S(1)}, f32[248,128]{1,0:T(8,128)S(1)}, u32[]{:S(2)}, u32[]{:S(2)}) collective-permute-start(f32[248,128]{1,0:T(8,128)S(1)} %shard_map.81.mine.unused), channel_id=1, source_target_pairs={{0,64},{32,96},{64,0},{96,32},{128,192},{160,224},{192,128},{224,1... | collective-permute-start | bytes 380936 | tf_op jit(solution)/shard_map/ppermute | solution.py:544
  36.1 0.5 shard_map.85
  36.7 0.2 shard_map.88
  36.9 4.2 %collective-permute-start.10 = (f32[248,128]{1,0:T(8,128)S(1)}, f32[248,128]{1,0:T(8,128)S(1)}, u32[]{:S(2)}, u32[]{:S(2)}) collective-permute-start(f32[248,128]{1,0:T(8,128)S(1)} %shard_map.88), channel_id=1, source_target_pairs={{32,0},{64,32},{96,64},{128,96},{160,128},{192,160},{224,192},{256... | collective-permute-start | bytes 380936 | tf_op jit(solution)/shard_map/ppermute | solution.py:532
  41.1 3.9 %collective-permute-done.5.theirs = f32[248,128]{1,0:T(8,128)S(1)} collective-permute-done((f32[248,128]{1,0:T(8,128)S(1)}, f32[248,128]{1,0:T(8,128)S(1)}, u32[]{:S(2)}, u32[]{:S(2)}) %collective-permute-start.5) | collective-permute-done | bytes 127008 | tf_op jit(solution)/shard_map/ppermute | solution.py:544
  45.0 0.3 shard_map.82.unused
  45.3 0.7 collective-permute-start.6
  46.0 0.4 shard_map.83.packed
  46.4 1.3 %collective-permute-start.9 = (f32[248,128]{1,0:T(8,128)S(1)}, f32[248,128]{1,0:T(8,128)S(1)}, u32[]{:S(2)}, u32[]{:S(2)}) collective-permute-start(f32[248,128]{1,0:T(8,128)S(1)} %shard_map.83.packed), channel_id=1, source_target_pairs={{256,448},{288,480},{320,384},{352,416},{257,449},{289,481},{321,3... | collective-permute-start | bytes 380936 | tf_op jit(solution)/shard_map/ppermute | solution.py:549
  47.7 0.3 shard_map.84
  48.0 1.4 %collective-permute-start.7 = (f32[48,128]{1,0:T(8,128)S(1)}, f32[48,128]{1,0:T(8,128)S(1)}, u32[]{:S(2)}, u32[]{:S(2)}) collective-permute-start(f32[48,128]{1,0:T(8,128)S(1)} %shard_map.84), channel_id=1, source_target_pairs={{128,320},{160,352},{192,256},{224,288},{129,321},{161,353},{193,2... | collective-permute-start | bytes 73736 | tf_op jit(solution)/shard_map/ppermute | solution.py:549
  49.5 0.7 collective-permute-start.8
  50.2 1.7 %shard_map.86 = (bf16[12,256,320]{2,1,0:T(8,128)(2,1)S(1)}, f32[12,16,320]{2,1,0:T(8,128)S(1)}, bf16[4,256,128]{2,1,0:T(8,128)(2,1)S(1)}, f32[4,16,128]{2,1,0:T(8,128)S(1)}, f32[16,128]{1,0:T(8,128)S(1)}) custom-call(f32[248,128]{1,0:T(8,128)S(1)} %collective-permute-done.4.theirs.pair, f32[248,128]{1,0:T(8,128)S(1)} %collective-permute-done.5.theirs, ...), custom_call_target="tpu_custom_call" | custom-call | flops 1000000000 | bytes 3600000 | tf_op jit(solution)/shard_map/pallas_call | solution.py:501
  51.8 3.9 %collective-permute-done.7.third = f32[48,128]{1,0:T(8,128)S(1)} collective-permute-done((f32[48,128]{1,0:T(8,128)S(1)}, f32[48,128]{1,0:T(8,128)S(1)}, u32[]{:S(2)}, u32[]{:S(2)}) %collective-permute-start.7) | collective-permute-done | bytes 24608 | tf_op jit(solution)/shard_map/ppermute | solution.py:549
  55.8 1.4 %shard_map.87 = (f32[12,16,320]{2,1,0:T(8,128)}, bf16[12,32,512]{2,1,0:T(8,128)(2,1)S(1)}, f32[6,16,128]{2,1,0:T(8,128)S(1)}, f32[6,16,128]{2,1,0:T(8,128)S(1)},...) custom-call(f32[16,128]{1,0:T(8,128)S(1)} %get-tuple-element.31.ups, ...), custom_call_target="tpu_custom_call" | custom-call | flops 1000000000 | bytes 3600000 | tf_op jit(solution)/shard_map/pallas_call | solution.py:501
  57.2 1.9 %collective-permute-start.11 = (f32[6,16,128]{2,1,0:T(8,128)S(1)}, f32[6,16,128]{2,1,0:T(8,128)S(1)}, u32[]{:S(2)}, u32[]{:S(2)}) collective-permute-start(f32[6,16,128]{2,1,0:T(8,128)S(1)} %get-tuple-element.55), channel_id=1, source_target_pairs={{2,4},{4,2},{6,8},{8,6},{10,12},{12,10},{14,16},{16,14},{18,20},{2... | collective-permute-start | bytes 147464 | tf_op jit(solution)/shard_map/ppermute | solution.py:537
  59.1 4.3 %collective-permute-start.12 = (f32[6,16,128]{2,1,0:T(8,128)S(1)}, f32[6,16,128]{2,1,0:T(8,128)S(1)}, u32[]{:S(2)}, u32[]{:S(2)}) collective-permute-start(f32[6,16,128]{2,1,0:T(8,128)S(1)} %get-tuple-element.56), channel_id=1, source_target_pairs={{0,2},{2,0},{4,6},{6,4},{8,10},{10,8},{12,14},{14,12},{16,18},{18,... | collective-permute-start | bytes 147464 | tf_op jit(solution)/shard_map/ppermute | solution.py:538
  63.4 5.6 %collective-permute-start.13 = (f32[6,16,128]{2,1,0:T(8,128)S(1)}, f32[6,16,128]{2,1,0:T(8,128)S(1)}, u32[]{:S(2)}, u32[]{:S(2)}) collective-permute-start(f32[6,16,128]{2,1,0:T(8,128)S(1)} %get-tuple-element.57), channel_id=1, source_target_pairs={{0,1},{1,0},{2,3},{3,2},{4,5},{5,4},{6,7},{7,6},{8,9},{9,8},{10,11... | collective-permute-start | bytes 147464 | tf_op jit(solution)/shard_map/ppermute | solution.py:539
  69.0 0.7 %shard_map.89.near = f32[12,16,320]{2,1,0:T(8,128)S(1)} custom-call(bf16[12,32,512]{2,1,0:T(8,128)(2,1)S(1)} %get-tuple-element.51.traces, bf16[8,32,128]{2,1,0:T(8,128)(2,1)S(1)} %get-tuple-element.52.down, f32[4,16,128]{2,1,0:T(8,128)S(1)} %get-tuple-element.53.leaving, f32[248,128]{1,0:T(8,128)S(1)} %collective-permute-done.10.ahead, ...), custom_call_target="tpu_custom_call" | custom-call | flops 1000000000 | bytes 3600000 | tf_op jit(solution)/shard_map/pallas_call | solution.py:501
  69.9 1.3 %shard_map.90 = f32[12,16,320]{2,1,0:T(8,128)} custom-call(f32[12,16,320]{2,1,0:T(8,128)S(1)} %shard_map.89.near, f32[6,16,128]{2,1,0:T(8,128)S(1)} %collective-permute-done.11.outer, f32[6,16,128]{2,1,0:T(8,128)S(1)} %collective-permute-done.12.inner, f32[6,16,128]{2,1,0:T(8,128)S(1)} %collective-permute-done.13.from_across, ...), custom_call_target="tpu_custom_call" | custom-call | flops 1000000000 | bytes 3600000 | tf_op jit(solution)/shard_map/pallas_call | solution.py:501
  (24 shorter events, 0.3 us)
Async XLA Ops:
  0.6 1.0 %copy-start.4 = (f32[3,2,2,16,320]{4,3,2,1,0:T(8,128)S(1)}, f32[3,2,2,16,320]{4,3,2,1,0:T(8,128)}, u32[]{:S(2)}) copy-start(f32[3,2,2,16,320]{4,3,2,1,0:T(8,128)} %param.7) | copy-start | bytes 737284
  1.6 0.7 copy-start.6
  1.6 22.6 %copy-start.1 = (bf16[3,2,2,80,480]{4,3,2,1,0:T(8,128)(2,1)S(1)}, bf16[3,2,2,80,480]{4,3,2,1,0:T(8,128)(2,1)}, u32[]{:S(2)}) copy-start(bf16[3,2,2,80,480]{4,3,2,1,0:T(8,128)(2,1)} %param.9) | copy-start | bytes 2764804
  2.0 22.2 %copy-start = (bf16[3,2,2,320,320]{4,3,2,1,0:T(8,128)(2,1)S(1)}, bf16[3,2,2,320,320]{4,3,2,1,0:T(8,128)(2,1)}, u32[]{:S(2)}) copy-start(bf16[3,2,2,320,320]{4,3,2,1,0:T(8,128)(2,1)} %param.8) | copy-start | bytes 7372804
  2.1 22.2 %copy-start.2 = (bf16[480,320]{0,1:T(8,128)(2,1)S(1)}, bf16[480,320]{0,1:T(8,128)(2,1)}, u32[]{:S(2)}) copy-start(bf16[480,320]{0,1:T(8,128)(2,1)} %param.10) | copy-start | bytes 921604
  2.4 23.4 %copy-start.3 = (f32[3,2,2,16,320]{4,3,2,1,0:T(8,128)S(1)}, f32[3,2,2,16,320]{4,3,2,1,0:T(8,128)}, u32[]{:S(2)}) copy-start(f32[3,2,2,16,320]{4,3,2,1,0:T(8,128)} %param.6) | copy-start | bytes 737284
  2.4 23.4 %collective-permute-start = (f32[6,16,128]{2,1,0:T(8,128)S(1)}, f32[6,16,128]{2,1,0:T(8,128)S(1)}, u32[]{:S(2)}, u32[]{:S(2)}) collective-permute-start(f32[6,16,128]{2,1,0:T(8,128)S(1)} %get-tuple-element.34.below), channel_id=1, source_target_pairs={{32,0},{64,32},{96,64},{128,96},{160,128},{192,160},{224,192},{256... | collective-permute-start | bytes 147464 | tf_op jit(solution)/shard_map/ppermute | solution.py:532
  7.9 17.9 %collective-permute-start.1 = (f32[6,16,128]{2,1,0:T(8,128)S(1)}, f32[6,16,128]{2,1,0:T(8,128)S(1)}, u32[]{:S(2)}, u32[]{:S(2)}) collective-permute-start(f32[6,16,128]{2,1,0:T(8,128)S(1)} %get-tuple-element.35), channel_id=1, source_target_pairs={{2,4},{4,2},{6,8},{8,6},{10,12},{12,10},{14,16},{16,14},{18,20},{2... | collective-permute-start | bytes 147464 | tf_op jit(solution)/shard_map/ppermute | solution.py:537
  19.2 6.7 %collective-permute-start.2 = (f32[6,16,128]{2,1,0:T(8,128)S(1)}, f32[6,16,128]{2,1,0:T(8,128)S(1)}, u32[]{:S(2)}, u32[]{:S(2)}) collective-permute-start(f32[6,16,128]{2,1,0:T(8,128)S(1)} %get-tuple-element.36), channel_id=1, source_target_pairs={{0,2},{2,0},{4,6},{6,4},{8,10},{10,8},{12,14},{14,12},{16,18},{18,... | collective-permute-start | bytes 147464 | tf_op jit(solution)/shard_map/ppermute | solution.py:538
  21.1 4.8 %collective-permute-start.3 = (f32[6,16,128]{2,1,0:T(8,128)S(1)}, f32[6,16,128]{2,1,0:T(8,128)S(1)}, u32[]{:S(2)}, u32[]{:S(2)}) collective-permute-start(f32[6,16,128]{2,1,0:T(8,128)S(1)} %get-tuple-element.37), channel_id=1, source_target_pairs={{0,1},{1,0},{2,3},{3,2},{4,5},{5,4},{6,7},{7,6},{8,9},{9,8},{10,11... | collective-permute-start | bytes 147464 | tf_op jit(solution)/shard_map/ppermute | solution.py:539
  27.4 6.3 %collective-permute-start.4 = (f32[248,128]{1,0:T(8,128)S(1)}, f32[248,128]{1,0:T(8,128)S(1)}, u32[]{:S(2)}, u32[]{:S(2)}) collective-permute-start(f32[248,128]{1,0:T(8,128)S(1)} %get-tuple-element.40.mine), channel_id=1, source_target_pairs={{0,32},{32,0},{64,96},{96,64},{128,160},{160,128},{192,224},{224,1... | collective-permute-start | bytes 380936 | tf_op jit(solution)/shard_map/ppermute | solution.py:544
  34.2 10.8 %collective-permute-start.5 = (f32[248,128]{1,0:T(8,128)S(1)}, f32[248,128]{1,0:T(8,128)S(1)}, u32[]{:S(2)}, u32[]{:S(2)}) collective-permute-start(f32[248,128]{1,0:T(8,128)S(1)} %shard_map.81.mine.unused), channel_id=1, source_target_pairs={{0,64},{32,96},{64,0},{96,32},{128,192},{160,224},{192,128},{224,1... | collective-permute-start | bytes 380936 | tf_op jit(solution)/shard_map/ppermute | solution.py:544
  36.9 32.1 %collective-permute-start.10 = (f32[248,128]{1,0:T(8,128)S(1)}, f32[248,128]{1,0:T(8,128)S(1)}, u32[]{:S(2)}, u32[]{:S(2)}) collective-permute-start(f32[248,128]{1,0:T(8,128)S(1)} %shard_map.88), channel_id=1, source_target_pairs={{32,0},{64,32},{96,64},{128,96},{160,128},{192,160},{224,192},{256... | collective-permute-start | bytes 380936 | tf_op jit(solution)/shard_map/ppermute | solution.py:532
  45.3 2.4 %collective-permute-start.6 = (f32[48,128]{1,0:T(8,128)S(1)}, f32[48,128]{1,0:T(8,128)S(1)}, u32[]{:S(2)}, u32[]{:S(2)}) collective-permute-start(f32[48,128]{1,0:T(8,128)S(1)} %shard_map.82.unused), channel_id=1, source_target_pairs={{0,192},{32,224},{64,128},{96,160},{1,193},{33,225},{65,129},{97,1... | collective-permute-start | bytes 73736 | tf_op jit(solution)/shard_map/ppermute | solution.py:549
  46.4 9.3 %collective-permute-start.9 = (f32[248,128]{1,0:T(8,128)S(1)}, f32[248,128]{1,0:T(8,128)S(1)}, u32[]{:S(2)}, u32[]{:S(2)}) collective-permute-start(f32[248,128]{1,0:T(8,128)S(1)} %shard_map.83.packed), channel_id=1, source_target_pairs={{256,448},{288,480},{320,384},{352,416},{257,449},{289,481},{321,3... | collective-permute-start | bytes 380936 | tf_op jit(solution)/shard_map/ppermute | solution.py:549
  48.0 7.7 %copy-start.5 = (f32[3,2,2,16,320]{4,3,2,1,0:T(8,128)S(1)}, f32[3,2,2,16,320]{4,3,2,1,0:T(8,128)}, u32[]{:S(2)}) copy-start(f32[3,2,2,16,320]{4,3,2,1,0:T(8,128)} %param.7) | copy-start | bytes 737284
  48.0 7.7 %collective-permute-start.7 = (f32[48,128]{1,0:T(8,128)S(1)}, f32[48,128]{1,0:T(8,128)S(1)}, u32[]{:S(2)}, u32[]{:S(2)}) collective-permute-start(f32[48,128]{1,0:T(8,128)S(1)} %shard_map.84), channel_id=1, source_target_pairs={{128,320},{160,352},{192,256},{224,288},{129,321},{161,353},{193,2... | collective-permute-start | bytes 73736 | tf_op jit(solution)/shard_map/ppermute | solution.py:549
  49.5 6.3 %collective-permute-start.8 = (f32[48,128]{1,0:T(8,128)S(1)}, f32[48,128]{1,0:T(8,128)S(1)}, u32[]{:S(2)}, u32[]{:S(2)}) collective-permute-start(f32[48,128]{1,0:T(8,128)S(1)} %shard_map.84), channel_id=1, source_target_pairs={{128,384},{160,416},{192,448},{224,480},{129,385},{161,417},{193,4... | collective-permute-start | bytes 73736 | tf_op jit(solution)/shard_map/ppermute | solution.py:549
  57.2 12.6 %collective-permute-start.11 = (f32[6,16,128]{2,1,0:T(8,128)S(1)}, f32[6,16,128]{2,1,0:T(8,128)S(1)}, u32[]{:S(2)}, u32[]{:S(2)}) collective-permute-start(f32[6,16,128]{2,1,0:T(8,128)S(1)} %get-tuple-element.55), channel_id=1, source_target_pairs={{2,4},{4,2},{6,8},{8,6},{10,12},{12,10},{14,16},{16,14},{18,20},{2... | collective-permute-start | bytes 147464 | tf_op jit(solution)/shard_map/ppermute | solution.py:537
  59.1 10.7 %collective-permute-start.12 = (f32[6,16,128]{2,1,0:T(8,128)S(1)}, f32[6,16,128]{2,1,0:T(8,128)S(1)}, u32[]{:S(2)}, u32[]{:S(2)}) collective-permute-start(f32[6,16,128]{2,1,0:T(8,128)S(1)} %get-tuple-element.56), channel_id=1, source_target_pairs={{0,2},{2,0},{4,6},{6,4},{8,10},{10,8},{12,14},{14,12},{16,18},{18,... | collective-permute-start | bytes 147464 | tf_op jit(solution)/shard_map/ppermute | solution.py:538
  63.4 6.5 %collective-permute-start.13 = (f32[6,16,128]{2,1,0:T(8,128)S(1)}, f32[6,16,128]{2,1,0:T(8,128)S(1)}, u32[]{:S(2)}, u32[]{:S(2)}) collective-permute-start(f32[6,16,128]{2,1,0:T(8,128)S(1)} %get-tuple-element.57), channel_id=1, source_target_pairs={{0,1},{1,0},{2,3},{3,2},{4,5},{5,4},{6,7},{7,6},{8,9},{9,8},{10,11... | collective-permute-start | bytes 147464 | tf_op jit(solution)/shard_map/ppermute | solution.py:539

commit v10 on v8

--- a/solution.py
+++ b/solution.py
@@ -317,18 +317,16 @@
 
 
 def source_kernel(
-    ups, rhs, traces, down, from_above, outer, inner, from_across, diag, coupling, lift, passing, composed,
+    ups, rest, from_above, outer, inner, from_across, diag, coupling, lift, passing, composed,
     solved, sources, packed, left, right,
 ):
     ups = ups_of(ups)
     stacks = [
-        near_slots(layer, e, traces, down) | far_slots(layer, e, from_above, outer, inner, from_across)
-        for layer in range(LAYERS)
-        for e in range(PATCH)
+        far_slots(layer, e, from_above, outer, inner, from_across) for layer in range(LAYERS) for e in range(PATCH)
     ]
     outflows = []
     for at, x in enumerate(lift_all(stacks, coupling, lift, left, right)):
-        y = halves(dot(stacked(rhs[at] - x), diag[at]))
+        y = halves(dot(stacked(rest[at] - x), diag[at]))
         solved[at] = y
         outflows.append(face_of(blocks_of(y), 1))
         sources[at] = outflows[at]
@@ -453,6 +451,12 @@
     copy.wait()
 
 
+def near_source_kernel(rhs, traces, down, coupling, lift, out, left, right):
+    stacks = [near_slots(layer, e, traces, down) for layer in range(LAYERS) for e in range(PATCH)]
+    for at, x in enumerate(lift_all(stacks, coupling, lift, left, right)):
+        out[at] = rhs[at] - x
+
+
 def near_residual_kernel(traces, down, leaving, ahead, coupling, lift, out, left, right):
     stacks = [near_slots(layer, e, traces, down) for layer in range(LAYERS) for e in range(PATCH)]
     maps, unused = unpack(ahead[...])
@@ -543,8 +547,9 @@
         [((CELLS, DEEP, ROWS), BF16), ((CELLS, DEEP, LANES), BF16), ((PATCH, TRACE, LANES), F32)],
         [pltpu.VMEM((CELLS, DEEP, LANES), BF16), pltpu.VMEM((PATCH, TRACE, LANES), F32)],
     )(ups, diag, blocks, lift)
+    (rest,) = call(near_source_kernel, [FIELD], FLUXES)(rhs, traces, down, blocks, lift)
     solved, sources, single = call(source_kernel, [FIELD, ((CELLS, VECS, LANES), F32), PACKED], FLUXES)(
-        ups, rhs, traces, down, *halos, diag, blocks, lift, passing, composed
+        ups, rest, *halos, diag, blocks, lift, passing, composed
     )
     partner = swapped(single, 1)
     (pair,) = call(pair_kernel, [PACKED])(single, partner)

time: 72.4 us -> 73.3 us (1.012)
  the two profiles are of different devices: /device:TPU:7 before, /device:TPU:22 now
where the time goes in v10:
time: 73.3 us; the launch traced here: 72.8 us
  starting transfers between devices  46.1 us (63%)
  waiting for transfers between devices  13 us (18%)
  Pallas kernels  11.5 us (16%)
  local copies, waits for them, and re-layouts  1.2 us (2%)
  between operations  0.94 us (1%)
    ppermute x2, starting transfers between devices, exchange_sides(): lax.ppermute(outer, 'cx', [(i, i + 1 if i % 2 else i - 1) for i in range(...  14.3 us
    pallas_call x15, Pallas kernels, run(): pl.pallas_call(kernel, in_specs=[VMEM] * len(args), out_specs=[FAR if i i...  11.5 us
    ppermute x4, starting transfers between devices, passed(): return lax.ppermute(states, 'sweep', pairs)  9.6 us
    ppermute x2, starting transfers between devices, swapped(): lax.ppermute(packed, 'sweep', [(i, i ^ by) for i in range(lax.axis_size('...  8.72 us
    ppermute x2, waiting for transfers between devices, swapped(): lax.ppermute(packed, 'sweep', [(i, i ^ by) for i in range(lax.axis_size('...  6.86 us
    ppermute x2, starting transfers between devices, exchange_sides(): inner = lax.ppermute(inner, 'cx', [(i, i ^ 1) for i in range(wide)])  5.25 us
    ppermute x4, waiting for transfers between devices, passed(): return lax.ppermute(states, 'sweep', pairs)  5.07 us
    ppermute x2, starting transfers between devices, from_next(): lax.ppermute(piece, 'sweep', [(i + 1, i) for i in range(lax.axis_size('sw...  4.41 us
  transfers between devices with their start and end apart: 14, of which 4 were waited for; matrix products, arithmetic and copies ran while one was open for 0% of the time, Pallas kernels for 11%

profile of v10, /device:TPU:22, one launch (start us, length us, event | category | flops | bytes accessed | tf_op | source)
XLA Modules:
  0.0 72.8 jit_solution(7600187594970652989)
XLA Ops:
  0.6 1.0 %copy-done.4 = f32[3,2,2,16,320]{4,3,2,1,0:T(8,128)S(1)} copy-done((f32[3,2,2,16,320]{4,3,2,1,0:T(8,128)S(1)}, f32[3,2,2,16,320]{4,3,2,1,0:T(8,128)}, u32[]{:S(2)}) %copy-start.4) | copy-done | bytes 245784
  1.6 0.4 shard_map.77
  2.4 2.5 %collective-permute-start = (f32[6,16,128]{2,1,0:T(8,128)S(1)}, f32[6,16,128]{2,1,0:T(8,128)S(1)}, u32[]{:S(2)}, u32[]{:S(2)}) collective-permute-start(f32[6,16,128]{2,1,0:T(8,128)S(1)} %get-tuple-element.34.below), channel_id=1, source_target_pairs={{32,0},{64,32},{96,64},{128,96},{160,128},{192,160},{224,192},{256... | collective-permute-start | bytes 147464 | tf_op jit(solution)/shard_map/ppermute | solution.py:514
  4.9 11.8 %collective-permute-start.1 = (f32[6,16,128]{2,1,0:T(8,128)S(1)}, f32[6,16,128]{2,1,0:T(8,128)S(1)}, u32[]{:S(2)}, u32[]{:S(2)}) collective-permute-start(f32[6,16,128]{2,1,0:T(8,128)S(1)} %get-tuple-element.35), channel_id=1, source_target_pairs={{2,4},{4,2},{6,8},{8,6},{10,12},{12,10},{14,16},{16,14},{18,20},{2... | collective-permute-start | bytes 147464 | tf_op jit(solution)/shard_map/ppermute | solution.py:519
  16.7 1.9 %collective-permute-start.2 = (f32[6,16,128]{2,1,0:T(8,128)S(1)}, f32[6,16,128]{2,1,0:T(8,128)S(1)}, u32[]{:S(2)}, u32[]{:S(2)}) collective-permute-start(f32[6,16,128]{2,1,0:T(8,128)S(1)} %get-tuple-element.36), channel_id=1, source_target_pairs={{0,2},{2,0},{4,6},{6,4},{8,10},{10,8},{12,14},{14,12},{16,18},{18,... | collective-permute-start | bytes 147464 | tf_op jit(solution)/shard_map/ppermute | solution.py:520
  18.7 1.9 %collective-permute-start.3 = (f32[6,16,128]{2,1,0:T(8,128)S(1)}, f32[6,16,128]{2,1,0:T(8,128)S(1)}, u32[]{:S(2)}, u32[]{:S(2)}) collective-permute-start(f32[6,16,128]{2,1,0:T(8,128)S(1)} %get-tuple-element.37), channel_id=1, source_target_pairs={{0,1},{1,0},{2,3},{3,2},{4,5},{5,4},{6,7},{7,6},{8,9},{9,8},{10,11... | collective-permute-start | bytes 147464 | tf_op jit(solution)/shard_map/ppermute | solution.py:521
  20.6 1.5 %shard_map.80 = (bf16[12,256,320]{2,1,0:T(8,128)(2,1)S(1)}, bf16[12,256,128]{2,1,0:T(8,128)(2,1)S(1)}, f32[4,80,128]{2,1,0:T(8,128)S(1)}) custom-call(f32[16,128]{1,0:T(8,128)S(1)} %get-tuple-element.31.ups, bf16[12,320,320]{2,1,0:T(8,128)(2,1)S(1)} %bitcast.8, bf16[12,80,480]{2,1,0:T(8,128)(2,1)S(1)} %bitcast.10, bf16[320,480]{1,0:T(8,128)(2,1)S(1)} %bitcast.16), custom_call_target="tpu_custom_call" | custom-call | flops 1000000000 | bytes 3600000 | tf_op jit(solution)/shard_map/pallas_call | solution.py:483
  22.2 0.6 shard_map.79.rest
  22.9 1.4 %shard_map.81 = (f32[12,16,320]{2,1,0:T(8,128)S(1)}, f32[12,16,128]{2,1,0:T(8,128)S(1)}, f32[248,128]{1,0:T(8,128)S(1)}) custom-call(f32[16,128]{1,0:T(8,128)S(1)} %get-tuple-element.31.ups, f32[12,16,320]{2,1,0:T(8,128)S(1)} %shard_map.79.rest, f32[6,16,128]{2,1,0:T(8,128)S(1)} %collective-permute-done.from_above, ...), custom_call_target="tpu_custom_call" | custom-call | flops 1000000000 | bytes 3600000 | tf_op jit(solution)/shard_map/pallas_call | solution.py:483
  24.2 3.5 %collective-permute-start.4 = (f32[248,128]{1,0:T(8,128)S(1)}, f32[248,128]{1,0:T(8,128)S(1)}, u32[]{:S(2)}, u32[]{:S(2)}) collective-permute-start(f32[248,128]{1,0:T(8,128)S(1)} %get-tuple-element.40.mine), channel_id=1, source_target_pairs={{0,32},{32,0},{64,96},{96,64},{128,160},{160,128},{192,224},{224,1... | collective-permute-start | bytes 380936 | tf_op jit(solution)/shard_map/ppermute | solution.py:526
  27.7 4.2 %collective-permute-done.4.theirs.pair = f32[248,128]{1,0:T(8,128)S(1)} collective-permute-done((f32[248,128]{1,0:T(8,128)S(1)}, f32[248,128]{1,0:T(8,128)S(1)}, u32[]{:S(2)}, u32[]{:S(2)}) %collective-permute-start.4) | collective-permute-done | bytes 127008 | tf_op jit(solution)/shard_map/ppermute | solution.py:526
  32.0 0.4 shard_map.82.mine.unused
  32.4 5.2 %collective-permute-start.5 = (f32[248,128]{1,0:T(8,128)S(1)}, f32[248,128]{1,0:T(8,128)S(1)}, u32[]{:S(2)}, u32[]{:S(2)}) collective-permute-start(f32[248,128]{1,0:T(8,128)S(1)} %shard_map.82.mine.unused), channel_id=1, source_target_pairs={{0,64},{32,96},{64,0},{96,32},{128,192},{160,224},{192,128},{224,1... | collective-permute-start | bytes 380936 | tf_op jit(solution)/shard_map/ppermute | solution.py:526
  37.6 0.5 shard_map.86
  38.4 1.9 %collective-permute-start.10 = (f32[248,128]{1,0:T(8,128)S(1)}, f32[248,128]{1,0:T(8,128)S(1)}, u32[]{:S(2)}, u32[]{:S(2)}) collective-permute-start(f32[248,128]{1,0:T(8,128)S(1)} %shard_map.89), channel_id=1, source_target_pairs={{32,0},{64,32},{96,64},{128,96},{160,128},{192,160},{224,192},{256... | collective-permute-start | bytes 380936 | tf_op jit(solution)/shard_map/ppermute | solution.py:514
  40.3 2.6 %collective-permute-done.5.theirs = f32[248,128]{1,0:T(8,128)S(1)} collective-permute-done((f32[248,128]{1,0:T(8,128)S(1)}, f32[248,128]{1,0:T(8,128)S(1)}, u32[]{:S(2)}, u32[]{:S(2)}) %collective-permute-start.5) | collective-permute-done | bytes 127008 | tf_op jit(solution)/shard_map/ppermute | solution.py:526
  43.0 0.3 shard_map.83.unused
  43.3 0.7 collective-permute-start.6
  44.0 0.4 shard_map.84.packed
  44.4 6.8 %collective-permute-start.9 = (f32[248,128]{1,0:T(8,128)S(1)}, f32[248,128]{1,0:T(8,128)S(1)}, u32[]{:S(2)}, u32[]{:S(2)}) collective-permute-start(f32[248,128]{1,0:T(8,128)S(1)} %shard_map.84.packed), channel_id=1, source_target_pairs={{256,448},{288,480},{320,384},{352,416},{257,449},{289,481},{321,3... | collective-permute-start | bytes 380936 | tf_op jit(solution)/shard_map/ppermute | solution.py:531
  51.3 0.3 shard_map.85
  51.6 1.4 %collective-permute-start.7 = (f32[48,128]{1,0:T(8,128)S(1)}, f32[48,128]{1,0:T(8,128)S(1)}, u32[]{:S(2)}, u32[]{:S(2)}) collective-permute-start(f32[48,128]{1,0:T(8,128)S(1)} %shard_map.85), channel_id=1, source_target_pairs={{128,320},{160,352},{192,256},{224,288},{129,321},{161,353},{193,2... | collective-permute-start | bytes 73736 | tf_op jit(solution)/shard_map/ppermute | solution.py:531
  53.0 0.7 collective-permute-start.8
  53.7 1.7 %shard_map.87 = (bf16[12,256,320]{2,1,0:T(8,128)(2,1)S(1)}, f32[12,16,320]{2,1,0:T(8,128)S(1)}, bf16[4,256,128]{2,1,0:T(8,128)(2,1)S(1)}, f32[4,16,128]{2,1,0:T(8,128)S(1)}, f32[16,128]{1,0:T(8,128)S(1)}) custom-call(f32[248,128]{1,0:T(8,128)S(1)} %collective-permute-done.4.theirs.pair, f32[248,128]{1,0:T(8,128)S(1)} %collective-permute-done.5.theirs, ...), custom_call_target="tpu_custom_call" | custom-call | flops 1000000000 | bytes 3600000 | tf_op jit(solution)/shard_map/pallas_call | solution.py:483
  55.4 5.1 %collective-permute-done.7.third = f32[48,128]{1,0:T(8,128)S(1)} collective-permute-done((f32[48,128]{1,0:T(8,128)S(1)}, f32[48,128]{1,0:T(8,128)S(1)}, u32[]{:S(2)}, u32[]{:S(2)}) %collective-permute-start.7) | collective-permute-done | bytes 24608 | tf_op jit(solution)/shard_map/ppermute | solution.py:531
  60.5 1.4 %shard_map.88 = (f32[12,16,320]{2,1,0:T(8,128)}, bf16[12,32,512]{2,1,0:T(8,128)(2,1)S(1)}, f32[6,16,128]{2,1,0:T(8,128)S(1)}, f32[6,16,128]{2,1,0:T(8,128)S(1)},...) custom-call(f32[16,128]{1,0:T(8,128)S(1)} %get-tuple-element.31.ups, ...), custom_call_target="tpu_custom_call" | custom-call | flops 1000000000 | bytes 3600000 | tf_op jit(solution)/shard_map/pallas_call | solution.py:483
  61.9 2.5 %collective-permute-start.11 = (f32[6,16,128]{2,1,0:T(8,128)S(1)}, f32[6,16,128]{2,1,0:T(8,128)S(1)}, u32[]{:S(2)}, u32[]{:S(2)}) collective-permute-start(f32[6,16,128]{2,1,0:T(8,128)S(1)} %get-tuple-element.55), channel_id=1, source_target_pairs={{2,4},{4,2},{6,8},{8,6},{10,12},{12,10},{14,16},{16,14},{18,20},{2... | collective-permute-start | bytes 147464 | tf_op jit(solution)/shard_map/ppermute | solution.py:519
  64.4 3.3 %collective-permute-start.12 = (f32[6,16,128]{2,1,0:T(8,128)S(1)}, f32[6,16,128]{2,1,0:T(8,128)S(1)}, u32[]{:S(2)}, u32[]{:S(2)}) collective-permute-start(f32[6,16,128]{2,1,0:T(8,128)S(1)} %get-tuple-element.56), channel_id=1, source_target_pairs={{0,2},{2,0},{4,6},{6,4},{8,10},{10,8},{12,14},{14,12},{16,18},{18,... | collective-permute-start | bytes 147464 | tf_op jit(solution)/shard_map/ppermute | solution.py:520
  67.7 1.9 %collective-permute-start.13 = (f32[6,16,128]{2,1,0:T(8,128)S(1)}, f32[6,16,128]{2,1,0:T(8,128)S(1)}, u32[]{:S(2)}, u32[]{:S(2)}) collective-permute-start(f32[6,16,128]{2,1,0:T(8,128)S(1)} %get-tuple-element.57), channel_id=1, source_target_pairs={{0,1},{1,0},{2,3},{3,2},{4,5},{5,4},{6,7},{7,6},{8,9},{9,8},{10,11... | collective-permute-start | bytes 147464 | tf_op jit(solution)/shard_map/ppermute | solution.py:521
  69.7 0.7 %shard_map.90.near = f32[12,16,320]{2,1,0:T(8,128)S(1)} custom-call(bf16[12,32,512]{2,1,0:T(8,128)(2,1)S(1)} %get-tuple-element.51.traces, bf16[8,32,128]{2,1,0:T(8,128)(2,1)S(1)} %get-tuple-element.52.down, f32[4,16,128]{2,1,0:T(8,128)S(1)} %get-tuple-element.53.leaving, f32[248,128]{1,0:T(8,128)S(1)} %collective-permute-done.10.ahead, ...), custom_call_target="tpu_custom_call" | custom-call | flops 1000000000 | bytes 3600000 | tf_op jit(solution)/shard_map/pallas_call | solution.py:483
  70.4 1.1 %collective-permute-done.11.outer = f32[6,16,128]{2,1,0:T(8,128)S(1)} collective-permute-done((f32[6,16,128]{2,1,0:T(8,128)S(1)}, f32[6,16,128]{2,1,0:T(8,128)S(1)}, u32[]{:S(2)}, u32[]{:S(2)}) %collective-permute-start.11) | collective-permute-done | bytes 49184 | tf_op jit(solution)/shard_map/ppermute | solution.py:519
  71.5 1.3 %shard_map.91 = f32[12,16,320]{2,1,0:T(8,128)} custom-call(f32[12,16,320]{2,1,0:T(8,128)S(1)} %shard_map.90.near, f32[6,16,128]{2,1,0:T(8,128)S(1)} %collective-permute-done.11.outer, f32[6,16,128]{2,1,0:T(8,128)S(1)} %collective-permute-done.12.inner, f32[6,16,128]{2,1,0:T(8,128)S(1)} %collective-permute-done.13.from_across, ...), custom_call_target="tpu_custom_call" | custom-call | flops 1000000000 | bytes 3600000 | tf_op jit(solution)/shard_map/pallas_call | solution.py:483
  (25 shorter events, 0.6 us)
Async XLA Ops:
  0.6 1.0 %copy-start.4 = (f32[3,2,2,16,320]{4,3,2,1,0:T(8,128)S(1)}, f32[3,2,2,16,320]{4,3,2,1,0:T(8,128)}, u32[]{:S(2)}) copy-start(f32[3,2,2,16,320]{4,3,2,1,0:T(8,128)} %param.7) | copy-start | bytes 737284
  1.6 0.7 copy-start.6
  1.6 19.0 %copy-start.1 = (bf16[3,2,2,80,480]{4,3,2,1,0:T(8,128)(2,1)S(1)}, bf16[3,2,2,80,480]{4,3,2,1,0:T(8,128)(2,1)}, u32[]{:S(2)}) copy-start(bf16[3,2,2,80,480]{4,3,2,1,0:T(8,128)(2,1)} %param.9) | copy-start | bytes 2764804
  2.0 18.6 %copy-start = (bf16[3,2,2,320,320]{4,3,2,1,0:T(8,128)(2,1)S(1)}, bf16[3,2,2,320,320]{4,3,2,1,0:T(8,128)(2,1)}, u32[]{:S(2)}) copy-start(bf16[3,2,2,320,320]{4,3,2,1,0:T(8,128)(2,1)} %param.8) | copy-start | bytes 7372804
  2.1 18.6 %copy-start.2 = (bf16[480,320]{0,1:T(8,128)(2,1)S(1)}, bf16[480,320]{0,1:T(8,128)(2,1)}, u32[]{:S(2)}) copy-start(bf16[480,320]{0,1:T(8,128)(2,1)} %param.10) | copy-start | bytes 921604
  2.4 19.7 %copy-start.3 = (f32[3,2,2,16,320]{4,3,2,1,0:T(8,128)S(1)}, f32[3,2,2,16,320]{4,3,2,1,0:T(8,128)}, u32[]{:S(2)}) copy-start(f32[3,2,2,16,320]{4,3,2,1,0:T(8,128)} %param.6) | copy-start | bytes 737284
  2.4 20.4 %collective-permute-start = (f32[6,16,128]{2,1,0:T(8,128)S(1)}, f32[6,16,128]{2,1,0:T(8,128)S(1)}, u32[]{:S(2)}, u32[]{:S(2)}) collective-permute-start(f32[6,16,128]{2,1,0:T(8,128)S(1)} %get-tuple-element.34.below), channel_id=1, source_target_pairs={{32,0},{64,32},{96,64},{128,96},{160,128},{192,160},{224,192},{256... | collective-permute-start | bytes 147464 | tf_op jit(solution)/shard_map/ppermute | solution.py:514
  4.9 17.9 %collective-permute-start.1 = (f32[6,16,128]{2,1,0:T(8,128)S(1)}, f32[6,16,128]{2,1,0:T(8,128)S(1)}, u32[]{:S(2)}, u32[]{:S(2)}) collective-permute-start(f32[6,16,128]{2,1,0:T(8,128)S(1)} %get-tuple-element.35), channel_id=1, source_target_pairs={{2,4},{4,2},{6,8},{8,6},{10,12},{12,10},{14,16},{16,14},{18,20},{2... | collective-permute-start | bytes 147464 | tf_op jit(solution)/shard_map/ppermute | solution.py:519
  16.7 6.1 %collective-permute-start.2 = (f32[6,16,128]{2,1,0:T(8,128)S(1)}, f32[6,16,128]{2,1,0:T(8,128)S(1)}, u32[]{:S(2)}, u32[]{:S(2)}) collective-permute-start(f32[6,16,128]{2,1,0:T(8,128)S(1)} %get-tuple-element.36), channel_id=1, source_target_pairs={{0,2},{2,0},{4,6},{6,4},{8,10},{10,8},{12,14},{14,12},{16,18},{18,... | collective-permute-start | bytes 147464 | tf_op jit(solution)/shard_map/ppermute | solution.py:520
  18.7 4.2 %collective-permute-start.3 = (f32[6,16,128]{2,1,0:T(8,128)S(1)}, f32[6,16,128]{2,1,0:T(8,128)S(1)}, u32[]{:S(2)}, u32[]{:S(2)}) collective-permute-start(f32[6,16,128]{2,1,0:T(8,128)S(1)} %get-tuple-element.37), channel_id=1, source_target_pairs={{0,1},{1,0},{2,3},{3,2},{4,5},{5,4},{6,7},{7,6},{8,9},{9,8},{10,11... | collective-permute-start | bytes 147464 | tf_op jit(solution)/shard_map/ppermute | solution.py:521
  24.2 7.7 %collective-permute-start.4 = (f32[248,128]{1,0:T(8,128)S(1)}, f32[248,128]{1,0:T(8,128)S(1)}, u32[]{:S(2)}, u32[]{:S(2)}) collective-permute-start(f32[248,128]{1,0:T(8,128)S(1)} %get-tuple-element.40.mine), channel_id=1, source_target_pairs={{0,32},{32,0},{64,96},{96,64},{128,160},{160,128},{192,224},{224,1... | collective-permute-start | bytes 380936 | tf_op jit(solution)/shard_map/ppermute | solution.py:526
  32.4 10.6 %collective-permute-start.5 = (f32[248,128]{1,0:T(8,128)S(1)}, f32[248,128]{1,0:T(8,128)S(1)}, u32[]{:S(2)}, u32[]{:S(2)}) collective-permute-start(f32[248,128]{1,0:T(8,128)S(1)} %shard_map.82.mine.unused), channel_id=1, source_target_pairs={{0,64},{32,96},{64,0},{96,32},{128,192},{160,224},{192,128},{224,1... | collective-permute-start | bytes 380936 | tf_op jit(solution)/shard_map/ppermute | solution.py:526
  38.4 31.3 %collective-permute-start.10 = (f32[248,128]{1,0:T(8,128)S(1)}, f32[248,128]{1,0:T(8,128)S(1)}, u32[]{:S(2)}, u32[]{:S(2)}) collective-permute-start(f32[248,128]{1,0:T(8,128)S(1)} %shard_map.89), channel_id=1, source_target_pairs={{32,0},{64,32},{96,64},{128,96},{160,128},{192,160},{224,192},{256... | collective-permute-start | bytes 380936 | tf_op jit(solution)/shard_map/ppermute | solution.py:514
  43.3 8.0 %collective-permute-start.6 = (f32[48,128]{1,0:T(8,128)S(1)}, f32[48,128]{1,0:T(8,128)S(1)}, u32[]{:S(2)}, u32[]{:S(2)}) collective-permute-start(f32[48,128]{1,0:T(8,128)S(1)} %shard_map.83.unused), channel_id=1, source_target_pairs={{0,192},{32,224},{64,128},{96,160},{1,193},{33,225},{65,129},{97,1... | collective-permute-start | bytes 73736 | tf_op jit(solution)/shard_map/ppermute | solution.py:531
  44.4 16.0 %collective-permute-start.9 = (f32[248,128]{1,0:T(8,128)S(1)}, f32[248,128]{1,0:T(8,128)S(1)}, u32[]{:S(2)}, u32[]{:S(2)}) collective-permute-start(f32[248,128]{1,0:T(8,128)S(1)} %shard_map.84.packed), channel_id=1, source_target_pairs={{256,448},{288,480},{320,384},{352,416},{257,449},{289,481},{321,3... | collective-permute-start | bytes 380936 | tf_op jit(solution)/shard_map/ppermute | solution.py:531
  51.6 8.9 %copy-start.5 = (f32[3,2,2,16,320]{4,3,2,1,0:T(8,128)S(1)}, f32[3,2,2,16,320]{4,3,2,1,0:T(8,128)}, u32[]{:S(2)}) copy-start(f32[3,2,2,16,320]{4,3,2,1,0:T(8,128)} %param.7) | copy-start | bytes 737284
  51.6 8.9 %collective-permute-start.7 = (f32[48,128]{1,0:T(8,128)S(1)}, f32[48,128]{1,0:T(8,128)S(1)}, u32[]{:S(2)}, u32[]{:S(2)}) collective-permute-start(f32[48,128]{1,0:T(8,128)S(1)} %shard_map.85), channel_id=1, source_target_pairs={{128,320},{160,352},{192,256},{224,288},{129,321},{161,353},{193,2... | collective-permute-start | bytes 73736 | tf_op jit(solution)/shard_map/ppermute | solution.py:531
  53.0 7.4 %collective-permute-start.8 = (f32[48,128]{1,0:T(8,128)S(1)}, f32[48,128]{1,0:T(8,128)S(1)}, u32[]{:S(2)}, u32[]{:S(2)}) collective-permute-start(f32[48,128]{1,0:T(8,128)S(1)} %shard_map.85), channel_id=1, source_target_pairs={{128,384},{160,416},{192,448},{224,480},{129,385},{161,417},{193,4... | collective-permute-start | bytes 73736 | tf_op jit(solution)/shard_map/ppermute | solution.py:531
  61.9 9.6 %collective-permute-start.11 = (f32[6,16,128]{2,1,0:T(8,128)S(1)}, f32[6,16,128]{2,1,0:T(8,128)S(1)}, u32[]{:S(2)}, u32[]{:S(2)}) collective-permute-start(f32[6,16,128]{2,1,0:T(8,128)S(1)} %get-tuple-element.55), channel_id=1, source_target_pairs={{2,4},{4,2},{6,8},{8,6},{10,12},{12,10},{14,16},{16,14},{18,20},{2... | collective-permute-start | bytes 147464 | tf_op jit(solution)/shard_map/ppermute | solution.py:519
  64.4 7.1 %collective-permute-start.12 = (f32[6,16,128]{2,1,0:T(8,128)S(1)}, f32[6,16,128]{2,1,0:T(8,128)S(1)}, u32[]{:S(2)}, u32[]{:S(2)}) collective-permute-start(f32[6,16,128]{2,1,0:T(8,128)S(1)} %get-tuple-element.56), channel_id=1, source_target_pairs={{0,2},{2,0},{4,6},{6,4},{8,10},{10,8},{12,14},{14,12},{16,18},{18,... | collective-permute-start | bytes 147464 | tf_op jit(solution)/shard_map/ppermute | solution.py:520
  67.7 3.8 %collective-permute-start.13 = (f32[6,16,128]{2,1,0:T(8,128)S(1)}, f32[6,16,128]{2,1,0:T(8,128)S(1)}, u32[]{:S(2)}, u32[]{:S(2)}) collective-permute-start(f32[6,16,128]{2,1,0:T(8,128)S(1)} %get-tuple-element.57), channel_id=1, source_target_pairs={{0,1},{1,0},{2,3},{3,2},{4,5},{5,4},{6,7},{7,6},{8,9},{9,8},{10,11... | collective-permute-start | bytes 147464 | tf_op jit(solution)/shard_map/ppermute | solution.py:521
